TPU v7x, 32 devices: a whole 2x2x4 slice. The times are simulated.
32 devices in a mesh: blk: 8 (over z, x), head: 4 (over y, core).
Axes of the slice: x: 2, y: 2, z: 4, core: 2. Of those that a mesh axis runs over, the one named last changes fastest.
Arguments:
- inward: float32 [3, 2048, 2048], P(None, 'blk', 'head'), may hold values from -0.125 to 0.125
- outward: float32 [2048, 2048], P('head', 'blk'), may hold values from -6 to 6
- expand: float32 [2048, 8192], P('blk', 'head'), may hold values from -0.125 to 0.125
- contract: float32 [8192, 2048], P('head', 'blk'), may hold values from -0.0625 to 0.0625
- image_table: float32 [8192, 2048], P('blk', 'head'), may hold values from -0.75 to 0.75
- code_table: float32 [1280, 2048], P('blk', 'head'), may hold values from -0.75 to 0.75
- readout: float32 [2048, 8192], P('blk', 'head')
- gains: float32 [3, 2048], P(None, 'blk'), may hold values from 0.5 to 1.5
- inward_first: float32 [3, 2048, 2048], P(None, 'blk', 'head'), may hold values from -6.67572e-06 to 6.67572e-06
- outward_first: float32 [2048, 2048], P('head', 'blk'), may hold values from -3.5762787e-07 to 3.5762787e-07
- expand_first: float32 [2048, 8192], P('blk', 'head'), may hold values from -1.4305115e-06 to 1.4305115e-06
- contract_first: float32 [8192, 2048], P('head', 'blk'), may hold values from -1.4305115e-06 to 1.4305115e-06
- image_first: float32 [8192, 2048], P('blk', 'head'), may hold values from -3.33786e-06 to 3.33786e-06
- code_first: float32 [1280, 2048], P('blk', 'head'), may hold values from -4.7683716e-06 to 4.7683716e-06
- readout_first: float32 [2048, 8192], P('blk', 'head'), may hold values from -3.8146973e-06 to 3.8146973e-06
- gains_first: float32 [3, 2048], P(None, 'blk'), may hold values from -1.335144e-05 to 1.335144e-05
- inward_second: float32 [3, 2048, 2048], P(None, 'blk', 'head'), may hold values from 8.1857047e-13 to 3.2742819e-12
- outward_second: float32 [2048, 2048], P('head', 'blk'), may hold values from 2.4318695e-15 to 9.7036365e-15
- expand_second: float32 [2048, 8192], P('blk', 'head'), may hold values from 4.053116e-14 to 1.6212464e-13
- contract_second: float32 [8192, 2048], P('head', 'blk'), may hold values from 3.618002e-14 to 1.4483929e-13
- image_second: float32 [8192, 2048], P('blk', 'head'), may hold values from 2.002716e-13 to 8.010864e-13
- code_second: float32 [1280, 2048], P('blk', 'head'), may hold values from 4.997253e-13 to 2.0027161e-12
- readout_second: float32 [2048, 8192], P('blk', 'head'), may hold values from 3.1292438e-13 to 1.2516975e-12
- gains_second: float32 [3, 2048], P(None, 'blk'), may hold values from 3.076172e-12 to 1.2304688e-11
- token_ids: int32 [2, 2048], P(None, 'blk'), may hold values from 0 to 8191, as said below
- modality: int32 [2, 2048], P(None, 'blk'), may hold values from 0 to 2
- clip_lengths: int32 [2], replicated, may hold values from 1024 to 2048, as said below
- loss_mask: int32 [2, 2048], P(None, 'blk'), may hold values from 0 to 1
- targets: int32 [2, 2048], P(None, 'blk'), may hold values from 0 to 8191
Outputs:
- inward_next: float32 [3, 2048, 2048], P(None, 'blk', 'head')
- inward_first_next: float32 [3, 2048, 2048], P(None, 'blk', 'head')
- inward_second_next: float32 [3, 2048, 2048], P(None, 'blk', 'head')
- outward_next: float32 [2048, 2048], P('head', 'blk')
- outward_first_next: float32 [2048, 2048], P('head', 'blk')
- outward_second_next: float32 [2048, 2048], P('head', 'blk')
- expand_next: float32 [2048, 8192], P('blk', 'head')
- expand_first_next: float32 [2048, 8192], P('blk', 'head')
- expand_second_next: float32 [2048, 8192], P('blk', 'head')
- contract_next: float32 [8192, 2048], P('head', 'blk')
- contract_first_next: float32 [8192, 2048], P('head', 'blk')
- contract_second_next: float32 [8192, 2048], P('head', 'blk')
- image_next: float32 [8192, 2048], P('blk', 'head')
- image_first_next: float32 [8192, 2048], P('blk', 'head')
- image_second_next: float32 [8192, 2048], P('blk', 'head')
- code_next: float32 [1280, 2048], P('blk', 'head')
- code_first_next: float32 [1280, 2048], P('blk', 'head')
- code_second_next: float32 [1280, 2048], P('blk', 'head')
- readout_next: float32 [2048, 8192], P('blk', 'head')
- readout_first_next: float32 [2048, 8192], P('blk', 'head')
- readout_second_next: float32 [2048, 8192], P('blk', 'head')
- gains_next: float32 [3, 2048], P(None, 'blk')
- gains_first_next: float32 [3, 2048], P(None, 'blk')
- gains_second_next: float32 [3, 2048], P(None, 'blk')
- loss_sum: float32 [], replicated
- loss_count: float32 [], replicated
- grad_norm: float32 [], replicated
Inputs may be any that keep to these rules, and one draw needn't show every extreme that they name: `token_ids`: ids are below 8192 at image positions, below 1024 at text positions and below 256 at action positions. `clip_lengths`: at least one clip uses all 2048 positions.
All inputs are finite; a program needn't handle non-finite values.
Results may differ from a plain program's by a relative error of at most 0.03.
Values may be sent and summed in bfloat16 or wider, within the bound.
No kernel may reach another device: no remote copies, remote signals or barrier semaphores. Data moves between devices by JAX's collectives and lax.ppermute only.
A program may use at most 256 MiB of HBM per device.

v0:
```python
import jax
import jax.numpy as jnp
from jax import lax
from jax.sharding import PartitionSpec as P

D = 2048
HD = 128
FF = 8192
VT = 1024
VA = 256
STEP = 10


EPS = 1e-05
ZCOEF = 0.01
CLIP = 0.02
BETA1 = 0.9
BETA2 = 0.95
ADAM_EPS = 1e-08
DECAY = 0.1
RATE_FACTOR = 1.5
GAIN_RATE = 0.8


def passed_along(value, axis, steps):
    count = lax.axis_size(axis)
    pairs = [(source, (source + steps) % count) for source in range(count)]
    return lax.ppermute(value, axis, pairs)


def from_behind(block, axis, distance):
    devices = range(lax.axis_size(axis))
    route = [(i - distance, i) for i in devices if i - distance in devices]
    return lax.ppermute(block, axis, route)


def combined_all(array, axis, combine):
    everything = jax.tree.map(lambda part: lax.all_gather(part, axis), array)
    leading = jax.tree.map(lambda part: part[0], everything)

    def turn(k, so_far):
        return combine(so_far, jax.tree.map(lambda part: part[k], everything))

    return lax.fori_loop(1, lax.axis_size(axis), turn, leading)


def rms_norm(hidden, gain):
    return hidden * lax.rsqrt(jnp.mean(hidden * hidden, axis=-1, keepdims=True) + EPS) * gain


def norm_back(hidden, gain, upstream):
    unused, pullback = jax.vjp(rms_norm, hidden, gain)
    return pullback(upstream)


def head_sum(partial_sum):
    return lax.psum(partial_sum.astype(jnp.bfloat16), "head").astype(jnp.float32)


def pass_grads(grad_keys, grad_values):
    return (
        passed_along(grad_keys.astype(jnp.bfloat16), "blk", 1).astype(grad_keys.dtype),
        passed_along(grad_values.astype(jnp.bfloat16), "blk", 1).astype(grad_values.dtype),
    )


def score_block(queries, keys_in):
    return HD ** (-0.5) * jnp.einsum(
        "cqhd,ckhd->chqk", queries, keys_in, preferred_element_type=jnp.float32
    )


def visible(query_pos, key_pos):
    return (key_pos[None, :] <= query_pos[:, None]) & (key_pos[None, :] >= 0)


def attend(queries, keys_in, values_in, query_pos, key_pos, running):
    top_now, total_now, summed = running
    seen = visible(query_pos, key_pos)
    scores = jnp.where(seen, score_block(queries, keys_in), -1e30)
    top_next = jnp.maximum(top_now, jnp.max(scores, axis=-1))
    weights = jnp.where(seen, jnp.exp(scores - top_next[..., None]), 0.0)
    fading = jnp.exp(top_now - top_next)
    total_next = total_now * fading + jnp.sum(weights, axis=-1)
    summed = summed * fading[..., None] + jnp.einsum(
        "chqk,ckhd->chqd",
        weights.astype(jnp.bfloat16),
        values_in,
        preferred_element_type=jnp.float32,
    )
    return (top_next, total_next, summed)


def attend_back(queries, keys_in, values_in, query_pos, key_pos, grad_out, log_total, inner):
    seen = visible(query_pos, key_pos)
    probs = jnp.where(seen, jnp.exp(score_block(queries, keys_in) - log_total[..., None]), 0.0)
    grad_values = jnp.einsum(
        "chqk,cqhd->ckhd", probs.astype(jnp.bfloat16), grad_out, preferred_element_type=jnp.float32
    )
    grad_probs = jnp.einsum(
        "cqhd,ckhd->chqk", grad_out, values_in, preferred_element_type=jnp.float32
    )
    grad_scores = (probs * (grad_probs - inner[..., None])).astype(jnp.bfloat16)
    grad_query = HD ** (-0.5) * jnp.einsum(
        "chqk,ckhd->cqhd", grad_scores, keys_in, preferred_element_type=jnp.float32
    )
    grad_keys = HD ** (-0.5) * jnp.einsum(
        "chqk,cqhd->ckhd", grad_scores, queries, preferred_element_type=jnp.float32
    )
    return (grad_query, grad_keys, grad_values)


def combine_vocab(left, right):
    top_both = jnp.maximum(left[0], right[0])
    total = left[1] * jnp.exp(left[0] - top_both) + right[1] * jnp.exp(right[0] - top_both)
    return (top_both, total)


def adamw(weight, first, second, grad, rate, decay):
    first = BETA1 * first + (1.0 - BETA1) * grad
    second = BETA2 * second + (1.0 - BETA2) * grad * grad
    first_hat = first / (1.0 - BETA1**STEP)
    second_hat = second / (1.0 - BETA2**STEP)
    weight = weight - rate * (first_hat / (jnp.sqrt(second_hat) + ADAM_EPS) + decay * weight)
    return (weight, first, second)


def shards(
    inward,
    outward,
    expand,
    contract,
    image_table,
    code_table,
    readout,
    gains,
    inward_first,
    outward_first,
    expand_first,
    contract_first,
    image_first,
    code_first,
    readout_first,
    gains_first,
    inward_second,
    outward_second,
    expand_second,
    contract_second,
    image_second,
    code_second,
    readout_second,
    gains_second,
    token_ids,
    modality,
    clip_lengths,
    loss_mask,
    targets,
):
    blocks_total = lax.axis_size("blk")
    blk_place = lax.axis_index("blk")
    head_place = lax.axis_index("head")
    clips, span = token_ids.shape
    half = jnp.bfloat16
    w_in, w_out, w_up, w_down, table_img, table_code, w_read = (
        lax.all_gather(inward.astype(half), "blk", axis=1, tiled=True),
        lax.all_gather(outward.astype(half), "blk", axis=1, tiled=True),
        lax.all_gather(expand.astype(half), "blk", axis=0, tiled=True),
        lax.all_gather(contract.astype(half), "blk", axis=1, tiled=True),
        lax.all_gather(image_table.astype(half), "blk", axis=0, tiled=True),
        lax.all_gather(code_table.astype(half), "blk", axis=0, tiled=True),
        lax.all_gather(readout.astype(half), "blk", axis=0, tiled=True),
    )
    gains_full = lax.all_gather(gains, "blk", axis=1, tiled=True)
    code_rows = jnp.clip(jnp.where(modality == 1, token_ids, VT + token_ids), 0, VT + VA - 1)
    image_pick = modality == 0
    local_cols = jnp.where(image_pick[..., None], table_img[token_ids], table_code[code_rows])
    embedded = lax.all_gather(local_cols, "head", axis=2, tiled=True).astype(jnp.float32)
    normed_in = rms_norm(embedded, gains_full[0]).astype(half)
    mixed = jnp.einsum("ctd,sde->scte", normed_in, w_in, preferred_element_type=jnp.float32).astype(
        half
    )
    head_count = w_in.shape[2] // HD
    queries = mixed[0].reshape(clips, span, head_count, HD)
    keys_own = mixed[1].reshape(clips, span, head_count, HD)
    values_own = mixed[2].reshape(clips, span, head_count, HD)
    offsets = jnp.arange(span)
    query_pos = blk_place * span + offsets
    start_state = (
        jnp.full((clips, head_count, span), -1e30, jnp.float32),
        jnp.zeros((clips, head_count, span), jnp.float32),
        jnp.zeros((clips, head_count, span, HD), jnp.float32),
    )
    running = attend(queries, keys_own, values_own, query_pos, query_pos, start_state)
    store = jnp.zeros((1,), half)

    def forward_turn(turn, state):
        keys_now, values_now, running, store = state
        keys_now, values_now = from_behind((keys_now, values_now), "blk", 1)
        key_pos = (blk_place - turn) * span + offsets
        running = attend(queries, keys_now, values_now, query_pos, key_pos, running)
        return (keys_now, values_now, running, store)

    unused_keys, unused_values, running, store = lax.fori_loop(
        1, blocks_total, forward_turn, (keys_own, values_own, running, store)
    )
    top_all, total_all, summed = running
    log_total = top_all + jnp.log(total_all)
    attn_heads = (summed / total_all[..., None]).transpose(0, 2, 1, 3).astype(half)
    flat_heads = attn_heads.reshape(clips, span, head_count * HD)
    first = embedded + head_sum(
        jnp.einsum("cte,ed->ctd", flat_heads, w_out, preferred_element_type=jnp.float32)
    )
    normed_mid = rms_norm(first, gains_full[1]).astype(half)
    hidden_up = jnp.einsum("ctd,df->ctf", normed_mid, w_up, preferred_element_type=jnp.float32)
    active = jax.nn.gelu(hidden_up).astype(half)
    second = first + head_sum(
        jnp.einsum("ctf,fd->ctd", active, w_down, preferred_element_type=jnp.float32)
    )
    final_in = rms_norm(second, gains_full[2]).astype(half)
    logits = jnp.einsum("ctd,dv->ctv", final_in, w_read, preferred_element_type=jnp.float32)
    vocab_local = logits.shape[2]
    column_ids = head_place * vocab_local + jnp.arange(vocab_local)
    match = column_ids[None, None, :] == targets[..., None]
    top_local = jnp.max(logits, axis=-1)
    sum_local = jnp.sum(jnp.exp(logits - top_local[..., None]), axis=-1)
    picked_local = jnp.sum(jnp.where(match, logits, 0.0), axis=-1)
    top_vocab, sum_vocab = combined_all((top_local, sum_local), "head", combine_vocab)
    log_norm = top_vocab + jnp.log(sum_vocab)
    weight_of = ((loss_mask == 1) & (query_pos[None, :] < clip_lengths[:, None])).astype(
        jnp.float32
    )
    leading = (head_place == 0).astype(jnp.float32)
    per_token = (leading * (log_norm + ZCOEF * log_norm * log_norm) - picked_local) * weight_of
    loss_sum, loss_count = lax.psum(
        (jnp.sum(per_token), leading * jnp.sum(weight_of)), ("blk", "head")
    )
    token_grad = weight_of / loss_count
    probs = jnp.exp(logits - log_norm[..., None])
    grad_logits = (
        token_grad[..., None]
        * (probs * (1.0 + 2.0 * ZCOEF * log_norm)[..., None] - match.astype(jnp.float32))
    ).astype(half)
    grad_read = jnp.einsum("ctd,ctv->dv", final_in, grad_logits, preferred_element_type=jnp.float32)
    grad_final = head_sum(
        jnp.einsum("ctv,dv->ctd", grad_logits, w_read, preferred_element_type=jnp.float32)
    )
    grad_second, gain_final = norm_back(second, gains_full[2], grad_final)
    branch_grad = grad_second.astype(half)
    grad_down = jnp.einsum("ctf,ctd->fd", active, branch_grad, preferred_element_type=jnp.float32)
    grad_active = jnp.einsum("ctd,fd->ctf", branch_grad, w_down, preferred_element_type=jnp.float32)
    unused_gelu, gelu_pull = jax.vjp(jax.nn.gelu, hidden_up)
    grad_hidden = gelu_pull(grad_active)[0].astype(half)
    grad_up = jnp.einsum("ctd,ctf->df", normed_mid, grad_hidden, preferred_element_type=jnp.float32)
    grad_mid = head_sum(
        jnp.einsum("ctf,df->ctd", grad_hidden, w_up, preferred_element_type=jnp.float32)
    )
    grad_mid_in, gain_mid = norm_back(first, gains_full[1], grad_mid)
    grad_first = grad_second + grad_mid_in
    attn_grad = grad_first.astype(half)
    grad_out_w = jnp.einsum(
        "cte,ctd->ed", flat_heads, attn_grad, preferred_element_type=jnp.float32
    )
    grad_heads = jnp.einsum(
        "ctd,ed->cte", attn_grad, w_out, preferred_element_type=jnp.float32
    ).astype(half)
    grad_heads = grad_heads.reshape(clips, span, head_count, HD)
    inner = jnp.einsum("cqhd,cqhd->chq", grad_heads, attn_heads, preferred_element_type=jnp.float32)
    grad_query, grad_keys, grad_values = attend_back(
        queries, keys_own, values_own, query_pos, query_pos, grad_heads, log_total, inner
    )

    def back_turn(turn, state):
        keys_now, values_now, grad_query, grad_keys, grad_values = state
        grad_keys, grad_values = pass_grads(grad_keys, grad_values)
        keys_now, values_now = from_behind((keys_now, values_now), "blk", 1)
        key_pos = (blk_place - turn) * span + offsets
        more_query, more_keys, more_values = attend_back(
            queries, keys_now, values_now, query_pos, key_pos, grad_heads, log_total, inner
        )
        return (
            keys_now,
            values_now,
            grad_query + more_query,
            grad_keys + more_keys,
            grad_values + more_values,
        )

    unused_keys, unused_values, grad_query, grad_keys, grad_values = lax.fori_loop(
        1, blocks_total, back_turn, (keys_own, values_own, grad_query, grad_keys, grad_values)
    )
    grad_keys, grad_values = pass_grads(grad_keys, grad_values)
    grad_mixed = (
        jnp.stack([grad_query, grad_keys, grad_values])
        .astype(half)
        .reshape(3, clips, span, head_count * HD)
    )
    grad_in = jnp.einsum("ctd,scte->sde", normed_in, grad_mixed, preferred_element_type=jnp.float32)
    grad_norm_in = head_sum(
        jnp.einsum("scte,sde->ctd", grad_mixed, w_in, preferred_element_type=jnp.float32)
    )
    grad_embed_in, gain_in = norm_back(embedded, gains_full[0], grad_norm_in)
    grad_embed = grad_first + grad_embed_in
    width_local = local_cols.shape[2]
    own_cols = lax.dynamic_slice_in_dim(grad_embed, head_place * width_local, width_local, 2)
    grad_img = (
        jnp.zeros(table_img.shape, jnp.float32)
        .at[token_ids]
        .add(jnp.where(image_pick[..., None], own_cols, 0.0))
    )
    grad_code = (
        jnp.zeros(table_code.shape, jnp.float32)
        .at[code_rows]
        .add(jnp.where(image_pick[..., None], 0.0, own_cols))
    )
    img_sum, code_sum = (
        lax.psum_scatter(
            grad_img.astype(jnp.bfloat16), "blk", scatter_dimension=0, tiled=True
        ).astype(jnp.float32),
        lax.psum_scatter(
            grad_code.astype(jnp.bfloat16), "blk", scatter_dimension=0, tiled=True
        ).astype(jnp.float32),
    )
    gain_stack = jnp.stack([gain_in, gain_mid, gain_final])
    in_sum, out_sum, up_sum, down_sum, read_sum, gain_sum = (
        lax.psum_scatter(
            grad_in.astype(jnp.bfloat16), "blk", scatter_dimension=1, tiled=True
        ).astype(jnp.float32),
        lax.psum_scatter(
            grad_out_w.astype(jnp.bfloat16), "blk", scatter_dimension=1, tiled=True
        ).astype(jnp.float32),
        lax.psum_scatter(
            grad_up.astype(jnp.bfloat16), "blk", scatter_dimension=0, tiled=True
        ).astype(jnp.float32),
        lax.psum_scatter(
            grad_down.astype(jnp.bfloat16), "blk", scatter_dimension=1, tiled=True
        ).astype(jnp.float32),
        lax.psum_scatter(
            grad_read.astype(jnp.bfloat16), "blk", scatter_dimension=0, tiled=True
        ).astype(jnp.float32),
        lax.psum_scatter(
            gain_stack.astype(jnp.bfloat16), "blk", scatter_dimension=1, tiled=True
        ).astype(jnp.float32),
    )
    reduced = [in_sum, out_sum, up_sum, down_sum, img_sum, code_sum, read_sum, gain_sum]
    local_squares = jnp.float32(0.0)
    for shard in reduced[:7]:
        local_squares = local_squares + jnp.sum(shard * shard)
    local_squares = local_squares + leading * jnp.sum(gain_sum * gain_sum)
    all_squares = lax.psum(local_squares, ("blk", "head"))
    grad_norm = jnp.sqrt(all_squares)
    factor = jnp.minimum(1.0, CLIP / grad_norm)
    length = span * blocks_total
    spreads = [
        D ** (-0.5),
        (length // 2) ** 0.5 * D ** (-0.5),
        D ** (-0.5),
        FF ** (-0.5),
        0.05,
        0.05,
        2.0 * D ** (-0.5),
    ]
    weights = [inward, outward, expand, contract, image_table, code_table, readout, gains]
    firsts = [
        inward_first,
        outward_first,
        expand_first,
        contract_first,
        image_first,
        code_first,
        readout_first,
        gains_first,
    ]
    seconds = [
        inward_second,
        outward_second,
        expand_second,
        contract_second,
        image_second,
        code_second,
        readout_second,
        gains_second,
    ]
    result = []
    for index in range(8):
        rate = GAIN_RATE if index == 7 else RATE_FACTOR * spreads[index]
        decay = 0.0 if index == 7 else DECAY
        result.append(
            adamw(
                weights[index], firsts[index], seconds[index], reduced[index] * factor, rate, decay
            )
        )
    return (
        result[0][0],
        result[0][1],
        result[0][2],
        result[1][0],
        result[1][1],
        result[1][2],
        result[2][0],
        result[2][1],
        result[2][2],
        result[3][0],
        result[3][1],
        result[3][2],
        result[4][0],
        result[4][1],
        result[4][2],
        result[5][0],
        result[5][1],
        result[5][2],
        result[6][0],
        result[6][1],
        result[6][2],
        result[7][0],
        result[7][1],
        result[7][2],
        loss_sum,
        loss_count,
        grad_norm,
    )


def solution(mesh):
    placed = (
        P(None, "blk", "head"),
        P("head", "blk"),
        P("blk", "head"),
        P("head", "blk"),
        P("blk", "head"),
        P("blk", "head"),
        P("blk", "head"),
        P(None, "blk"),
        P(None, "blk", "head"),
        P("head", "blk"),
        P("blk", "head"),
        P("head", "blk"),
        P("blk", "head"),
        P("blk", "head"),
        P("blk", "head"),
        P(None, "blk"),
        P(None, "blk", "head"),
        P("head", "blk"),
        P("blk", "head"),
        P("head", "blk"),
        P("blk", "head"),
        P("blk", "head"),
        P("blk", "head"),
        P(None, "blk"),
        P(None, "blk"),
        P(None, "blk"),
        P(),
        P(None, "blk"),
        P(None, "blk"),
    )
    return jax.shard_map(
        shards,
        mesh=mesh,
        in_specs=placed,
        out_specs=(
            P(None, "blk", "head"),
            P(None, "blk", "head"),
            P(None, "blk", "head"),
            P("head", "blk"),
            P("head", "blk"),
            P("head", "blk"),
            P("blk", "head"),
            P("blk", "head"),
            P("blk", "head"),
            P("head", "blk"),
            P("head", "blk"),
            P("head", "blk"),
            P("blk", "head"),
            P("blk", "head"),
            P("blk", "head"),
            P("blk", "head"),
            P("blk", "head"),
            P("blk", "head"),
            P("blk", "head"),
            P("blk", "head"),
            P("blk", "head"),
            P(None, "blk"),
            P(None, "blk"),
            P(None, "blk"),
            P(),
            P(),
            P(),
        ),
        check_vma=False,
    )
```

profile of v0, /device:TPU:0, one launch (start us, length us, event | category | flops | bytes accessed | tf_op | source)
XLA Modules:
  0.0 2748.7 jit_solution(9286766374316284267)
XLA Ops:
  11.9 43.7 %all-gather.15.cloned.1.call-done = bf16[1280,512]{1,0:T(8,128)(2,1)} async-done(((bf16[160,512]{1,0:T(8,128)(2,1)}), bf16[1280,512]{1,0:T(8,128)(2,1)}) %all-gather.15.cloned.1.call-update) | async-done | bytes 1310736 | tf_op jit(solution)/shard_map/all_gather | solution.py:170
  59.1 122.8 %all-gather.13.cloned.1.call-done = bf16[8192,512]{1,0:T(8,128)(2,1)} async-done(((bf16[1024,512]{1,0:T(8,128)(2,1)}), bf16[8192,512]{1,0:T(8,128)(2,1)}) %all-gather.13.cloned.1.call-update) | async-done | bytes 8388624 | tf_op jit(solution)/shard_map/all_gather | solution.py:169
  181.9 6.4 gather_fusion
  191.9 30.6 %all_gather.42 = f32[3,2048]{1,0:T(4,128)S(1)} all-gather(f32[3,256]{1,0:T(4,128)S(1)} %copy-done.66), channel_id=1, replica_groups=mesh['blk'=8,'head'=4] {'blk'}, dimensions={1}, use_global_device_ids=true | all-gather | bytes 27648 | tf_op jit(solution)/shard_map/all_gather | solution.py:173
  224.9 87.0 %all-gather.19.cloned.1.call-done = bf16[3,2048,512]{2,1,0:T(8,128)(2,1)} async-done(((bf16[3,256,512]{2,1,0:T(8,128)(2,1)}), bf16[3,2048,512]{2,1,0:T(8,128)(2,1)}) %all-gather.19.cloned.1.call-update) | async-done | bytes 6291472 | tf_op jit(solution)/shard_map/all_gather | solution.py:165
  312.0 6.2 fusion.111
  331.3 210.7 %while.62 = (s32[]{:T(128)}, bf16[2,256,4,128]{3,1,2,0:T(8,128)(2,1)}, bf16[2,256,4,128]{3,1,2,0:T(8,128)(2,1)}, f32[2,4,256]{2,1,0:T(4,128)S(1)}, f32[2,4,256]{...) while((s32[]{:T(128)}, ...), condition=%wide.region_6.7_spmd.clone, body=%wide.region_3.6_spmd.clone.sunk | while | flops 275911680 | bytes 25039640 | solution.py:203
  337.6 12.7 collective-permute-done
  352.2 15.0 collective-permute-done.1
  377.6 6.1 collective-permute-start.1
  383.9 6.4 collective-permute-done
  408.0 6.1 collective-permute-start.1
  414.2 6.4 collective-permute-done
  443.7 6.4 collective-permute-done
  466.0 6.1 collective-permute-start.1
  493.5 6.1 collective-permute-start.1
  520.0 6.3 collective-permute-start.1
  556.3 57.5 %all-reduce.7.cloned.1.call-done = bf16[2,256,2048]{2,1,0:T(8,128)(2,1)} async-done(((bf16[2,256,2048]{2,1,0:T(8,128)(2,1)}), bf16[2,256,2048]{2,1,0:T(8,128)(2,1)}) %all-reduce.7.cloned.1.call-update) | async-done | bytes 2097168 | tf_op jit(solution)/shard_map/psum | solution.py:57
  616.1 125.6 %all-gather.23.cloned.1.call-done = bf16[2048,2048]{1,0:T(8,128)(2,1)} async-done(((bf16[256,2048]{1,0:T(8,128)(2,1)}), bf16[2048,2048]{1,0:T(8,128)(2,1)}) %all-gather.23.cloned.1.call-update) | async-done | bytes 8388624 | tf_op jit(solution)/shard_map/all_gather | solution.py:167
  741.7 10.6 fusion.36
  752.3 115.9 %all-gather.25.cloned.1.call-done = bf16[2048,2048]{1,0:T(8,128)(2,1)} async-done(((bf16[2048,256]{1,0:T(8,128)(2,1)}), bf16[2048,2048]{1,0:T(8,128)(2,1)}) %all-gather.25.cloned.1.call-update) | async-done | bytes 8388624 | tf_op jit(solution)/shard_map/all_gather | solution.py:168
  868.2 10.8 fusion.71
  881.9 46.9 %all-reduce.9.cloned.1.call-done = bf16[2,256,2048]{2,1,0:T(8,128)(2,1)} async-done(((bf16[2,256,2048]{2,1,0:T(8,128)(2,1)}), bf16[2,256,2048]{2,1,0:T(8,128)(2,1)}) %all-reduce.9.cloned.1.call-update) | async-done | bytes 2097168 | tf_op jit(solution)/shard_map/psum | solution.py:57
  932.0 124.3 %all-gather.27.cloned.1.call-done = bf16[2048,2048]{1,0:T(8,128)(2,1)} async-done(((bf16[256,2048]{1,0:T(8,128)(2,1)}), bf16[2048,2048]{1,0:T(8,128)(2,1)}) %all-gather.27.cloned.1.call-update) | async-done | bytes 8388624 | tf_op jit(solution)/shard_map/all_gather | solution.py:171
  1056.3 8.4 fusion.197
  1078.6 38.4 %psum.56 = f32[]{:T(128)} all-reduce(f32[]{:T(128)S(6)} %mul.741), channel_id=1, replica_groups=mesh['blk'=8,'head'=4] {'blk','head'}, use_global_device_ids=true, to_apply=%region_8.9 | all-reduce | flops 1 | bytes 8 | tf_op jit(solution)/shard_map/psum | solution.py:234
  1117.8 10.7 fusion.74
  1128.6 52.4 %all-reduce.11.cloned.1.call-done = bf16[2,256,2048]{2,1,0:T(8,128)(2,1)} async-done(((bf16[2,256,2048]{2,1,0:T(8,128)(2,1)}), bf16[2,256,2048]{2,1,0:T(8,128)(2,1)}) %all-reduce.11.cloned.1.call-update) | async-done | bytes 2097168 | tf_op jit(solution)/shard_map/psum | solution.py:57
  1188.9 11.8 fusion.64
  1208.4 51.1 %all-reduce.13.cloned.1.call-done = bf16[2,256,2048]{2,1,0:T(8,128)(2,1)} async-done(((bf16[2,256,2048]{2,1,0:T(8,128)(2,1)}), bf16[2,256,2048]{2,1,0:T(8,128)(2,1)}) %all-reduce.13.cloned.1.call-update) | async-done | bytes 2097168 | tf_op jit(solution)/shard_map/psum | solution.py:57
  1293.3 346.7 %while.63 = (s32[]{:T(128)}, bf16[2,256,4,128]{3,1,2,0:T(8,128)(2,1)}, bf16[2,256,4,128]{3,1,2,0:T(8,128)(2,1)}, f32[2,256,4,128]{3,1,2,0:T(8,128)}, bf16[2,256,...) while((s32[]{:T(128)}, ...), condition=%wide.region_22.23_spmd.clone, body=%wide.region_21.22_spmd.clone.sunk | while | flops 677250048 | bytes 36328320 | solution.py:288
  1311.2 9.4 collective-permute-done.3
  1325.6 6.2 collective-permute-done.4
  1335.7 6.1 collective-permute-done.5
  1363.1 9.4 collective-permute-done.3
  1377.5 6.2 collective-permute-done.4
  1414.1 9.4 collective-permute-done.3
  1428.5 6.2 collective-permute-done.4
  1464.9 9.4 collective-permute-done.3
  1479.3 6.2 collective-permute-done.4
  1495.1 6.1 collective-permute-start.2
  1514.9 9.4 collective-permute-done.3
  1529.3 6.2 collective-permute-done.4
  1564.0 9.4 collective-permute-done.3
  1592.3 6.1 collective-permute-start.2
  1612.1 9.4 collective-permute-done.3
  1648.4 8.7 collective-permute-done.6
  1664.8 7.8 bitcast_convert_fusion.4
  1675.2 50.0 %all-reduce.15.cloned.1.call-done = bf16[2,256,2048]{2,1,0:T(8,128)(2,1)} async-done(((bf16[2,256,2048]{2,1,0:T(8,128)(2,1)}), bf16[2,256,2048]{2,1,0:T(8,128)(2,1)}) %all-reduce.15.cloned.1.call-update) | async-done | bytes 2097168 | tf_op jit(solution)/shard_map/psum | solution.py:57
  1750.0 6.7 fusion.40
  1756.7 12.4 bitcast_convert_fusion
  1769.6 10.4 bitcast_convert_fusion.2
  1781.5 10.1 bitcast_convert_fusion.1
  1793.0 10.6 scatter_custom_fusion
  1803.7 9.0 convert_element_type.266
  1822.7 38.2 %reduce-scatter.21.cloned.1.call-done = bf16[160,512]{1,0:T(8,128)(2,1)} async-done(((bf16[1280,512]{1,0:T(8,128)(2,1)}), bf16[160,512]{1,0:T(8,128)(2,1)}) %reduce-scatter.21.cloned.1.call-update) | async-done | bytes 163856 | tf_op jit(solution)/shard_map/reduce_scatter | solution.py:319
  1862.5 69.6 %reduce-scatter.13.cloned.1.call-done = bf16[512,256]{1,0:T(8,128)(2,1)} async-done(((bf16[512,2048]{1,0:T(8,128)(2,1)}), bf16[512,256]{1,0:T(8,128)(2,1)}) %reduce-scatter.13.cloned.1.call-update) | async-done | bytes 262160 | tf_op jit(solution)/shard_map/reduce_scatter | solution.py:328
  1933.8 119.2 %reduce-scatter.11.cloned.1.call-done = bf16[3,256,512]{1,2,0:T(8,128)(2,1)} async-done(((bf16[3,2048,512]{1,2,0:T(8,128)(2,1)}), bf16[3,256,512]{1,2,0:T(8,128)(2,1)}) %reduce-scatter.11.cloned.1.call-update) | async-done | bytes 786448 | tf_op jit(solution)/shard_map/reduce_scatter | solution.py:325
  2056.5 148.2 %reduce-scatter.23.cloned.1.call-done = bf16[256,2048]{1,0:T(8,128)(2,1)} async-done(((bf16[2048,2048]{1,0:T(8,128)(2,1)}), bf16[256,2048]{1,0:T(8,128)(2,1)}) %reduce-scatter.23.cloned.1.call-update) | async-done | bytes 1048592 | tf_op jit(solution)/shard_map/reduce_scatter | solution.py:337
  2207.0 149.8 %reduce-scatter.15.cloned.1.call-done = bf16[256,2048]{1,0:T(8,128)(2,1)} async-done(((bf16[2048,2048]{1,0:T(8,128)(2,1)}), bf16[256,2048]{1,0:T(8,128)(2,1)}) %reduce-scatter.15.cloned.1.call-update) | async-done | bytes 1048592 | tf_op jit(solution)/shard_map/reduce_scatter | solution.py:331
  2359.9 148.9 %reduce-scatter.17.cloned.1.call-done = bf16[2048,256]{1,0:T(8,128)(2,1)} async-done(((bf16[2048,2048]{1,0:T(8,128)(2,1)}), bf16[2048,256]{1,0:T(8,128)(2,1)}) %reduce-scatter.17.cloned.1.call-update) | async-done | bytes 1048592 | tf_op jit(solution)/shard_map/reduce_scatter | solution.py:334
  2511.7 149.1 %reduce-scatter.19.cloned.1.call-done = bf16[1024,512]{1,0:T(8,128)(2,1)} async-done(((bf16[8192,512]{1,0:T(8,128)(2,1)}), bf16[1024,512]{1,0:T(8,128)(2,1)}) %reduce-scatter.19.cloned.1.call-update) | async-done | bytes 1048592 | tf_op jit(solution)/shard_map/reduce_scatter | solution.py:316
  2665.2 39.3 %all-reduce = (f32[]{:T(128)}, f32[]{:T(128)}) all-reduce(f32[]{:T(128)S(6)} %add.473, f32[]{:T(128)} %get-tuple-element.757), channel_id=1, replica_groups=mesh['blk'=8,'head'=4] {'blk','head'}, use_global_device_ids=true, to_apply=%region_46.47 | all-reduce | flops 2 | bytes 16 | tf_op jit(solution)/shard_map/psum | solution.py:349
  2719.9 6.2 multiply_subtract_fusion.1
  (590 shorter events, 576.0 us)
Async XLA Ops:
  7.2 48.4 %all-gather.15.cloned.1.call-start = ((), (), s32[]{:S(2)}) async-start(), calls=%async_computation.9 | async-start | bytes 1474560 | tf_op jit(solution)/shard_map/all_gather | solution.py:170
  9.0 172.9 %all-gather.13.cloned.1.call-start = ((), (), s32[]{:S(2)}) async-start(), calls=%async_computation.8 | async-start | bytes 9437184 | tf_op jit(solution)/shard_map/all_gather | solution.py:169
  11.7 210.9 %all-gather.17.cloned.1.call-start = ((), (), s32[]{:S(2)}) async-start(), calls=%async_computation.10 | async-start | bytes 2621440 | tf_op jit(solution)/shard_map/all_gather | solution.py:177
  189.3 122.6 %all-gather.19.cloned.1.call-start = ((), (), s32[]{:S(2)}) async-start(), calls=%async_computation.11 | async-start | bytes 7077888 | tf_op jit(solution)/shard_map/all_gather | solution.py:165
  191.0 354.9 %all-gather.21.cloned.1.call-start = ((), (), s32[]{:S(2)}) async-start(), calls=%async_computation.12 | async-start | bytes 2359296 | tf_op jit(solution)/shard_map/all_gather | solution.py:166
  191.8 422.0 %all-reduce.7.cloned.1.call-start = ((), (), s32[]{:S(2)}) async-start(), calls=%async_computation.13 | async-start | bytes 4194304 | tf_op jit(solution)/shard_map/psum | solution.py:57
  331.3 19.0 collective-permute-start
  333.8 33.4 %collective-permute-start.1 = (bf16[2,256,4,128]{3,1,2,0:T(8,128)(2,1)}, bf16[2,256,4,128]{3,1,2,0:T(8,128)(2,1)}, u32[]{:S(2)}, u32[]{:S(2)}) collective-permute-start(bf16[2,256,4,128]{3,1,2,0:T(8,128)(2,1)} %get-tuple-element.1059), channel_id=1, source_target_pairs={{0,4},{4,8},{8,12},{12,16},{16,20},{20,24},{24,28},{1,5},{5,9},{9,... | collective-permute-start | bytes 1572872 | tf_op jit(solution)/shard_map/while/body/eval_jaxpr/ppermute | solution.py:34
  372.2 18.0 collective-permute-start
  377.6 20.3 collective-permute-start.1
  402.9 17.7 collective-permute-start
  408.0 19.1 collective-permute-start.1
  432.1 17.9 collective-permute-start
  437.5 18.2 collective-permute-start.1
  460.7 17.0 collective-permute-start
  466.0 17.3 collective-permute-start.1
  493.5 16.3 collective-permute-start.1
  514.8 16.6 collective-permute-start
  520.0 17.0 collective-permute-start.1
  550.3 191.5 %all-gather.23.cloned.1.call-start = ((), (), s32[]{:S(2)}) async-start(), calls=%async_computation.14 | async-start | bytes 9437184 | tf_op jit(solution)/shard_map/all_gather | solution.py:167
  553.1 315.1 %all-gather.25.cloned.1.call-start = ((), (), s32[]{:S(2)}) async-start(), calls=%async_computation.15 | async-start | bytes 9437184 | tf_op jit(solution)/shard_map/all_gather | solution.py:168
  555.8 372.9 %all-reduce.9.cloned.1.call-start = ((), (), s32[]{:S(2)}) async-start(), calls=%async_computation.16 | async-start | bytes 4194304 | tf_op jit(solution)/shard_map/psum | solution.py:57
  879.0 177.3 %all-gather.27.cloned.1.call-start = ((), (), s32[]{:S(2)}) async-start(), calls=%async_computation.17 | async-start | bytes 9437184 | tf_op jit(solution)/shard_map/all_gather | solution.py:171
  881.8 299.2 %all-reduce.11.cloned.1.call-start = ((), (), s32[]{:S(2)}) async-start(), calls=%async_computation.18 | async-start | bytes 4194304 | tf_op jit(solution)/shard_map/psum | solution.py:57
  1128.5 131.0 %all-reduce.13.cloned.1.call-start = ((), (), s32[]{:S(2)}) async-start(), calls=%async_computation.19 | async-start | bytes 4194304 | tf_op jit(solution)/shard_map/psum | solution.py:57
  1207.9 517.3 %all-reduce.15.cloned.1.call-start = ((), (), s32[]{:S(2)}) async-start(), calls=%async_computation.24 | async-start | bytes 4194304 | tf_op jit(solution)/shard_map/psum | solution.py:57
  1293.3 16.0 collective-permute-start.2
  1297.5 23.1 collective-permute-start.3
  1300.9 30.9 %collective-permute-start.4 = (bf16[2,256,4,128]{3,1,2,0:T(8,128)(2,1)}, bf16[2,256,4,128]{3,1,2,0:T(8,128)(2,1)}, u32[]{:S(2)}, u32[]{:S(2)}) collective-permute-start(bf16[2,256,4,128]{3,1,2,0:T(8,128)(2,1)} %get-tuple-element.1121), channel_id=1, source_target_pairs={{0,4},{4,8},{8,12},{12,16},{16,20},{20,24},{24,28},{28,0},{1,5},{5... | collective-permute-start | bytes 1572872 | tf_op jit(solution)/shard_map/while/body/eval_jaxpr/ppermute | solution.py:28
  1301.6 40.2 %collective-permute-start.5 = (bf16[2,256,4,128]{3,1,2,0:T(8,128)(2,1)}, bf16[2,256,4,128]{3,1,2,0:T(8,128)(2,1)}, u32[]{:S(2)}, u32[]{:S(2)}) collective-permute-start(bf16[2,256,4,128]{3,1,2,0:T(8,128)(2,1)} %get-tuple-element.1122), channel_id=1, source_target_pairs={{0,4},{4,8},{8,12},{12,16},{16,20},{20,24},{24,28},{28,0},{1,5},{5... | collective-permute-start | bytes 1572872 | tf_op jit(solution)/shard_map/while/body/eval_jaxpr/ppermute | solution.py:28
  1344.1 17.1 collective-permute-start.2
  1349.3 23.1 collective-permute-start.3
  1353.6 30.0 %collective-permute-start.4 = (bf16[2,256,4,128]{3,1,2,0:T(8,128)(2,1)}, bf16[2,256,4,128]{3,1,2,0:T(8,128)(2,1)}, u32[]{:S(2)}, u32[]{:S(2)}) collective-permute-start(bf16[2,256,4,128]{3,1,2,0:T(8,128)(2,1)} %get-tuple-element.1121), channel_id=1, source_target_pairs={{0,4},{4,8},{8,12},{12,16},{16,20},{20,24},{24,28},{28,0},{1,5},{5... | collective-permute-start | bytes 1572872 | tf_op jit(solution)/shard_map/while/body/eval_jaxpr/ppermute | solution.py:28
  1353.6 39.1 %collective-permute-start.5 = (bf16[2,256,4,128]{3,1,2,0:T(8,128)(2,1)}, bf16[2,256,4,128]{3,1,2,0:T(8,128)(2,1)}, u32[]{:S(2)}, u32[]{:S(2)}) collective-permute-start(bf16[2,256,4,128]{3,1,2,0:T(8,128)(2,1)} %get-tuple-element.1122), channel_id=1, source_target_pairs={{0,4},{4,8},{8,12},{12,16},{16,20},{20,24},{24,28},{28,0},{1,5},{5... | collective-permute-start | bytes 1572872 | tf_op jit(solution)/shard_map/while/body/eval_jaxpr/ppermute | solution.py:28
  1395.1 17.1 collective-permute-start.2
  1400.3 23.1 collective-permute-start.3
  1405.5 29.2 %collective-permute-start.4 = (bf16[2,256,4,128]{3,1,2,0:T(8,128)(2,1)}, bf16[2,256,4,128]{3,1,2,0:T(8,128)(2,1)}, u32[]{:S(2)}, u32[]{:S(2)}) collective-permute-start(bf16[2,256,4,128]{3,1,2,0:T(8,128)(2,1)} %get-tuple-element.1121), channel_id=1, source_target_pairs={{0,4},{4,8},{8,12},{12,16},{16,20},{20,24},{24,28},{28,0},{1,5},{5... | collective-permute-start | bytes 1572872 | tf_op jit(solution)/shard_map/while/body/eval_jaxpr/ppermute | solution.py:28
  1405.5 37.3 %collective-permute-start.5 = (bf16[2,256,4,128]{3,1,2,0:T(8,128)(2,1)}, bf16[2,256,4,128]{3,1,2,0:T(8,128)(2,1)}, u32[]{:S(2)}, u32[]{:S(2)}) collective-permute-start(bf16[2,256,4,128]{3,1,2,0:T(8,128)(2,1)} %get-tuple-element.1122), channel_id=1, source_target_pairs={{0,4},{4,8},{8,12},{12,16},{16,20},{20,24},{24,28},{28,0},{1,5},{5... | collective-permute-start | bytes 1572872 | tf_op jit(solution)/shard_map/while/body/eval_jaxpr/ppermute | solution.py:28
  1445.2 17.8 collective-permute-start.2
  1451.1 23.1 collective-permute-start.3
  1456.4 29.0 %collective-permute-start.4 = (bf16[2,256,4,128]{3,1,2,0:T(8,128)(2,1)}, bf16[2,256,4,128]{3,1,2,0:T(8,128)(2,1)}, u32[]{:S(2)}, u32[]{:S(2)}) collective-permute-start(bf16[2,256,4,128]{3,1,2,0:T(8,128)(2,1)} %get-tuple-element.1121), channel_id=1, source_target_pairs={{0,4},{4,8},{8,12},{12,16},{16,20},{20,24},{24,28},{28,0},{1,5},{5... | collective-permute-start | bytes 1572872 | tf_op jit(solution)/shard_map/while/body/eval_jaxpr/ppermute | solution.py:28
  1456.4 36.3 %collective-permute-start.5 = (bf16[2,256,4,128]{3,1,2,0:T(8,128)(2,1)}, bf16[2,256,4,128]{3,1,2,0:T(8,128)(2,1)}, u32[]{:S(2)}, u32[]{:S(2)}) collective-permute-start(bf16[2,256,4,128]{3,1,2,0:T(8,128)(2,1)} %get-tuple-element.1122), channel_id=1, source_target_pairs={{0,4},{4,8},{8,12},{12,16},{16,20},{20,24},{24,28},{28,0},{1,5},{5... | collective-permute-start | bytes 1572872 | tf_op jit(solution)/shard_map/while/body/eval_jaxpr/ppermute | solution.py:28
  1495.1 18.0 collective-permute-start.2
  1501.1 23.1 collective-permute-start.3
  1506.5 29.0 %collective-permute-start.4 = (bf16[2,256,4,128]{3,1,2,0:T(8,128)(2,1)}, bf16[2,256,4,128]{3,1,2,0:T(8,128)(2,1)}, u32[]{:S(2)}, u32[]{:S(2)}) collective-permute-start(bf16[2,256,4,128]{3,1,2,0:T(8,128)(2,1)} %get-tuple-element.1121), channel_id=1, source_target_pairs={{0,4},{4,8},{8,12},{12,16},{16,20},{20,24},{24,28},{28,0},{1,5},{5... | collective-permute-start | bytes 1572872 | tf_op jit(solution)/shard_map/while/body/eval_jaxpr/ppermute | solution.py:28
  1506.5 35.3 %collective-permute-start.5 = (bf16[2,256,4,128]{3,1,2,0:T(8,128)(2,1)}, bf16[2,256,4,128]{3,1,2,0:T(8,128)(2,1)}, u32[]{:S(2)}, u32[]{:S(2)}) collective-permute-start(bf16[2,256,4,128]{3,1,2,0:T(8,128)(2,1)} %get-tuple-element.1122), channel_id=1, source_target_pairs={{0,4},{4,8},{8,12},{12,16},{16,20},{20,24},{24,28},{28,0},{1,5},{5... | collective-permute-start | bytes 1572872 | tf_op jit(solution)/shard_map/while/body/eval_jaxpr/ppermute | solution.py:28
  1544.1 18.0 collective-permute-start.2
  1550.2 23.1 collective-permute-start.3
  1555.5 28.8 %collective-permute-start.4 = (bf16[2,256,4,128]{3,1,2,0:T(8,128)(2,1)}, bf16[2,256,4,128]{3,1,2,0:T(8,128)(2,1)}, u32[]{:S(2)}, u32[]{:S(2)}) collective-permute-start(bf16[2,256,4,128]{3,1,2,0:T(8,128)(2,1)} %get-tuple-element.1121), channel_id=1, source_target_pairs={{0,4},{4,8},{8,12},{12,16},{16,20},{20,24},{24,28},{28,0},{1,5},{5... | collective-permute-start | bytes 1572872 | tf_op jit(solution)/shard_map/while/body/eval_jaxpr/ppermute | solution.py:28
  1555.5 34.4 %collective-permute-start.5 = (bf16[2,256,4,128]{3,1,2,0:T(8,128)(2,1)}, bf16[2,256,4,128]{3,1,2,0:T(8,128)(2,1)}, u32[]{:S(2)}, u32[]{:S(2)}) collective-permute-start(bf16[2,256,4,128]{3,1,2,0:T(8,128)(2,1)} %get-tuple-element.1122), channel_id=1, source_target_pairs={{0,4},{4,8},{8,12},{12,16},{16,20},{20,24},{24,28},{28,0},{1,5},{5... | collective-permute-start | bytes 1572872 | tf_op jit(solution)/shard_map/while/body/eval_jaxpr/ppermute | solution.py:28
  1592.3 18.0 collective-permute-start.2
  1598.4 23.1 collective-permute-start.3
  1603.7 27.9 %collective-permute-start.4 = (bf16[2,256,4,128]{3,1,2,0:T(8,128)(2,1)}, bf16[2,256,4,128]{3,1,2,0:T(8,128)(2,1)}, u32[]{:S(2)}, u32[]{:S(2)}) collective-permute-start(bf16[2,256,4,128]{3,1,2,0:T(8,128)(2,1)} %get-tuple-element.1121), channel_id=1, source_target_pairs={{0,4},{4,8},{8,12},{12,16},{16,20},{20,24},{24,28},{28,0},{1,5},{5... | collective-permute-start | bytes 1572872 | tf_op jit(solution)/shard_map/while/body/eval_jaxpr/ppermute | solution.py:28
  1603.7 33.9 %collective-permute-start.5 = (bf16[2,256,4,128]{3,1,2,0:T(8,128)(2,1)}, bf16[2,256,4,128]{3,1,2,0:T(8,128)(2,1)}, u32[]{:S(2)}, u32[]{:S(2)}) collective-permute-start(bf16[2,256,4,128]{3,1,2,0:T(8,128)(2,1)} %get-tuple-element.1122), channel_id=1, source_target_pairs={{0,4},{4,8},{8,12},{12,16},{16,20},{20,24},{24,28},{28,0},{1,5},{5... | collective-permute-start | bytes 1572872 | tf_op jit(solution)/shard_map/while/body/eval_jaxpr/ppermute | solution.py:28
  1640.0 17.1 collective-permute-start.6
  1643.4 19.3 collective-permute-start.7
  1672.6 148.0 %reduce-scatter.25.cloned.1.call-start = ((), (), s32[]{:S(2)}) async-start(), calls=%async_computation.28 | async-start | bytes 589824
  1731.6 129.3 %reduce-scatter.21.cloned.1.call-start = ((), (), s32[]{:S(2)}) async-start(), calls=%async_computation.26 | async-start | bytes 1474560 | tf_op jit(solution)/shard_map/reduce_scatter | solution.py:319
  1744.1 188.0 %reduce-scatter.13.cloned.1.call-start = ((), (), s32[]{:S(2)}) async-start(), calls=%async_computation.21 | async-start | bytes 2359296 | tf_op jit(solution)/shard_map/reduce_scatter | solution.py:328
  1749.0 304.1 %reduce-scatter.11.cloned.1.call-start = ((), (), s32[]{:S(2)}) async-start(), calls=%async_computation.20 | async-start | bytes 7077888 | tf_op jit(solution)/shard_map/reduce_scatter | solution.py:325
  1756.7 448.0 %reduce-scatter.23.cloned.1.call-start = ((), (), s32[]{:S(2)}) async-start(), calls=%async_computation.27 | async-start | bytes 9437184 | tf_op jit(solution)/shard_map/reduce_scatter | solution.py:337
  1769.1 587.7 %reduce-scatter.15.cloned.1.call-start = ((), (), s32[]{:S(2)}) async-start(), calls=%async_computation.22 | async-start | bytes 9437184 | tf_op jit(solution)/shard_map/reduce_scatter | solution.py:331
  1780.0 728.8 %reduce-scatter.17.cloned.1.call-start = ((), (), s32[]{:S(2)}) async-start(), calls=%async_computation.23 | async-start | bytes 9437184 | tf_op jit(solution)/shard_map/reduce_scatter | solution.py:334
  1791.7 869.2 %reduce-scatter.19.cloned.1.call-start = ((), (), s32[]{:S(2)}) async-start(), calls=%async_computation.25 | async-start | bytes 9437184 | tf_op jit(solution)/shard_map/reduce_scatter | solution.py:316
  (108 other events, 2635.6 us)
Sparse Core Ops, SparseCore 0:
  10.8 44.7 all-gather.14
  58.3 123.5 all-gather.12
  189.5 20.7 all-gather.16
  212.9 99.0 all-gather.18
  314.4 60.5 all-gather.20
  550.4 63.3 all-reduce.6
  616.7 124.9 all-gather.22
  744.6 123.5 all-gather.24
  879.1 49.5 all-reduce.8
  931.3 124.9 all-gather.26
  1128.6 52.2 all-reduce.10
  1208.0 51.4 all-reduce.12
  1672.7 52.4 all-reduce.14
  1731.7 61.9 reduce-scatter.24
  1797.4 63.4 reduce-scatter.20
  1864.9 67.2 reduce-scatter.12
  1935.6 117.3 reduce-scatter.10
  2056.5 148.1 reduce-scatter.22
  2208.7 148.0 reduce-scatter.14
  2360.3 148.3 reduce-scatter.16
  2512.8 147.9 reduce-scatter.18
where the time goes:
time: 2760 us; the launch traced here: 2750 us
  waiting for transfers between devices  1970 us (71%)
  matrix products  219 us (8%)
  starting transfers between devices  171 us (6%)
  other arithmetic  132 us (5%)
  blocking collectives  119 us (4%)
  local copies, waits for them, and re-layouts  116 us (4%)
    psum x5, waiting for transfers between devices, head_sum(): lax.psum(partial_sum.astype(jnp.bfloat16), 'head').astype(jnp.float32)  258 us
    ppermute x28, waiting for transfers between devices, from_behind(): return lax.ppermute(block, axis, route)  186 us
    reduce_scatter x1, waiting for transfers between devices, shards(): lax.psum_scatter(grad_up.astype(jnp.bfloat16), 'blk', scatter_dimension=0...  150 us
    reduce_scatter x1, waiting for transfers between devices, shards(): lax.psum_scatter(grad_img.astype(jnp.bfloat16), 'blk', scatter_dimension=...  149 us
    reduce_scatter x1, waiting for transfers between devices, shards(): lax.psum_scatter(grad_down.astype(jnp.bfloat16), 'blk', scatter_dimension...  149 us
    reduce_scatter x1, waiting for transfers between devices, shards(): lax.psum_scatter(grad_read.astype(jnp.bfloat16), 'blk', scatter_dimension...  148 us
    ppermute x28, starting transfers between devices, from_behind(): return lax.ppermute(block, axis, route)  147 us
    all_gather x1, waiting for transfers between devices, shards(): lax.all_gather(expand.astype(half), 'blk', axis=0, tiled=True)  126 us
  transfers between devices with their start and end apart: 65, of which 62 were waited for; matrix products, arithmetic and copies ran while one was open for 10% of the time, Pallas kernels for 0%

commit v1 on v0

v1 whole, which is shorter than its diff:
```python
import jax
import jax.numpy as jnp
from jax import lax
from jax.sharding import PartitionSpec as P

D = 2048
HD = 128
FF = 8192
VT = 1024
VA = 256
STEP = 10


EPS = 1e-05
ZCOEF = 0.01
CLIP = 0.02
BETA1 = 0.9
BETA2 = 0.95
ADAM_EPS = 1e-08
DECAY = 0.1
RATE_FACTOR = 1.5
GAIN_RATE = 0.8

HALF = jnp.bfloat16
F32 = jnp.float32
NEG = -1e30
PAIR = 2


def flip(value, bit):
    count = lax.axis_size("blk")
    return lax.ppermute(value, "blk", [(i, i ^ bit) for i in range(count)])


def rms_norm(hidden, gain):
    return hidden * lax.rsqrt(jnp.mean(hidden * hidden, axis=-1, keepdims=True) + EPS) * gain


def norm_back(hidden, gain, upstream):
    unused, pullback = jax.vjp(rms_norm, hidden, gain)
    return pullback(upstream)


def dot(left, right, dims, out=F32):
    return lax.dot_general(left, right, (dims, ((), ())), preferred_element_type=F32).astype(out)


def adamw(weight, first, second, grad, rate, decay):
    first = BETA1 * first + (1.0 - BETA1) * grad
    second = BETA2 * second + (1.0 - BETA2) * grad * grad
    first_hat = first / (1.0 - BETA1**STEP)
    second_hat = second / (1.0 - BETA2**STEP)
    weight = weight - rate * (first_hat / (jnp.sqrt(second_hat) + ADAM_EPS) + decay * weight)
    return (weight, first, second)


def visible(query_pos, key_pos):
    return (key_pos[None, :] <= query_pos[:, None]) & (key_pos[None, :] >= 0)


def scores_of(queries, keys):
    return HD ** (-0.5) * jnp.einsum("qhd,khd->hqk", queries, keys, preferred_element_type=F32)


def attend(queries, keys, values, query_pos, key_pos, running):
    top_now, total_now, summed = running
    seen = visible(query_pos, key_pos)
    scores = jnp.where(seen, scores_of(queries, keys), NEG)
    top_next = jnp.maximum(top_now, jnp.max(scores, axis=-1))
    weights = jnp.where(seen, jnp.exp(scores - top_next[..., None]), 0.0)
    fading = jnp.exp(top_now - top_next)
    total_next = total_now * fading + jnp.sum(weights, axis=-1)
    summed = summed * fading[..., None] + jnp.einsum(
        "hqk,khd->hqd", weights.astype(HALF), values, preferred_element_type=F32
    )
    return (top_next, total_next, summed)


def attend_back(queries, keys, values, query_pos, key_pos, grad_out, log_total, inner):
    seen = visible(query_pos, key_pos)
    probs = jnp.where(seen, jnp.exp(scores_of(queries, keys) - log_total[..., None]), 0.0)
    grad_values = jnp.einsum(
        "hqk,qhd->khd", probs.astype(HALF), grad_out, preferred_element_type=F32
    )
    grad_probs = jnp.einsum("qhd,khd->hqk", grad_out, values, preferred_element_type=F32)
    grad_scores = (probs * (grad_probs - inner[..., None])).astype(HALF)
    grad_query = HD ** (-0.5) * jnp.einsum(
        "hqk,khd->qhd", grad_scores, keys, preferred_element_type=F32
    )
    grad_keys = HD ** (-0.5) * jnp.einsum(
        "hqk,qhd->khd", grad_scores, queries, preferred_element_type=F32
    )
    return (grad_query, grad_keys, grad_values)


def shards(
    inward,
    outward,
    expand,
    contract,
    image_table,
    code_table,
    readout,
    gains,
    inward_first,
    outward_first,
    expand_first,
    contract_first,
    image_first,
    code_first,
    readout_first,
    gains_first,
    inward_second,
    outward_second,
    expand_second,
    contract_second,
    image_second,
    code_second,
    readout_second,
    gains_second,
    token_ids,
    modality,
    clip_lengths,
    loss_mask,
    targets,
):
    blocks = lax.axis_size("blk")
    heads = lax.axis_size("head")
    blk = lax.axis_index("blk")
    head = lax.axis_index("head")
    clips, span = token_ids.shape
    length = span * blocks
    rows = D // blocks
    low = blk % 2
    side = (blk // 2) % 2
    high = blk // 4
    highs = blocks // 4
    groups = blocks // 2
    group = high * 2 + low
    per_clip = groups // clips
    clip = group // per_clip
    place = group % per_clip
    ranks = 2 * heads
    rank = side * heads + head
    team = clips * length // groups
    own = team // ranks
    high_bits = [1 << k for k in range(2, blocks.bit_length() - 1)]
    all_bits = [1, 2] + high_bits
    teams = [
        [i * heads + h for i in (base, base + PAIR) for h in range(heads)]
        for base in range(blocks)
        if not base & PAIR
    ]
    both = ("blk", "head")

    def gathered(block):
        return lax.all_gather(block, both, axis=0, tiled=True, axis_index_groups=teams)

    def reduced(partial):
        return lax.psum_scatter(
            partial, both, scatter_dimension=0, tiled=True, axis_index_groups=teams
        ).astype(F32)

    def index_of(shift):
        pairs = []
        for i in range(blocks):
            g = (i // 4) * 2 + i % 2
            far = g + shift
            if 0 <= far < groups and far // per_clip == g // per_clip:
                pairs.append((i, (far // 2) * 4 + (i & PAIR) + far % 2))
        return pairs

    small = jnp.concatenate(
        [part.astype(F32).reshape(-1) for part in (token_ids, modality, loss_mask, targets, gains)]
    )[None]
    for bit in all_bits:
        small = jnp.concatenate([small, flip(small, bit)])
    order = blk ^ jnp.arange(blocks)
    small = small[order]
    cells = clips * span
    ids_all, modality_all, mask_all, targets_all = (
        small[:, k * cells : (k + 1) * cells]
        .astype(jnp.int32)
        .reshape(blocks, clips, span)
        .transpose(1, 0, 2)
        .reshape(clips, length)
        for k in range(4)
    )
    gains_full = small[:, 4 * cells :].reshape(blocks, 3, rows).transpose(1, 0, 2).reshape(3, D)

    def sided(weight):
        return weight.astype(HALF).reshape(rows, 2, -1)

    qkv_local = inward.astype(HALF).reshape(3, rows, 2, -1).transpose(1, 2, 0, 3)
    local = [
        jnp.concatenate(
            [qkv_local.reshape(rows, 2, -1), sided(outward.astype(HALF).T)], axis=-1
        ),
        sided(expand),
        sided(contract.astype(HALF).T),
        sided(readout),
    ]

    def gathered_weight(halves):
        keep = lax.dynamic_index_in_dim(halves, side, 1, keepdims=False)
        send = lax.dynamic_index_in_dim(halves, 1 - side, 1, keepdims=False)
        came = flip(send, PAIR)
        mine = jnp.where(side == 0, jnp.stack([keep, came]), jnp.stack([came, keep]))
        pieces = {0: mine}
        for bit in high_bits + [1]:
            for mask in list(pieces):
                pieces[mask | bit] = flip(pieces[mask], bit)
        columns = mine.shape[-1]
        whole = jnp.zeros((highs, 2, 2, rows, columns), HALF)
        for mask, piece in pieces.items():
            whole = lax.dynamic_update_slice(
                whole,
                piece[None, :, None],
                (high ^ (mask >> 2), 0, low ^ (mask & 1), 0, 0),
            )
        return whole.reshape(D, columns)

    w_first, w_up, w_down, w_read = [gathered_weight(part) for part in local]
    head_columns = w_first.shape[-1] // 4
    w_in, w_out = w_first[:, : 3 * head_columns], w_first[:, 3 * head_columns :]
    local_heads = head_columns // HD

    def by_device(array):
        split = array.reshape(highs, 2, 2, team // 2)
        return split.transpose(0, 2, 1, 3).reshape(blocks, team // 2)

    image_rows = image_table.shape[0]
    code_local = code_table.shape[0]
    table = jnp.concatenate([image_table.astype(HALF), code_table.astype(HALF)])
    ids_dev, modality_dev = by_device(ids_all)[order], by_device(modality_all)[order]
    code_rows = jnp.clip(jnp.where(modality_dev == 1, ids_dev, VT + ids_dev), 0, VT + VA - 1)
    image_at = ids_dev - blk * image_rows
    code_at = code_rows - blk * code_local
    image_at = jnp.where((image_at >= 0) & (image_at < image_rows), image_at, -1)
    code_at = jnp.where((code_at >= 0) & (code_at < code_local), code_at + image_rows, -1)
    table_at = jnp.where(modality_dev == 0, image_at, code_at)
    table_rows = image_rows + code_local
    pick = (table_at.reshape(-1)[:, None] == jnp.arange(table_rows)[None, :]).astype(HALF)
    picked = dot(pick, table, ((1,), (0,)), HALF)
    width = table.shape[1]
    levels = len(all_bits)
    picked = picked.reshape((2,) * levels + (team // 2, width))

    def token_sum(part, bits):
        left = sorted(all_bits, reverse=True)
        for bit in bits:
            axis = left.index(bit)
            left.remove(bit)
            keep = lax.index_in_dim(part, 0, axis, keepdims=False)
            send = lax.index_in_dim(part, 1, axis, keepdims=False)
            part = keep + flip(send, bit)
        return part

    bits_a = [1, 2] + high_bits[::-1]
    bits_b = [2, 1] + high_bits[::-1]
    mid = width // 2
    block = jnp.concatenate(
        [token_sum(picked[..., :mid], bits_a), token_sum(picked[..., mid:], bits_b)], axis=-1
    )
    embedded = (
        gathered(block)
        .reshape(2, heads, team // 2, width)
        .transpose(0, 2, 1, 3)
        .reshape(team, heads * width)
    )
    embedded_own = lax.dynamic_slice_in_dim(embedded, rank * own, own, 0).astype(F32)

    normed_in = rms_norm(embedded.astype(F32), gains_full[0]).astype(HALF)
    mixed = dot(normed_in, w_in, ((1,), (0,)), HALF)
    queries, keys_own, values_own = (
        mixed[:, k * head_columns : (k + 1) * head_columns].reshape(team, local_heads, HD)
        for k in range(3)
    )
    offsets = jnp.arange(team)
    query_pos = place * team + offsets
    running = (
        jnp.full((local_heads, team), NEG, F32),
        jnp.zeros((local_heads, team), F32),
        jnp.zeros((local_heads, team, HD), F32),
    )
    earlier = []
    for back in range(1, per_clip):
        earlier.append(lax.ppermute((keys_own, values_own), "blk", index_of(back)))
    running = attend(queries, keys_own, values_own, query_pos, query_pos, running)
    for back in range(1, per_clip):
        keys_now, values_now = earlier[back - 1]
        running = attend(
            queries, keys_now, values_now, query_pos, query_pos - back * team, running
        )
    top_all, total_all, summed = running
    log_total = top_all + jnp.log(total_all)
    attn_heads = (summed / total_all[..., None]).transpose(1, 0, 2).astype(HALF)
    flat_heads = attn_heads.reshape(team, head_columns)
    first = embedded_own + reduced(dot(flat_heads, w_out, ((1,), (1,)), HALF))
    normed_mid = gathered(rms_norm(first, gains_full[1]).astype(HALF))
    hidden_up = dot(normed_mid, w_up, ((1,), (0,)))
    active = jax.nn.gelu(hidden_up).astype(HALF)
    second = first + reduced(dot(active, w_down, ((1,), (1,)), HALF))
    final_in = gathered(rms_norm(second, gains_full[2]).astype(HALF))
    logits = dot(final_in, w_read, ((1,), (0,)))

    def of_team(array):
        return lax.dynamic_slice(array, (clip, place * team), (1, team))[0]

    weight_all = (
        (mask_all == 1) & (jnp.arange(length)[None, :] < clip_lengths[:, None])
    ).astype(F32)
    loss_count = jnp.sum(weight_all)
    weight_of = of_team(weight_all)
    targets_own = of_team(targets_all)
    vocab_local = logits.shape[1]
    column_ids = (head * 2 + side) * vocab_local + jnp.arange(vocab_local)
    match = column_ids[None, :] == targets_own[:, None]
    top_vocab = jnp.max(logits, axis=-1)
    sum_vocab = jnp.sum(jnp.exp(logits - top_vocab[:, None]), axis=-1)
    hit_vocab = jnp.sum(jnp.where(match, logits, 0.0), axis=-1)
    stats = jnp.stack([top_vocab, sum_vocab, hit_vocab])
    steps = [("blk", PAIR)] + [("head", 1 << k) for k in range(heads.bit_length() - 1)]
    for axis, bit in steps:
        pairs = [(i, i ^ bit) for i in range(lax.axis_size(axis))]
        other = lax.ppermute(stats, axis, pairs)
        top = jnp.maximum(stats[0], other[0])
        total = stats[1] * jnp.exp(stats[0] - top) + other[1] * jnp.exp(other[0] - top)
        stats = jnp.stack([top, total, stats[2] + other[2]])
    log_norm = stats[0] + jnp.log(stats[1])
    per_token = (log_norm + ZCOEF * log_norm * log_norm - stats[2]) * weight_of
    loss_part = jnp.sum(per_token) * (rank == 0).astype(F32)

    token_grad = weight_of / loss_count
    probs = jnp.exp(logits - log_norm[:, None])
    grad_logits = (
        token_grad[:, None]
        * (probs * (1.0 + 2.0 * ZCOEF * log_norm)[:, None] - match.astype(F32))
    ).astype(HALF)

    def weight_grad(left, right):
        split = left.reshape(team, highs, 2, 2, rows)

        def part(at):
            chosen = lax.dynamic_index_in_dim(split, at, 3, keepdims=False)
            made = dot(chosen.reshape(team, highs * 2 * rows), right, ((0,), (0,)))
            return made.reshape((2,) * len(high_bits) + (2, rows, right.shape[1]))

        came = flip(part(1 - low).astype(HALF), 1)
        total = part(low) + came.astype(F32)
        for bit in high_bits[::-1]:
            at = (blk // bit) % 2
            send = lax.dynamic_index_in_dim(total, 1 - at, 0, keepdims=False)
            keep = lax.dynamic_index_in_dim(total, at, 0, keepdims=False)
            total = keep + flip(send.astype(HALF), bit).astype(F32)
        send = lax.dynamic_index_in_dim(total, 1 - side, 0, keepdims=False)
        keep = lax.dynamic_index_in_dim(total, side, 0, keepdims=False)
        came = flip(send.astype(HALF), PAIR).astype(F32)
        return jnp.where(
            side == 0, jnp.stack([keep, came], axis=1), jnp.stack([came, keep], axis=1)
        )

    grad_final = reduced(dot(grad_logits, w_read, ((1,), (1,)), HALF))
    grad_read = weight_grad(final_in, grad_logits)
    grad_second, gain_final = norm_back(second, gains_full[2], grad_final)
    branch_grad = gathered(grad_second.astype(HALF))
    grad_active = dot(branch_grad, w_down, ((1,), (0,)))
    unused_gelu, gelu_pull = jax.vjp(jax.nn.gelu, hidden_up)
    grad_hidden = gelu_pull(grad_active)[0].astype(HALF)
    grad_mid = reduced(dot(grad_hidden, w_up, ((1,), (1,)), HALF))
    grad_down = weight_grad(branch_grad, active)
    grad_up = weight_grad(normed_mid, grad_hidden)
    grad_mid_in, gain_mid = norm_back(first, gains_full[1], grad_mid)
    grad_first = grad_second + grad_mid_in
    attn_grad = gathered(grad_first.astype(HALF))
    grad_heads = dot(attn_grad, w_out, ((1,), (0,)), HALF).reshape(team, local_heads, HD)
    grad_out_w = weight_grad(attn_grad, flat_heads)
    inner = jnp.einsum("qhd,qhd->hq", grad_heads, attn_heads, preferred_element_type=F32)
    returned = []
    grad_query = jnp.zeros((), F32)
    for back in range(1, per_clip):
        keys_now, values_now = earlier[back - 1]
        more_query, far_keys, far_values = attend_back(
            queries,
            keys_now,
            values_now,
            query_pos,
            query_pos - back * team,
            grad_heads,
            log_total,
            inner,
        )
        grad_query = grad_query + more_query
        returned.append(
            lax.ppermute(
                (far_keys.astype(HALF), far_values.astype(HALF)), "blk", index_of(-back)
            )
        )
    more_query, grad_keys, grad_values = attend_back(
        queries, keys_own, values_own, query_pos, query_pos, grad_heads, log_total, inner
    )
    grad_query = grad_query + more_query
    for far_keys, far_values in returned:
        grad_keys = grad_keys + far_keys.astype(F32)
        grad_values = grad_values + far_values.astype(F32)
    grad_mixed = jnp.concatenate(
        [
            part.astype(HALF).reshape(team, head_columns)
            for part in (grad_query, grad_keys, grad_values)
        ],
        axis=1,
    )
    grad_norm_in = reduced(dot(grad_mixed, w_in, ((1,), (1,)), HALF))
    grad_in = weight_grad(normed_in, grad_mixed)
    grad_embed_in, gain_in = norm_back(embedded_own, gains_full[0], grad_norm_in)
    grad_embed = (grad_first + grad_embed_in).astype(HALF)

    columns_own = lax.all_to_all(grad_embed, "head", 1, 0, tiled=True)

    def token_spread(part, bits):
        pieces = {0: part}
        for bit in bits:
            for mask in list(pieces):
                pieces[mask | bit] = flip(pieces[mask], bit)
        return jnp.concatenate([pieces[mask] for mask in range(blocks)])

    columns_all = jnp.concatenate(
        [
            token_spread(columns_own[:, :mid], bits_a[::-1]),
            token_spread(columns_own[:, mid:], bits_b[::-1]),
        ],
        axis=1,
    )
    grad_table = dot(pick, columns_all, ((0,), (0,)))
    img_sum, code_sum = grad_table[:image_rows], grad_table[image_rows:]

    gain_stack = jnp.stack([gain_in, gain_mid, gain_final])
    gain_parts = jnp.broadcast_to(
        gain_stack.reshape(3, blocks, rows).transpose(1, 0, 2)[:, None],
        (blocks, heads, 3, rows),
    ).reshape(blocks * heads, 3 * rows)
    gain_sum = jnp.sum(lax.all_to_all(gain_parts, both, 0, 0, tiled=True), axis=0).reshape(3, rows)

    in_sum = grad_in.reshape(rows, 2, 3, head_columns).transpose(2, 0, 1, 3).reshape(inward.shape)
    out_sum = grad_out_w.reshape(rows, -1).T
    up_sum = grad_up.reshape(rows, -1)
    down_sum = grad_down.reshape(rows, -1).T
    read_sum = grad_read.reshape(rows, -1)
    sums = [in_sum, out_sum, up_sum, down_sum, img_sum, code_sum, read_sum, gain_sum]
    local_squares = jnp.float32(0.0)
    for shard in sums[:7]:
        local_squares = local_squares + jnp.sum(shard * shard)
    local_squares = local_squares + (head == 0).astype(F32) * jnp.sum(gain_sum * gain_sum)
    mine = jnp.broadcast_to(
        jnp.stack([local_squares, loss_part])[None, :, None], (blocks * heads, 2, 128)
    )
    totals = jnp.sum(lax.all_to_all(mine, both, 0, 0, tiled=True), axis=0)
    grad_norm = jnp.sqrt(totals[0, 0])
    loss_sum = totals[1, 0]
    factor = jnp.minimum(1.0, CLIP / grad_norm)
    spreads = [
        D ** (-0.5),
        (length // 2) ** 0.5 * D ** (-0.5),
        D ** (-0.5),
        FF ** (-0.5),
        0.05,
        0.05,
        2.0 * D ** (-0.5),
    ]
    weights = [inward, outward, expand, contract, image_table, code_table, readout, gains]
    firsts = [
        inward_first,
        outward_first,
        expand_first,
        contract_first,
        image_first,
        code_first,
        readout_first,
        gains_first,
    ]
    seconds = [
        inward_second,
        outward_second,
        expand_second,
        contract_second,
        image_second,
        code_second,
        readout_second,
        gains_second,
    ]
    result = []
    for index in range(8):
        rate = GAIN_RATE if index == 7 else RATE_FACTOR * spreads[index]
        decay = 0.0 if index == 7 else DECAY
        result.extend(
            adamw(weights[index], firsts[index], seconds[index], sums[index] * factor, rate, decay)
        )
    return (*result, loss_sum, loss_count, grad_norm)


def solution(mesh):
    matrices = (
        P(None, "blk", "head"),
        P("head", "blk"),
        P("blk", "head"),
        P("head", "blk"),
        P("blk", "head"),
        P("blk", "head"),
        P("blk", "head"),
        P(None, "blk"),
    )
    tokens = P(None, "blk")
    return jax.shard_map(
        shards,
        mesh=mesh,
        in_specs=matrices * 3 + (tokens, tokens, P(), tokens, tokens),
        out_specs=tuple(spec for spec in matrices for _ in range(3)) + (P(), P(), P()),
        check_vma=False,
    )
```

time: 2760 us -> 1440 us (0.52)
  waiting for transfers between devices: 1970 us -> 667 us
  local copies, waits for them, and re-layouts: 116 us -> 345 us
  blocking collectives: 119 us -> 0 us
  starting transfers between devices: 171 us -> 92 us
  matrix products: 219 us -> 174 us
    reduce_scatter x7 -> x5, waiting for transfers between devices: 823 us -> 153 us  [reduced(): lax.psum_scatter(partial, both, scatter_dimension=0, tiled=True, axis_ind...]
    all_gather x8 -> x5, waiting for transfers between devices: 619 us -> 31.1 us  [gathered(): lax.all_gather(block, both, axis=0, tiled=True, axis_index_groups=teams)]
    psum x5 -> x0, waiting for transfers between devices: 258 us -> none  [head_sum(): lax.psum(partial_sum.astype(jnp.bfloat16), 'head').astype(jnp.float32)]
    ppermute x44 -> x61, waiting for transfers between devices: 266 us -> 483 us  [the longest x54 445 us: flip(): return lax.ppermute(value, 'blk', [(i, i ^ bit) for i in range(count)])]
    unnamed x176 -> x248, local copies, waits for them, and re-layouts: 42.4 us -> 155 us
    ppermute x44 -> x61, starting transfers between devices: 169 us -> 76.3 us  [the longest x54 68.3 us: flip(): return lax.ppermute(value, 'blk', [(i, i ^ bit) for i in range(count)])]
    dynamic_slice x0 -> x22, local copies, waits for them, and re-layouts: none -> 87.1 us  [the longest x7 76.5 us: part(): chosen = lax.dynamic_index_in_dim(split, at, 3, keepdims=False)]
    psum x2 -> x0, blocking collectives: 77.8 us -> none  [the longest x1 39.3 us: shards(): all_squares = lax.psum(local_squares, ('blk', 'head'))]
  transfers between devices with their start and end apart: 65 -> 74, of which waited for: 62 -> 43; matrix products, arithmetic and copies ran while one was open for 10% -> 31% of each run, Pallas kernels for 0% -> 0%
where the time goes in v1:
time: 1440 us; the launch traced here: 1430 us
  waiting for transfers between devices  667 us (46%)
  local copies, waits for them, and re-layouts  345 us (24%)
  matrix products  174 us (12%)
  other arithmetic  127 us (9%)
  starting transfers between devices  92 us (6%)
  between operations  24.2 us (2%)
    ppermute x54, waiting for transfers between devices, flip(): return lax.ppermute(value, 'blk', [(i, i ^ bit) for i in range(count)])  445 us
    unnamed x248, local copies, waits for them, and re-layouts  155 us
    reduce_scatter x5, waiting for transfers between devices, reduced(): lax.psum_scatter(partial, both, scatter_dimension=0, tiled=True, axis_ind...  153 us
    dot_general x22, matrix products, dot(): lax.dot_general(left, right, (dims, ((), ())), preferred_element_type=F32)  135 us
    dynamic_slice x7, local copies, waits for them, and re-layouts, part(): chosen = lax.dynamic_index_in_dim(split, at, 3, keepdims=False)  76.5 us
    ppermute x54, starting transfers between devices, flip(): return lax.ppermute(value, 'blk', [(i, i ^ bit) for i in range(count)])  68.3 us
    reshape x4, local copies, waits for them, and re-layouts, weight_grad(): split = left.reshape(team, highs, 2, 2, rows)  31.3 us
    all_gather x5, waiting for transfers between devices, gathered(): lax.all_gather(block, both, axis=0, tiled=True, axis_index_groups=teams)  31.1 us
  transfers between devices with their start and end apart: 74, of which 43 were waited for; matrix products, arithmetic and copies ran while one was open for 31% of the time, Pallas kernels for 0%

profile of v1, /device:TPU:0, one launch (start us, length us, event | category | flops | bytes accessed | tf_op | source)
XLA Modules:
  0.0 1429.0 jit_solution(3019519504359895358)
XLA Ops:
  36.9 19.0 %collective-permute-done.6 = bf16[2,2,512,256]{3,2,1,0:T(8,128)(2,1)S(1)} collective-permute-done((bf16[2,2,512,256]{3,2,1,0:T(8,128)(2,1)S(1)}, bf16[2,2,512,256]{3,2,1,0:T(8,128)(2,1)S(1)}, u32[]{:S(2)}, u32[]{:S(2)}) %collective-permute-start.6) | collective-permute-done | bytes 1048608 | tf_op jit(solution)/shard_map/ppermute | solution.py:32
  60.0 8.6 collective-permute-done.7
  74.2 13.9 collective-permute-done.8
  96.1 28.8 %collective-permute-done.9 = bf16[256,1024]{1,0:T(8,128)(2,1)S(1)} collective-permute-done((bf16[256,1024]{1,0:T(8,128)(2,1)S(1)}, bf16[256,1024]{1,0:T(8,128)(2,1)S(1)}, u32[]{:S(2)}, u32[]{:S(2)}) %collective-permute-start.9) | collective-permute-done | bytes 524320 | tf_op jit(solution)/shard_map/ppermute | solution.py:32
  126.4 31.8 %collective-permute-done.10 = bf16[2,256,1024]{2,1,0:T(8,128)(2,1)S(1)} collective-permute-done((bf16[2,256,1024]{2,1,0:T(8,128)(2,1)S(1)}, bf16[2,256,1024]{2,1,0:T(8,128)(2,1)S(1)}, u32[]{:S(2)}, u32[]{:S(2)}) %collective-permute-start.10) | collective-permute-done | bytes 1048608 | tf_op jit(solution)/shard_map/ppermute | solution.py:32
  166.6 6.9 collective-permute-done.12
  175.8 11.3 fusion.253
  193.3 7.2 fusion.107
  228.5 49.3 %reduce-scatter.6.cloned.1.call-done = bf16[128,2048]{1,0:T(8,128)(2,1)} async-done(((bf16[1024,2048]{1,0:T(8,128)(2,1)}), bf16[128,2048]{1,0:T(8,128)(2,1)}) %reduce-scatter.6.cloned.1.call-update) | async-done | bytes 524304 | tf_op jit(solution)/shard_map/reduce_scatter | solution.py:160
  291.3 13.4 collective-permute-done.15
  307.2 35.9 %collective-permute-done.19 = bf16[256,1024]{1,0:T(8,128)(2,1)S(1)} collective-permute-done((bf16[256,1024]{1,0:T(8,128)(2,1)}, bf16[256,1024]{1,0:T(8,128)(2,1)S(1)}, u32[]{:S(2)}, u32[]{:S(2)}) %collective-permute-start.19) | collective-permute-done | bytes 524320 | tf_op jit(solution)/shard_map/ppermute | solution.py:32
  354.0 44.5 %collective-permute-done.20 = bf16[2,256,1024]{2,1,0:T(8,128)(2,1)S(1)} collective-permute-done((bf16[2,256,1024]{2,1,0:T(8,128)(2,1)S(1)}, bf16[2,256,1024]{2,1,0:T(8,128)(2,1)S(1)}, u32[]{:S(2)}, u32[]{:S(2)}) %collective-permute-start.20) | collective-permute-done | bytes 1048608 | tf_op jit(solution)/shard_map/ppermute | solution.py:32
  404.1 9.5 collective-permute-done.18
  414.7 21.4 %collective-permute-done.22 = bf16[2,256,1024]{2,1,0:T(8,128)(2,1)S(1)} collective-permute-done((bf16[2,256,1024]{2,1,0:T(8,128)(2,1)S(1)}, bf16[2,256,1024]{2,1,0:T(8,128)(2,1)S(1)}, u32[]{:S(2)}, u32[]{:S(2)}) %collective-permute-start.22) | collective-permute-done | bytes 1048608 | tf_op jit(solution)/shard_map/ppermute | solution.py:32
  437.1 7.5 fusion.260
  446.7 8.5 convolution_convert_fusion.4
  455.3 46.9 %reduce-scatter.8.cloned.1.call-done = bf16[128,2048]{1,0:T(8,128)(2,1)} async-done(((bf16[1024,2048]{1,0:T(8,128)(2,1)}), bf16[128,2048]{1,0:T(8,128)(2,1)}) %reduce-scatter.8.cloned.1.call-update) | async-done | bytes 524304 | tf_op jit(solution)/shard_map/reduce_scatter | solution.py:160
  512.3 16.9 %collective-permute-done.23 = bf16[256,1024]{1,0:T(8,128)(2,1)S(1)} collective-permute-done((bf16[256,1024]{1,0:T(8,128)(2,1)S(1)}, bf16[256,1024]{1,0:T(8,128)(2,1)S(1)}, u32[]{:S(2)}, u32[]{:S(2)}) %collective-permute-start.23) | collective-permute-done | bytes 524320 | tf_op jit(solution)/shard_map/ppermute | solution.py:32
  533.2 42.7 %collective-permute-done.24 = bf16[2,256,1024]{2,1,0:T(8,128)(2,1)} collective-permute-done((bf16[2,256,1024]{2,1,0:T(8,128)(2,1)S(1)}, bf16[2,256,1024]{2,1,0:T(8,128)(2,1)}, u32[]{:S(2)}, u32[]{:S(2)}) %collective-permute-start.24) | collective-permute-done | bytes 1048608 | tf_op jit(solution)/shard_map/ppermute | solution.py:32
  586.1 14.1 collective-permute-done.26
  602.5 7.6 fusion.259
  625.0 8.3 convolution_convert_fusion.3
  633.4 46.2 %reduce-scatter.10.cloned.1.call-done = bf16[128,2048]{1,0:T(8,128)(2,1)} async-done(((bf16[1024,2048]{1,0:T(8,128)(2,1)}), bf16[128,2048]{1,0:T(8,128)(2,1)}) %reduce-scatter.10.cloned.1.call-update) | async-done | bytes 524304 | tf_op jit(solution)/shard_map/reduce_scatter | solution.py:160
  683.9 31.1 %all-gather.12.cloned.1.call-done = bf16[1024,2048]{1,0:T(8,128)(2,1)} async-done(((bf16[128,2048]{1,0:T(8,128)(2,1)}), bf16[1024,2048]{1,0:T(8,128)(2,1)}) %all-gather.12.cloned.1.call-update) | async-done | bytes 4194320 | tf_op jit(solution)/shard_map/all_gather | solution.py:157
  715.0 11.3 fusion.21
  726.3 9.0 convolution_convert_fusion.2
  735.4 7.9 reshape.930
  743.3 11.4 constant_dynamic-slice_fusion.1
  754.7 10.5 copy.620
  772.8 10.4 reduce-scatter.12.cloned.1.call-done
  788.3 11.9 reshape.933
  800.2 9.1 copy.619
  809.3 10.2 collective-permute-done.58
  826.9 6.2 multiply_convert_fusion.3
  833.1 7.8 reshape.924
  840.9 11.4 constant_dynamic-slice_fusion.5
  852.4 10.5 copy.616
  862.9 10.5 copy.615
  883.1 7.8 reshape.927
  890.9 11.4 constant_dynamic-slice_fusion.3
  902.3 10.9 copy.618
  913.2 6.6 fusion.92
  920.3 10.5 copy.617
  935.0 6.7 fusion.147
  958.8 27.9 %collective-permute-done.31 = bf16[1024,2,128]{0,2,1:T(8,128)(2,1)} collective-permute-done((bf16[1024,2,128]{0,2,1:T(8,128)(2,1)}, bf16[1024,2,128]{0,2,1:T(8,128)(2,1)}, u32[]{:S(2)}, u32[]{:S(2)}) %collective-permute-start.31) | collective-permute-done | bytes 524320 | tf_op jit(solution)/shard_map/ppermute | solution.py:395
  986.7 6.3 add_convert_fusion
  999.9 7.9 convolution_convert_fusion.1
  1023.9 10.0 constant_dynamic-slice_fusion.17
  1033.9 10.5 copy.530
  1044.4 10.5 copy.479
  1058.1 27.0 %collective-permute-done.39 = bf16[2,256,1024]{2,1,0:T(8,128)(2,1)} collective-permute-done((bf16[2,256,1024]{2,1,0:T(8,128)(2,1)}, bf16[2,256,1024]{2,1,0:T(8,128)(2,1)}, u32[]{:S(2)}, u32[]{:S(2)}) %collective-permute-start.39) | collective-permute-done | bytes 1048608 | tf_op jit(solution)/shard_map/ppermute | solution.py:32
  1087.7 18.4 %collective-permute-done.42 = bf16[2,256,1024]{2,1,0:T(8,128)(2,1)} collective-permute-done((bf16[2,256,1024]{2,1,0:T(8,128)(2,1)}, bf16[2,256,1024]{2,1,0:T(8,128)(2,1)}, u32[]{:S(2)}, u32[]{:S(2)}) %collective-permute-start.42) | collective-permute-done | bytes 1048608 | tf_op jit(solution)/shard_map/ppermute | solution.py:32
  1109.8 7.8 reshape.921
  1117.6 11.3 constant_dynamic-slice_fusion.6
  1128.9 10.5 copy.614
  1144.8 10.5 copy.613
  1169.4 6.7 collective-permute-done.36
  1182.7 11.3 collective-permute-done.32
  1210.0 24.0 %collective-permute-done.33 = bf16[2,256,768]{2,1,0:T(8,128)(2,1)} collective-permute-done((bf16[2,256,768]{2,1,0:T(8,128)(2,1)}, bf16[2,256,768]{2,1,0:T(8,128)(2,1)}, u32[]{:S(2)}, u32[]{:S(2)}) %collective-permute-start.33) | collective-permute-done | bytes 786464 | tf_op jit(solution)/shard_map/ppermute | solution.py:32
  1271.6 7.4 collective-permute-done.45
  1310.3 11.0 fusion
  1371.2 6.5 multiply_subtract_fusion.3
  1391.3 6.5 multiply_subtract_fusion
  1406.1 6.9 multiply_subtract_fusion.1
  (589 shorter events, 442.4 us)
Async XLA Ops:
  7.2 168.6 %all-gather.6.cloned.1.call-start = ((), (), s32[]{:S(2)}) async-start(), calls=%async_computation.8 | async-start | bytes 4718592 | tf_op jit(solution)/shard_map/all_gather | solution.py:157
  33.5 22.4 %collective-permute-start.6 = (bf16[2,2,512,256]{3,2,1,0:T(8,128)(2,1)S(1)}, bf16[2,2,512,256]{3,2,1,0:T(8,128)(2,1)S(1)}, u32[]{:S(2)}, u32[]{:S(2)}) collective-permute-start(bf16[2,2,512,256]{3,2,1,0:T(8,128)(2,1)S(1)} %slice_bitcast_fusion), channel_id=1, source_target_pairs={{0,8},{4,12},{8,0},{12,4},{16,24},{20,28},{24,16},{28,20},{1,9},{5... | collective-permute-start | bytes 3145736 | tf_op jit(solution)/shard_map/ppermute | solution.py:32
  35.3 24.5 %collective-permute-start.3 = (bf16[2,2,512,256]{3,2,0,1:T(8,128)(2,1)S(1)}, bf16[2,2,512,256]{3,2,0,1:T(8,128)(2,1)S(1)}, u32[]{:S(2)}, u32[]{:S(2)}) collective-permute-start(bf16[2,2,512,256]{3,2,0,1:T(8,128)(2,1)S(1)} %bitcast.605), channel_id=1, source_target_pairs={{0,4},{4,0},{8,12},{12,8},{16,20},{20,16},{24,28},{28,24},{1,5},{5... | collective-permute-start | bytes 3145736 | tf_op jit(solution)/shard_map/ppermute | solution.py:32
  56.0 12.7 collective-permute-start.7
  68.8 19.3 %collective-permute-start.8 = (bf16[512,256]{1,0:T(8,128)(2,1)S(1)}, bf16[512,256]{1,0:T(8,128)(2,1)S(1)}, u32[]{:S(2)}, u32[]{:S(2)}) collective-permute-start(bf16[512,256]{1,0:T(8,128)(2,1)S(1)} %slice_bitcast_fusion.6), channel_id=1, source_target_pairs={{0,16},{4,20},{8,24},{12,28},{16,0},{20,4},{24,8},{28,12},{1,17},{... | collective-permute-start | bytes 786440 | tf_op jit(solution)/shard_map/ppermute | solution.py:32
  70.6 21.4 %collective-permute-start.5 = (bf16[512,256]{1,0:T(8,128)(2,1)S(1)}, bf16[512,256]{1,0:T(8,128)(2,1)S(1)}, u32[]{:S(2)}, u32[]{:S(2)}) collective-permute-start(bf16[512,256]{1,0:T(8,128)(2,1)S(1)} %slice_bitcast_fusion.8), channel_id=1, source_target_pairs={{0,16},{4,20},{8,24},{12,28},{16,0},{20,4},{24,8},{28,12},{1,17},{... | collective-permute-start | bytes 786440 | tf_op jit(solution)/shard_map/ppermute | solution.py:32
  92.9 184.9 %reduce-scatter.6.cloned.1.call-start = ((), (), s32[]{:S(2)}) async-start(), calls=%async_computation.9 | async-start | bytes 4718592 | tf_op jit(solution)/shard_map/reduce_scatter | solution.py:160
  95.8 29.1 %collective-permute-start.9 = (bf16[256,1024]{1,0:T(8,128)(2,1)S(1)}, bf16[256,1024]{1,0:T(8,128)(2,1)S(1)}, u32[]{:S(2)}, u32[]{:S(2)}) collective-permute-start(bf16[256,1024]{1,0:T(8,128)(2,1)S(1)} %bitcast.607), channel_id=1, source_target_pairs={{0,8},{4,12},{8,0},{12,4},{16,24},{20,28},{24,16},{28,20},{1,9},{5... | collective-permute-start | bytes 1572872 | tf_op jit(solution)/shard_map/ppermute | solution.py:32
  125.0 33.2 %collective-permute-start.10 = (bf16[2,256,1024]{2,1,0:T(8,128)(2,1)S(1)}, bf16[2,256,1024]{2,1,0:T(8,128)(2,1)S(1)}, u32[]{:S(2)}, u32[]{:S(2)}) collective-permute-start(bf16[2,256,1024]{2,1,0:T(8,128)(2,1)S(1)} %maximum_select_fusion.5), channel_id=1, source_target_pairs={{0,16},{4,20},{8,24},{12,28},{16,0},{20,4},{24,8},{28,12},{1,17},{... | collective-permute-start | bytes 3145736 | tf_op jit(solution)/shard_map/ppermute | solution.py:32
  125.1 39.3 %collective-permute-start.11 = (bf16[2,256,1024]{2,1,0:T(8,128)(2,1)S(1)}, bf16[2,256,1024]{2,1,0:T(8,128)(2,1)}, u32[]{:S(2)}, u32[]{:S(2)}) collective-permute-start(bf16[2,256,1024]{2,1,0:T(8,128)(2,1)S(1)} %maximum_select_fusion.5), channel_id=1, source_target_pairs={{0,4},{4,0},{8,12},{12,8},{16,20},{20,16},{24,28},{28,24},{1,5},{5... | collective-permute-start | bytes 3145736 | tf_op jit(solution)/shard_map/ppermute | solution.py:32
  158.2 15.3 %collective-permute-start.12 = (bf16[2,256,1024]{2,1,0:T(8,128)(2,1)S(1)}, bf16[2,256,1024]{2,1,0:T(8,128)(2,1)}, u32[]{:S(2)}, u32[]{:S(2)}) collective-permute-start(bf16[2,256,1024]{2,1,0:T(8,128)(2,1)S(1)} %collective-permute-done.10), channel_id=1, source_target_pairs={{0,4},{4,0},{8,12},{12,8},{16,20},{20,16},{24,28},{28,24},{1,5},{5... | collective-permute-start | bytes 3145736 | tf_op jit(solution)/shard_map/ppermute | solution.py:32
  205.7 14.2 collective-permute-start.14
  228.5 208.7 %all-gather.8.cloned.1.call-start = ((), (), s32[]{:S(2)}) async-start(), calls=%async_computation.10 | async-start | bytes 4718592 | tf_op jit(solution)/shard_map/all_gather | solution.py:157
  281.5 220.7 %reduce-scatter.8.cloned.1.call-start = ((), (), s32[]{:S(2)}) async-start(), calls=%async_computation.11 | async-start | bytes 4718592 | tf_op jit(solution)/shard_map/reduce_scatter | solution.py:160
  286.0 18.7 %collective-permute-start.15 = (bf16[256,1024]{1,0:T(8,128)(2,1)}, bf16[256,1024]{1,0:T(8,128)(2,1)S(1)}, u32[]{:S(2)}, u32[]{:S(2)}) collective-permute-start(bf16[256,1024]{1,0:T(8,128)(2,1)} %bitcast.63), channel_id=1, source_target_pairs={{0,8},{4,12},{8,0},{12,4},{16,24},{20,28},{24,16},{28,20},{1,9},{5... | collective-permute-start | bytes 1572872 | tf_op jit(solution)/shard_map/ppermute | solution.py:32
  289.7 53.4 %collective-permute-start.19 = (bf16[256,1024]{1,0:T(8,128)(2,1)}, bf16[256,1024]{1,0:T(8,128)(2,1)S(1)}, u32[]{:S(2)}, u32[]{:S(2)}) collective-permute-start(bf16[256,1024]{1,0:T(8,128)(2,1)} %bitcast.78), channel_id=1, source_target_pairs={{0,8},{4,12},{8,0},{12,4},{16,24},{20,28},{24,16},{28,20},{1,9},{5... | collective-permute-start | bytes 1572872 | tf_op jit(solution)/shard_map/ppermute | solution.py:32
  304.9 48.1 %collective-permute-start.16 = (bf16[2,256,1024]{2,1,0:T(8,128)(2,1)S(1)}, bf16[2,256,1024]{2,1,0:T(8,128)(2,1)S(1)}, u32[]{:S(2)}, u32[]{:S(2)}) collective-permute-start(bf16[2,256,1024]{2,1,0:T(8,128)(2,1)S(1)} %maximum_select_fusion.7), channel_id=1, source_target_pairs={{0,16},{4,20},{8,24},{12,28},{16,0},{20,4},{24,8},{28,12},{1,17},{... | collective-permute-start | bytes 3145736 | tf_op jit(solution)/shard_map/ppermute | solution.py:32
  343.3 55.2 %collective-permute-start.20 = (bf16[2,256,1024]{2,1,0:T(8,128)(2,1)S(1)}, bf16[2,256,1024]{2,1,0:T(8,128)(2,1)S(1)}, u32[]{:S(2)}, u32[]{:S(2)}) collective-permute-start(bf16[2,256,1024]{2,1,0:T(8,128)(2,1)S(1)} %maximum_select_fusion.9), channel_id=1, source_target_pairs={{0,16},{4,20},{8,24},{12,28},{16,0},{20,4},{24,8},{28,12},{1,17},{... | collective-permute-start | bytes 3145736 | tf_op jit(solution)/shard_map/ppermute | solution.py:32
  343.4 58.6 %collective-permute-start.17 = (bf16[2,256,1024]{2,1,0:T(8,128)(2,1)S(1)}, bf16[2,256,1024]{2,1,0:T(8,128)(2,1)S(1)}, u32[]{:S(2)}, u32[]{:S(2)}) collective-permute-start(bf16[2,256,1024]{2,1,0:T(8,128)(2,1)S(1)} %maximum_select_fusion.7), channel_id=1, source_target_pairs={{0,4},{4,0},{8,12},{12,8},{16,20},{20,16},{24,28},{28,24},{1,5},{5... | collective-permute-start | bytes 3145736 | tf_op jit(solution)/shard_map/ppermute | solution.py:32
  344.5 58.5 %collective-permute-start.21 = (bf16[2,256,1024]{2,1,0:T(8,128)(2,1)S(1)}, bf16[2,256,1024]{2,1,0:T(8,128)(2,1)S(1)}, u32[]{:S(2)}, u32[]{:S(2)}) collective-permute-start(bf16[2,256,1024]{2,1,0:T(8,128)(2,1)S(1)} %maximum_select_fusion.9), channel_id=1, source_target_pairs={{0,4},{4,0},{8,12},{12,8},{16,20},{20,16},{24,28},{28,24},{1,5},{5... | collective-permute-start | bytes 3145736 | tf_op jit(solution)/shard_map/ppermute | solution.py:32
  353.0 60.7 %collective-permute-start.18 = (bf16[2,256,1024]{2,1,0:T(8,128)(2,1)S(1)}, bf16[2,256,1024]{2,1,0:T(8,128)(2,1)S(1)}, u32[]{:S(2)}, u32[]{:S(2)}) collective-permute-start(bf16[2,256,1024]{2,1,0:T(8,128)(2,1)S(1)} %collective-permute-done.16), channel_id=1, source_target_pairs={{0,4},{4,0},{8,12},{12,8},{16,20},{20,16},{24,28},{28,24},{1,5},{5... | collective-permute-start | bytes 3145736 | tf_op jit(solution)/shard_map/ppermute | solution.py:32
  398.5 37.6 %collective-permute-start.22 = (bf16[2,256,1024]{2,1,0:T(8,128)(2,1)S(1)}, bf16[2,256,1024]{2,1,0:T(8,128)(2,1)S(1)}, u32[]{:S(2)}, u32[]{:S(2)}) collective-permute-start(bf16[2,256,1024]{2,1,0:T(8,128)(2,1)S(1)} %collective-permute-done.20), channel_id=1, source_target_pairs={{0,4},{4,0},{8,12},{12,8},{16,20},{20,16},{24,28},{28,24},{1,5},{5... | collective-permute-start | bytes 3145736 | tf_op jit(solution)/shard_map/ppermute | solution.py:32
  455.2 147.2 %all-gather.10.cloned.1.call-start = ((), (), s32[]{:S(2)}) async-start(), calls=%async_computation.12 | async-start | bytes 4718592 | tf_op jit(solution)/shard_map/all_gather | solution.py:157
  504.7 174.9 %reduce-scatter.10.cloned.1.call-start = ((), (), s32[]{:S(2)}) async-start(), calls=%async_computation.13 | async-start | bytes 4718592 | tf_op jit(solution)/shard_map/reduce_scatter | solution.py:160
  510.0 19.2 %collective-permute-start.23 = (bf16[256,1024]{1,0:T(8,128)(2,1)S(1)}, bf16[256,1024]{1,0:T(8,128)(2,1)S(1)}, u32[]{:S(2)}, u32[]{:S(2)}) collective-permute-start(bf16[256,1024]{1,0:T(8,128)(2,1)S(1)} %bitcast.608), channel_id=1, source_target_pairs={{0,8},{4,12},{8,0},{12,4},{16,24},{20,28},{24,16},{28,20},{1,9},{5... | collective-permute-start | bytes 1572872 | tf_op jit(solution)/shard_map/ppermute | solution.py:32
  529.4 46.5 %collective-permute-start.24 = (bf16[2,256,1024]{2,1,0:T(8,128)(2,1)S(1)}, bf16[2,256,1024]{2,1,0:T(8,128)(2,1)}, u32[]{:S(2)}, u32[]{:S(2)}) collective-permute-start(bf16[2,256,1024]{2,1,0:T(8,128)(2,1)S(1)} %maximum_select_fusion.11), channel_id=1, source_target_pairs={{0,16},{4,20},{8,24},{12,28},{16,0},{20,4},{24,8},{28,12},{1,17},{... | collective-permute-start | bytes 3145736 | tf_op jit(solution)/shard_map/ppermute | solution.py:32
  531.4 52.5 %collective-permute-start.25 = (bf16[2,256,1024]{2,1,0:T(8,128)(2,1)S(1)}, bf16[2,256,1024]{2,1,0:T(8,128)(2,1)}, u32[]{:S(2)}, u32[]{:S(2)}) collective-permute-start(bf16[2,256,1024]{2,1,0:T(8,128)(2,1)S(1)} %maximum_select_fusion.11), channel_id=1, source_target_pairs={{0,4},{4,0},{8,12},{12,8},{16,20},{20,16},{24,28},{28,24},{1,5},{5... | collective-permute-start | bytes 3145736 | tf_op jit(solution)/shard_map/ppermute | solution.py:32
  575.8 24.3 %collective-permute-start.26 = (bf16[2,256,1024]{2,1,0:T(8,128)(2,1)}, bf16[2,256,1024]{2,1,0:T(8,128)(2,1)}, u32[]{:S(2)}, u32[]{:S(2)}) collective-permute-start(bf16[2,256,1024]{2,1,0:T(8,128)(2,1)} %collective-permute-done.24), channel_id=1, source_target_pairs={{0,4},{4,0},{8,12},{12,8},{16,20},{20,16},{24,28},{28,24},{1,5},{5... | collective-permute-start | bytes 3145736 | tf_op jit(solution)/shard_map/ppermute | solution.py:32
  633.4 81.6 %all-gather.12.cloned.1.call-start = ((), (), s32[]{:S(2)}) async-start(), calls=%async_computation.14 | async-start | bytes 4718592 | tf_op jit(solution)/shard_map/all_gather | solution.py:157
  683.7 99.4 %reduce-scatter.12.cloned.1.call-start = ((), (), s32[]{:S(2)}) async-start(), calls=%async_computation.15 | async-start | bytes 4718592 | tf_op jit(solution)/shard_map/reduce_scatter | solution.py:160
  735.4 195.5 %all-gather.14.cloned.1.call-start = ((), (), s32[]{:S(2)}) async-start(), calls=%async_computation.16 | async-start | bytes 4718592 | tf_op jit(solution)/shard_map/all_gather | solution.py:157
  771.3 48.1 %collective-permute-start.58 = (bf16[2,2,256,1024]{3,2,1,0:T(8,128)(2,1)}, bf16[2,2,256,1024]{3,2,1,0:T(8,128)(2,1)}, u32[]{:S(2)}, u32[]{:S(2)}) collective-permute-start(bf16[2,2,256,1024]{3,2,1,0:T(8,128)(2,1)} %fusion.97), channel_id=1, source_target_pairs={{0,4},{4,0},{8,12},{12,8},{16,20},{20,16},{24,28},{28,24},{1,5},{5... | collective-permute-start | bytes 6291464 | tf_op jit(solution)/shard_map/ppermute | solution.py:32
  788.0 413.4 %reduce-scatter.14.cloned.1.call-start = ((), (), s32[]{:S(2)}) async-start(), calls=%async_computation.17 | async-start | bytes 4718592 | tf_op jit(solution)/shard_map/reduce_scatter | solution.py:160
  824.4 49.0 %collective-permute-start.59 = (bf16[2,256,1024]{2,1,0:T(8,128)(2,1)S(1)}, bf16[2,256,1024]{2,1,0:T(8,128)(2,1)}, u32[]{:S(2)}, u32[]{:S(2)}) collective-permute-start(bf16[2,256,1024]{2,1,0:T(8,128)(2,1)S(1)} %fusion.169), channel_id=1, source_target_pairs={{0,16},{4,20},{8,24},{12,28},{16,0},{20,4},{24,8},{28,12},{1,17},{... | collective-permute-start | bytes 3145736 | tf_op jit(solution)/shard_map/ppermute | solution.py:32
  876.8 178.8 %collective-permute-start.60 = (bf16[256,1024]{1,0:T(8,128)(2,1)}, bf16[256,1024]{1,0:T(8,128)(2,1)}, u32[]{:S(2)}, u32[]{:S(2)}) collective-permute-start(bf16[256,1024]{1,0:T(8,128)(2,1)} %fusion.185), channel_id=1, source_target_pairs={{0,8},{4,12},{8,0},{12,4},{16,24},{20,28},{24,16},{28,20},{1,9},{5... | collective-permute-start | bytes 1572872 | tf_op jit(solution)/shard_map/ppermute | solution.py:32
  881.6 126.2 %collective-permute-start.38 = (bf16[2,2,256,1024]{3,2,1,0:T(8,128)(2,1)}, bf16[2,2,256,1024]{3,2,1,0:T(8,128)(2,1)}, u32[]{:S(2)}, u32[]{:S(2)}) collective-permute-start(bf16[2,2,256,1024]{3,2,1,0:T(8,128)(2,1)} %fusion.87), channel_id=1, source_target_pairs={{0,4},{4,0},{8,12},{12,8},{16,20},{20,16},{24,28},{28,24},{1,5},{5... | collective-permute-start | bytes 6291464 | tf_op jit(solution)/shard_map/ppermute | solution.py:32
  919.8 96.4 %collective-permute-start.41 = (bf16[2,2,256,1024]{3,2,1,0:T(8,128)(2,1)}, bf16[2,2,256,1024]{3,2,1,0:T(8,128)(2,1)}, u32[]{:S(2)}, u32[]{:S(2)}) collective-permute-start(bf16[2,2,256,1024]{3,2,1,0:T(8,128)(2,1)} %fusion.92), channel_id=1, source_target_pairs={{0,4},{4,0},{8,12},{12,8},{16,20},{20,16},{24,28},{28,24},{1,5},{5... | collective-permute-start | bytes 6291464 | tf_op jit(solution)/shard_map/ppermute | solution.py:32
  941.7 45.0 %collective-permute-start.31 = (bf16[1024,2,128]{0,2,1:T(8,128)(2,1)}, bf16[1024,2,128]{0,2,1:T(8,128)(2,1)}, u32[]{:S(2)}, u32[]{:S(2)}) collective-permute-start(bf16[1024,2,128]{0,2,1:T(8,128)(2,1)} %fusion.147), channel_id=1, source_target_pairs={{4,0},{12,8},{20,16},{28,24},{5,1},{13,9},{21,17},{29,25},{6,2},{1... | collective-permute-start | bytes 1572872 | tf_op jit(solution)/shard_map/ppermute | solution.py:395
  954.6 41.3 %collective-permute-start.30 = (bf16[1024,2,128]{0,2,1:T(8,128)(2,1)}, bf16[1024,2,128]{0,2,1:T(8,128)(2,1)}, u32[]{:S(2)}, u32[]{:S(2)}) collective-permute-start(bf16[1024,2,128]{0,2,1:T(8,128)(2,1)} %fusion.150), channel_id=1, source_target_pairs={{4,0},{12,8},{20,16},{28,24},{5,1},{13,9},{21,17},{29,25},{6,2},{1... | collective-permute-start | bytes 1572872 | tf_op jit(solution)/shard_map/ppermute | solution.py:395
  1014.4 70.8 %collective-permute-start.39 = (bf16[2,256,1024]{2,1,0:T(8,128)(2,1)}, bf16[2,256,1024]{2,1,0:T(8,128)(2,1)}, u32[]{:S(2)}, u32[]{:S(2)}) collective-permute-start(bf16[2,256,1024]{2,1,0:T(8,128)(2,1)} %fusion.167), channel_id=1, source_target_pairs={{0,16},{4,20},{8,24},{12,28},{16,0},{20,4},{24,8},{28,12},{1,17},{... | collective-permute-start | bytes 3145736 | tf_op jit(solution)/shard_map/ppermute | solution.py:32
  1022.0 84.2 %collective-permute-start.42 = (bf16[2,256,1024]{2,1,0:T(8,128)(2,1)}, bf16[2,256,1024]{2,1,0:T(8,128)(2,1)}, u32[]{:S(2)}, u32[]{:S(2)}) collective-permute-start(bf16[2,256,1024]{2,1,0:T(8,128)(2,1)} %fusion.168), channel_id=1, source_target_pairs={{0,16},{4,20},{8,24},{12,28},{16,0},{20,4},{24,8},{28,12},{1,17},{... | collective-permute-start | bytes 3145736 | tf_op jit(solution)/shard_map/ppermute | solution.py:32
  1087.7 54.9 %collective-permute-start.40 = (bf16[256,1024]{1,0:T(8,128)(2,1)}, bf16[256,1024]{1,0:T(8,128)(2,1)}, u32[]{:S(2)}, u32[]{:S(2)}) collective-permute-start(bf16[256,1024]{1,0:T(8,128)(2,1)} %fusion.183), channel_id=1, source_target_pairs={{0,8},{4,12},{8,0},{12,4},{16,24},{20,28},{24,16},{28,20},{1,9},{5... | collective-permute-start | bytes 1572872 | tf_op jit(solution)/shard_map/ppermute | solution.py:32
  1108.7 57.2 %collective-permute-start.43 = (bf16[256,1024]{1,0:T(8,128)(2,1)}, bf16[256,1024]{1,0:T(8,128)(2,1)}, u32[]{:S(2)}, u32[]{:S(2)}) collective-permute-start(bf16[256,1024]{1,0:T(8,128)(2,1)} %fusion.184), channel_id=1, source_target_pairs={{0,8},{4,12},{8,0},{12,4},{16,24},{20,28},{24,16},{28,20},{1,9},{5... | collective-permute-start | bytes 1572872 | tf_op jit(solution)/shard_map/ppermute | solution.py:32
  1142.6 18.7 %collective-permute-start.35 = (bf16[2,2,256,256]{2,3,1,0:T(8,128)(2,1)}, bf16[2,2,256,256]{2,3,1,0:T(8,128)(2,1)}, u32[]{:S(2)}, u32[]{:S(2)}) collective-permute-start(bf16[2,2,256,256]{2,3,1,0:T(8,128)(2,1)} %fusion.138), channel_id=1, source_target_pairs={{0,4},{4,0},{8,12},{12,8},{16,20},{20,16},{24,28},{28,24},{1,5},{5... | collective-permute-start | bytes 1572872 | tf_op jit(solution)/shard_map/ppermute | solution.py:32
  1159.2 34.9 %collective-permute-start.32 = (bf16[2,2,256,768]{3,2,1,0:T(8,128)(2,1)S(1)}, bf16[2,2,256,768]{3,2,1,0:T(8,128)(2,1)S(1)}, u32[]{:S(2)}, u32[]{:S(2)}) collective-permute-start(bf16[2,2,256,768]{3,2,1,0:T(8,128)(2,1)S(1)} %fusion.104), channel_id=1, source_target_pairs={{0,4},{4,0},{8,12},{12,8},{16,20},{20,16},{24,28},{28,24},{1,5},{5... | collective-permute-start | bytes 4718600 | tf_op jit(solution)/shard_map/ppermute | solution.py:32
  1163.2 13.0 collective-permute-start.36
  1198.5 35.5 %collective-permute-start.33 = (bf16[2,256,768]{2,1,0:T(8,128)(2,1)}, bf16[2,256,768]{2,1,0:T(8,128)(2,1)}, u32[]{:S(2)}, u32[]{:S(2)}) collective-permute-start(bf16[2,256,768]{2,1,0:T(8,128)(2,1)} %fusion.181), channel_id=1, source_target_pairs={{0,16},{4,20},{8,24},{12,28},{16,0},{20,4},{24,8},{28,12},{1,17},{... | collective-permute-start | bytes 2359304 | tf_op jit(solution)/shard_map/ppermute | solution.py:32
  1205.9 32.8 %all-to-all-start = ((bf16[128,4,512]{2,0,1:T(8,128)(2,1)}), bf16[128,4,512]{2,0,1:T(8,128)(2,1)}, u32[]{:S(2)}, u32[]{:S(2)}) async-start(bf16[128,4,512]{2,0,1:T(8,128)(2,1)} %bitcast.602), calls=%async_computation.5 | async-start | bytes 1048576 | tf_op jit(solution)/shard_map/all_to_all | solution.py:418
  1237.8 13.0 collective-permute-start.34
  1238.6 22.7 %all-to-all-start.1 = ((f32[32,1,768]{2,1,0:T(1,128)}), f32[32,1,768]{2,1,0:T(1,128)S(1)}, u32[]{:S(2)}, u32[]{:S(2)}) async-start(f32[32,1,768]{2,1,0:T(1,128)} %all_to_all.30), calls=%async_computation.6 | async-start | bytes 196608 | tf_op jit(solution)/shard_map/all_to_all | solution.py:442
  1245.7 19.1 %collective-permute-start.51 = (bf16[512,256]{1,0:T(8,128)(2,1)}, bf16[512,256]{1,0:T(8,128)(2,1)}, u32[]{:S(2)}, u32[]{:S(2)}) collective-permute-start(bf16[512,256]{1,0:T(8,128)(2,1)} %get-tuple-element.231), channel_id=1, source_target_pairs={{0,4},{4,0},{8,12},{12,8},{16,20},{20,16},{24,28},{28,24},{1,5},{5... | collective-permute-start | bytes 786440 | tf_op jit(solution)/shard_map/ppermute | solution.py:32
  1252.8 15.3 %collective-permute-start.54 = (bf16[512,256]{1,0:T(8,128)(2,1)}, bf16[512,256]{1,0:T(8,128)(2,1)}, u32[]{:S(2)}, u32[]{:S(2)}) collective-permute-start(bf16[512,256]{1,0:T(8,128)(2,1)} %get-tuple-element.231), channel_id=1, source_target_pairs={{0,16},{4,20},{8,24},{12,28},{16,0},{20,4},{24,8},{28,12},{1,17},{... | collective-permute-start | bytes 786440 | tf_op jit(solution)/shard_map/ppermute | solution.py:32
  1255.2 13.3 collective-permute-start.44
  1261.4 17.7 %collective-permute-start.45 = (bf16[512,256]{1,0:T(8,128)(2,1)}, bf16[512,256]{1,0:T(8,128)(2,1)}, u32[]{:S(2)}, u32[]{:S(2)}) collective-permute-start(bf16[512,256]{1,0:T(8,128)(2,1)} %get-tuple-element.228), channel_id=1, source_target_pairs={{0,8},{4,12},{8,0},{12,4},{16,24},{20,28},{24,16},{28,20},{1,9},{5... | collective-permute-start | bytes 786440 | tf_op jit(solution)/shard_map/ppermute | solution.py:32
  1264.2 20.3 %collective-permute-start.52 = (bf16[512,256]{1,0:T(8,128)(2,1)}, bf16[512,256]{1,0:T(8,128)(2,1)S(1)}, u32[]{:S(2)}, u32[]{:S(2)}) collective-permute-start(bf16[512,256]{1,0:T(8,128)(2,1)} %get-tuple-element.231), channel_id=1, source_target_pairs={{0,8},{4,12},{8,0},{12,4},{16,24},{20,28},{24,16},{28,20},{1,9},{5... | collective-permute-start | bytes 786440 | tf_op jit(solution)/shard_map/ppermute | solution.py:32
  1264.8 20.1 %collective-permute-start.47 = (bf16[512,256]{1,0:T(8,128)(2,1)}, bf16[512,256]{1,0:T(8,128)(2,1)S(1)}, u32[]{:S(2)}, u32[]{:S(2)}) collective-permute-start(bf16[512,256]{1,0:T(8,128)(2,1)} %get-tuple-element.228), channel_id=1, source_target_pairs={{0,16},{4,20},{8,24},{12,28},{16,0},{20,4},{24,8},{28,12},{1,17},{... | collective-permute-start | bytes 786440 | tf_op jit(solution)/shard_map/ppermute | solution.py:32
  1268.1 22.0 %collective-permute-start.53 = (bf16[512,256]{1,0:T(8,128)(2,1)}, bf16[512,256]{1,0:T(8,128)(2,1)S(1)}, u32[]{:S(2)}, u32[]{:S(2)}) collective-permute-start(bf16[512,256]{1,0:T(8,128)(2,1)} %collective-permute-done.51), channel_id=1, source_target_pairs={{0,8},{4,12},{8,0},{12,4},{16,24},{20,28},{24,16},{28,20},{1,9},{5... | collective-permute-start | bytes 786440 | tf_op jit(solution)/shard_map/ppermute | solution.py:32
  1268.5 21.7 %collective-permute-start.55 = (bf16[512,256]{1,0:T(8,128)(2,1)}, bf16[512,256]{1,0:T(8,128)(2,1)S(1)}, u32[]{:S(2)}, u32[]{:S(2)}) collective-permute-start(bf16[512,256]{1,0:T(8,128)(2,1)} %collective-permute-done.54), channel_id=1, source_target_pairs={{0,4},{4,0},{8,12},{12,8},{16,20},{20,16},{24,28},{28,24},{1,5},{5... | collective-permute-start | bytes 786440 | tf_op jit(solution)/shard_map/ppermute | solution.py:32
  1279.0 24.2 %collective-permute-start.56 = (bf16[512,256]{1,0:T(8,128)(2,1)}, bf16[512,256]{1,0:T(8,128)(2,1)S(1)}, u32[]{:S(2)}, u32[]{:S(2)}) collective-permute-start(bf16[512,256]{1,0:T(8,128)(2,1)} %collective-permute-done.54), channel_id=1, source_target_pairs={{0,8},{4,12},{8,0},{12,4},{16,24},{20,28},{24,16},{28,20},{1,9},{5... | collective-permute-start | bytes 786440 | tf_op jit(solution)/shard_map/ppermute | solution.py:32
  1284.6 10.8 collective-permute-start.46
  1284.9 16.9 %collective-permute-start.48 = (bf16[512,256]{1,0:T(8,128)(2,1)S(1)}, bf16[512,256]{1,0:T(8,128)(2,1)S(1)}, u32[]{:S(2)}, u32[]{:S(2)}) collective-permute-start(bf16[512,256]{1,0:T(8,128)(2,1)S(1)} %collective-permute-done.47), channel_id=1, source_target_pairs={{0,4},{4,0},{8,12},{12,8},{16,20},{20,16},{24,28},{28,24},{1,5},{5... | collective-permute-start | bytes 786440 | tf_op jit(solution)/shard_map/ppermute | solution.py:32
  1290.2 11.2 collective-permute-start.49
  1290.2 16.8 %collective-permute-start.57 = (bf16[512,256]{1,0:T(8,128)(2,1)S(1)}, bf16[512,256]{1,0:T(8,128)(2,1)S(1)}, u32[]{:S(2)}, u32[]{:S(2)}) collective-permute-start(bf16[512,256]{1,0:T(8,128)(2,1)S(1)} %collective-permute-done.55), channel_id=1, source_target_pairs={{0,8},{4,12},{8,0},{12,4},{16,24},{20,28},{24,16},{28,20},{1,9},{5... | collective-permute-start | bytes 786440 | tf_op jit(solution)/shard_map/ppermute | solution.py:32
  1326.1 22.4 %all-to-all-start.2 = ((f32[32,2,128]{2,1,0:T(2,128)}), f32[32,2,128]{2,1,0:T(2,128)S(1)}, u32[]{:S(2)}, u32[]{:S(2)}) async-start(f32[32,2,128]{2,1,0:T(2,128)} %broadcast_in_dim.171), calls=%async_computation.7 | async-start | bytes 65536 | tf_op jit(solution)/shard_map/all_to_all | solution.py:457
  (105 other events, 979.6 us)
Sparse Core Ops, SparseCore 0:
  93.0 44.2 all-gather.5
  228.6 49.1 reduce-scatter.5
  281.6 63.6 all-gather.7
  455.4 46.7 reduce-scatter.7
  504.8 48.0 all-gather.9
  633.5 46.0 reduce-scatter.9
  683.8 31.1 all-gather.11
  735.5 47.6 reduce-scatter.11
  788.1 30.9 all-gather.13
  1008.0 59.9 reduce-scatter.13

commit v2 on v1

--- a/solution.py
+++ b/solution.py
@@ -1,6 +1,9 @@
 import jax
 import jax.numpy as jnp
 from jax import lax
+from jax.experimental import pallas as pl
+from jax.experimental.layout import Layout, with_layout_constraint
+from jax.experimental.pallas import tpu as pltpu
 from jax.sharding import PartitionSpec as P
 
 D = 2048
@@ -91,6 +94,103 @@
         "hqk,qhd->khd", grad_scores, queries, preferred_element_type=F32
     )
     return (grad_query, grad_keys, grad_values)
+
+
+def joined_norm_kernel(blocks_ref, gain_ref, out_ref):
+    count, unused, width = blocks_ref.shape
+    parts = [blocks_ref[k].astype(F32) for k in range(count)]
+    squares = sum(jnp.sum(part * part, axis=-1, keepdims=True) for part in parts)
+    scale = lax.rsqrt(squares / (count * width) + EPS)
+    for k, part in enumerate(parts):
+        at = slice(k * width, (k + 1) * width)
+        out_ref[:, at] = (part * scale * gain_ref[:, at]).astype(HALF)
+
+
+def joined_norm(blocks, gain, count):
+    total, tokens, width = blocks.shape
+    sides, step = total // count, min(tokens, 128)
+    steps = tokens // step
+    return pl.pallas_call(
+        joined_norm_kernel,
+        grid=(sides, steps),
+        in_specs=[
+            pl.BlockSpec((count, step, width), lambda s, m: (s, m, 0)),
+            pl.BlockSpec((1, count * width), lambda s, m: (0, 0)),
+        ],
+        out_specs=pl.BlockSpec((step, count * width), lambda s, m: (s * steps + m, 0)),
+        out_shape=jax.ShapeDtypeStruct((sides * tokens, count * width), HALF),
+        cost_estimate=pl.CostEstimate(
+            flops=5 * blocks.size, bytes_accessed=4 * blocks.size, transcendentals=0
+        ),
+    )(blocks, gain[None])
+
+
+def table_grad_kernel(count, at_ref, *refs):
+    pieces, out_ref = refs[:-1], refs[-1]
+    split = len(pieces) // count
+    tokens, width = pieces[0].shape
+    step = out_ref.shape[0]
+    row = pl.program_id(0) * step + lax.broadcasted_iota(jnp.int32, (step, tokens), 0)
+    for part in range(split):
+        total = jnp.zeros((step, width), F32)
+        for k in range(count):
+            pick = (row == at_ref[k][None, :]).astype(F32).astype(HALF)
+            total += jnp.dot(
+                pick, pieces[part * count + k][...], preferred_element_type=F32
+            )
+        out_ref[:, part * width : (part + 1) * width] = total
+
+
+def table_grad(at, pieces, rows, step):
+    count, tokens = at.shape
+    width = pieces[0].shape[1]
+    columns = width * len(pieces) // count
+    return pl.pallas_call(
+        lambda *refs: table_grad_kernel(count, *refs),
+        grid=(rows // step,),
+        in_specs=[pl.BlockSpec((count, tokens), lambda i: (0, 0))]
+        + [pl.BlockSpec((tokens, width), lambda i: (0, 0)) for unused in pieces],
+        out_specs=pl.BlockSpec((step, columns), lambda i: (i, 0)),
+        out_shape=jax.ShapeDtypeStruct((rows, columns), F32),
+        compiler_params=pltpu.CompilerParams(vmem_limit_bytes=56 * 2**20),
+        cost_estimate=pl.CostEstimate(
+            flops=2 * rows * count * tokens * columns,
+            bytes_accessed=2 * count * tokens * columns + 4 * rows * columns,
+            transcendentals=0,
+        ),
+    )(at, *pieces)
+
+
+def assembled_kernel(count, at_ref, *refs):
+    pieces, out_ref = refs[:count], refs[count]
+    for k, piece in enumerate(pieces):
+
+        @pl.when(pl.program_id(0) == k)
+        def write():
+            out_ref[0, :, 0] = piece[...]
+
+
+def assembled_at(places, pieces):
+    count = len(pieces)
+    unused, rows, columns = pieces[0].shape
+    grid = pltpu.PrefetchScalarGridSpec(
+        num_scalar_prefetch=1,
+        grid=(count,),
+        in_specs=[pl.BlockSpec((2, rows, columns), lambda i, at: (0, 0, 0)) for piece in pieces],
+        out_specs=pl.BlockSpec(
+            (1, 2, 1, rows, columns), lambda i, at: (at[2 * i], 0, at[2 * i + 1], 0, 0)
+        ),
+    )
+    whole = pl.pallas_call(
+        lambda *refs: assembled_kernel(count, *refs),
+        grid_spec=grid,
+        out_shape=jax.ShapeDtypeStruct((count // 2, 2, 2, rows, columns), HALF),
+        compiler_params=pltpu.CompilerParams(vmem_limit_bytes=40 * 2**20),
+        cost_estimate=pl.CostEstimate(
+            flops=0, bytes_accessed=4 * count * pieces[0].size, transcendentals=0
+        ),
+    )(places, *pieces)
+    return whole.reshape(count * 2 * rows, columns)
 
 
 def shards(
@@ -170,13 +270,34 @@
                 pairs.append((i, (far // 2) * 4 + (i & PAIR) + far % 2))
         return pairs
 
+    def tie(*values):
+        return lax.optimization_barrier(values)
+
+    def sided(weight):
+        return weight.astype(HALF).reshape(rows, 2, -1)
+
+    qkv_local = inward.astype(HALF).reshape(3, rows, 2, -1).transpose(1, 2, 0, 3)
+    local_first = jnp.concatenate(
+        [qkv_local.reshape(rows, 2, -1), sided(outward.astype(HALF).T)], axis=-1
+    )
+    local = [
+        None,
+        sided(expand),
+        sided(contract.astype(HALF).T),
+        sided(readout),
+    ]
+
     small = jnp.concatenate(
         [part.astype(F32).reshape(-1) for part in (token_ids, modality, loss_mask, targets, gains)]
     )[None]
-    for bit in all_bits:
+    small = jnp.concatenate([small, flip(small, PAIR)])
+    local_first, small = tie(local_first, small)
+    masks = [0, PAIR]
+    for bit in high_bits + [1]:
         small = jnp.concatenate([small, flip(small, bit)])
+        masks = masks + [mask | bit for mask in masks]
     order = blk ^ jnp.arange(blocks)
-    small = small[order]
+    small = small[jnp.array([masks.index(mask) for mask in range(blocks)])[order]]
     cells = clips * span
     ids_all, modality_all, mask_all, targets_all = (
         small[:, k * cells : (k + 1) * cells]
@@ -188,42 +309,31 @@
     )
     gains_full = small[:, 4 * cells :].reshape(blocks, 3, rows).transpose(1, 0, 2).reshape(3, D)
 
-    def sided(weight):
-        return weight.astype(HALF).reshape(rows, 2, -1)
-
-    qkv_local = inward.astype(HALF).reshape(3, rows, 2, -1).transpose(1, 2, 0, 3)
-    local = [
-        jnp.concatenate(
-            [qkv_local.reshape(rows, 2, -1), sided(outward.astype(HALF).T)], axis=-1
-        ),
-        sided(expand),
-        sided(contract.astype(HALF).T),
-        sided(readout),
-    ]
-
-    def gathered_weight(halves):
+    def paired(halves):
         keep = lax.dynamic_index_in_dim(halves, side, 1, keepdims=False)
         send = lax.dynamic_index_in_dim(halves, 1 - side, 1, keepdims=False)
         came = flip(send, PAIR)
-        mine = jnp.where(side == 0, jnp.stack([keep, came]), jnp.stack([came, keep]))
-        pieces = {0: mine}
-        for bit in high_bits + [1]:
-            for mask in list(pieces):
-                pieces[mask | bit] = flip(pieces[mask], bit)
-        columns = mine.shape[-1]
-        whole = jnp.zeros((highs, 2, 2, rows, columns), HALF)
-        for mask, piece in pieces.items():
-            whole = lax.dynamic_update_slice(
-                whole,
-                piece[None, :, None],
-                (high ^ (mask >> 2), 0, low ^ (mask & 1), 0, 0),
-            )
-        return whole.reshape(D, columns)
-
-    w_first, w_up, w_down, w_read = [gathered_weight(part) for part in local]
-    head_columns = w_first.shape[-1] // 4
-    w_in, w_out = w_first[:, : 3 * head_columns], w_first[:, 3 * head_columns :]
-    local_heads = head_columns // HD
+        return jnp.where(side == 0, jnp.stack([keep, came]), jnp.stack([came, keep]))
+
+    def spread_high(mine):
+        pieces = [mine]
+        for bit in high_bits:
+            pieces = pieces + [flip(piece, bit) for piece in pieces]
+        return tuple(pieces[1:])
+
+    def spread_low(pieces):
+        return tuple(flip(piece, 1) for piece in pieces)
+
+    def assembled(mine, far, near):
+        pieces = (mine, *far, *near)
+        places = [high ^ (k % highs) if side_at == 0 else low ^ (k // highs)
+                  for k in range(len(pieces)) for side_at in range(2)]
+        return assembled_at(jnp.stack(places).astype(jnp.int32), pieces)
+
+    mine = [paired(local_first), None, None, None]
+    far = [None] * 4
+    near = [None] * 4
+    mine[1] = paired(local[1])
 
     def by_device(array):
         split = array.reshape(highs, 2, 2, team // 2)
@@ -246,32 +356,47 @@
     levels = len(all_bits)
     picked = picked.reshape((2,) * levels + (team // 2, width))
 
-    def token_sum(part, bits):
-        left = sorted(all_bits, reverse=True)
-        for bit in bits:
-            axis = left.index(bit)
-            left.remove(bit)
-            keep = lax.index_in_dim(part, 0, axis, keepdims=False)
-            send = lax.index_in_dim(part, 1, axis, keepdims=False)
-            part = keep + flip(send, bit)
-        return part
-
-    bits_a = [1, 2] + high_bits[::-1]
-    bits_b = [2, 1] + high_bits[::-1]
+    def token_hop(part, bit, left):
+        axis = left.index(bit)
+        keep = lax.index_in_dim(part, 0, axis, keepdims=False)
+        send = lax.index_in_dim(part, 1, axis, keepdims=False)
+        return keep + flip(send, bit)
+
+    left = sorted(all_bits, reverse=True)
     mid = width // 2
-    block = jnp.concatenate(
-        [token_sum(picked[..., :mid], bits_a), token_sum(picked[..., mid:], bits_b)], axis=-1
-    )
-    embedded = (
-        gathered(block)
-        .reshape(2, heads, team // 2, width)
-        .transpose(0, 2, 1, 3)
-        .reshape(team, heads * width)
-    )
-    embedded_own = lax.dynamic_slice_in_dim(embedded, rank * own, own, 0).astype(F32)
-
-    normed_in = rms_norm(embedded.astype(F32), gains_full[0]).astype(HALF)
+    picked, mine[0] = tie(picked, mine[0])
+    far[0] = spread_high(mine[0])
+    part_a = token_hop(picked[..., :mid], 1, left)
+    part_b = token_hop(picked[..., mid:], PAIR, left)
+    part_a = token_hop(part_a, PAIR, left[:-1])
+    part_b = token_hop(part_b, 1, left[:-2] + left[-1:])
+    part_a, part_b, mine[0], mine[1], *far[0] = tie(part_a, part_b, mine[0], mine[1], *far[0])
+    near_own = spread_low(mine[:1])
+    for k, bit in enumerate(high_bits[::-1]):
+        part_a = token_hop(part_a, bit, left[k:-2])
+        part_b = token_hop(part_b, bit, left[k:-2])
+    block = jnp.concatenate([part_a, part_b], axis=-1)
+    block, mine[1], *near_own = tie(block, mine[1], *near_own)
+    far[1] = spread_high(mine[1])
+    near[0] = (*near_own, *spread_low(tie(*far[0], block)[:-1]))
+    near_own = spread_low(tie(mine[1], block)[:1])
+    columns_in = gathered(block).reshape(ranks, team // 2, width)
+    normed_in = joined_norm(columns_in, gains_full[0], heads)
+    embedded_own = (
+        lax.dynamic_slice(columns_in, (side * heads, head * own, 0), (heads, own, width))
+        .transpose(1, 0, 2)
+        .reshape(own, heads * width)
+        .astype(F32)
+    )
+    w_first = assembled(mine[0], far[0], near[0])
+    head_columns = w_first.shape[-1] // 4
+    w_in, w_out = w_first[:, : 3 * head_columns], w_first[:, 3 * head_columns :]
+    local_heads = head_columns // HD
     mixed = dot(normed_in, w_in, ((1,), (0,)), HALF)
+    mixed, mine[1], local[2], local[3], near_own, *far[1] = tie(
+        mixed, mine[1], local[2], local[3], *near_own, *far[1]
+    )
+    mine[2], mine[3] = paired(local[2]), paired(local[3])
     queries, keys_own, values_own = (
         mixed[:, k * head_columns : (k + 1) * head_columns].reshape(team, local_heads, HD)
         for k in range(3)
@@ -287,6 +412,10 @@
     for back in range(1, per_clip):
         earlier.append(lax.ppermute((keys_own, values_own), "blk", index_of(back)))
     running = attend(queries, keys_own, values_own, query_pos, query_pos, running)
+    *far[1], mine[2], earlier = tie(*far[1], mine[2], earlier)
+    near[1] = (near_own, *spread_low(far[1]))
+    far[2] = spread_high(mine[2])
+    near_own = spread_low(mine[2:3])
     for back in range(1, per_clip):
         keys_now, values_now = earlier[back - 1]
         running = attend(
@@ -296,12 +425,22 @@
     log_total = top_all + jnp.log(total_all)
     attn_heads = (summed / total_all[..., None]).transpose(1, 0, 2).astype(HALF)
     flat_heads = attn_heads.reshape(team, head_columns)
+    flat_heads, mine[3] = tie(flat_heads, mine[3])
     first = embedded_own + reduced(dot(flat_heads, w_out, ((1,), (1,)), HALF))
-    normed_mid = gathered(rms_norm(first, gains_full[1]).astype(HALF))
+    w_up = assembled(mine[1], far[1], near[1])
+    first, w_up, mine[3], near_own, *far[2] = tie(first, w_up, mine[3], *near_own, *far[2])
+    far[3] = spread_high(mine[3])
+    near[2] = (near_own, *spread_low(far[2]))
+    normed_mid, *near_2 = tie(gathered(rms_norm(first, gains_full[1]).astype(HALF)), *near[2])
+    w_down = assembled(mine[2], far[2], near_2)
     hidden_up = dot(normed_mid, w_up, ((1,), (0,)))
     active = jax.nn.gelu(hidden_up).astype(HALF)
+    active, mine[3], *far[3] = tie(active, mine[3], *far[3])
+    near[3] = spread_low((mine[3], *far[3]))
     second = first + reduced(dot(active, w_down, ((1,), (1,)), HALF))
-    final_in = gathered(rms_norm(second, gains_full[2]).astype(HALF))
+    second, *near_3 = tie(second, *near[3])
+    w_read = assembled(mine[3], far[3], near_3)
+    final_in, w_read = tie(gathered(rms_norm(second, gains_full[2]).astype(HALF)), w_read)
     logits = dot(final_in, w_read, ((1,), (0,)))
 
     def of_team(array):
@@ -338,46 +477,75 @@
         * (probs * (1.0 + 2.0 * ZCOEF * log_norm)[:, None] - match.astype(F32))
     ).astype(HALF)
 
-    def weight_grad(left, right):
-        split = left.reshape(team, highs, 2, 2, rows)
-
-        def part(at):
-            chosen = lax.dynamic_index_in_dim(split, at, 3, keepdims=False)
-            made = dot(chosen.reshape(team, highs * 2 * rows), right, ((0,), (0,)))
-            return made.reshape((2,) * len(high_bits) + (2, rows, right.shape[1]))
-
-        came = flip(part(1 - low).astype(HALF), 1)
-        total = part(low) + came.astype(F32)
-        for bit in high_bits[::-1]:
+    top_bit = high_bits[-1]
+    top = (blk // top_bit) % 2
+
+    def made_of(left, right):
+        return dot(left, right, ((0,), (0,)), HALF).reshape(
+            2, highs // 2, 2, 2, rows, right.shape[1]
+        )
+
+    def low_part(made, at_top, at_low):
+        chosen = lax.dynamic_index_in_dim(made, at_top, 0, keepdims=False)
+        return lax.dynamic_index_in_dim(chosen, at_low, 2, keepdims=False)
+
+    def send_low(made, at_top):
+        return flip(low_part(made, at_top, 1 - low), 1)
+
+    def add_low(made, at_top, came):
+        return low_part(made, at_top, low).astype(F32) + came.astype(F32)
+
+    def send_high(made, came):
+        return flip(add_low(made, 1 - top, came).astype(HALF), top_bit)
+
+    def add_high(made, came_low, came_high):
+        total = add_low(made, top, came_low) + came_high.astype(F32)
+        total = total.reshape((2,) * (len(high_bits) - 1) + total.shape[1:])
+        for bit in high_bits[-2::-1] if len(high_bits) > 1 else []:
             at = (blk // bit) % 2
             send = lax.dynamic_index_in_dim(total, 1 - at, 0, keepdims=False)
             keep = lax.dynamic_index_in_dim(total, at, 0, keepdims=False)
             total = keep + flip(send.astype(HALF), bit).astype(F32)
+        return total
+
+    def sum_sides(total):
         send = lax.dynamic_index_in_dim(total, 1 - side, 0, keepdims=False)
         keep = lax.dynamic_index_in_dim(total, side, 0, keepdims=False)
         came = flip(send.astype(HALF), PAIR).astype(F32)
-        return jnp.where(
-            side == 0, jnp.stack([keep, came], axis=1), jnp.stack([came, keep], axis=1)
-        )
+        return jnp.where(side == 0, keep, came), jnp.where(side == 0, came, keep)
 
     grad_final = reduced(dot(grad_logits, w_read, ((1,), (1,)), HALF))
-    grad_read = weight_grad(final_in, grad_logits)
+    read_made = made_of(final_in, grad_logits)
+    read_far = send_low(read_made, 1 - top)
+    grad_final, read_made, read_far = tie(grad_final, read_made, read_far)
+    read_near = send_low(read_made, top)
+    read_high = send_high(read_made, read_far)
     grad_second, gain_final = norm_back(second, gains_full[2], grad_final)
     branch_grad = gathered(grad_second.astype(HALF))
+    branch_grad, read_near = tie(branch_grad, read_near)
     grad_active = dot(branch_grad, w_down, ((1,), (0,)))
     unused_gelu, gelu_pull = jax.vjp(jax.nn.gelu, hidden_up)
     grad_hidden = gelu_pull(grad_active)[0].astype(HALF)
+    grad_hidden, read_high = tie(grad_hidden, read_high)
     grad_mid = reduced(dot(grad_hidden, w_up, ((1,), (1,)), HALF))
-    grad_down = weight_grad(branch_grad, active)
-    grad_up = weight_grad(normed_mid, grad_hidden)
+    read_total = add_high(read_made, read_near, read_high)
+    down_made = made_of(branch_grad, active)
+    down_far = send_low(down_made, 1 - top)
+    grad_mid, read_total, down_made, down_far = tie(grad_mid, read_total, down_made, down_far)
+    down_near = send_low(down_made, top)
+    down_high = send_high(down_made, down_far)
     grad_mid_in, gain_mid = norm_back(first, gains_full[1], grad_mid)
     grad_first = grad_second + grad_mid_in
     attn_grad = gathered(grad_first.astype(HALF))
+    up_made = made_of(normed_mid, grad_hidden)
+    attn_grad, up_made, down_near = tie(attn_grad, up_made, down_near)
+    up_far = send_low(up_made, 1 - top)
+    grad_read = sum_sides(read_total)
     grad_heads = dot(attn_grad, w_out, ((1,), (0,)), HALF).reshape(team, local_heads, HD)
-    grad_out_w = weight_grad(attn_grad, flat_heads)
     inner = jnp.einsum("qhd,qhd->hq", grad_heads, attn_heads, preferred_element_type=F32)
     returned = []
     grad_query = jnp.zeros((), F32)
+    grad_down = sum_sides(add_high(down_made, down_near, down_high))
     for back in range(1, per_clip):
         keys_now, values_now = earlier[back - 1]
         more_query, far_keys, far_values = attend_back(
@@ -410,42 +578,87 @@
         ],
         axis=1,
     )
+    grad_mixed, up_made, up_far, grad_down, grad_read = tie(
+        grad_mixed, up_made, up_far, grad_down, grad_read
+    )
+    up_near = send_low(up_made, top)
+    up_high = send_high(up_made, up_far)
     grad_norm_in = reduced(dot(grad_mixed, w_in, ((1,), (1,)), HALF))
-    grad_in = weight_grad(normed_in, grad_mixed)
+    in_made = made_of(normed_in, grad_mixed)
+    out_made = made_of(attn_grad, flat_heads)
+    in_far, out_far = send_low(in_made, 1 - top), send_low(out_made, 1 - top)
+    grad_norm_in, up_near, up_high, in_made, out_made, in_far, out_far = tie(
+        grad_norm_in, up_near, up_high, in_made, out_made, in_far, out_far
+    )
+    grad_up = sum_sides(add_high(up_made, up_near, up_high))
     grad_embed_in, gain_in = norm_back(embedded_own, gains_full[0], grad_norm_in)
     grad_embed = (grad_first + grad_embed_in).astype(HALF)
 
     columns_own = lax.all_to_all(grad_embed, "head", 1, 0, tiled=True)
 
-    def token_spread(part, bits):
-        pieces = {0: part}
-        for bit in bits:
-            for mask in list(pieces):
-                pieces[mask | bit] = flip(pieces[mask], bit)
-        return jnp.concatenate([pieces[mask] for mask in range(blocks)])
-
-    columns_all = jnp.concatenate(
+    gain_sum = jnp.stack([gain_in, gain_mid, gain_final]).reshape(
+        (3,) + (2,) * len(all_bits) + (rows,)
+    )
+
+    def gain_hop(total, bit, left):
+        axis = 1 + left.index(bit)
+        at = (blk // bit) % 2
+        send = lax.dynamic_index_in_dim(total, 1 - at, axis, keepdims=False)
+        keep = lax.dynamic_index_in_dim(total, at, axis, keepdims=False)
+        return keep + flip(send, bit)
+
+    def spread(pieces, bit):
+        return pieces + [flip(piece, bit) for piece in pieces]
+
+    pieces_a, pieces_b = [columns_own[:, :mid]], [columns_own[:, mid:]]
+    in_near, out_near = send_low(in_made, top), send_low(out_made, top)
+    for k, bit in enumerate(high_bits[::-1]):
+        pieces_a, pieces_b = spread(pieces_a, bit), spread(pieces_b, bit)
+        gain_sum = gain_hop(gain_sum, bit, left[k:])
+    pieces_a, pieces_b, gain_sum, in_far, out_far, in_near, out_near, grad_up = tie(
+        pieces_a, pieces_b, gain_sum, in_far, out_far, in_near, out_near, grad_up
+    )
+    in_high, out_high = send_high(in_made, in_far), send_high(out_made, out_far)
+    pieces_a, pieces_b = spread(pieces_a, PAIR), spread(pieces_b, 1)
+    gain_sum = gain_hop(gain_sum, 1, left[-2:])
+    pieces_a, pieces_b, gain_sum = tie(pieces_a, pieces_b, gain_sum)
+    pieces_a, pieces_b = spread(pieces_a, 1), spread(pieces_b, PAIR)
+    gain_sum = gain_hop(gain_sum, PAIR, left[-2:-1])
+    pieces_a, pieces_b, gain_sum, in_high, out_high = tie(
+        pieces_a, pieces_b, gain_sum, in_high, out_high
+    )
+    grad_in = sum_sides(add_high(in_made, in_near, in_high))
+    grad_out_w = sum_sides(add_high(out_made, out_near, out_high))
+    for k in range(heads.bit_length() - 1):
+        pairs = [(i, i ^ (1 << k)) for i in range(heads)]
+        gain_sum = gain_sum + lax.ppermute(gain_sum, "head", pairs)
+    masks_a, masks_b = [0], [0]
+    for bit_a, bit_b in zip(high_bits[::-1] + [PAIR, 1], high_bits[::-1] + [1, PAIR]):
+        masks_a = masks_a + [mask | bit_a for mask in masks_a]
+        masks_b = masks_b + [mask | bit_b for mask in masks_b]
+    token_pieces = [pieces_a[masks_a.index(mask)] for mask in range(blocks)] + [
+        pieces_b[masks_b.index(mask)] for mask in range(blocks)
+    ]
+    row_step = max(s for s in range(8, 321, 8) if table_rows % s == 0)
+    grad_table = table_grad(table_at, token_pieces, table_rows, row_step)
+    img_sum, code_sum = grad_table[:image_rows], grad_table[image_rows:]
+
+    in_sum = jnp.stack(
         [
-            token_spread(columns_own[:, :mid], bits_a[::-1]),
-            token_spread(columns_own[:, mid:], bits_b[::-1]),
-        ],
-        axis=1,
-    )
-    grad_table = dot(pick, columns_all, ((0,), (0,)))
-    img_sum, code_sum = grad_table[:image_rows], grad_table[image_rows:]
-
-    gain_stack = jnp.stack([gain_in, gain_mid, gain_final])
-    gain_parts = jnp.broadcast_to(
-        gain_stack.reshape(3, blocks, rows).transpose(1, 0, 2)[:, None],
-        (blocks, heads, 3, rows),
-    ).reshape(blocks * heads, 3 * rows)
-    gain_sum = jnp.sum(lax.all_to_all(gain_parts, both, 0, 0, tiled=True), axis=0).reshape(3, rows)
-
-    in_sum = grad_in.reshape(rows, 2, 3, head_columns).transpose(2, 0, 1, 3).reshape(inward.shape)
-    out_sum = grad_out_w.reshape(rows, -1).T
-    up_sum = grad_up.reshape(rows, -1)
-    down_sum = grad_down.reshape(rows, -1).T
-    read_sum = grad_read.reshape(rows, -1)
+            jnp.concatenate(
+                [part[:, k * head_columns : (k + 1) * head_columns] for part in grad_in], axis=1
+            )
+            for k in range(3)
+        ]
+    )
+    out_sum = jnp.concatenate([part.T for part in grad_out_w])
+    down_sum = jnp.concatenate([part.T for part in grad_down])
+    up_sum = jnp.concatenate(grad_up, axis=1)
+    read_sum = jnp.concatenate(grad_read, axis=1)
+    in_sum, out_sum, up_sum, down_sum, read_sum = (
+        with_layout_constraint(total, Layout(major_to_minor=tuple(range(total.ndim))))
+        for total in (in_sum, out_sum, up_sum, down_sum, read_sum)
+    )
     sums = [in_sum, out_sum, up_sum, down_sum, img_sum, code_sum, read_sum, gain_sum]
     local_squares = jnp.float32(0.0)
     for shard in sums[:7]:

time: 1440 us -> 1070 us (0.74)
  local copies, waits for them, and re-layouts: 345 us -> 85.5 us
  waiting for transfers between devices: 667 us -> 559 us
  matrix products: 174 us -> 141 us
  Pallas kernels: 0 us -> 27.8 us
    ppermute x54 -> x62, waiting for transfers between devices: 445 us -> 253 us  [flip(): return lax.ppermute(value, 'blk', [(i, i ^ bit) for i in range(count)])]
    unnamed x248 -> x262, local copies, waits for them, and re-layouts: 155 us -> 36 us
    dynamic_slice x20 -> x10, local copies, waits for them, and re-layouts: 86.5 us -> 4.39 us  [the longest x3 2.44 us: paired(): keep = lax.dynamic_index_in_dim(halves, side, 1, keepdims=False)]
    all_gather x5, waiting for transfers between devices: 31.1 us -> 90.6 us  [gathered(): lax.all_gather(block, both, axis=0, tiled=True, axis_index_groups=teams)]
    reduce_scatter x5, waiting for transfers between devices: 153 us -> 183 us  [reduced(): lax.psum_scatter(partial, both, scatter_dimension=0, tiled=True, axis_ind...]
    reshape x7 -> x2, local copies, waits for them, and re-layouts: 33.5 us -> 3.44 us  [sided(): return weight.astype(HALF).reshape(rows, 2, -1)]
    pallas_call x0 -> x6, Pallas kernels: none -> 27.8 us  [the longest x4 11.4 us: assembled_at(): pl.pallas_call(lambda *refs: assembled_kernel(count, *refs), grid_spec=gr...]
    dot_general x22 -> x16, matrix products: 135 us -> 111 us  [dot(): lax.dot_general(left, right, (dims, ((), ())), preferred_element_type=F32)]
  transfers between devices with their start and end apart: 74 -> 82, of which waited for: 43 -> 48; matrix products, arithmetic and copies ran while one was open for 31% -> 20% of each run, Pallas kernels for 0% -> 2%
where the time goes in v2:
time: 1070 us; the launch traced here: 1060 us
  waiting for transfers between devices  559 us (52%)
  matrix products  141 us (13%)
  other arithmetic  117 us (11%)
  starting transfers between devices  94.1 us (9%)
  local copies, waits for them, and re-layouts  85.5 us (8%)
  Pallas kernels  27.8 us (3%)
  between operations  24.4 us (2%)
  blocking collectives  10.9 us (1%)
    ppermute x62, waiting for transfers between devices, flip(): return lax.ppermute(value, 'blk', [(i, i ^ bit) for i in range(count)])  253 us
    reduce_scatter x5, waiting for transfers between devices, reduced(): lax.psum_scatter(partial, both, scatter_dimension=0, tiled=True, axis_ind...  183 us
    dot_general x16, matrix products, dot(): lax.dot_general(left, right, (dims, ((), ())), preferred_element_type=F32)  111 us
    all_gather x5, waiting for transfers between devices, gathered(): lax.all_gather(block, both, axis=0, tiled=True, axis_index_groups=teams)  90.6 us
    ppermute x62, starting transfers between devices, flip(): return lax.ppermute(value, 'blk', [(i, i ^ bit) for i in range(count)])  77.1 us
    unnamed x262, local copies, waits for them, and re-layouts  36 us
    sub x8, other arithmetic, adamw(): weight - rate * (first_hat / (jnp.sqrt(second_hat) + ADAM_EPS) + decay *...  26.5 us
  transfers between devices with their start and end apart: 82, of which 48 were waited for; matrix products, arithmetic and copies ran while one was open for 20% of the time, Pallas kernels for 2%

profile of v2, /device:TPU:0, one launch (start us, length us, event | category | flops | bytes accessed | tf_op | source)
XLA Modules:
  0.0 1060.3 jit_solution(18077359748433151351)
XLA Ops:
  31.5 7.3 fusion.4
  50.5 13.1 %collective-permute-done.4 = bf16[2,2,512,256]{3,2,0,1:T(8,128)(2,1)} collective-permute-done((bf16[2,2,512,256]{3,2,0,1:T(8,128)(2,1)}, bf16[2,2,512,256]{3,2,0,1:T(8,128)(2,1)}, u32[]{:S(2)}, u32[]{:S(2)}) %collective-permute-start.4) | collective-permute-done | bytes 1048608 | tf_op jit(solution)/shard_map/ppermute | solution.py:35
  65.8 25.7 %collective-permute-done.6 = bf16[2,2,512,256]{3,2,0,1:T(8,128)(2,1)} collective-permute-done((bf16[2,2,512,256]{3,2,0,1:T(8,128)(2,1)}, bf16[2,2,512,256]{3,2,0,1:T(8,128)(2,1)}, u32[]{:S(2)}, u32[]{:S(2)}) %collective-permute-start.6) | collective-permute-done | bytes 1048608 | tf_op jit(solution)/shard_map/ppermute | solution.py:35
  94.3 8.3 collective-permute-done.8
  102.8 7.5 collective-permute-done.5
  114.6 14.2 %collective-permute-done.11 = bf16[512,256]{1,0:T(8,128)(2,1)S(1)} collective-permute-done((bf16[512,256]{1,0:T(8,128)(2,1)S(1)}, bf16[512,256]{1,0:T(8,128)(2,1)S(1)}, u32[]{:S(2)}, u32[]{:S(2)}) %collective-permute-start.11) | collective-permute-done | bytes 262176 | tf_op jit(solution)/shard_map/ppermute | solution.py:35
  128.8 4.9 collective-permute-done.10
  147.7 13.4 %collective-permute-done.13.refs_4_ = bf16[2,256,1024]{2,1,0:T(8,128)(2,1)} collective-permute-done((bf16[2,256,1024]{2,1,0:T(8,128)(2,1)S(1)}, bf16[2,256,1024]{2,1,0:T(8,128)(2,1)}, u32[]{:S(2)}, u32[]{:S(2)}) %collective-permute-start.13) | collective-permute-done | bytes 1048608 | tf_op jit(solution)/shard_map/ppermute | solution.py:35
  166.0 8.3 all-gather.6.cloned.1.call-done
  174.3 7.5 shard_map.493
  181.8 7.8 fusion.46
  189.6 3.3 collective-permute-done.15.refs_2_
  213.9 5.1 collective-permute-done.18
  219.0 8.7 collective-permute-done.17
  243.2 4.6 convolution_convert_fusion
  250.3 5.3 collective-permute-start.22
  263.0 11.7 %collective-permute-done.20.refs_4_ = bf16[2,256,1024]{2,1,0:T(8,128)(2,1)} collective-permute-done((bf16[2,256,1024]{2,1,0:T(8,128)(2,1)}, bf16[2,256,1024]{2,1,0:T(8,128)(2,1)}, u32[]{:S(2)}, u32[]{:S(2)}) %collective-permute-start.20) | collective-permute-done | bytes 1048608 | tf_op jit(solution)/shard_map/ppermute | solution.py:35
  279.9 33.1 %reduce-scatter.6.cloned.1.call-done = bf16[128,2048]{1,0:T(8,128)(2,1)} async-done(((bf16[1024,2048]{1,0:T(8,128)(2,1)}), bf16[128,2048]{1,0:T(8,128)(2,1)}) %reduce-scatter.6.cloned.1.call-update) | async-done | bytes 524304 | tf_op jit(solution)/shard_map/reduce_scatter | solution.py:260
  319.4 22.7 %collective-permute-done.23.refs_4_ = bf16[2,256,1024]{2,1,0:T(8,128)(2,1)S(1)} collective-permute-done((bf16[2,256,1024]{2,1,0:T(8,128)(2,1)}, bf16[2,256,1024]{2,1,0:T(8,128)(2,1)S(1)}, u32[]{:S(2)}, u32[]{:S(2)}) %collective-permute-start.23) | collective-permute-done | bytes 1048608 | tf_op jit(solution)/shard_map/ppermute | solution.py:35
  343.0 17.7 %all-gather.8.cloned.1.call-done = bf16[1024,2048]{1,0:T(8,128)(2,1)} async-done(((bf16[128,2048]{1,0:T(8,128)(2,1)}), bf16[1024,2048]{1,0:T(8,128)(2,1)}) %all-gather.8.cloned.1.call-update) | async-done | bytes 4194320 | tf_op jit(solution)/shard_map/all_gather | solution.py:257
  360.7 10.6 multiply_convert_fusion.2
  376.3 6.1 convolution_convert_fusion.7
  384.6 52.2 %reduce-scatter.8.cloned.1.call-done = bf16[128,2048]{1,0:T(8,128)(2,1)} async-done(((bf16[1024,2048]{1,0:T(8,128)(2,1)}), bf16[128,2048]{1,0:T(8,128)(2,1)}) %reduce-scatter.8.cloned.1.call-update) | async-done | bytes 524304 | tf_op jit(solution)/shard_map/reduce_scatter | solution.py:260
  445.7 26.7 %all-gather.10.cloned.1.call-done = bf16[1024,2048]{1,0:T(8,128)(2,1)} async-done(((bf16[128,2048]{1,0:T(8,128)(2,1)}), bf16[1024,2048]{1,0:T(8,128)(2,1)}) %all-gather.10.cloned.1.call-update) | async-done | bytes 4194320 | tf_op jit(solution)/shard_map/all_gather | solution.py:257
  472.4 7.6 fusion.167
  491.7 7.0 convolution_convert_fusion.6
  499.1 8.3 convolution_convert_fusion.5
  511.9 33.6 %reduce-scatter.10.cloned.1.call-done = bf16[128,2048]{1,0:T(8,128)(2,1)} async-done(((bf16[1024,2048]{1,0:T(8,128)(2,1)}), bf16[128,2048]{1,0:T(8,128)(2,1)}) %reduce-scatter.10.cloned.1.call-update) | async-done | bytes 524304 | tf_op jit(solution)/shard_map/reduce_scatter | solution.py:260
  557.4 17.1 %collective-permute-done.31 = bf16[1,2,256,1024]{3,2,1,0:T(8,128)(2,1)} collective-permute-done((bf16[1,2,256,1024]{3,2,1,0:T(8,128)(2,1)}, bf16[1,2,256,1024]{3,2,1,0:T(8,128)(2,1)}, u32[]{:S(2)}, u32[]{:S(2)}) %collective-permute-start.31) | collective-permute-done | bytes 1048608 | tf_op jit(solution)/shard_map/ppermute | solution.py:35
  574.5 20.3 %all-gather.12.cloned.1.call-done = bf16[1024,2048]{1,0:T(8,128)(2,1)} async-done(((bf16[128,2048]{1,0:T(8,128)(2,1)}), bf16[1024,2048]{1,0:T(8,128)(2,1)}) %all-gather.12.cloned.1.call-update) | async-done | bytes 4194320 | tf_op jit(solution)/shard_map/all_gather | solution.py:257
  594.9 11.4 %fusion.19 = bf16[1024,1024]{1,0:T(8,128)(2,1)S(1)} fusion(f32[1024,1024]{1,0:T(8,128)} %get-tuple-element.357, bf16[1024,2048]{1,0:T(8,128)(2,1)} %all-gather.12.cloned.1.call-done, bf16[2048,1024]{1,0:T(8,128)(2,1)} %bitcast.384), kind=kOutput, calls=%fused_computation.36 | convolution fusion | flops 4315938816 | bytes 14680064 | tf_op jit(solution)/shard_map/dot_general | solution.py:48
  607.6 6.2 convolution_convert_fusion.4
  614.4 7.5 convolution_convert_fusion.3
  626.5 3.5 fusion.44
  630.0 33.4 %reduce-scatter.12.cloned.1.call-done = bf16[128,2048]{1,0:T(8,128)(2,1)} async-done(((bf16[1024,2048]{1,0:T(8,128)(2,1)}), bf16[128,2048]{1,0:T(8,128)(2,1)}) %reduce-scatter.12.cloned.1.call-update) | async-done | bytes 524304 | tf_op jit(solution)/shard_map/reduce_scatter | solution.py:260
  672.2 9.4 convolution_convert_fusion.2
  688.6 6.9 collective-permute-done.34
  695.5 17.6 %all-gather.14.cloned.1.call-done = bf16[1024,2048]{1,0:T(8,128)(2,1)} async-done(((bf16[128,2048]{1,0:T(8,128)(2,1)}), bf16[1024,2048]{1,0:T(8,128)(2,1)}) %all-gather.14.cloned.1.call-update) | async-done | bytes 4194320 | tf_op jit(solution)/shard_map/all_gather | solution.py:257
  713.0 3.9 fusion.90
  717.1 6.7 fusion.77
  742.5 13.8 %collective-permute-done.36 = bf16[1024,2,128]{0,2,1:T(8,128)(2,1)S(1)} collective-permute-done((bf16[1024,2,128]{0,2,1:T(8,128)(2,1)}, bf16[1024,2,128]{0,2,1:T(8,128)(2,1)S(1)}, u32[]{:S(2)}, u32[]{:S(2)}) %collective-permute-start.36) | collective-permute-done | bytes 524320 | tf_op jit(solution)/shard_map/ppermute | solution.py:563
  760.7 17.8 %collective-permute-done.37 = bf16[1,2,256,1024]{3,2,1,0:T(8,128)(2,1)} collective-permute-done((bf16[1,2,256,1024]{3,2,1,0:T(8,128)(2,1)S(1)}, bf16[1,2,256,1024]{3,2,1,0:T(8,128)(2,1)}, u32[]{:S(2)}, u32[]{:S(2)}) %collective-permute-start.37) | collective-permute-done | bytes 1048608 | tf_op jit(solution)/shard_map/ppermute | solution.py:35
  778.5 5.1 convolution_convert_fusion.1
  786.2 4.0 convolution_convert_fusion.9
  791.3 3.4 fusion.40
  796.7 4.2 convolution_convert_fusion.8
  815.7 31.1 %reduce-scatter.14.cloned.1.call-done = bf16[128,2048]{1,0:T(8,128)(2,1)} async-done(((bf16[1024,2048]{1,0:T(8,128)(2,1)}), bf16[128,2048]{1,0:T(8,128)(2,1)}) %reduce-scatter.14.cloned.1.call-update) | async-done | bytes 524304 | tf_op jit(solution)/shard_map/reduce_scatter | solution.py:260
  851.9 4.1 all-to-all-start
  873.6 6.0 collective-permute-done.50
  881.2 9.2 collective-permute-done.49
  892.0 4.0 collective-permute-done.45.refs_5_
  903.4 11.9 %collective-permute-done.51.refs_3_ = bf16[512,256]{1,0:T(8,128)(2,1)S(1)} collective-permute-done((bf16[512,256]{1,0:T(8,128)(2,1)S(1)}, bf16[512,256]{1,0:T(8,128)(2,1)S(1)}, u32[]{:S(2)}, u32[]{:S(2)}) %collective-permute-start.51) | collective-permute-done | bytes 262176 | tf_op jit(solution)/shard_map/ppermute | solution.py:35
  923.2 12.5 %collective-permute-done.66 = bf16[1,2,256,256]{2,3,1,0:T(8,128)(2,1)S(1)} collective-permute-done((bf16[1,2,256,256]{2,3,1,0:T(8,128)(2,1)S(1)}, bf16[1,2,256,256]{2,3,1,0:T(8,128)(2,1)S(1)}, u32[]{:S(2)}, u32[]{:S(2)}) %collective-permute-start.66) | collective-permute-done | bytes 262176 | tf_op jit(solution)/shard_map/ppermute | solution.py:35
  946.9 7.3 collective-permute-done.60.refs_11_
  954.3 5.6 collective-permute-done.61.refs_15_
  959.9 5.6 collective-permute-done.62.refs_12_
  965.5 4.9 collective-permute-done.63.refs_16_
  971.1 9.0 shard_map.498
  993.8 6.1 collective-permute-done.67
  1008.1 10.9 %all_to_all.24 = f32[32,2,128]{2,1,0:T(2,128)S(1)} all-to-all(f32[32,2,128]{2,1,0:T(2,128)S(1)} %broadcast_in_dim.115), channel_id=1, replica_groups=mesh['blk'=8,'head'=4] {'blk','head'}, dimensions={0} | all-to-all | bytes 65536 | tf_op jit(solution)/shard_map/all_to_all | solution.py:670
  1031.0 3.9 multiply_subtract_fusion.1
  1036.0 5.8 multiply_subtract_fusion
  1041.9 3.8 multiply_subtract_fusion.2
  1047.5 4.0 multiply_subtract_fusion.3
  (602 shorter events, 315.9 us)
Async XLA Ops:
  7.2 167.1 %all-gather.6.cloned.1.call-start = ((), (), s32[]{:S(2)}) async-start(), calls=%async_computation.7 | async-start | bytes 4718592 | tf_op jit(solution)/shard_map/all_gather | solution.py:257
  40.6 23.0 %collective-permute-start.4 = (bf16[2,2,512,256]{3,2,0,1:T(8,128)(2,1)}, bf16[2,2,512,256]{3,2,0,1:T(8,128)(2,1)}, u32[]{:S(2)}, u32[]{:S(2)}) collective-permute-start(bf16[2,2,512,256]{3,2,0,1:T(8,128)(2,1)} %slice_bitcast_fusion.2), channel_id=1, source_target_pairs={{0,4},{4,0},{8,12},{12,8},{16,20},{20,16},{24,28},{28,24},{1,5},{5... | collective-permute-start | bytes 3145736 | tf_op jit(solution)/shard_map/ppermute | solution.py:35
  42.6 48.9 %collective-permute-start.6 = (bf16[2,2,512,256]{3,2,0,1:T(8,128)(2,1)}, bf16[2,2,512,256]{3,2,0,1:T(8,128)(2,1)}, u32[]{:S(2)}, u32[]{:S(2)}) collective-permute-start(bf16[2,2,512,256]{3,2,0,1:T(8,128)(2,1)} %slice_bitcast_fusion), channel_id=1, source_target_pairs={{0,8},{4,12},{8,0},{12,4},{16,24},{20,28},{24,16},{28,20},{1,9},{5... | collective-permute-start | bytes 3145736 | tf_op jit(solution)/shard_map/ppermute | solution.py:35
  46.3 56.4 %collective-permute-start.8 = (bf16[256,1024]{1,0:T(8,128)(2,1)S(1)}, bf16[256,1024]{1,0:T(8,128)(2,1)S(1)}, u32[]{:S(2)}, u32[]{:S(2)}) collective-permute-start(bf16[256,1024]{1,0:T(8,128)(2,1)S(1)} %bitcast.439), channel_id=1, source_target_pairs={{0,8},{4,12},{8,0},{12,4},{16,24},{20,28},{24,16},{28,20},{1,9},{5... | collective-permute-start | bytes 1572872 | tf_op jit(solution)/shard_map/ppermute | solution.py:35
  48.0 62.4 %collective-permute-start.9 = (bf16[2,256,1024]{2,1,0:T(8,128)(2,1)S(1)}, bf16[2,256,1024]{2,1,0:T(8,128)(2,1)S(1)}, u32[]{:S(2)}, u32[]{:S(2)}) collective-permute-start(bf16[2,256,1024]{2,1,0:T(8,128)(2,1)S(1)} %maximum_select_fusion.refs_1_), channel_id=1, source_target_pairs={{0,16},{4,20},{8,24},{12,28},{16,0},{20,4},{24,8},{28,12},{1,17},{... | collective-permute-start | bytes 3145736 | tf_op jit(solution)/shard_map/ppermute | solution.py:35
  65.2 45.1 %collective-permute-start.5 = (bf16[2,512,256]{2,1,0:T(8,128)(2,1)S(1)}, bf16[2,512,256]{2,1,0:T(8,128)(2,1)S(1)}, u32[]{:S(2)}, u32[]{:S(2)}) collective-permute-start(bf16[2,512,256]{2,1,0:T(8,128)(2,1)S(1)} %slice_bitcast_fusion.6), channel_id=1, source_target_pairs={{0,8},{4,12},{8,0},{12,4},{16,24},{20,28},{24,16},{28,20},{1,9},{5... | collective-permute-start | bytes 1572872 | tf_op jit(solution)/shard_map/ppermute | solution.py:35
  93.0 17.3 %collective-permute-start.7 = (bf16[2,512,256]{2,1,0:T(8,128)(2,1)S(1)}, bf16[2,512,256]{2,1,0:T(8,128)(2,1)S(1)}, u32[]{:S(2)}, u32[]{:S(2)}) collective-permute-start(bf16[2,512,256]{2,1,0:T(8,128)(2,1)S(1)} %slice_bitcast_fusion.4), channel_id=1, source_target_pairs={{0,4},{4,0},{8,12},{12,8},{16,20},{20,16},{24,28},{28,24},{1,5},{5... | collective-permute-start | bytes 1572872 | tf_op jit(solution)/shard_map/ppermute | solution.py:35
  110.4 24.1 %collective-permute-start.12 = (bf16[2,256,1024]{2,1,0:T(8,128)(2,1)S(1)}, bf16[2,256,1024]{2,1,0:T(8,128)(2,1)}, u32[]{:S(2)}, u32[]{:S(2)}) collective-permute-start(bf16[2,256,1024]{2,1,0:T(8,128)(2,1)S(1)} %maximum_select_fusion.refs_1_), channel_id=1, source_target_pairs={{0,4},{4,0},{8,12},{12,8},{16,20},{20,16},{24,28},{28,24},{1,5},{5... | collective-permute-start | bytes 3145736 | tf_op jit(solution)/shard_map/ppermute | solution.py:35
  111.5 17.3 %collective-permute-start.11 = (bf16[512,256]{1,0:T(8,128)(2,1)S(1)}, bf16[512,256]{1,0:T(8,128)(2,1)S(1)}, u32[]{:S(2)}, u32[]{:S(2)}) collective-permute-start(bf16[512,256]{1,0:T(8,128)(2,1)S(1)} %slice_bitcast_fusion.9), channel_id=1, source_target_pairs={{0,16},{4,20},{8,24},{12,28},{16,0},{20,4},{24,8},{28,12},{1,17},{... | collective-permute-start | bytes 786440 | tf_op jit(solution)/shard_map/ppermute | solution.py:35
  113.2 20.5 %collective-permute-start.10 = (bf16[512,256]{1,0:T(8,128)(2,1)S(1)}, bf16[512,256]{1,0:T(8,128)(2,1)S(1)}, u32[]{:S(2)}, u32[]{:S(2)}) collective-permute-start(bf16[512,256]{1,0:T(8,128)(2,1)S(1)} %slice_bitcast_fusion.10), channel_id=1, source_target_pairs={{0,16},{4,20},{8,24},{12,28},{16,0},{20,4},{24,8},{28,12},{1,17},{... | collective-permute-start | bytes 786440 | tf_op jit(solution)/shard_map/ppermute | solution.py:35
  134.6 178.4 %reduce-scatter.6.cloned.1.call-start = ((), (), s32[]{:S(2)}) async-start(), calls=%async_computation.8 | async-start | bytes 4718592 | tf_op jit(solution)/shard_map/reduce_scatter | solution.py:260
  134.8 26.3 %collective-permute-start.13 = (bf16[2,256,1024]{2,1,0:T(8,128)(2,1)S(1)}, bf16[2,256,1024]{2,1,0:T(8,128)(2,1)}, u32[]{:S(2)}, u32[]{:S(2)}) collective-permute-start(bf16[2,256,1024]{2,1,0:T(8,128)(2,1)S(1)} %collective-permute-done.9.refs_2_), channel_id=1, source_target_pairs={{0,4},{4,0},{8,12},{12,8},{16,20},{20,16},{24,28},{28,24},{1,5},{5... | collective-permute-start | bytes 3145736 | tf_op jit(solution)/shard_map/ppermute | solution.py:35
  145.5 47.3 %collective-permute-start.15 = (bf16[2,256,1024]{2,1,0:T(8,128)(2,1)S(1)}, bf16[2,256,1024]{2,1,0:T(8,128)(2,1)}, u32[]{:S(2)}, u32[]{:S(2)}) collective-permute-start(bf16[2,256,1024]{2,1,0:T(8,128)(2,1)S(1)} %maximum_select_fusion.1.refs_1_), channel_id=1, source_target_pairs={{0,16},{4,20},{8,24},{12,28},{16,0},{20,4},{24,8},{28,12},{1,17},{... | collective-permute-start | bytes 3145736 | tf_op jit(solution)/shard_map/ppermute | solution.py:35
  145.5 44.0 %collective-permute-start.14 = (bf16[2,256,1024]{2,1,0:T(8,128)(2,1)S(1)}, bf16[2,256,1024]{2,1,0:T(8,128)(2,1)}, u32[]{:S(2)}, u32[]{:S(2)}) collective-permute-start(bf16[2,256,1024]{2,1,0:T(8,128)(2,1)S(1)} %maximum_select_fusion.1.refs_1_), channel_id=1, source_target_pairs={{0,4},{4,0},{8,12},{12,8},{16,20},{20,16},{24,28},{28,24},{1,5},{5... | collective-permute-start | bytes 3145736 | tf_op jit(solution)/shard_map/ppermute | solution.py:35
  197.9 29.9 %collective-permute-start.19 = (bf16[256,1024]{1,0:T(8,128)(2,1)}, bf16[256,1024]{1,0:T(8,128)(2,1)}, u32[]{:S(2)}, u32[]{:S(2)}) collective-permute-start(bf16[256,1024]{1,0:T(8,128)(2,1)} %get-tuple-element.300), channel_id=1, source_target_pairs={{0,8},{4,12},{8,0},{12,4},{16,24},{20,28},{24,16},{28,20},{1,9},{5... | collective-permute-start | bytes 1572872 | tf_op jit(solution)/shard_map/ppermute | solution.py:35
  206.6 21.1 %collective-permute-start.17 = (bf16[1024,2,128]{0,2,1:T(8,128)(2,1)S(1)}, bf16[1024,2,128]{0,2,1:T(8,128)(2,1)S(1)}, u32[]{:S(2)}, u32[]{:S(2)}) collective-permute-start(bf16[1024,2,128]{0,2,1:T(8,128)(2,1)S(1)} %bitcast.394), channel_id=1, source_target_pairs={{0,4},{8,12},{16,20},{24,28},{1,5},{9,13},{17,21},{25,29},{2,6},{1... | collective-permute-start | bytes 1572872 | tf_op jit(solution)/shard_map/ppermute | solution.py:413
  247.7 112.9 %all-gather.8.cloned.1.call-start = ((), (), s32[]{:S(2)}) async-start(), calls=%async_computation.9 | async-start | bytes 4718592 | tf_op jit(solution)/shard_map/all_gather | solution.py:257
  247.8 26.9 %collective-permute-start.20 = (bf16[2,256,1024]{2,1,0:T(8,128)(2,1)}, bf16[2,256,1024]{2,1,0:T(8,128)(2,1)}, u32[]{:S(2)}, u32[]{:S(2)}) collective-permute-start(bf16[2,256,1024]{2,1,0:T(8,128)(2,1)} %collective-permute-done.15.refs_2_), channel_id=1, source_target_pairs={{0,4},{4,0},{8,12},{12,8},{16,20},{20,16},{24,28},{28,24},{1,5},{5... | collective-permute-start | bytes 3145736 | tf_op jit(solution)/shard_map/ppermute | solution.py:35
  250.3 64.1 %collective-permute-start.22 = (bf16[2,256,1024]{2,1,0:T(8,128)(2,1)S(1)}, bf16[2,256,1024]{2,1,0:T(8,128)(2,1)}, u32[]{:S(2)}, u32[]{:S(2)}) collective-permute-start(bf16[2,256,1024]{2,1,0:T(8,128)(2,1)S(1)} %maximum_select_fusion.2.refs_1_), channel_id=1, source_target_pairs={{0,16},{4,20},{8,24},{12,28},{16,0},{20,4},{24,8},{28,12},{1,17},{... | collective-permute-start | bytes 3145736 | tf_op jit(solution)/shard_map/ppermute | solution.py:35
  255.7 58.8 %collective-permute-start.21 = (bf16[2,256,1024]{2,1,0:T(8,128)(2,1)S(1)}, bf16[2,256,1024]{2,1,0:T(8,128)(2,1)}, u32[]{:S(2)}, u32[]{:S(2)}) collective-permute-start(bf16[2,256,1024]{2,1,0:T(8,128)(2,1)S(1)} %maximum_select_fusion.2.refs_1_), channel_id=1, source_target_pairs={{0,4},{4,0},{8,12},{12,8},{16,20},{20,16},{24,28},{28,24},{1,5},{5... | collective-permute-start | bytes 3145736 | tf_op jit(solution)/shard_map/ppermute | solution.py:35
  316.4 120.4 %reduce-scatter.8.cloned.1.call-start = ((), (), s32[]{:S(2)}) async-start(), calls=%async_computation.10 | async-start | bytes 4718592 | tf_op jit(solution)/shard_map/reduce_scatter | solution.py:260
  316.6 25.4 %collective-permute-start.23 = (bf16[2,256,1024]{2,1,0:T(8,128)(2,1)}, bf16[2,256,1024]{2,1,0:T(8,128)(2,1)S(1)}, u32[]{:S(2)}, u32[]{:S(2)}) collective-permute-start(bf16[2,256,1024]{2,1,0:T(8,128)(2,1)} %collective-permute-done.22.refs_2_), channel_id=1, source_target_pairs={{0,4},{4,0},{8,12},{12,8},{16,20},{20,16},{24,28},{28,24},{1,5},{5... | collective-permute-start | bytes 3145736 | tf_op jit(solution)/shard_map/ppermute | solution.py:35
  319.0 52.2 %collective-permute-start.24 = (bf16[2,256,1024]{2,1,0:T(8,128)(2,1)S(1)}, bf16[2,256,1024]{2,1,0:T(8,128)(2,1)S(1)}, u32[]{:S(2)}, u32[]{:S(2)}) collective-permute-start(bf16[2,256,1024]{2,1,0:T(8,128)(2,1)S(1)} %maximum_select_fusion.3.refs_1_), channel_id=1, source_target_pairs={{0,16},{4,20},{8,24},{12,28},{16,0},{20,4},{24,8},{28,12},{1,17},{... | collective-permute-start | bytes 3145736 | tf_op jit(solution)/shard_map/ppermute | solution.py:35
  382.4 89.9 %all-gather.10.cloned.1.call-start = ((), (), s32[]{:S(2)}) async-start(), calls=%async_computation.11 | async-start | bytes 4718592 | tf_op jit(solution)/shard_map/all_gather | solution.py:257
  382.5 55.8 %collective-permute-start.25 = (bf16[2,256,1024]{2,1,0:T(8,128)(2,1)S(1)}, bf16[2,256,1024]{2,1,0:T(8,128)(2,1)S(1)}, u32[]{:S(2)}, u32[]{:S(2)}) collective-permute-start(bf16[2,256,1024]{2,1,0:T(8,128)(2,1)S(1)} %maximum_select_fusion.3.refs_1_), channel_id=1, source_target_pairs={{0,4},{4,0},{8,12},{12,8},{16,20},{20,16},{24,28},{28,24},{1,5},{5... | collective-permute-start | bytes 3145736 | tf_op jit(solution)/shard_map/ppermute | solution.py:35
  384.0 54.2 %collective-permute-start.26 = (bf16[2,256,1024]{2,1,0:T(8,128)(2,1)S(1)}, bf16[2,256,1024]{2,1,0:T(8,128)(2,1)}, u32[]{:S(2)}, u32[]{:S(2)}) collective-permute-start(bf16[2,256,1024]{2,1,0:T(8,128)(2,1)S(1)} %collective-permute-done.24.refs_2_), channel_id=1, source_target_pairs={{0,4},{4,0},{8,12},{12,8},{16,20},{20,16},{24,28},{28,24},{1,5},{5... | collective-permute-start | bytes 3145736 | tf_op jit(solution)/shard_map/ppermute | solution.py:35
  440.2 105.4 %reduce-scatter.10.cloned.1.call-start = ((), (), s32[]{:S(2)}) async-start(), calls=%async_computation.12 | async-start | bytes 4718592 | tf_op jit(solution)/shard_map/reduce_scatter | solution.py:260
  498.8 96.1 %all-gather.12.cloned.1.call-start = ((), (), s32[]{:S(2)}) async-start(), calls=%async_computation.13 | async-start | bytes 4718592 | tf_op jit(solution)/shard_map/all_gather | solution.py:257
  510.4 36.2 %collective-permute-start.30 = (bf16[1,2,256,1024]{3,2,1,0:T(8,128)(2,1)}, bf16[1,2,256,1024]{3,2,1,0:T(8,128)(2,1)S(1)}, u32[]{:S(2)}, u32[]{:S(2)}) collective-permute-start(bf16[1,2,256,1024]{3,2,1,0:T(8,128)(2,1)} %dynamic-slice_bitcast_fusion.5), channel_id=1, source_target_pairs={{0,4},{4,0},{8,12},{12,8},{16,20},{20,16},{24,28},{28,24},{1,5},{5... | collective-permute-start | bytes 3145736 | tf_op jit(solution)/shard_map/ppermute | solution.py:35
  548.1 115.2 %reduce-scatter.12.cloned.1.call-start = ((), (), s32[]{:S(2)}) async-start(), calls=%async_computation.14 | async-start | bytes 4718592 | tf_op jit(solution)/shard_map/reduce_scatter | solution.py:260
  550.7 23.8 %collective-permute-start.31 = (bf16[1,2,256,1024]{3,2,1,0:T(8,128)(2,1)}, bf16[1,2,256,1024]{3,2,1,0:T(8,128)(2,1)}, u32[]{:S(2)}, u32[]{:S(2)}) collective-permute-start(bf16[1,2,256,1024]{3,2,1,0:T(8,128)(2,1)} %dynamic-slice_bitcast_fusion.4), channel_id=1, source_target_pairs={{0,4},{4,0},{8,12},{12,8},{16,20},{20,16},{24,28},{28,24},{1,5},{5... | collective-permute-start | bytes 3145736 | tf_op jit(solution)/shard_map/ppermute | solution.py:35
  555.0 51.3 %collective-permute-start.32 = (bf16[1,2,256,1024]{3,2,1,0:T(8,128)(2,1)}, bf16[1,2,256,1024]{3,2,1,0:T(8,128)(2,1)S(1)}, u32[]{:S(2)}, u32[]{:S(2)}) collective-permute-start(bf16[1,2,256,1024]{3,2,1,0:T(8,128)(2,1)} %fusion.45), channel_id=1, source_target_pairs={{0,16},{4,20},{8,24},{12,28},{16,0},{20,4},{24,8},{28,12},{1,17},{... | collective-permute-start | bytes 3145736 | tf_op jit(solution)/shard_map/ppermute | solution.py:35
  613.8 99.2 %all-gather.14.cloned.1.call-start = ((), (), s32[]{:S(2)}) async-start(), calls=%async_computation.15 | async-start | bytes 4718592 | tf_op jit(solution)/shard_map/all_gather | solution.py:257
  625.1 39.4 %collective-permute-start.33 = (bf16[1,2,256,1024]{3,2,1,0:T(8,128)(2,1)}, bf16[1,2,256,1024]{3,2,1,0:T(8,128)(2,1)}, u32[]{:S(2)}, u32[]{:S(2)}) collective-permute-start(bf16[1,2,256,1024]{3,2,1,0:T(8,128)(2,1)} %dynamic-slice_bitcast_fusion.3), channel_id=1, source_target_pairs={{0,4},{4,0},{8,12},{12,8},{16,20},{20,16},{24,28},{28,24},{1,5},{5... | collective-permute-start | bytes 3145736 | tf_op jit(solution)/shard_map/ppermute | solution.py:35
  666.6 180.1 %reduce-scatter.14.cloned.1.call-start = ((), (), s32[]{:S(2)}) async-start(), calls=%async_computation.16 | async-start | bytes 4718592 | tf_op jit(solution)/shard_map/reduce_scatter | solution.py:260
  668.2 18.9 %collective-permute-start.40 = (bf16[256,1024]{1,0:T(8,128)(2,1)S(1)}, bf16[256,1024]{1,0:T(8,128)(2,1)S(1)}, u32[]{:S(2)}, u32[]{:S(2)}) collective-permute-start(bf16[256,1024]{1,0:T(8,128)(2,1)S(1)} %fusion.97), channel_id=1, source_target_pairs={{0,8},{4,12},{8,0},{12,4},{16,24},{20,28},{24,16},{28,20},{1,9},{5... | collective-permute-start | bytes 1572872 | tf_op jit(solution)/shard_map/ppermute | solution.py:35
  670.7 24.8 %collective-permute-start.34 = (bf16[1,2,256,1024]{3,2,1,0:T(8,128)(2,1)S(1)}, bf16[1,2,256,1024]{3,2,1,0:T(8,128)(2,1)}, u32[]{:S(2)}, u32[]{:S(2)}) collective-permute-start(bf16[1,2,256,1024]{3,2,1,0:T(8,128)(2,1)S(1)} %dynamic-slice_bitcast_fusion.2), channel_id=1, source_target_pairs={{0,4},{4,0},{8,12},{12,8},{16,20},{20,16},{24,28},{28,24},{1,5},{5... | collective-permute-start | bytes 3145736 | tf_op jit(solution)/shard_map/ppermute | solution.py:35
  684.6 54.4 %collective-permute-start.38 = (bf16[1,2,256,1024]{3,2,1,0:T(8,128)(2,1)}, bf16[1,2,256,1024]{3,2,1,0:T(8,128)(2,1)}, u32[]{:S(2)}, u32[]{:S(2)}) collective-permute-start(bf16[1,2,256,1024]{3,2,1,0:T(8,128)(2,1)} %fusion.41), channel_id=1, source_target_pairs={{0,16},{4,20},{8,24},{12,28},{16,0},{20,4},{24,8},{28,12},{1,17},{... | collective-permute-start | bytes 3145736 | tf_op jit(solution)/shard_map/ppermute | solution.py:35
  728.4 30.4 %collective-permute-start.35 = (bf16[1024,2,128]{0,2,1:T(8,128)(2,1)S(1)}, bf16[1024,2,128]{0,2,1:T(8,128)(2,1)S(1)}, u32[]{:S(2)}, u32[]{:S(2)}) collective-permute-start(bf16[1024,2,128]{0,2,1:T(8,128)(2,1)S(1)} %fusion.80), channel_id=1, source_target_pairs={{4,0},{12,8},{20,16},{28,24},{5,1},{13,9},{21,17},{29,25},{6,2},{1... | collective-permute-start | bytes 1572872 | tf_op jit(solution)/shard_map/ppermute | solution.py:563
  729.7 26.6 %collective-permute-start.36 = (bf16[1024,2,128]{0,2,1:T(8,128)(2,1)}, bf16[1024,2,128]{0,2,1:T(8,128)(2,1)S(1)}, u32[]{:S(2)}, u32[]{:S(2)}) collective-permute-start(bf16[1024,2,128]{0,2,1:T(8,128)(2,1)} %fusion.77), channel_id=1, source_target_pairs={{4,0},{12,8},{20,16},{28,24},{5,1},{13,9},{21,17},{29,25},{6,2},{1... | collective-permute-start | bytes 1572872 | tf_op jit(solution)/shard_map/ppermute | solution.py:563
  732.3 46.2 %collective-permute-start.37 = (bf16[1,2,256,1024]{3,2,1,0:T(8,128)(2,1)S(1)}, bf16[1,2,256,1024]{3,2,1,0:T(8,128)(2,1)}, u32[]{:S(2)}, u32[]{:S(2)}) collective-permute-start(bf16[1,2,256,1024]{3,2,1,0:T(8,128)(2,1)S(1)} %dynamic-slice_bitcast_fusion.1), channel_id=1, source_target_pairs={{0,4},{4,0},{8,12},{12,8},{16,20},{20,16},{24,28},{28,24},{1,5},{5... | collective-permute-start | bytes 3145736 | tf_op jit(solution)/shard_map/ppermute | solution.py:35
  741.6 18.9 %collective-permute-start.39 = (bf16[256,1024]{1,0:T(8,128)(2,1)S(1)}, bf16[256,1024]{1,0:T(8,128)(2,1)S(1)}, u32[]{:S(2)}, u32[]{:S(2)}) collective-permute-start(bf16[256,1024]{1,0:T(8,128)(2,1)S(1)} %fusion.96), channel_id=1, source_target_pairs={{0,8},{4,12},{8,0},{12,4},{16,24},{20,28},{24,16},{28,20},{1,9},{5... | collective-permute-start | bytes 1572872 | tf_op jit(solution)/shard_map/ppermute | solution.py:35
  791.3 56.6 %collective-permute-start.41 = (bf16[1,2,256,1024]{3,2,1,0:T(8,128)(2,1)}, bf16[1,2,256,1024]{3,2,1,0:T(8,128)(2,1)}, u32[]{:S(2)}, u32[]{:S(2)}) collective-permute-start(bf16[1,2,256,1024]{3,2,1,0:T(8,128)(2,1)} %dynamic-slice_bitcast_fusion), channel_id=1, source_target_pairs={{0,4},{4,0},{8,12},{12,8},{16,20},{20,16},{24,28},{28,24},{1,5},{5... | collective-permute-start | bytes 3145736 | tf_op jit(solution)/shard_map/ppermute | solution.py:35
  794.7 53.2 %collective-permute-start.42 = (bf16[1,2,256,1024]{3,2,1,0:T(8,128)(2,1)}, bf16[1,2,256,1024]{3,2,1,0:T(8,128)(2,1)}, u32[]{:S(2)}, u32[]{:S(2)}) collective-permute-start(bf16[1,2,256,1024]{3,2,1,0:T(8,128)(2,1)} %fusion.40), channel_id=1, source_target_pairs={{0,16},{4,20},{8,24},{12,28},{16,0},{20,4},{24,8},{28,12},{1,17},{... | collective-permute-start | bytes 3145736 | tf_op jit(solution)/shard_map/ppermute | solution.py:35
  803.5 44.5 %collective-permute-start.43 = (bf16[1,2,256,768]{3,2,1,0:T(8,128)(2,1)}, bf16[1,2,256,768]{3,2,1,0:T(8,128)(2,1)}, u32[]{:S(2)}, u32[]{:S(2)}) collective-permute-start(bf16[1,2,256,768]{3,2,1,0:T(8,128)(2,1)} %dynamic-slice_bitcast_fusion.7), channel_id=1, source_target_pairs={{0,4},{4,0},{8,12},{12,8},{16,20},{20,16},{24,28},{28,24},{1,5},{5... | collective-permute-start | bytes 2359304 | tf_op jit(solution)/shard_map/ppermute | solution.py:35
  805.6 42.3 %collective-permute-start.44 = (bf16[1,2,256,256]{2,3,1,0:T(8,128)(2,1)}, bf16[1,2,256,256]{2,3,1,0:T(8,128)(2,1)S(1)}, u32[]{:S(2)}, u32[]{:S(2)}) collective-permute-start(bf16[1,2,256,256]{2,3,1,0:T(8,128)(2,1)} %bitcast.112), channel_id=1, source_target_pairs={{0,4},{4,0},{8,12},{12,8},{16,20},{20,16},{24,28},{28,24},{1,5},{5... | collective-permute-start | bytes 786440 | tf_op jit(solution)/shard_map/ppermute | solution.py:35
  851.9 17.5 %all-to-all-start = ((bf16[128,4,512]{2,0,1:T(8,128)(2,1)}), bf16[128,4,512]{2,0,1:T(8,128)(2,1)}, u32[]{:S(2)}, u32[]{:S(2)}) async-start(bf16[128,4,512]{2,0,1:T(8,128)(2,1)} %bitcast.369), calls=%async_computation.5 | async-start | bytes 1048576 | tf_op jit(solution)/shard_map/all_to_all | solution.py:597
  860.9 18.7 %collective-permute-start.50 = (bf16[256,1024]{1,0:T(8,128)(2,1)}, bf16[256,1024]{1,0:T(8,128)(2,1)}, u32[]{:S(2)}, u32[]{:S(2)}) collective-permute-start(bf16[256,1024]{1,0:T(8,128)(2,1)} %fusion.98), channel_id=1, source_target_pairs={{0,8},{4,12},{8,0},{12,4},{16,24},{20,28},{24,16},{28,20},{1,9},{5... | collective-permute-start | bytes 1572872 | tf_op jit(solution)/shard_map/ppermute | solution.py:35
  865.1 30.9 %collective-permute-start.48 = (bf16[1,2,256,768]{3,2,1,0:T(8,128)(2,1)}, bf16[1,2,256,768]{3,2,1,0:T(8,128)(2,1)}, u32[]{:S(2)}, u32[]{:S(2)}) collective-permute-start(bf16[1,2,256,768]{3,2,1,0:T(8,128)(2,1)} %dynamic-slice_bitcast_fusion.6), channel_id=1, source_target_pairs={{0,4},{4,0},{8,12},{12,8},{16,20},{20,16},{24,28},{28,24},{1,5},{5... | collective-permute-start | bytes 2359304 | tf_op jit(solution)/shard_map/ppermute | solution.py:35
  868.5 21.8 %collective-permute-start.49 = (bf16[1,2,256,256]{2,3,1,0:T(8,128)(2,1)}, bf16[1,2,256,256]{2,3,1,0:T(8,128)(2,1)}, u32[]{:S(2)}, u32[]{:S(2)}) collective-permute-start(bf16[1,2,256,256]{2,3,1,0:T(8,128)(2,1)} %bitcast.444), channel_id=1, source_target_pairs={{0,4},{4,0},{8,12},{12,8},{16,20},{20,16},{24,28},{28,24},{1,5},{5... | collective-permute-start | bytes 786440 | tf_op jit(solution)/shard_map/ppermute | solution.py:35
  870.6 21.4 %collective-permute-start.46 = (bf16[512,256]{1,0:T(8,128)(2,1)S(1)}, bf16[512,256]{1,0:T(8,128)(2,1)S(1)}, u32[]{:S(2)}, u32[]{:S(2)}) collective-permute-start(bf16[512,256]{1,0:T(8,128)(2,1)S(1)} %get-tuple-element.234.refs_9_), channel_id=1, source_target_pairs={{0,16},{4,20},{8,24},{12,28},{16,0},{20,4},{24,8},{28,12},{1,17},{... | collective-permute-start | bytes 786440 | tf_op jit(solution)/shard_map/ppermute | solution.py:35
  871.3 24.6 %collective-permute-start.45 = (bf16[512,256]{1,0:T(8,128)(2,1)S(1)}, bf16[512,256]{1,0:T(8,128)(2,1)S(1)}, u32[]{:S(2)}, u32[]{:S(2)}) collective-permute-start(bf16[512,256]{1,0:T(8,128)(2,1)S(1)} %get-tuple-element.226.refs_1_), channel_id=1, source_target_pairs={{0,16},{4,20},{8,24},{12,28},{16,0},{20,4},{24,8},{28,12},{1,17},{... | collective-permute-start | bytes 786440 | tf_op jit(solution)/shard_map/ppermute | solution.py:35
  898.7 16.6 %collective-permute-start.51 = (bf16[512,256]{1,0:T(8,128)(2,1)S(1)}, bf16[512,256]{1,0:T(8,128)(2,1)S(1)}, u32[]{:S(2)}, u32[]{:S(2)}) collective-permute-start(bf16[512,256]{1,0:T(8,128)(2,1)S(1)} %get-tuple-element.226.refs_1_), channel_id=1, source_target_pairs={{0,8},{4,12},{8,0},{12,4},{16,24},{20,28},{24,16},{28,20},{1,9},{5... | collective-permute-start | bytes 786440 | tf_op jit(solution)/shard_map/ppermute | solution.py:35
  898.7 19.4 %collective-permute-start.52 = (bf16[512,256]{1,0:T(8,128)(2,1)S(1)}, bf16[512,256]{1,0:T(8,128)(2,1)S(1)}, u32[]{:S(2)}, u32[]{:S(2)}) collective-permute-start(bf16[512,256]{1,0:T(8,128)(2,1)S(1)} %collective-permute-done.45.refs_5_), channel_id=1, source_target_pairs={{0,8},{4,12},{8,0},{12,4},{16,24},{20,28},{24,16},{28,20},{1,9},{5... | collective-permute-start | bytes 786440 | tf_op jit(solution)/shard_map/ppermute | solution.py:35
  900.8 17.3 %collective-permute-start.53 = (bf16[512,256]{1,0:T(8,128)(2,1)S(1)}, bf16[512,256]{1,0:T(8,128)(2,1)S(1)}, u32[]{:S(2)}, u32[]{:S(2)}) collective-permute-start(bf16[512,256]{1,0:T(8,128)(2,1)S(1)} %get-tuple-element.234.refs_9_), channel_id=1, source_target_pairs={{0,4},{4,0},{8,12},{12,8},{16,20},{20,16},{24,28},{28,24},{1,5},{5... | collective-permute-start | bytes 786440 | tf_op jit(solution)/shard_map/ppermute | solution.py:35
  901.5 16.6 %collective-permute-start.54 = (bf16[512,256]{1,0:T(8,128)(2,1)S(1)}, bf16[512,256]{1,0:T(8,128)(2,1)S(1)}, u32[]{:S(2)}, u32[]{:S(2)}) collective-permute-start(bf16[512,256]{1,0:T(8,128)(2,1)S(1)} %collective-permute-done.46.refs_13_), channel_id=1, source_target_pairs={{0,4},{4,0},{8,12},{12,8},{16,20},{20,16},{24,28},{28,24},{1,5},{5... | collective-permute-start | bytes 786440 | tf_op jit(solution)/shard_map/ppermute | solution.py:35
  902.9 32.8 %collective-permute-start.66 = (bf16[1,2,256,256]{2,3,1,0:T(8,128)(2,1)S(1)}, bf16[1,2,256,256]{2,3,1,0:T(8,128)(2,1)S(1)}, u32[]{:S(2)}, u32[]{:S(2)}) collective-permute-start(bf16[1,2,256,256]{2,3,1,0:T(8,128)(2,1)S(1)} %fusion.102), channel_id=1, source_target_pairs={{0,16},{4,20},{8,24},{12,28},{16,0},{20,4},{24,8},{28,12},{1,17},{... | collective-permute-start | bytes 786440 | tf_op jit(solution)/shard_map/ppermute | solution.py:35
  915.3 55.1 %collective-permute-start.65 = (bf16[1,2,256,768]{3,2,1,0:T(8,128)(2,1)S(1)}, bf16[1,2,256,768]{3,2,1,0:T(8,128)(2,1)S(1)}, u32[]{:S(2)}, u32[]{:S(2)}) collective-permute-start(bf16[1,2,256,768]{3,2,1,0:T(8,128)(2,1)S(1)} %fusion.50), channel_id=1, source_target_pairs={{0,16},{4,20},{8,24},{12,28},{16,0},{20,4},{24,8},{28,12},{1,17},{... | collective-permute-start | bytes 2359304 | tf_op jit(solution)/shard_map/ppermute | solution.py:35
  918.2 18.3 %collective-permute-start.64 = (f32[3,256]{1,0:T(4,128)S(1)}, f32[3,256]{1,0:T(4,128)S(1)}, u32[]{:S(2)}, u32[]{:S(2)}) collective-permute-start(f32[3,256]{1,0:T(4,128)S(1)} %bitcast.495), channel_id=1, source_target_pairs={{0,8},{4,12},{8,0},{12,4},{16,24},{20,28},{24,16},{28,20},{1,9},{5... | collective-permute-start | bytes 9224 | tf_op jit(solution)/shard_map/ppermute | solution.py:35
  921.1 16.8 %collective-permute-start.56 = (bf16[512,256]{1,0:T(8,128)(2,1)S(1)}, bf16[512,256]{1,0:T(8,128)(2,1)S(1)}, u32[]{:S(2)}, u32[]{:S(2)}) collective-permute-start(bf16[512,256]{1,0:T(8,128)(2,1)S(1)} %get-tuple-element.226.refs_1_), channel_id=1, source_target_pairs={{0,4},{4,0},{8,12},{12,8},{16,20},{20,16},{24,28},{28,24},{1,5},{5... | collective-permute-start | bytes 786440 | tf_op jit(solution)/shard_map/ppermute | solution.py:35
  938.0 16.3 %collective-permute-start.60 = (bf16[512,256]{1,0:T(8,128)(2,1)S(1)}, bf16[512,256]{1,0:T(8,128)(2,1)S(1)}, u32[]{:S(2)}, u32[]{:S(2)}) collective-permute-start(bf16[512,256]{1,0:T(8,128)(2,1)S(1)} %get-tuple-element.234.refs_9_), channel_id=1, source_target_pairs={{0,8},{4,12},{8,0},{12,4},{16,24},{20,28},{24,16},{28,20},{1,9},{5... | collective-permute-start | bytes 786440 | tf_op jit(solution)/shard_map/ppermute | solution.py:35
  938.1 21.8 %collective-permute-start.61 = (bf16[512,256]{1,0:T(8,128)(2,1)S(1)}, bf16[512,256]{1,0:T(8,128)(2,1)S(1)}, u32[]{:S(2)}, u32[]{:S(2)}) collective-permute-start(bf16[512,256]{1,0:T(8,128)(2,1)S(1)} %collective-permute-done.46.refs_13_), channel_id=1, source_target_pairs={{0,8},{4,12},{8,0},{12,4},{16,24},{20,28},{24,16},{28,20},{1,9},{5... | collective-permute-start | bytes 786440 | tf_op jit(solution)/shard_map/ppermute | solution.py:35
  942.0 23.5 %collective-permute-start.62 = (bf16[512,256]{1,0:T(8,128)(2,1)S(1)}, bf16[512,256]{1,0:T(8,128)(2,1)S(1)}, u32[]{:S(2)}, u32[]{:S(2)}) collective-permute-start(bf16[512,256]{1,0:T(8,128)(2,1)S(1)} %collective-permute-done.53.refs_10_), channel_id=1, source_target_pairs={{0,8},{4,12},{8,0},{12,4},{16,24},{20,28},{24,16},{28,20},{1,9},{5... | collective-permute-start | bytes 786440 | tf_op jit(solution)/shard_map/ppermute | solution.py:35
  945.6 24.9 %collective-permute-start.63 = (bf16[512,256]{1,0:T(8,128)(2,1)S(1)}, bf16[512,256]{1,0:T(8,128)(2,1)S(1)}, u32[]{:S(2)}, u32[]{:S(2)}) collective-permute-start(bf16[512,256]{1,0:T(8,128)(2,1)S(1)} %collective-permute-done.54.refs_14_), channel_id=1, source_target_pairs={{0,8},{4,12},{8,0},{12,4},{16,24},{20,28},{24,16},{28,20},{1,9},{5... | collective-permute-start | bytes 786440 | tf_op jit(solution)/shard_map/ppermute | solution.py:35
  (135 other events, 1491.8 us)
Sparse Core Ops, SparseCore 0:
  134.7 39.5 all-gather.5
  247.9 65.0 reduce-scatter.5
  316.5 44.0 all-gather.7
  382.5 54.1 reduce-scatter.7
  440.3 32.0 all-gather.9
  498.9 46.6 reduce-scatter.9
  548.2 46.6 all-gather.11
  614.0 49.3 reduce-scatter.11
  666.7 46.2 all-gather.13
  783.7 62.9 reduce-scatter.13

commit v3 on v2

v3 whole, which is shorter than its diff:
```python
import jax
import jax.numpy as jnp
import numpy as np
from jax import lax
from jax.experimental import pallas as pl
from jax.experimental.layout import Layout, with_layout_constraint
from jax.experimental.pallas import tpu as pltpu
from jax.sharding import PartitionSpec as P

D = 2048
HD = 128
FF = 8192
VT = 1024
VA = 256
STEP = 10


EPS = 1e-05
ZCOEF = 0.01
CLIP = 0.02
BETA1 = 0.9
BETA2 = 0.95
ADAM_EPS = 1e-08
DECAY = 0.1
RATE_FACTOR = 1.5
GAIN_RATE = 0.8

HALF = jnp.bfloat16
F32 = jnp.float32
NEG = -1e30
LOG2E = 1.4426950408889634
SCORE = HD ** (-0.5) * LOG2E
PAIR = 2


def flip(value, bit):
    count = lax.axis_size("blk")
    return lax.ppermute(value, "blk", [(i, i ^ bit) for i in range(count)])


def rms_norm(hidden, gain):
    return hidden * lax.rsqrt(jnp.mean(hidden * hidden, axis=-1, keepdims=True) + EPS) * gain


def norm_back(hidden, gain, upstream):
    unused, pullback = jax.vjp(rms_norm, hidden, gain)
    return pullback(upstream)


def dot(left, right, dims, out=F32):
    return lax.dot_general(left, right, (dims, ((), ())), preferred_element_type=F32).astype(out)


def adamw(weight, first, second, grad, rate, decay):
    first = BETA1 * first + (1.0 - BETA1) * grad
    second = BETA2 * second + (1.0 - BETA2) * grad * grad
    first_hat = first / (1.0 - BETA1**STEP)
    second_hat = second / (1.0 - BETA2**STEP)
    weight = weight - rate * (first_hat / (jnp.sqrt(second_hat) + ADAM_EPS) + decay * weight)
    return (weight, first, second)


def dot_last(left, right):
    return lax.dot_general(left, right, (((1,), (1,)), ((), ())), preferred_element_type=F32)


def dot_first(left, right):
    return lax.dot_general(left, right, (((0,), (0,)), ((), ())), preferred_element_type=F32)


def attend_kernel(opening, closing, qpos_ref, kpos_ref, q_ref, k_ref, v_ref, *refs):
    scores = dot_last(k_ref[...], q_ref[...]) * SCORE
    scores = jnp.where(kpos_ref[...] <= qpos_ref[...], scores, NEG)
    top = jnp.max(scores, axis=0, keepdims=True)
    if not opening:
        acc_in, top_in, total_in = refs[:3]
        refs = refs[3:]
        top = jnp.maximum(top, top_in[0])
    weights = jnp.exp2(scores - top)
    total = jnp.sum(weights, axis=0, keepdims=True)
    acc = dot_first(v_ref[...], weights.astype(HALF))
    if not opening:
        fading = jnp.exp2(top_in[0] - top)
        total = total + total_in[0] * fading
        acc = acc + acc_in[0] * fading
    if closing:
        out_ref, log_ref = refs
        out_ref[...] = (acc / total).T.astype(HALF)
        log_ref[0] = top + jnp.log2(total)
    else:
        acc_ref, top_ref, total_ref = refs
        acc_ref[0] = acc
        top_ref[0] = top
        total_ref[0] = total


def attend(queries, pairs, at, query_pos, key_pos, state, closing, count):
    team = queries.shape[0]
    step = min(team, 256)
    row = pl.BlockSpec((1, 1, step), lambda h, i: (h, 0, i))
    wide = pl.BlockSpec((1, HD, step), lambda h, i: (h, 0, i))
    rows = jax.ShapeDtypeStruct((count, 1, team), F32)
    if closing:
        out_specs = [pl.BlockSpec((step, HD), lambda h, i: (i, h)), row]
        out_shape = [jax.ShapeDtypeStruct((team, count * HD), HALF), rows]
    else:
        out_specs = [wide, row, row]
        out_shape = [jax.ShapeDtypeStruct((count, HD, team), F32), rows, rows]
    return pl.pallas_call(
        lambda *refs: attend_kernel(not state, closing, *refs),
        grid=(count, team // step),
        in_specs=[
            pl.BlockSpec((1, step), lambda h, i: (0, i)),
            pl.BlockSpec((team, 1), lambda h, i: (0, 0)),
            pl.BlockSpec((step, HD), lambda h, i: (i, h)),
            pl.BlockSpec((team, HD), lambda h, i: (0, at + h)),
            pl.BlockSpec((team, HD), lambda h, i: (0, at + count + h)),
        ]
        + ([wide, row, row] if state else []),
        out_specs=out_specs,
        out_shape=out_shape,
        compiler_params=pltpu.CompilerParams(vmem_limit_bytes=40 * 2**20),
        cost_estimate=pl.CostEstimate(
            flops=4 * count * team * team * HD,
            bytes_accessed=10 * count * team * HD,
            transcendentals=count * team * team,
        ),
    )(query_pos[None], key_pos[:, None], queries, pairs, pairs, *state)


def attend_back_kernel(opening, closing, qpos_ref, kpos_ref, q_ref, k_ref, v_ref, *refs):
    out_ref, grad_ref, log_ref = refs[:3]
    query_in, (query_ref, pair_ref, keys_acc, values_acc) = refs[3:-4], refs[-4:]
    head, step = pl.program_id(0), pl.program_id(1)
    grad = grad_ref[...]
    inner = (grad.astype(F32) * out_ref[...].astype(F32)).T
    inner = jnp.sum(inner, axis=0, keepdims=True)
    scores = dot_last(k_ref[...], q_ref[...]) * SCORE
    seen = kpos_ref[...] <= qpos_ref[...]
    probs = jnp.where(seen, jnp.exp2(scores - log_ref[0]), 0.0)
    grad_probs = dot_last(v_ref[...], grad)
    grad_scores = (probs * (grad_probs - inner)).astype(HALF)
    grad_query = dot_first(k_ref[...], grad_scores)
    if not opening:
        grad_query = grad_query + query_in[0][0]
    if closing:
        query_ref[...] = (grad_query * HD ** (-0.5)).T.astype(HALF)
    else:
        query_ref[0] = grad_query

    @pl.when(step == 0)
    def clear():
        keys_acc[...] = jnp.zeros_like(keys_acc)
        values_acc[...] = jnp.zeros_like(values_acc)

    keys_acc[...] += jnp.dot(grad_scores, q_ref[...], preferred_element_type=F32)
    values_acc[...] += jnp.dot(probs.astype(HALF), grad, preferred_element_type=F32)

    @pl.when(step == pl.num_programs(1) - 1)
    def write():
        half = pair_ref.shape[1] // 2
        at = pl.multiple_of(head * HD, HD)
        pair_ref[:, pl.ds(at, HD)] = (keys_acc[...] * HD ** (-0.5)).astype(pair_ref.dtype)
        pair_ref[:, pl.ds(half + at, HD)] = values_acc[...].astype(pair_ref.dtype)


def attend_back(queries, pairs, at, query_pos, key_pos, out, grad, log_total, state, closing, count):
    team = queries.shape[0]
    step = min(team, 256)
    wide = pl.BlockSpec((1, HD, step), lambda h, i: (h, 0, i))
    block = pl.BlockSpec((step, HD), lambda h, i: (i, h))
    if closing:
        query_spec, query_shape = block, jax.ShapeDtypeStruct((team, count * HD), HALF)
    else:
        query_spec, query_shape = wide, jax.ShapeDtypeStruct((count, HD, team), F32)
    return pl.pallas_call(
        lambda *refs: attend_back_kernel(state is None, closing, *refs),
        grid=(count, team // step),
        in_specs=[
            pl.BlockSpec((1, step), lambda h, i: (0, i)),
            pl.BlockSpec((team, 1), lambda h, i: (0, 0)),
            block,
            pl.BlockSpec((team, HD), lambda h, i: (0, at + h)),
            pl.BlockSpec((team, HD), lambda h, i: (0, at + count + h)),
            block,
            block,
            pl.BlockSpec((1, 1, step), lambda h, i: (h, 0, i)),
        ]
        + ([] if state is None else [wide]),
        out_specs=[query_spec, pl.BlockSpec((team, 2 * count * HD), lambda h, i: (0, 0))],
        out_shape=[
            query_shape,
            jax.ShapeDtypeStruct((team, 2 * count * HD), F32 if closing else HALF),
        ],
        scratch_shapes=[pltpu.VMEM((team, HD), F32), pltpu.VMEM((team, HD), F32)],
        compiler_params=pltpu.CompilerParams(vmem_limit_bytes=48 * 2**20),
        cost_estimate=pl.CostEstimate(
            flops=10 * count * team * team * HD,
            bytes_accessed=20 * count * team * HD,
            transcendentals=count * team * team,
        ),
    )(
        query_pos[None],
        key_pos[:, None],
        queries,
        pairs,
        pairs,
        out,
        grad,
        log_total,
        *([] if state is None else [state]),
    )


def joined_norm_kernel(sides, at_ref, gain_ref, *refs):
    pieces, out_ref, first_ref = refs[:-2], refs[-2], refs[-1]
    count = len(pieces) // sides
    width = pieces[0].shape[1]
    is_first = (pl.program_id(0) == 0) & (pl.program_id(1) == 0)
    for side in range(sides):
        parts = [ref[...].astype(F32) for ref in pieces[side * count : (side + 1) * count]]
        squares = sum(jnp.sum(part * part, axis=-1, keepdims=True) for part in parts)
        scale = lax.rsqrt(squares / (count * width) + EPS)
        for k, part in enumerate(parts):
            at = pl.ds(pl.multiple_of(at_ref[k] * width, width), width)
            out_ref[0, side, 0, :, at] = (part * scale * gain_ref[:, at]).astype(HALF)
            if side == 0:

                @pl.when(is_first)
                def keep():
                    first_ref[:, at] = part


def joined_norm(pieces, at, gain, own):
    ys = len(pieces[0][0])
    width = pieces[0][0][0].shape[1]
    columns = 2 * ys * width
    flat, specs = [], []
    for of_side in pieces:
        for core, of_core in enumerate(of_side):
            for y, piece in enumerate(of_core):
                flat.append(piece)
                specs.append(
                    pl.BlockSpec(
                        (own, width),
                        lambda c, k, at, core=core, y=y: ((c ^ core) * ys + (k ^ y), 0),
                    )
                )
    grid = pltpu.PrefetchScalarGridSpec(
        num_scalar_prefetch=1,
        grid=(2, ys),
        in_specs=[pl.BlockSpec((1, columns), lambda c, k, at: (0, 0))] + specs,
        out_specs=[
            pl.BlockSpec((1, 2, 1, own, columns), lambda c, k, at: (c, 0, k, 0, 0)),
            pl.BlockSpec((own, columns), lambda c, k, at: (0, 0)),
        ],
    )
    normed, first = pl.pallas_call(
        lambda *refs: joined_norm_kernel(2, *refs),
        grid_spec=grid,
        out_shape=[
            jax.ShapeDtypeStruct((2, 2, ys, own, columns), HALF),
            jax.ShapeDtypeStruct((own, columns), F32),
        ],
        compiler_params=pltpu.CompilerParams(vmem_limit_bytes=60 * 2**20),
        cost_estimate=pl.CostEstimate(
            flops=20 * ys * own * columns, bytes_accessed=16 * ys * own * columns, transcendentals=0
        ),
    )(at, gain[None], *flat)
    return normed.reshape(4 * ys * own, columns), first


def table_grad_kernel(places, at_ref, *refs):
    parts, out_ref = refs[:-1], refs[-1]
    tokens = at_ref.shape[1]
    width = parts[0].shape[2]
    step = out_ref.shape[0]
    row = pl.program_id(0) * step + lax.broadcasted_iota(jnp.int32, (step, tokens), 0)
    for part, order in enumerate(places):
        total = jnp.zeros((step, width), F32)
        for k, place in enumerate(order):
            pieces, at = parts[2 * part + place // (len(order) // 2)], place % (len(order) // 2)
            pick = (row == at_ref[k][None, :]).astype(F32).astype(HALF)
            total += jnp.dot(pick, pieces[at, :tokens], preferred_element_type=F32)
        out_ref[:, part * width : (part + 1) * width] = total


def table_grad(at, parts, places, rows, step):
    count, tokens = at.shape
    columns = parts[0].shape[2] * len(places)
    return pl.pallas_call(
        lambda *refs: table_grad_kernel(places, *refs),
        grid=(rows // step,),
        in_specs=[pl.BlockSpec((count, tokens), lambda i: (0, 0))]
        + [pl.BlockSpec(part.shape, lambda i: (0, 0, 0)) for part in parts],
        out_specs=pl.BlockSpec((step, columns), lambda i: (i, 0)),
        out_shape=jax.ShapeDtypeStruct((rows, columns), F32),
        compiler_params=pltpu.CompilerParams(vmem_limit_bytes=56 * 2**20),
        cost_estimate=pl.CostEstimate(
            flops=2 * rows * count * tokens * columns,
            bytes_accessed=2 * count * tokens * columns + 4 * rows * columns,
            transcendentals=0,
        ),
    )(at, *parts)


def assembled_kernel(count, at_ref, *refs):
    pieces, out_ref = refs[:count], refs[count]
    for k, piece in enumerate(pieces):

        @pl.when(pl.program_id(0) == k)
        def write():
            out_ref[0, :, 0] = piece[...]


def assembled_at(places, pieces):
    count = len(pieces)
    unused, rows, columns = pieces[0].shape
    grid = pltpu.PrefetchScalarGridSpec(
        num_scalar_prefetch=1,
        grid=(count,),
        in_specs=[pl.BlockSpec((2, rows, columns), lambda i, at: (0, 0, 0)) for piece in pieces],
        out_specs=pl.BlockSpec(
            (1, 2, 1, rows, columns), lambda i, at: (at[2 * i], 0, at[2 * i + 1], 0, 0)
        ),
    )
    whole = pl.pallas_call(
        lambda *refs: assembled_kernel(count, *refs),
        grid_spec=grid,
        out_shape=jax.ShapeDtypeStruct((count // 2, 2, 2, rows, columns), HALF),
        compiler_params=pltpu.CompilerParams(vmem_limit_bytes=60 * 2**20),
        cost_estimate=pl.CostEstimate(
            flops=0, bytes_accessed=4 * count * pieces[0].size, transcendentals=0
        ),
    )(places, *pieces)
    return whole.reshape(count * 2 * rows, columns)


def shards(
    inward,
    outward,
    expand,
    contract,
    image_table,
    code_table,
    readout,
    gains,
    inward_first,
    outward_first,
    expand_first,
    contract_first,
    image_first,
    code_first,
    readout_first,
    gains_first,
    inward_second,
    outward_second,
    expand_second,
    contract_second,
    image_second,
    code_second,
    readout_second,
    gains_second,
    token_ids,
    modality,
    clip_lengths,
    loss_mask,
    targets,
):
    blocks = lax.axis_size("blk")
    heads = lax.axis_size("head")
    blk = lax.axis_index("blk")
    head = lax.axis_index("head")
    clips, span = token_ids.shape
    length = span * blocks
    rows = D // blocks
    low = blk % 2
    side = (blk // 2) % 2
    high = blk // 4
    highs = blocks // 4
    groups = blocks // 2
    group = high * 2 + low
    per_clip = groups // clips
    clip = group // per_clip
    place = group % per_clip
    ranks = 2 * heads
    core, y_at, ys = head % 2, head // 2, heads // 2
    rank = side * heads + head
    team = clips * length // groups
    half = team // 2
    own = team // ranks
    high_bits = [1 << k for k in range(2, blocks.bit_length() - 1)]
    all_bits = [1, 2] + high_bits
    both = ("blk", "head")
    near_peers = [(side_bit, 2 * y) for side_bit in (0, PAIR) for y in range(ys)][1:]

    def hop(value, blk_bits, head_bits):
        pairs = [
            (i * heads + h, (i ^ blk_bits) * heads + (h ^ head_bits))
            for i in range(blocks)
            for h in range(heads)
        ]
        return lax.ppermute(value, both, pairs)

    def tie(*values):
        return lax.optimization_barrier(values)

    def gathered(block, *riders):
        parts, riders = tie([hop(block, *bits) for bits in near_peers], riders)
        mine = jnp.concatenate([block] + parts)
        return ((mine, hop(mine, 0, 1)), *riders)

    def core_sum(mine, other, weight, dims):
        came = hop(dot(other, weight, dims, HALF), 0, 1)
        (made,) = tie(dot(mine, weight, dims, HALF))
        made = (made.astype(F32) + came.astype(F32)).astype(HALF)
        return made.reshape(ranks // 2, own, D)

    def group_sum(made, *riders):
        parts = [hop(made[k + 1], *bits) for k, bits in enumerate(near_peers)]
        parts, riders = tie(parts, riders)
        return (sum((part.astype(F32) for part in parts), made[0].astype(F32)), *riders)

    def index_of(shift):
        pairs = []
        for i in range(blocks):
            g = (i // 4) * 2 + i % 2
            far = g + shift
            if 0 <= far < groups and far // per_clip == g // per_clip:
                pairs.append((i, (far // 2) * 4 + (i & PAIR) + far % 2))
        return pairs

    def sided(weight):
        return weight.astype(HALF).reshape(rows, 2, -1)

    qkv_local = inward.astype(HALF).reshape(3, rows, 2, -1).transpose(1, 2, 0, 3)
    local_first = jnp.concatenate(
        [qkv_local.reshape(rows, 2, -1), sided(outward.astype(HALF).T)], axis=-1
    )
    local = [
        None,
        sided(expand),
        sided(contract.astype(HALF).T),
        sided(readout),
    ]

    def sides_of(halves):
        return tuple(
            lax.dynamic_index_in_dim(halves, at, 1, keepdims=False) for at in (side, 1 - side)
        )

    def paired(keep, send):
        came = flip(send, PAIR)
        return jnp.where(side == 0, jnp.stack([keep, came]), jnp.stack([came, keep]))

    small = jnp.concatenate(
        [part.astype(F32).reshape(-1) for part in (token_ids, modality, loss_mask, targets, gains)]
    )[None]
    small = jnp.concatenate([small, flip(small, PAIR)])
    local_first, small = tie(local_first, small)
    masks = [0, PAIR]
    for bit in high_bits + [1]:
        small = jnp.concatenate([small, flip(small, bit)])
        masks = masks + [mask | bit for mask in masks]
    order = blk ^ jnp.arange(blocks)
    mine_first = paired(*sides_of(local_first))
    small = small[jnp.array([masks.index(mask) for mask in range(blocks)])[order]]
    cells = clips * span
    ids_all, modality_all, mask_all, targets_all = (
        small[:, k * cells : (k + 1) * cells]
        .astype(jnp.int32)
        .reshape(blocks, clips, span)
        .transpose(1, 0, 2)
        .reshape(clips, length)
        for k in range(4)
    )
    gains_full = small[:, 4 * cells :].reshape(blocks, 3, rows).transpose(1, 0, 2).reshape(3, D)

    def spread_high(mine, at=slice(None)):
        pieces = [mine[at]]
        for bit in high_bits:
            pieces = pieces + [flip(piece, bit) for piece in pieces]
        return tuple(pieces[1:])

    def both_sides(first, second):
        return tuple(jnp.stack(pair) for pair in zip(first, second))

    def spread_low(pieces):
        return tuple(flip(piece, 1) for piece in pieces)

    def assembled(mine, far, near):
        pieces = (mine, *far, *near)
        places = [high ^ (k % highs) if side_at == 0 else low ^ (k // highs)
                  for k in range(len(pieces)) for side_at in range(2)]
        return assembled_at(jnp.stack(places).astype(jnp.int32), pieces)

    mine = [mine_first, None, None, None]
    far = [None] * 4
    near = [None] * 4

    head_order = ((core ^ jnp.arange(2))[:, None] * ys + (y_at ^ jnp.arange(ys))[None]).reshape(-1)

    def by_device(array):
        split = array.reshape(highs, 2, 2, 2, ys, own).transpose(0, 3, 1, 2, 4, 5)
        split = split.reshape(blocks, 2 * ys, own)[:, head_order]
        return split.reshape(blocks, half)

    image_rows = image_table.shape[0]
    code_local = code_table.shape[0]
    table = jnp.concatenate([image_table.astype(HALF), code_table.astype(HALF)])
    ids_dev, modality_dev = by_device(ids_all)[order], by_device(modality_all)[order]
    code_rows = jnp.clip(jnp.where(modality_dev == 1, ids_dev, VT + ids_dev), 0, VT + VA - 1)
    image_at = ids_dev - blk * image_rows
    code_at = code_rows - blk * code_local
    image_at = jnp.where((image_at >= 0) & (image_at < image_rows), image_at, -1)
    code_at = jnp.where((code_at >= 0) & (code_at < code_local), code_at + image_rows, -1)
    table_at = jnp.where(modality_dev == 0, image_at, code_at)
    table_rows = image_rows + code_local
    pick = (table_at.reshape(-1)[:, None] == jnp.arange(table_rows)[None, :]).astype(HALF)
    picked = dot(pick, table, ((1,), (0,)), HALF)
    width = table.shape[1]
    levels = len(all_bits)
    picked = picked.reshape((2,) * levels + (half, width))

    def token_hop(part, bit, left):
        axis = left.index(bit)
        keep = lax.index_in_dim(part, 0, axis, keepdims=False)
        send = lax.index_in_dim(part, 1, axis, keepdims=False)
        return keep + flip(send, bit)

    left = sorted(all_bits, reverse=True)
    mid = 3 * width // 4
    picked, mine[0] = tie(picked, mine[0])
    far[0] = spread_high(mine[0])
    part_a = token_hop(picked[..., :mid], 1, left)
    part_b = token_hop(picked[..., mid:], PAIR, left)
    local[1:] = [sides_of(halves) for halves in local[1:]]
    part_a = token_hop(part_a, PAIR, left[:-1])
    part_b = token_hop(part_b, 1, left[:-2] + left[-1:])
    part_a, part_b, mine[0], far[0], local[1] = tie(part_a, part_b, mine[0], far[0], local[1])
    mine[1] = paired(*local[1])
    near_own = spread_low(mine[:1])
    for k, bit in enumerate(high_bits[::-1]):
        part_a = token_hop(part_a, bit, left[k:-2])
        part_b = token_hop(part_b, bit, left[k:-2])
    block = jnp.concatenate([part_a, part_b], axis=-1)
    block, mine[1], far[0], near_own, local[2:] = tie(block, mine[1], far[0], near_own, local[2:])
    far_side, near_far = spread_high(mine[1], 0), spread_low(far[0])
    of_core = [
        [block if not bits else hop(block, *bits) for bits in row]
        for row in ([()] + near_peers[: ys - 1], near_peers[ys - 1 :])
    ]
    of_core, far_side, near_far, mine[1], local[2] = tie(
        of_core, far_side, near_far, mine[1], local[2]
    )
    near[0] = (*near_own, *near_far)
    far_other, near_own = spread_high(mine[1], 1), spread_low(mine[1:2])
    mine[2] = paired(*local[2])
    column_pieces = [[row, [hop(piece, 0, 1) for piece in row]] for row in of_core]
    column_at = jnp.stack([head ^ (2 * y + c) for c in range(2) for y in range(ys)])
    normed_in, embedded_own = joined_norm(column_pieces, column_at, gains_full[0], own)
    w_first = assembled(mine[0], far[0], near[0])
    head_columns = w_first.shape[-1] // 4
    w_in, w_out = w_first[:, : 3 * head_columns], w_first[:, 3 * head_columns :]
    local_heads = head_columns // HD
    mixed = dot(normed_in, w_in, ((1,), (0,)), HALF)
    mixed, near_own, far_other, mine[2], local[3] = tie(
        mixed, near_own, far_other, mine[2], local[3]
    )
    mine[3] = paired(*local[3])
    far[1] = both_sides(far_side, far_other)
    far_side = spread_high(mine[2], 0)
    block_order = (
        ((core ^ jnp.arange(2))[:, None, None] * 2 + (side ^ jnp.arange(2))[None, :, None]) * ys
        + (y_at ^ jnp.arange(ys))[None, None]
    ).reshape(-1)
    query_pos = place * team + (block_order[:, None] * own + jnp.arange(own)[None]).reshape(-1)
    query_pos = query_pos.astype(jnp.int32)

    def key_pos(back):
        return jnp.where(query_pos >= back * team, query_pos - back * team, length)

    pairs_own = mixed[:, head_columns:]
    earlier = [lax.ppermute(pairs_own, "blk", index_of(back)) for back in range(1, per_clip)]
    running = attend(
        mixed, mixed, local_heads, query_pos, query_pos, (), per_clip == 1, local_heads
    )
    running, earlier, far_side, far[1], mine[2], mine[3] = tie(
        running, earlier, far_side, far[1], mine[2], mine[3]
    )
    far_other, near_far = spread_high(mine[2], 1), spread_low(far[1])
    for back in range(1, per_clip):
        running = attend(
            mixed,
            earlier[back - 1],
            0,
            query_pos,
            key_pos(back),
            running,
            back == per_clip - 1,
            local_heads,
        )
    flat_heads, log_total = running
    made = core_sum(flat_heads[:half], flat_heads[half:], w_out, ((1,), (1,)))
    made, mine[2] = tie(made, mine[2])
    near_next = spread_low(mine[2:3])
    first, near_far, far_other = group_sum(made, near_far, far_other)
    near[1] = (*near_own, *near_far)
    w_up = assembled(mine[1], far[1], near[1])
    first = embedded_own + first
    far[2] = both_sides(far_side, far_other)
    far_side, near_far = spread_high(mine[3], 0), spread_low(far[2])
    normed_mid, far_side, near_far, near_next, w_up, mine[3] = gathered(
        rms_norm(first, gains_full[1]).astype(HALF), far_side, near_far, near_next, w_up, mine[3]
    )
    near[2] = (*near_next, *near_far)
    w_down = assembled(mine[2], far[2], near[2])
    hidden_up = [dot(part, w_up, ((1,), (0,))) for part in normed_mid]
    active = [jax.nn.gelu(part).astype(HALF) for part in hidden_up]
    near_own, far_other = spread_low(mine[3:]), spread_high(mine[3], 1)
    made = core_sum(*active, w_down, ((1,), (1,)))
    second, near_own, far_other = group_sum(made, near_own, far_other)
    far[3] = both_sides(far_side, far_other)
    second = first + second
    final_in, *near_far = gathered(
        rms_norm(second, gains_full[2]).astype(HALF), *spread_low(far[3])
    )
    w_read = assembled(mine[3], far[3], (*near_own, *near_far))
    logits = [dot(part, w_read, ((1,), (0,))) for part in final_in]

    def of_team(array):
        taken = lax.dynamic_slice(array, (clip, place * team), (1, team))
        return taken.reshape(ranks, own)[block_order].reshape(team)

    weight_all = (
        (mask_all == 1) & (jnp.arange(length)[None, :] < clip_lengths[:, None])
    ).astype(F32)
    loss_count = jnp.sum(weight_all)
    weight_of = of_team(weight_all)
    targets_own = of_team(targets_all)
    vocab_local = logits[0].shape[1]
    column_ids = (head * 2 + side) * vocab_local + jnp.arange(vocab_local)
    halves = (slice(0, half), slice(half, team))
    match = [column_ids[None, :] == targets_own[at][:, None] for at in halves]
    parts = []
    for part, hit in zip(logits, match):
        top = jnp.max(part, axis=-1)
        total = jnp.sum(jnp.exp(part - top[:, None]), axis=-1)
        parts.append(jnp.stack([top, total, jnp.sum(jnp.where(hit, part, 0.0), axis=-1)]))
    stats = jnp.concatenate(parts, axis=1)
    for axis, bits in [(2, (PAIR, 0)), (1, (0, 1))] + [
        (3, (0, 2 << k)) for k in range(ys.bit_length() - 1)
    ]:
        other = hop(stats, *bits).reshape(3, 2, 2, ys, own)
        flipped = np.arange(other.shape[axis]) ^ (bits[1] // 2 if axis == 3 else 1)
        other = jnp.stack(
            [lax.index_in_dim(other, k, axis, keepdims=False) for k in flipped], axis=axis
        ).reshape(3, team)
        top = jnp.maximum(stats[0], other[0])
        total = stats[1] * jnp.exp(stats[0] - top) + other[1] * jnp.exp(other[0] - top)
        stats = jnp.stack([top, total, stats[2] + other[2]])
    log_norm = stats[0] + jnp.log(stats[1])
    per_token = (log_norm + ZCOEF * log_norm * log_norm - stats[2]) * weight_of
    loss_part = jnp.sum(per_token) * (rank == 0).astype(F32)

    token_grad = weight_of / loss_count
    grad_logits = []
    for part, hit, at in zip(logits, match, halves):
        probs = jnp.exp(part - log_norm[at][:, None])
        scaled = probs * (1.0 + 2.0 * ZCOEF * log_norm[at])[:, None] - hit.astype(F32)
        grad_logits.append((token_grad[at][:, None] * scaled).astype(HALF))

    top_bit = high_bits[-1]
    top = (blk // top_bit) % 2

    def made_of(left, right):
        return dot(left, right, ((0,), (0,)), HALF).reshape(
            2, highs // 2, 2, 2, rows, right.shape[1]
        )

    def low_part(made, at_top, at_low):
        chosen = lax.dynamic_index_in_dim(made, at_top, 0, keepdims=False)
        return lax.dynamic_index_in_dim(chosen, at_low, 2, keepdims=False)

    def send_low(made, at_top):
        return flip(low_part(made, at_top, 1 - low), 1)

    def add_low(made, at_top, came):
        return low_part(made, at_top, low).astype(F32) + came.astype(F32)

    def for_top(made, came):
        total = add_low(made, 1 - top, came).astype(HALF)
        return total[:, 0], total[:, 1]

    def send_high(part):
        return flip(part, top_bit)

    def add_high(made, came_low, came_high):
        total = add_low(made, top, came_low) + jnp.stack(came_high, axis=1).astype(F32)
        total = total.reshape((2,) * (len(high_bits) - 1) + total.shape[1:])
        for bit in high_bits[-2::-1] if len(high_bits) > 1 else []:
            at = (blk // bit) % 2
            send = lax.dynamic_index_in_dim(total, 1 - at, 0, keepdims=False)
            keep = lax.dynamic_index_in_dim(total, at, 0, keepdims=False)
            total = keep + flip(send.astype(HALF), bit).astype(F32)
        return total

    def sum_sides(total):
        send = lax.dynamic_index_in_dim(total, 1 - side, 0, keepdims=False)
        keep = lax.dynamic_index_in_dim(total, side, 0, keepdims=False)
        came = flip(send.astype(HALF), PAIR).astype(F32)
        return jnp.where(side == 0, keep, came), jnp.where(side == 0, came, keep)

    def joined(parts):
        return jnp.concatenate(parts)

    made = core_sum(*grad_logits, w_read, ((1,), (1,)))
    made, read_made = tie(made, made_of(joined(final_in), joined(grad_logits)))
    read_far = send_low(read_made, 1 - top)
    grad_final, read_made, read_far = group_sum(made, read_made, read_far)
    read_near = send_low(read_made, top)
    read_top = for_top(read_made, read_far)
    read_first = send_high(read_top[0])
    grad_second, gain_final = norm_back(second, gains_full[2], grad_final)
    branch_grad, read_near, read_first, read_top = gathered(
        grad_second.astype(HALF), read_near, read_first, read_top
    )
    read_second = send_high(read_top[1])
    grad_hidden = []
    for part, up in zip(branch_grad, hidden_up):
        unused_gelu, gelu_pull = jax.vjp(jax.nn.gelu, up)
        grad_hidden.append(gelu_pull(dot(part, w_down, ((1,), (0,))))[0].astype(HALF))
    made = core_sum(*grad_hidden, w_up, ((1,), (1,)))
    made, normed_mid, grad_hidden, read_second, down_made = tie(
        made,
        normed_mid,
        grad_hidden,
        read_second,
        made_of(joined(branch_grad), joined(active)),
    )
    read_total = add_high(read_made, read_near, (read_first, read_second))
    down_far = send_low(down_made, 1 - top)
    grad_mid, down_made, down_far, up_made = group_sum(
        made, down_made, down_far, made_of(joined(normed_mid), joined(grad_hidden))
    )
    down_near = send_low(down_made, top)
    down_top = for_top(down_made, down_far)
    down_first = send_high(down_top[0])
    grad_mid_in, gain_mid = norm_back(first, gains_full[1], grad_mid)
    grad_first = grad_second + grad_mid_in
    attn_grad, up_made, down_near, down_first, down_top, read_total = gathered(
        grad_first.astype(HALF), up_made, down_near, down_first, down_top, read_total
    )
    down_second = send_high(down_top[1])
    up_far = send_low(up_made, 1 - top)
    attn_grad = joined(attn_grad)
    grad_heads = dot(attn_grad, w_out, ((1,), (0,)), HALF)
    returned = []
    grad_query = None
    for back in range(1, per_clip):
        grad_query, far_pairs = attend_back(
            mixed,
            earlier[back - 1],
            0,
            query_pos,
            key_pos(back),
            flat_heads,
            grad_heads,
            log_total,
            grad_query,
            False,
            local_heads,
        )
        if back == 1:
            far_pairs, up_made, up_far, down_second, read_total = tie(
                far_pairs, up_made, up_far, down_second, read_total
            )
            grad_read = sum_sides(read_total)
            grad_down = sum_sides(add_high(down_made, down_near, (down_first, down_second)))
            up_near = send_low(up_made, top)
            up_top = for_top(up_made, up_far)
            up_first = send_high(up_top[0])
        returned.append(lax.ppermute(far_pairs, "blk", index_of(-back)))
    grad_query, grad_pairs = attend_back(
        mixed,
        mixed,
        local_heads,
        query_pos,
        query_pos,
        flat_heads,
        grad_heads,
        log_total,
        grad_query,
        True,
        local_heads,
    )
    for far_pairs in returned:
        grad_pairs = grad_pairs + far_pairs.astype(F32)
    grad_mixed = jnp.concatenate([grad_query, grad_pairs.astype(HALF)], axis=1)
    grad_mixed, up_first, up_top, grad_read = tie(grad_mixed, up_first, up_top, grad_read)
    up_second = send_high(up_top[1])
    made = core_sum(grad_mixed[:half], grad_mixed[half:], w_in, ((1,), (1,)))
    made, in_made, out_made, up_near, grad_down = tie(
        made,
        made_of(normed_in, grad_mixed),
        made_of(attn_grad, flat_heads),
        up_near,
        grad_down,
    )
    in_far, out_far = send_low(in_made, 1 - top), send_low(out_made, 1 - top)
    grad_norm_in, in_made, out_made, in_far, out_far, up_second = group_sum(
        made, in_made, out_made, in_far, out_far, up_second
    )
    in_near, out_near = send_low(in_made, top), send_low(out_made, top)
    in_top, out_top = for_top(in_made, in_far), for_top(out_made, out_far)
    in_first, out_first = send_high(in_top[0]), send_high(out_top[0])
    grad_embed_in, gain_in = norm_back(embedded_own, gains_full[0], grad_norm_in)
    grad_embed = (grad_first + grad_embed_in).astype(HALF)

    def columns_of(head_bits):
        at = (head ^ head_bits) * width
        return lax.dynamic_slice(grad_embed, (0, at), (own, width))

    head_bits = [2 * y + c for c in range(2) for y in range(ys)]
    head_parts = [
        columns_of(bits) if bits == 0 else hop(columns_of(bits), 0, bits) for bits in head_bits
    ]
    grad_up = sum_sides(add_high(up_made, up_near, (up_first, up_second)))
    columns_own = jnp.concatenate(head_parts)
    gain_own = jnp.stack([gain_in, gain_mid, gain_final])
    for k in range(heads.bit_length() - 1):
        gain_own = gain_own + hop(gain_own, 0, 1 << k)

    def spread(pieces, bit):
        return jnp.concatenate([pieces, flip(pieces, bit)])

    mid = width // 2
    gain_rows = gain_own.astype(HALF).reshape(-1, width - mid)
    gain_rows = jnp.pad(gain_rows, ((0, -gain_rows.shape[0] % 16), (0, 0)))
    pieces_a, pieces_b = tie(
        columns_own[None, :, :mid], jnp.concatenate([columns_own[:, mid:], gain_rows])[None]
    )
    for bit in high_bits[::-1]:
        pieces_a, pieces_b = spread(pieces_a, bit), spread(pieces_b, bit)
    pieces_a, pieces_b, in_first, out_first, in_top, out_top, in_near, out_near = tie(
        pieces_a, pieces_b, in_first, out_first, in_top, out_top, in_near, out_near
    )
    in_second, out_second = send_high(in_top[1]), send_high(out_top[1])
    pieces_a, pieces_b = spread(pieces_a, PAIR), spread(pieces_b, 1)
    pieces_a, pieces_b, in_second, out_second, grad_up = tie(
        pieces_a, pieces_b, in_second, out_second, grad_up
    )
    pieces = (pieces_a, flip(pieces_a, 1), pieces_b, flip(pieces_b, PAIR))
    pieces, in_total, out_total = tie(
        pieces,
        add_high(in_made, in_near, (in_first, in_second)),
        add_high(out_made, out_near, (out_first, out_second)),
    )
    grad_in, grad_out_w = sum_sides(in_total), sum_sides(out_total)
    gain_sum = sum(jnp.sum(part[:, half:].astype(F32), axis=0) for part in pieces[2:])
    gain_sum = gain_sum.reshape(-1)[: 3 * D].reshape(3, D)
    gain_sum = lax.dynamic_slice_in_dim(gain_sum, blk * rows, rows, 1)
    masks_a, masks_b = [0], [0]
    for bit_a, bit_b in zip(high_bits[::-1] + [PAIR, 1], high_bits[::-1] + [1, PAIR]):
        masks_a = masks_a + [mask | bit_a for mask in masks_a]
        masks_b = masks_b + [mask | bit_b for mask in masks_b]
    places = [[masks.index(mask) for mask in range(blocks)] for masks in (masks_a, masks_b)]
    row_step = max(s for s in range(8, 321, 8) if table_rows % s == 0)
    grad_table = table_grad(table_at, pieces, places, table_rows, row_step)
    img_sum, code_sum = grad_table[:image_rows], grad_table[image_rows:]

    in_sum = jnp.stack(
        [
            jnp.concatenate(
                [part[:, k * head_columns : (k + 1) * head_columns] for part in grad_in], axis=1
            )
            for k in range(3)
        ]
    )
    out_sum = jnp.concatenate([part.T for part in grad_out_w])
    down_sum = jnp.concatenate([part.T for part in grad_down])
    up_sum = jnp.concatenate(grad_up, axis=1)
    read_sum = jnp.concatenate(grad_read, axis=1)
    in_sum, out_sum, up_sum, down_sum, read_sum = (
        with_layout_constraint(total, Layout(major_to_minor=tuple(range(total.ndim))))
        for total in (in_sum, out_sum, up_sum, down_sum, read_sum)
    )
    sums = [in_sum, out_sum, up_sum, down_sum, img_sum, code_sum, read_sum, gain_sum]
    local_squares = jnp.float32(0.0)
    for shard in sums[:7]:
        local_squares = local_squares + jnp.sum(shard * shard)
    local_squares = local_squares + (head == 0).astype(F32) * jnp.sum(gain_sum * gain_sum)
    mine = jnp.broadcast_to(
        jnp.stack([local_squares, loss_part])[None, :, None], (blocks * heads, 2, 128)
    )
    totals = jnp.sum(lax.all_to_all(mine, both, 0, 0, tiled=True), axis=0)
    grad_norm = jnp.sqrt(totals[0, 0])
    loss_sum = totals[1, 0]
    factor = jnp.minimum(1.0, CLIP / grad_norm)
    spreads = [
        D ** (-0.5),
        (length // 2) ** 0.5 * D ** (-0.5),
        D ** (-0.5),
        FF ** (-0.5),
        0.05,
        0.05,
        2.0 * D ** (-0.5),
    ]
    weights = [inward, outward, expand, contract, image_table, code_table, readout, gains]
    firsts = [
        inward_first,
        outward_first,
        expand_first,
        contract_first,
        image_first,
        code_first,
        readout_first,
        gains_first,
    ]
    seconds = [
        inward_second,
        outward_second,
        expand_second,
        contract_second,
        image_second,
        code_second,
        readout_second,
        gains_second,
    ]
    result = []
    for index in range(8):
        rate = GAIN_RATE if index == 7 else RATE_FACTOR * spreads[index]
        decay = 0.0 if index == 7 else DECAY
        result.extend(
            adamw(weights[index], firsts[index], seconds[index], sums[index] * factor, rate, decay)
        )
    return (*result, loss_sum, loss_count, grad_norm)


def solution(mesh):
    matrices = (
        P(None, "blk", "head"),
        P("head", "blk"),
        P("blk", "head"),
        P("head", "blk"),
        P("blk", "head"),
        P("blk", "head"),
        P("blk", "head"),
        P(None, "blk"),
    )
    tokens = P(None, "blk")
    return jax.shard_map(
        shards,
        mesh=mesh,
        in_specs=matrices * 3 + (tokens, tokens, P(), tokens, tokens),
        out_specs=tuple(spec for spec in matrices for _ in range(3)) + (P(), P(), P()),
        check_vma=False,
    )
```

time: 1070 us -> 984 us (0.920)
  waiting for transfers between devices: 559 us -> 459 us
  matrix products: 141 us -> 90.7 us
  Pallas kernels: 27.8 us -> 75.3 us
  starting transfers between devices: 94.1 us -> 115 us
  between operations: 24.4 us -> 11.1 us
    reduce_scatter x5 -> x0, waiting for transfers between devices: 183 us -> none  [reduced(): lax.psum_scatter(partial, both, scatter_dimension=0, tiled=True, axis_ind...]
    ppermute x9 -> x53, waiting for transfers between devices: 32.5 us -> 186 us  [the longest x51 185 us: hop(): return lax.ppermute(value, both, pairs)]
    all_gather x5 -> x0, waiting for transfers between devices: 90.6 us -> none  [gathered(): lax.all_gather(block, both, axis=0, tiled=True, axis_index_groups=teams)]
    pallas_call x2 -> x6, Pallas kernels: 16.4 us -> 53.4 us  [the longest x2 23 us: attend_back(): pl.pallas_call(lambda *refs: attend_back_kernel(state is None, closing, *...]
    ppermute x9 -> x53, starting transfers between devices: 10.6 us -> 47.6 us  [the longest x51 44 us: hop(): return lax.ppermute(value, both, pairs)]
    dot_general x12 -> x0, matrix products: 29.8 us -> none  [the longest x2 9.21 us: attend_back(): jnp.einsum('hqk,qhd->khd', probs.astype(HALF), grad_out, preferred_elemen...]
    dot_general x16 -> x24, matrix products: 111 us -> 90.7 us  [dot(): lax.dot_general(left, right, (dims, ((), ())), preferred_element_type=F32)]
    ppermute x62 -> x59, waiting for transfers between devices: 253 us -> 273 us  [flip(): return lax.ppermute(value, 'blk', [(i, i ^ bit) for i in range(count)])]
  transfers between devices with their start and end apart: 82 -> 112, of which waited for: 48 -> 57; matrix products, arithmetic and copies ran while one was open for 20% -> 20% of each run, Pallas kernels for 2% -> 7%
where the time goes in v3:
time: 984 us; the launch traced here: 971 us
  waiting for transfers between devices  459 us (47%)
  other arithmetic  124 us (13%)
  starting transfers between devices  115 us (12%)
  matrix products  90.7 us (9%)
  local copies, waits for them, and re-layouts  85.5 us (9%)
  Pallas kernels  75.3 us (8%)
  blocking collectives  11.3 us (1%)
  between operations  11.1 us (1%)
    ppermute x59, waiting for transfers between devices, flip(): return lax.ppermute(value, 'blk', [(i, i ^ bit) for i in range(count)])  273 us
    ppermute x51, waiting for transfers between devices, hop(): return lax.ppermute(value, both, pairs)  185 us
    dot_general x24, matrix products, dot(): lax.dot_general(left, right, (dims, ((), ())), preferred_element_type=F32)  90.7 us
    ppermute x59, starting transfers between devices, flip(): return lax.ppermute(value, 'blk', [(i, i ^ bit) for i in range(count)])  67.2 us
    ppermute x51, starting transfers between devices, hop(): return lax.ppermute(value, both, pairs)  44 us
    unnamed x302, local copies, waits for them, and re-layouts  32.8 us
    sub x8, other arithmetic, adamw(): weight - rate * (first_hat / (jnp.sqrt(second_hat) + ADAM_EPS) + decay *...  24.8 us
    pallas_call x2, Pallas kernels, attend_back(): pl.pallas_call(lambda *refs: attend_back_kernel(state is None, closing, *...  23 us
  transfers between devices with their start and end apart: 112, of which 57 were waited for; matrix products, arithmetic and copies ran while one was open for 20% of the time, Pallas kernels for 7%

profile of v3, /device:TPU:0, one launch (start us, length us, event | category | flops | bytes accessed | tf_op | source)
XLA Modules:
  0.0 971.5 jit_solution(12880867908308750140)
XLA Ops:
  26.3 6.0 fusion.2
  46.7 23.6 %collective-permute-done.4 = bf16[2,2,512,384]{3,2,0,1:T(8,128)(2,1)} collective-permute-done((bf16[2,2,512,384]{3,2,0,1:T(8,128)(2,1)}, bf16[2,2,512,384]{3,2,0,1:T(8,128)(2,1)}, u32[]{:S(2)}, u32[]{:S(2)}) %collective-permute-start.4) | collective-permute-done | bytes 1572896 | tf_op jit(solution)/shard_map/ppermute | solution.py:38
  75.3 5.1 constant_dynamic-slice_fusion.7
  82.3 18.2 %collective-permute-done.5 = bf16[2,512,384]{2,1,0:T(8,128)(2,1)S(1)} collective-permute-done((bf16[2,512,384]{2,1,0:T(8,128)(2,1)S(1)}, bf16[2,512,384]{2,1,0:T(8,128)(2,1)S(1)}, u32[]{:S(2)}, u32[]{:S(2)}) %collective-permute-start.5) | collective-permute-done | bytes 786464 | tf_op jit(solution)/shard_map/ppermute | solution.py:38
  113.8 9.7 collective-permute-done.10
  125.6 7.5 collective-permute-done.11
  139.0 20.1 %collective-permute-done.16 = bf16[256,1024]{1,0:T(8,128)(2,1)S(1)} collective-permute-done((bf16[256,1024]{1,0:T(8,128)(2,1)S(1)}, bf16[256,1024]{1,0:T(8,128)(2,1)S(1)}, u32[]{:S(2)}, u32[]{:S(2)}) %collective-permute-start.16) | collective-permute-done | bytes 524320 | tf_op jit(solution)/shard_map/ppermute | solution.py:38
  161.0 10.3 %collective-permute-done.14.refs_6_ = bf16[512,512]{1,0:T(8,128)(2,1)S(1)} collective-permute-done((bf16[512,512]{1,0:T(8,128)(2,1)S(1)}, bf16[512,512]{1,0:T(8,128)(2,1)S(1)}, u32[]{:S(2)}, u32[]{:S(2)}) %collective-permute-start.14) | collective-permute-done | bytes 524320 | tf_op jit(solution)/shard_map/ppermute | solution.py:403
  177.6 5.4 shard_map.494
  186.4 7.6 shard_map.493
  196.4 6.6 fusion.56.refs_2_.refs_3_.refs_4_
  203.0 7.1 collective-permute-done.23
  217.8 6.5 shard_map.495
  225.6 10.8 %collective-permute-done.27 = bf16[256,1024]{1,0:T(8,128)(2,1)S(1)} collective-permute-done((bf16[256,1024]{1,0:T(8,128)(2,1)}, bf16[256,1024]{1,0:T(8,128)(2,1)S(1)}, u32[]{:S(2)}, u32[]{:S(2)}) %collective-permute-start.27) | collective-permute-done | bytes 524320 | tf_op jit(solution)/shard_map/ppermute | solution.py:38
  239.8 7.3 shard_map.496
  256.9 18.3 %collective-permute-done.33 = bf16[256,1024]{1,0:T(8,128)(2,1)S(1)} collective-permute-done((bf16[256,1024]{1,0:T(8,128)(2,1)S(1)}, bf16[256,1024]{1,0:T(8,128)(2,1)S(1)}, u32[]{:S(2)}, u32[]{:S(2)}) %collective-permute-start.33) | collective-permute-done | bytes 524320 | tf_op jit(solution)/shard_map/ppermute | solution.py:38
  275.2 12.7 %collective-permute-done.31 = bf16[128,2048]{1,0:T(8,128)(2,1)S(1)} collective-permute-done((bf16[128,2048]{1,0:T(8,128)(2,1)S(1)}, bf16[128,2048]{1,0:T(8,128)(2,1)S(1)}, u32[]{:S(2)}, u32[]{:S(2)}) %collective-permute-start.31) | collective-permute-done | bytes 524320 | tf_op jit(solution)/shard_map/ppermute | solution.py:403
  287.9 13.3 %collective-permute-done.30 = bf16[128,2048]{1,0:T(8,128)(2,1)S(1)} collective-permute-done((bf16[128,2048]{1,0:T(8,128)(2,1)S(1)}, bf16[128,2048]{1,0:T(8,128)(2,1)S(1)}, u32[]{:S(2)}, u32[]{:S(2)}) %collective-permute-start.30) | collective-permute-done | bytes 524320 | tf_op jit(solution)/shard_map/ppermute | solution.py:403
  306.8 5.4 shard_map.497
  312.1 7.0 collective-permute-done.36
  319.1 5.8 collective-permute-done.35
  328.1 5.5 shard_map.498
  333.6 6.9 multiply_convert_fusion
  348.5 5.4 multiply_convert_fusion.1
  361.2 10.9 %collective-permute-done.46 = bf16[256,1024]{1,0:T(8,128)(2,1)S(1)} collective-permute-done((bf16[256,1024]{1,0:T(8,128)(2,1)S(1)}, bf16[256,1024]{1,0:T(8,128)(2,1)S(1)}, u32[]{:S(2)}, u32[]{:S(2)}) %collective-permute-start.46) | collective-permute-done | bytes 524320 | tf_op jit(solution)/shard_map/ppermute | solution.py:38
  372.2 11.0 %collective-permute-done.44 = bf16[128,2048]{1,0:T(8,128)(2,1)S(1)} collective-permute-done((bf16[128,2048]{1,0:T(8,128)(2,1)S(1)}, bf16[128,2048]{1,0:T(8,128)(2,1)S(1)}, u32[]{:S(2)}, u32[]{:S(2)}) %collective-permute-start.44) | collective-permute-done | bytes 524320 | tf_op jit(solution)/shard_map/ppermute | solution.py:403
  383.2 9.2 collective-permute-done.43
  401.0 12.3 %collective-permute-done.49 = bf16[128,2048]{1,0:T(8,128)(2,1)S(1)} collective-permute-done((bf16[128,2048]{1,0:T(8,128)(2,1)S(1)}, bf16[128,2048]{1,0:T(8,128)(2,1)S(1)}, u32[]{:S(2)}, u32[]{:S(2)}) %collective-permute-start.49) | collective-permute-done | bytes 524320 | tf_op jit(solution)/shard_map/ppermute | solution.py:403
  413.3 8.3 collective-permute-done.48
  426.9 5.7 shard_map.499
  432.6 5.1 fusion.172
  437.7 4.8 fusion.173
  464.1 5.4 convolution_convert_fusion.1
  477.8 12.4 %collective-permute-done.58 = bf16[128,2048]{1,0:T(8,128)(2,1)S(1)} collective-permute-done((bf16[128,2048]{1,0:T(8,128)(2,1)}, bf16[128,2048]{1,0:T(8,128)(2,1)S(1)}, u32[]{:S(2)}, u32[]{:S(2)}) %collective-permute-start.58) | collective-permute-done | bytes 524320 | tf_op jit(solution)/shard_map/ppermute | solution.py:403
  490.3 10.3 %collective-permute-done.57 = bf16[128,2048]{1,0:T(8,128)(2,1)} collective-permute-done((bf16[128,2048]{1,0:T(8,128)(2,1)}, bf16[128,2048]{1,0:T(8,128)(2,1)}, u32[]{:S(2)}, u32[]{:S(2)}) %collective-permute-start.57) | collective-permute-done | bytes 524320 | tf_op jit(solution)/shard_map/ppermute | solution.py:403
  513.9 17.1 %collective-permute-done.64 = bf16[1,256,1024]{2,1,0:T(8,128)(2,1)S(1)} collective-permute-done((bf16[1,256,1024]{2,1,0:T(8,128)(2,1)S(1)}, bf16[1,256,1024]{2,1,0:T(8,128)(2,1)S(1)}, u32[]{:S(2)}, u32[]{:S(2)}) %collective-permute-start.64) | collective-permute-done | bytes 524320 | tf_op jit(solution)/shard_map/ppermute | solution.py:38
  531.0 5.5 collective-permute-done.62
  536.5 9.5 collective-permute-done.61
  548.2 5.4 fusion.28
  563.6 4.9 convolution_convert_fusion
  576.5 8.7 fusion.7
  588.7 9.7 collective-permute-done.69
  611.4 18.2 %collective-permute-done.74 = bf16[128,2048]{1,0:T(8,128)(2,1)S(1)} collective-permute-done((bf16[128,2048]{1,0:T(8,128)(2,1)S(1)}, bf16[128,2048]{1,0:T(8,128)(2,1)S(1)}, u32[]{:S(2)}, u32[]{:S(2)}) %collective-permute-start.74) | collective-permute-done | bytes 524320 | tf_op jit(solution)/shard_map/ppermute | solution.py:403
  629.6 9.6 collective-permute-done.73
  655.4 10.5 %shard_map.500 = (f32[2,128,1024]{2,1,0:T(8,128)S(1)}, bf16[1024,512]{1,0:T(8,128)(2,1)S(1)}) custom-call(s32[1,1024]{1,0:T(1,128)S(1)} %bitcast.426, s32[1024,1]{1,0:T(8,128)S(1)} %copy-done.3, bf16[1024,768]{1,0:T(8,128)(2,1)} %copy-done, bf16[1024,512]{1,0:T(8,128)(2,1)S(1)} %collective-permute-done.25.refs_3_.refs_4_, ...), custom_call_target="tpu_custom_call" | custom-call | flops 2684354560 | bytes 5242880 | tf_op jit(solution)/shard_map/pallas_call | solution.py:176
  666.0 7.3 collective-permute-done.79
  684.9 12.5 %shard_map.501 = (bf16[1024,256]{1,0:T(8,128)(2,1)S(1)}, f32[1024,512]{1,0:T(8,128)}) custom-call(s32[1,1024]{1,0:T(1,128)S(1)} %bitcast.427, s32[1024,1]{1,0:T(8,128)S(1)} %copy.178.refs_1_, bf16[1024,768]{1,0:T(8,128)(2,1)S(1)} %copy-done.1, bf16[1024,768]{1,0:T(8,128)(2,1)S(1)} %copy-done.1, bf16[1024,768]{1,0:T(8,128)(2,1)S(1)} %copy-done.1, ...), custom_call_target="tpu_custom_call" | custom-call | flops 2684354560 | bytes 5242880 | tf_op jit(solution)/shard_map/pallas_call | solution.py:176
  697.4 7.3 collective-permute-done.82
  708.7 4.1 collective-permute-done.81
  726.1 3.8 convolution_convert_fusion.2
  730.8 10.8 %collective-permute-done.84 = bf16[1,2,256,1024]{3,2,1,0:T(8,128)(2,1)S(1)} collective-permute-done((bf16[1,2,256,1024]{3,2,1,0:T(8,128)(2,1)S(1)}, bf16[1,2,256,1024]{3,2,1,0:T(8,128)(2,1)S(1)}, u32[]{:S(2)}, u32[]{:S(2)}) %collective-permute-start.84) | collective-permute-done | bytes 1048608 | tf_op jit(solution)/shard_map/ppermute | solution.py:38
  752.4 15.3 %collective-permute-done.90 = bf16[1,2,256,256]{2,3,1,0:T(8,128)(2,1)S(1)} collective-permute-done((bf16[1,2,256,256]{2,3,1,0:T(8,128)(2,1)}, bf16[1,2,256,256]{2,3,1,0:T(8,128)(2,1)S(1)}, u32[]{:S(2)}, u32[]{:S(2)}) %collective-permute-start.90) | collective-permute-done | bytes 262176 | tf_op jit(solution)/shard_map/ppermute | solution.py:38
  802.1 25.6 %collective-permute-done.97 = bf16[1,512,256]{2,1,0:T(8,128)(2,1)S(1)} collective-permute-done((bf16[1,512,256]{2,1,0:T(8,128)(2,1)S(1)}, bf16[1,512,256]{2,1,0:T(8,128)(2,1)S(1)}, u32[]{:S(2)}, u32[]{:S(2)}) %collective-permute-start.97) | collective-permute-done | bytes 262176 | tf_op jit(solution)/shard_map/ppermute | solution.py:38
  827.8 8.7 collective-permute-done.98
  846.4 13.6 %collective-permute-done.107 = bf16[256,1024]{1,0:T(8,128)(2,1)} collective-permute-done((bf16[256,1024]{1,0:T(8,128)(2,1)}, bf16[256,1024]{1,0:T(8,128)(2,1)}, u32[]{:S(2)}, u32[]{:S(2)}) %collective-permute-start.107) | collective-permute-done | bytes 524320 | tf_op jit(solution)/shard_map/ppermute | solution.py:38
  861.9 8.2 collective-permute-done.103
  881.0 14.8 %collective-permute-done.108.refs_2_ = bf16[4,512,256]{2,1,0:T(8,128)(2,1)S(1)} collective-permute-done((bf16[4,512,256]{2,1,0:T(8,128)(2,1)S(1)}, bf16[4,512,256]{2,1,0:T(8,128)(2,1)S(1)}, u32[]{:S(2)}, u32[]{:S(2)}) %collective-permute-start.108) | collective-permute-done | bytes 1048608 | tf_op jit(solution)/shard_map/ppermute | solution.py:38
  902.1 8.9 shard_map.502
  925.6 11.3 %all_to_all.5 = f32[32,2,128]{2,1,0:T(2,128)S(1)} all-to-all(f32[32,2,128]{2,1,0:T(2,128)S(1)} %broadcast_in_dim.41), channel_id=1, replica_groups=mesh['blk'=8,'head'=4] {'blk','head'}, dimensions={0} | all-to-all | bytes 65536 | tf_op jit(solution)/shard_map/all_to_all | solution.py:896
  944.0 4.6 multiply_subtract_fusion.4
  949.7 3.9 multiply_subtract_fusion.1
  955.4 4.1 multiply_subtract_fusion
  960.4 3.8 multiply_subtract_fusion.2
  966.1 4.0 multiply_subtract_fusion.3
  (733 shorter events, 360.9 us)
Async XLA Ops:
  36.0 34.3 %collective-permute-start.4 = (bf16[2,2,512,384]{3,2,0,1:T(8,128)(2,1)}, bf16[2,2,512,384]{3,2,0,1:T(8,128)(2,1)}, u32[]{:S(2)}, u32[]{:S(2)}) collective-permute-start(bf16[2,2,512,384]{3,2,0,1:T(8,128)(2,1)} %slice_bitcast_fusion), channel_id=1, source_target_pairs={{0,4},{4,0},{8,12},{12,8},{16,20},{20,16},{24,28},{28,24},{1,5},{5... | collective-permute-start | bytes 4718600 | tf_op jit(solution)/shard_map/ppermute | solution.py:38
  43.9 29.5 %collective-permute-start.6 = (bf16[2,2,512,128]{3,2,0,1:T(8,128)(2,1)S(1)}, bf16[2,2,512,128]{3,2,0,1:T(8,128)(2,1)S(1)}, u32[]{:S(2)}, u32[]{:S(2)}) collective-permute-start(bf16[2,2,512,128]{3,2,0,1:T(8,128)(2,1)S(1)} %slice_bitcast_fusion.10), channel_id=1, source_target_pairs={{0,8},{4,12},{8,0},{12,4},{16,24},{20,28},{24,16},{28,20},{1,9},{5... | collective-permute-start | bytes 1572872 | tf_op jit(solution)/shard_map/ppermute | solution.py:38
  44.1 56.5 %collective-permute-start.8 = (bf16[2,256,1024]{2,1,0:T(8,128)(2,1)}, bf16[2,256,1024]{2,1,0:T(8,128)(2,1)S(1)}, u32[]{:S(2)}, u32[]{:S(2)}) collective-permute-start(bf16[2,256,1024]{2,1,0:T(8,128)(2,1)} %maximum_select_fusion.refs_1_), channel_id=1, source_target_pairs={{0,16},{4,20},{8,24},{12,28},{16,0},{20,4},{24,8},{28,12},{1,17},{... | collective-permute-start | bytes 3145736 | tf_op jit(solution)/shard_map/ppermute | solution.py:38
  72.7 27.8 %collective-permute-start.5 = (bf16[2,512,384]{2,1,0:T(8,128)(2,1)S(1)}, bf16[2,512,384]{2,1,0:T(8,128)(2,1)S(1)}, u32[]{:S(2)}, u32[]{:S(2)}) collective-permute-start(bf16[2,512,384]{2,1,0:T(8,128)(2,1)S(1)} %slice_bitcast_fusion.2), channel_id=1, source_target_pairs={{0,8},{4,12},{8,0},{12,4},{16,24},{20,28},{24,16},{28,20},{1,9},{5... | collective-permute-start | bytes 2359304 | tf_op jit(solution)/shard_map/ppermute | solution.py:38
  101.7 31.6 %collective-permute-start.12 = (bf16[2,256,1024]{2,1,0:T(8,128)(2,1)}, bf16[2,256,1024]{2,1,0:T(8,128)(2,1)}, u32[]{:S(2)}, u32[]{:S(2)}) collective-permute-start(bf16[2,256,1024]{2,1,0:T(8,128)(2,1)} %maximum_select_fusion.refs_1_), channel_id=1, source_target_pairs={{0,4},{4,0},{8,12},{12,8},{16,20},{20,16},{24,28},{28,24},{1,5},{5... | collective-permute-start | bytes 3145736 | tf_op jit(solution)/shard_map/ppermute | solution.py:38
  133.3 38.0 %collective-permute-start.17 = (bf16[2,256,1024]{2,1,0:T(8,128)(2,1)S(1)}, bf16[2,256,1024]{2,1,0:T(8,128)(2,1)S(1)}, u32[]{:S(2)}, u32[]{:S(2)}) collective-permute-start(bf16[2,256,1024]{2,1,0:T(8,128)(2,1)S(1)} %copy-done.87), channel_id=1, source_target_pairs={{0,4},{4,0},{8,12},{12,8},{16,20},{20,16},{24,28},{28,24},{1,5},{5... | collective-permute-start | bytes 3145736 | tf_op jit(solution)/shard_map/ppermute | solution.py:38
  134.4 24.7 %collective-permute-start.16 = (bf16[256,1024]{1,0:T(8,128)(2,1)S(1)}, bf16[256,1024]{1,0:T(8,128)(2,1)S(1)}, u32[]{:S(2)}, u32[]{:S(2)}) collective-permute-start(bf16[256,1024]{1,0:T(8,128)(2,1)S(1)} %slice_bitcast_fusion.29), channel_id=1, source_target_pairs={{0,16},{4,20},{8,24},{12,28},{16,0},{20,4},{24,8},{28,12},{1,17},{... | collective-permute-start | bytes 1572872 | tf_op jit(solution)/shard_map/ppermute | solution.py:38
  134.8 26.2 %collective-permute-start.15 = (bf16[512,512]{1,0:T(8,128)(2,1)S(1)}, bf16[512,512]{1,0:T(8,128)(2,1)S(1)}, u32[]{:S(2)}, u32[]{:S(2)}) collective-permute-start(bf16[512,512]{1,0:T(8,128)(2,1)S(1)} %pad_maximum_fusion.14.refs_2_), channel_id=1, source_target_pairs={{0,10},{1,11},{2,8},{3,9},{4,14},{5,15},{6,12},{7,13},{8,2},{9,3},... | collective-permute-start | bytes 1572872 | tf_op jit(solution)/shard_map/ppermute | solution.py:403
  138.4 32.9 %collective-permute-start.14 = (bf16[512,512]{1,0:T(8,128)(2,1)S(1)}, bf16[512,512]{1,0:T(8,128)(2,1)S(1)}, u32[]{:S(2)}, u32[]{:S(2)}) collective-permute-start(bf16[512,512]{1,0:T(8,128)(2,1)S(1)} %pad_maximum_fusion.14.refs_2_), channel_id=1, source_target_pairs={{0,8},{1,9},{2,10},{3,11},{4,12},{5,13},{6,14},{7,15},{8,0},{9,1},... | collective-permute-start | bytes 1572872 | tf_op jit(solution)/shard_map/ppermute | solution.py:403
  138.4 32.9 %collective-permute-start.13 = (bf16[512,512]{1,0:T(8,128)(2,1)S(1)}, bf16[512,512]{1,0:T(8,128)(2,1)S(1)}, u32[]{:S(2)}, u32[]{:S(2)}) collective-permute-start(bf16[512,512]{1,0:T(8,128)(2,1)S(1)} %pad_maximum_fusion.14.refs_2_), channel_id=1, source_target_pairs={{0,2},{1,3},{2,0},{3,1},{4,6},{5,7},{6,4},{7,5},{8,10},{9,11},{10,... | collective-permute-start | bytes 1572872 | tf_op jit(solution)/shard_map/ppermute | solution.py:403
  175.8 34.2 %collective-permute-start.22 = (bf16[2,256,1024]{2,1,0:T(8,128)(2,1)S(1)}, bf16[2,256,1024]{2,1,0:T(8,128)(2,1)}, u32[]{:S(2)}, u32[]{:S(2)}) collective-permute-start(bf16[2,256,1024]{2,1,0:T(8,128)(2,1)S(1)} %maximum_select_fusion.1.refs_1_), channel_id=1, source_target_pairs={{0,4},{4,0},{8,12},{12,8},{16,20},{20,16},{24,28},{28,24},{1,5},{5... | collective-permute-start | bytes 3145736 | tf_op jit(solution)/shard_map/ppermute | solution.py:38
  182.9 27.1 %collective-permute-start.23 = (bf16[256,1024]{1,0:T(8,128)(2,1)}, bf16[256,1024]{1,0:T(8,128)(2,1)}, u32[]{:S(2)}, u32[]{:S(2)}) collective-permute-start(bf16[256,1024]{1,0:T(8,128)(2,1)} %slice_bitcast_fusion.28), channel_id=1, source_target_pairs={{0,16},{4,20},{8,24},{12,28},{16,0},{20,4},{24,8},{28,12},{1,17},{... | collective-permute-start | bytes 1572872 | tf_op jit(solution)/shard_map/ppermute | solution.py:38
  211.1 28.7 %collective-permute-start.25 = (bf16[1024,512]{1,0:T(8,128)(2,1)}, bf16[1024,512]{1,0:T(8,128)(2,1)S(1)}, u32[]{:S(2)}, u32[]{:S(2)}) collective-permute-start(bf16[1024,512]{1,0:T(8,128)(2,1)} %slice.371), channel_id=1, source_target_pairs={{0,4},{8,12},{16,20},{24,28},{1,5},{9,13},{17,21},{25,29},{2,6},{1... | collective-permute-start | bytes 3145736 | tf_op jit(solution)/shard_map/ppermute | solution.py:584
  214.9 24.9 %collective-permute-start.26 = (bf16[256,1024]{1,0:T(8,128)(2,1)S(1)}, bf16[256,1024]{1,0:T(8,128)(2,1)S(1)}, u32[]{:S(2)}, u32[]{:S(2)}) collective-permute-start(bf16[256,1024]{1,0:T(8,128)(2,1)S(1)} %slice_bitcast_fusion.27), channel_id=1, source_target_pairs={{0,16},{4,20},{8,24},{12,28},{16,0},{20,4},{24,8},{28,12},{1,17},{... | collective-permute-start | bytes 1572872 | tf_op jit(solution)/shard_map/ppermute | solution.py:38
  249.1 26.0 %collective-permute-start.33 = (bf16[256,1024]{1,0:T(8,128)(2,1)S(1)}, bf16[256,1024]{1,0:T(8,128)(2,1)S(1)}, u32[]{:S(2)}, u32[]{:S(2)}) collective-permute-start(bf16[256,1024]{1,0:T(8,128)(2,1)S(1)} %slice_bitcast_fusion.23), channel_id=1, source_target_pairs={{0,16},{4,20},{8,24},{12,28},{16,0},{20,4},{24,8},{28,12},{1,17},{... | collective-permute-start | bytes 1572872 | tf_op jit(solution)/shard_map/ppermute | solution.py:38
  249.2 25.9 %collective-permute-start.32 = (bf16[2,256,1024]{2,1,0:T(8,128)(2,1)S(1)}, bf16[2,256,1024]{2,1,0:T(8,128)(2,1)S(1)}, u32[]{:S(2)}, u32[]{:S(2)}) collective-permute-start(bf16[2,256,1024]{2,1,0:T(8,128)(2,1)S(1)} %pad_maximum_fusion.9.refs_2_), channel_id=1, source_target_pairs={{0,4},{4,0},{8,12},{12,8},{16,20},{20,16},{24,28},{28,24},{1,5},{5... | collective-permute-start | bytes 3145736 | tf_op jit(solution)/shard_map/ppermute | solution.py:38
  253.3 34.7 %collective-permute-start.31 = (bf16[128,2048]{1,0:T(8,128)(2,1)S(1)}, bf16[128,2048]{1,0:T(8,128)(2,1)S(1)}, u32[]{:S(2)}, u32[]{:S(2)}) collective-permute-start(bf16[128,2048]{1,0:T(8,128)(2,1)S(1)} %get-tuple-element.413), channel_id=1, source_target_pairs={{0,10},{1,11},{2,8},{3,9},{4,14},{5,15},{6,12},{7,13},{8,2},{9,3},... | collective-permute-start | bytes 1572872 | tf_op jit(solution)/shard_map/ppermute | solution.py:403
  254.3 46.9 %collective-permute-start.30 = (bf16[128,2048]{1,0:T(8,128)(2,1)S(1)}, bf16[128,2048]{1,0:T(8,128)(2,1)S(1)}, u32[]{:S(2)}, u32[]{:S(2)}) collective-permute-start(bf16[128,2048]{1,0:T(8,128)(2,1)S(1)} %get-tuple-element.414), channel_id=1, source_target_pairs={{0,8},{1,9},{2,10},{3,11},{4,12},{5,13},{6,14},{7,15},{8,0},{9,1},... | collective-permute-start | bytes 1572872 | tf_op jit(solution)/shard_map/ppermute | solution.py:403
  255.7 45.6 %collective-permute-start.29 = (bf16[128,2048]{1,0:T(8,128)(2,1)S(1)}, bf16[128,2048]{1,0:T(8,128)(2,1)S(1)}, u32[]{:S(2)}, u32[]{:S(2)}) collective-permute-start(bf16[128,2048]{1,0:T(8,128)(2,1)S(1)} %get-tuple-element.415), channel_id=1, source_target_pairs={{0,2},{1,3},{2,0},{3,1},{4,6},{5,7},{6,4},{7,5},{8,10},{9,11},{10,... | collective-permute-start | bytes 1572872 | tf_op jit(solution)/shard_map/ppermute | solution.py:403
  275.1 30.8 %collective-permute-start.37 = (bf16[256,1024]{1,0:T(8,128)(2,1)S(1)}, bf16[256,1024]{1,0:T(8,128)(2,1)S(1)}, u32[]{:S(2)}, u32[]{:S(2)}) collective-permute-start(bf16[256,1024]{1,0:T(8,128)(2,1)S(1)} %slice_bitcast_fusion.22), channel_id=1, source_target_pairs={{0,16},{4,20},{8,24},{12,28},{16,0},{20,4},{24,8},{28,12},{1,17},{... | collective-permute-start | bytes 1572872 | tf_op jit(solution)/shard_map/ppermute | solution.py:38
  275.1 37.0 %collective-permute-start.39 = (bf16[2,256,1024]{2,1,0:T(8,128)(2,1)}, bf16[2,256,1024]{2,1,0:T(8,128)(2,1)}, u32[]{:S(2)}, u32[]{:S(2)}) collective-permute-start(bf16[2,256,1024]{2,1,0:T(8,128)(2,1)} %maximum_select_fusion.2.refs_1_), channel_id=1, source_target_pairs={{0,4},{4,0},{8,12},{12,8},{16,20},{20,16},{24,28},{28,24},{1,5},{5... | collective-permute-start | bytes 3145736 | tf_op jit(solution)/shard_map/ppermute | solution.py:38
  344.5 27.7 %collective-permute-start.45 = (bf16[2,256,1024]{2,1,0:T(8,128)(2,1)S(1)}, bf16[2,256,1024]{2,1,0:T(8,128)(2,1)S(1)}, u32[]{:S(2)}, u32[]{:S(2)}) collective-permute-start(bf16[2,256,1024]{2,1,0:T(8,128)(2,1)S(1)} %copy-done.15), channel_id=1, source_target_pairs={{0,4},{4,0},{8,12},{12,8},{16,20},{20,16},{24,28},{28,24},{1,5},{5... | collective-permute-start | bytes 3145736 | tf_op jit(solution)/shard_map/ppermute | solution.py:38
  346.2 25.9 %collective-permute-start.46 = (bf16[256,1024]{1,0:T(8,128)(2,1)S(1)}, bf16[256,1024]{1,0:T(8,128)(2,1)S(1)}, u32[]{:S(2)}, u32[]{:S(2)}) collective-permute-start(bf16[256,1024]{1,0:T(8,128)(2,1)S(1)} %slice_bitcast_fusion.21), channel_id=1, source_target_pairs={{0,16},{4,20},{8,24},{12,28},{16,0},{20,4},{24,8},{28,12},{1,17},{... | collective-permute-start | bytes 1572872 | tf_op jit(solution)/shard_map/ppermute | solution.py:38
  357.3 25.9 %collective-permute-start.44 = (bf16[128,2048]{1,0:T(8,128)(2,1)S(1)}, bf16[128,2048]{1,0:T(8,128)(2,1)S(1)}, u32[]{:S(2)}, u32[]{:S(2)}) collective-permute-start(bf16[128,2048]{1,0:T(8,128)(2,1)S(1)} %get-tuple-element.410), channel_id=1, source_target_pairs={{0,10},{1,11},{2,8},{3,9},{4,14},{5,15},{6,12},{7,13},{8,2},{9,3},... | collective-permute-start | bytes 1572872 | tf_op jit(solution)/shard_map/ppermute | solution.py:403
  360.0 32.4 %collective-permute-start.43 = (bf16[128,2048]{1,0:T(8,128)(2,1)S(1)}, bf16[128,2048]{1,0:T(8,128)(2,1)S(1)}, u32[]{:S(2)}, u32[]{:S(2)}) collective-permute-start(bf16[128,2048]{1,0:T(8,128)(2,1)S(1)} %get-tuple-element.411), channel_id=1, source_target_pairs={{0,8},{1,9},{2,10},{3,11},{4,12},{5,13},{6,14},{7,15},{8,0},{9,1},... | collective-permute-start | bytes 1572872 | tf_op jit(solution)/shard_map/ppermute | solution.py:403
  360.1 32.4 %collective-permute-start.42 = (bf16[128,2048]{1,0:T(8,128)(2,1)S(1)}, bf16[128,2048]{1,0:T(8,128)(2,1)S(1)}, u32[]{:S(2)}, u32[]{:S(2)}) collective-permute-start(bf16[128,2048]{1,0:T(8,128)(2,1)S(1)} %get-tuple-element.412), channel_id=1, source_target_pairs={{0,2},{1,3},{2,0},{3,1},{4,6},{5,7},{6,4},{7,5},{8,10},{9,11},{10,... | collective-permute-start | bytes 1572872 | tf_op jit(solution)/shard_map/ppermute | solution.py:403
  392.5 29.3 %collective-permute-start.50 = (bf16[2,256,1024]{2,1,0:T(8,128)(2,1)S(1)}, bf16[2,256,1024]{2,1,0:T(8,128)(2,1)}, u32[]{:S(2)}, u32[]{:S(2)}) collective-permute-start(bf16[2,256,1024]{2,1,0:T(8,128)(2,1)S(1)} %pad_maximum_fusion.11.refs_2_), channel_id=1, source_target_pairs={{0,4},{4,0},{8,12},{12,8},{16,20},{20,16},{24,28},{28,24},{1,5},{5... | collective-permute-start | bytes 3145736 | tf_op jit(solution)/shard_map/ppermute | solution.py:38
  397.7 23.9 %collective-permute-start.48 = (bf16[128,2048]{1,0:T(8,128)(2,1)S(1)}, bf16[128,2048]{1,0:T(8,128)(2,1)S(1)}, u32[]{:S(2)}, u32[]{:S(2)}) collective-permute-start(bf16[128,2048]{1,0:T(8,128)(2,1)S(1)} %get-tuple-element.383), channel_id=1, source_target_pairs={{0,8},{1,9},{2,10},{3,11},{4,12},{5,13},{6,14},{7,15},{8,0},{9,1},... | collective-permute-start | bytes 1572872 | tf_op jit(solution)/shard_map/ppermute | solution.py:403
  472.4 28.4 %collective-permute-start.59 = (bf16[1,2,256,1024]{3,2,1,0:T(8,128)(2,1)}, bf16[1,2,256,1024]{3,2,1,0:T(8,128)(2,1)}, u32[]{:S(2)}, u32[]{:S(2)}) collective-permute-start(bf16[1,2,256,1024]{3,2,1,0:T(8,128)(2,1)} %dynamic-slice_bitcast_fusion.5), channel_id=1, source_target_pairs={{0,4},{4,0},{8,12},{12,8},{16,20},{20,16},{24,28},{28,24},{1,5},{5... | collective-permute-start | bytes 3145736 | tf_op jit(solution)/shard_map/ppermute | solution.py:38
  474.9 25.6 %collective-permute-start.57 = (bf16[128,2048]{1,0:T(8,128)(2,1)}, bf16[128,2048]{1,0:T(8,128)(2,1)}, u32[]{:S(2)}, u32[]{:S(2)}) collective-permute-start(bf16[128,2048]{1,0:T(8,128)(2,1)} %get-tuple-element.408), channel_id=1, source_target_pairs={{0,8},{1,9},{2,10},{3,11},{4,12},{5,13},{6,14},{7,15},{8,0},{9,1},... | collective-permute-start | bytes 1572872 | tf_op jit(solution)/shard_map/ppermute | solution.py:403
  476.9 23.9 %collective-permute-start.56 = (bf16[128,2048]{1,0:T(8,128)(2,1)}, bf16[128,2048]{1,0:T(8,128)(2,1)}, u32[]{:S(2)}, u32[]{:S(2)}) collective-permute-start(bf16[128,2048]{1,0:T(8,128)(2,1)} %get-tuple-element.409), channel_id=1, source_target_pairs={{0,2},{1,3},{2,0},{3,1},{4,6},{5,7},{6,4},{7,5},{8,10},{9,11},{10,... | collective-permute-start | bytes 1572872 | tf_op jit(solution)/shard_map/ppermute | solution.py:403
  504.8 26.1 %collective-permute-start.64 = (bf16[1,256,1024]{2,1,0:T(8,128)(2,1)S(1)}, bf16[1,256,1024]{2,1,0:T(8,128)(2,1)S(1)}, u32[]{:S(2)}, u32[]{:S(2)}) collective-permute-start(bf16[1,256,1024]{2,1,0:T(8,128)(2,1)S(1)} %get-tuple-element.424), channel_id=1, source_target_pairs={{0,16},{4,20},{8,24},{12,28},{16,0},{20,4},{24,8},{28,12},{1,17},{... | collective-permute-start | bytes 1572872 | tf_op jit(solution)/shard_map/ppermute | solution.py:38
  507.0 39.0 %collective-permute-start.63 = (bf16[1,2,256,1024]{3,2,1,0:T(8,128)(2,1)S(1)}, bf16[1,2,256,1024]{3,2,1,0:T(8,128)(2,1)S(1)}, u32[]{:S(2)}, u32[]{:S(2)}) collective-permute-start(bf16[1,2,256,1024]{3,2,1,0:T(8,128)(2,1)S(1)} %dynamic-slice_bitcast_fusion.4), channel_id=1, source_target_pairs={{0,4},{4,0},{8,12},{12,8},{16,20},{20,16},{24,28},{28,24},{1,5},{5... | collective-permute-start | bytes 3145736 | tf_op jit(solution)/shard_map/ppermute | solution.py:38
  510.4 26.2 %collective-permute-start.62 = (bf16[128,2048]{1,0:T(8,128)(2,1)S(1)}, bf16[128,2048]{1,0:T(8,128)(2,1)S(1)}, u32[]{:S(2)}, u32[]{:S(2)}) collective-permute-start(bf16[128,2048]{1,0:T(8,128)(2,1)S(1)} %get-tuple-element.380), channel_id=1, source_target_pairs={{0,10},{1,11},{2,8},{3,9},{4,14},{5,15},{6,12},{7,13},{8,2},{9,3},... | collective-permute-start | bytes 1572872 | tf_op jit(solution)/shard_map/ppermute | solution.py:403
  513.1 32.9 %collective-permute-start.61 = (bf16[128,2048]{1,0:T(8,128)(2,1)S(1)}, bf16[128,2048]{1,0:T(8,128)(2,1)S(1)}, u32[]{:S(2)}, u32[]{:S(2)}) collective-permute-start(bf16[128,2048]{1,0:T(8,128)(2,1)S(1)} %get-tuple-element.380), channel_id=1, source_target_pairs={{0,8},{1,9},{2,10},{3,11},{4,12},{5,13},{6,14},{7,15},{8,0},{9,1},... | collective-permute-start | bytes 1572872 | tf_op jit(solution)/shard_map/ppermute | solution.py:403
  513.1 32.9 %collective-permute-start.60 = (bf16[128,2048]{1,0:T(8,128)(2,1)S(1)}, bf16[128,2048]{1,0:T(8,128)(2,1)S(1)}, u32[]{:S(2)}, u32[]{:S(2)}) collective-permute-start(bf16[128,2048]{1,0:T(8,128)(2,1)S(1)} %get-tuple-element.380), channel_id=1, source_target_pairs={{0,2},{1,3},{2,0},{3,1},{4,6},{5,7},{6,4},{7,5},{8,10},{9,11},{10,... | collective-permute-start | bytes 1572872 | tf_op jit(solution)/shard_map/ppermute | solution.py:403
  546.2 26.3 %collective-permute-start.67 = (bf16[1,256,1024]{2,1,0:T(8,128)(2,1)S(1)}, bf16[1,256,1024]{2,1,0:T(8,128)(2,1)S(1)}, u32[]{:S(2)}, u32[]{:S(2)}) collective-permute-start(bf16[1,256,1024]{2,1,0:T(8,128)(2,1)S(1)} %get-tuple-element.264), channel_id=1, source_target_pairs={{0,16},{4,20},{8,24},{12,28},{16,0},{20,4},{24,8},{28,12},{1,17},{... | collective-permute-start | bytes 1572872 | tf_op jit(solution)/shard_map/ppermute | solution.py:38
  572.6 26.4 %collective-permute-start.71 = (bf16[1,2,256,1024]{3,2,1,0:T(8,128)(2,1)S(1)}, bf16[1,2,256,1024]{3,2,1,0:T(8,128)(2,1)S(1)}, u32[]{:S(2)}, u32[]{:S(2)}) collective-permute-start(bf16[1,2,256,1024]{3,2,1,0:T(8,128)(2,1)S(1)} %dynamic-slice_bitcast_fusion.3), channel_id=1, source_target_pairs={{0,4},{4,0},{8,12},{12,8},{16,20},{20,16},{24,28},{28,24},{1,5},{5... | collective-permute-start | bytes 3145736 | tf_op jit(solution)/shard_map/ppermute | solution.py:38
  573.0 25.4 %collective-permute-start.69 = (bf16[128,2048]{1,0:T(8,128)(2,1)S(1)}, bf16[128,2048]{1,0:T(8,128)(2,1)S(1)}, u32[]{:S(2)}, u32[]{:S(2)}) collective-permute-start(bf16[128,2048]{1,0:T(8,128)(2,1)S(1)} %get-tuple-element.405), channel_id=1, source_target_pairs={{0,8},{1,9},{2,10},{3,11},{4,12},{5,13},{6,14},{7,15},{8,0},{9,1},... | collective-permute-start | bytes 1572872 | tf_op jit(solution)/shard_map/ppermute | solution.py:403
  575.3 23.7 %collective-permute-start.68 = (bf16[128,2048]{1,0:T(8,128)(2,1)S(1)}, bf16[128,2048]{1,0:T(8,128)(2,1)S(1)}, u32[]{:S(2)}, u32[]{:S(2)}) collective-permute-start(bf16[128,2048]{1,0:T(8,128)(2,1)S(1)} %get-tuple-element.406), channel_id=1, source_target_pairs={{0,2},{1,3},{2,0},{3,1},{4,6},{5,7},{6,4},{7,5},{8,10},{9,11},{10,... | collective-permute-start | bytes 1572872 | tf_op jit(solution)/shard_map/ppermute | solution.py:403
  602.6 27.0 %collective-permute-start.74 = (bf16[128,2048]{1,0:T(8,128)(2,1)S(1)}, bf16[128,2048]{1,0:T(8,128)(2,1)S(1)}, u32[]{:S(2)}, u32[]{:S(2)}) collective-permute-start(bf16[128,2048]{1,0:T(8,128)(2,1)S(1)} %get-tuple-element.377), channel_id=1, source_target_pairs={{0,10},{1,11},{2,8},{3,9},{4,14},{5,15},{6,12},{7,13},{8,2},{9,3},... | collective-permute-start | bytes 1572872 | tf_op jit(solution)/shard_map/ppermute | solution.py:403
  602.9 36.3 %collective-permute-start.73 = (bf16[128,2048]{1,0:T(8,128)(2,1)S(1)}, bf16[128,2048]{1,0:T(8,128)(2,1)S(1)}, u32[]{:S(2)}, u32[]{:S(2)}) collective-permute-start(bf16[128,2048]{1,0:T(8,128)(2,1)S(1)} %get-tuple-element.377), channel_id=1, source_target_pairs={{0,8},{1,9},{2,10},{3,11},{4,12},{5,13},{6,14},{7,15},{8,0},{9,1},... | collective-permute-start | bytes 1572872 | tf_op jit(solution)/shard_map/ppermute | solution.py:403
  604.9 34.3 %collective-permute-start.72 = (bf16[128,2048]{1,0:T(8,128)(2,1)S(1)}, bf16[128,2048]{1,0:T(8,128)(2,1)S(1)}, u32[]{:S(2)}, u32[]{:S(2)}) collective-permute-start(bf16[128,2048]{1,0:T(8,128)(2,1)S(1)} %get-tuple-element.377), channel_id=1, source_target_pairs={{0,2},{1,3},{2,0},{3,1},{4,6},{5,7},{6,4},{7,5},{8,10},{9,11},{10,... | collective-permute-start | bytes 1572872 | tf_op jit(solution)/shard_map/ppermute | solution.py:403
  606.2 33.1 %collective-permute-start.75 = (bf16[1,2,256,1024]{3,2,1,0:T(8,128)(2,1)S(1)}, bf16[1,2,256,1024]{3,2,1,0:T(8,128)(2,1)S(1)}, u32[]{:S(2)}, u32[]{:S(2)}) collective-permute-start(bf16[1,2,256,1024]{3,2,1,0:T(8,128)(2,1)S(1)} %dynamic-slice_bitcast_fusion.2), channel_id=1, source_target_pairs={{0,4},{4,0},{8,12},{12,8},{16,20},{20,16},{24,28},{28,24},{1,5},{5... | collective-permute-start | bytes 3145736 | tf_op jit(solution)/shard_map/ppermute | solution.py:38
  609.3 30.0 %collective-permute-start.76 = (bf16[1,256,1024]{2,1,0:T(8,128)(2,1)S(1)}, bf16[1,256,1024]{2,1,0:T(8,128)(2,1)S(1)}, u32[]{:S(2)}, u32[]{:S(2)}) collective-permute-start(bf16[1,256,1024]{2,1,0:T(8,128)(2,1)S(1)} %get-tuple-element.421), channel_id=1, source_target_pairs={{0,16},{4,20},{8,24},{12,28},{16,0},{20,4},{24,8},{28,12},{1,17},{... | collective-permute-start | bytes 1572872 | tf_op jit(solution)/shard_map/ppermute | solution.py:38
  643.1 30.2 %collective-permute-start.78 = (bf16[1,2,256,1024]{3,2,1,0:T(8,128)(2,1)S(1)}, bf16[1,2,256,1024]{3,2,1,0:T(8,128)(2,1)S(1)}, u32[]{:S(2)}, u32[]{:S(2)}) collective-permute-start(bf16[1,2,256,1024]{3,2,1,0:T(8,128)(2,1)S(1)} %dynamic-slice_bitcast_fusion.1), channel_id=1, source_target_pairs={{0,4},{4,0},{8,12},{12,8},{16,20},{20,16},{24,28},{28,24},{1,5},{5... | collective-permute-start | bytes 3145736 | tf_op jit(solution)/shard_map/ppermute | solution.py:38
  647.4 25.8 %collective-permute-start.79 = (bf16[1,256,1024]{2,1,0:T(8,128)(2,1)S(1)}, bf16[1,256,1024]{2,1,0:T(8,128)(2,1)S(1)}, u32[]{:S(2)}, u32[]{:S(2)}) collective-permute-start(bf16[1,256,1024]{2,1,0:T(8,128)(2,1)S(1)} %copy-done.107), channel_id=1, source_target_pairs={{0,16},{4,20},{8,24},{12,28},{16,0},{20,4},{24,8},{28,12},{1,17},{... | collective-permute-start | bytes 1572872 | tf_op jit(solution)/shard_map/ppermute | solution.py:38
  678.4 26.3 %collective-permute-start.82 = (bf16[256,1024]{1,0:T(8,128)(2,1)}, bf16[256,1024]{1,0:T(8,128)(2,1)}, u32[]{:S(2)}, u32[]{:S(2)}) collective-permute-start(bf16[256,1024]{1,0:T(8,128)(2,1)} %fusion.87), channel_id=1, source_target_pairs={{0,8},{4,12},{8,0},{12,4},{16,24},{20,28},{24,16},{28,20},{1,9},{5... | collective-permute-start | bytes 1572872 | tf_op jit(solution)/shard_map/ppermute | solution.py:38
  678.4 39.5 %collective-permute-start.85 = (bf16[256,1024]{1,0:T(8,128)(2,1)}, bf16[256,1024]{1,0:T(8,128)(2,1)}, u32[]{:S(2)}, u32[]{:S(2)}) collective-permute-start(bf16[256,1024]{1,0:T(8,128)(2,1)} %fusion.88), channel_id=1, source_target_pairs={{0,8},{4,12},{8,0},{12,4},{16,24},{20,28},{24,16},{28,20},{1,9},{5... | collective-permute-start | bytes 1572872 | tf_op jit(solution)/shard_map/ppermute | solution.py:38
  680.4 26.5 %collective-permute-start.80 = (bf16[1024,512]{1,0:T(8,128)(2,1)S(1)}, bf16[1024,512]{1,0:T(8,128)(2,1)}, u32[]{:S(2)}, u32[]{:S(2)}) collective-permute-start(bf16[1024,512]{1,0:T(8,128)(2,1)S(1)} %get-tuple-element.291), channel_id=1, source_target_pairs={{4,0},{12,8},{20,16},{28,24},{5,1},{13,9},{21,17},{29,25},{6,2},{1... | collective-permute-start | bytes 3145736 | tf_op jit(solution)/shard_map/ppermute | solution.py:783
  684.4 28.5 %collective-permute-start.81 = (bf16[1,256,1024]{2,1,0:T(8,128)(2,1)}, bf16[1,256,1024]{2,1,0:T(8,128)(2,1)}, u32[]{:S(2)}, u32[]{:S(2)}) collective-permute-start(bf16[1,256,1024]{2,1,0:T(8,128)(2,1)} %get-tuple-element.419), channel_id=1, source_target_pairs={{0,16},{4,20},{8,24},{12,28},{16,0},{20,4},{24,8},{28,12},{1,17},{... | collective-permute-start | bytes 1572872 | tf_op jit(solution)/shard_map/ppermute | solution.py:38
  716.1 25.6 %collective-permute-start.84 = (bf16[1,2,256,1024]{3,2,1,0:T(8,128)(2,1)S(1)}, bf16[1,2,256,1024]{3,2,1,0:T(8,128)(2,1)S(1)}, u32[]{:S(2)}, u32[]{:S(2)}) collective-permute-start(bf16[1,2,256,1024]{3,2,1,0:T(8,128)(2,1)S(1)} %dynamic-slice_bitcast_fusion), channel_id=1, source_target_pairs={{0,4},{4,0},{8,12},{12,8},{16,20},{20,16},{24,28},{28,24},{1,5},{5... | collective-permute-start | bytes 3145736 | tf_op jit(solution)/shard_map/ppermute | solution.py:38
  720.9 28.7 %collective-permute-start.91 = (bf16[1,256,1024]{2,1,0:T(8,128)(2,1)}, bf16[1,256,1024]{2,1,0:T(8,128)(2,1)}, u32[]{:S(2)}, u32[]{:S(2)}) collective-permute-start(bf16[1,256,1024]{2,1,0:T(8,128)(2,1)} %get-tuple-element.302), channel_id=1, source_target_pairs={{0,16},{4,20},{8,24},{12,28},{16,0},{20,4},{24,8},{28,12},{1,17},{... | collective-permute-start | bytes 1572872 | tf_op jit(solution)/shard_map/ppermute | solution.py:38
  742.7 28.1 %collective-permute-start.89 = (bf16[1,2,256,768]{3,2,1,0:T(8,128)(2,1)}, bf16[1,2,256,768]{3,2,1,0:T(8,128)(2,1)}, u32[]{:S(2)}, u32[]{:S(2)}) collective-permute-start(bf16[1,2,256,768]{3,2,1,0:T(8,128)(2,1)} %dynamic-slice_bitcast_fusion.7), channel_id=1, source_target_pairs={{0,4},{4,0},{8,12},{12,8},{16,20},{20,16},{24,28},{28,24},{1,5},{5... | collective-permute-start | bytes 2359304 | tf_op jit(solution)/shard_map/ppermute | solution.py:38
  786.6 51.2 %collective-permute-start.102 = (bf16[1,2,256,256]{2,3,1,0:T(8,128)(2,1)S(1)}, bf16[1,2,256,256]{2,3,1,0:T(8,128)(2,1)S(1)}, u32[]{:S(2)}, u32[]{:S(2)}) collective-permute-start(bf16[1,2,256,256]{2,3,1,0:T(8,128)(2,1)S(1)} %bitcast.510), channel_id=1, source_target_pairs={{0,4},{4,0},{8,12},{12,8},{16,20},{20,16},{24,28},{28,24},{1,5},{5... | collective-permute-start | bytes 786440 | tf_op jit(solution)/shard_map/ppermute | solution.py:38
  789.8 48.1 %collective-permute-start.99 = (bf16[1,256,768]{2,1,0:T(8,128)(2,1)}, bf16[1,256,768]{2,1,0:T(8,128)(2,1)}, u32[]{:S(2)}, u32[]{:S(2)}) collective-permute-start(bf16[1,256,768]{2,1,0:T(8,128)(2,1)} %get-tuple-element.440), channel_id=1, source_target_pairs={{0,16},{4,20},{8,24},{12,28},{16,0},{20,4},{24,8},{28,12},{1,17},{... | collective-permute-start | bytes 1179656 | tf_op jit(solution)/shard_map/ppermute | solution.py:38
  793.2 44.6 %collective-permute-start.101 = (bf16[1,2,256,768]{3,2,1,0:T(8,128)(2,1)S(1)}, bf16[1,2,256,768]{3,2,1,0:T(8,128)(2,1)S(1)}, u32[]{:S(2)}, u32[]{:S(2)}) collective-permute-start(bf16[1,2,256,768]{3,2,1,0:T(8,128)(2,1)S(1)} %copy-done.96), channel_id=1, source_target_pairs={{0,4},{4,0},{8,12},{12,8},{16,20},{20,16},{24,28},{28,24},{1,5},{5... | collective-permute-start | bytes 2359304 | tf_op jit(solution)/shard_map/ppermute | solution.py:38
  796.1 31.7 %collective-permute-start.97 = (bf16[1,512,256]{2,1,0:T(8,128)(2,1)S(1)}, bf16[1,512,256]{2,1,0:T(8,128)(2,1)S(1)}, u32[]{:S(2)}, u32[]{:S(2)}) collective-permute-start(bf16[1,512,256]{2,1,0:T(8,128)(2,1)S(1)} %get-tuple-element.306), channel_id=1, source_target_pairs={{0,16},{4,20},{8,24},{12,28},{16,0},{20,4},{24,8},{28,12},{1,17},{... | collective-permute-start | bytes 786440 | tf_op jit(solution)/shard_map/ppermute | solution.py:38
  796.5 39.9 %collective-permute-start.98 = (bf16[1,544,256]{2,1,0:T(8,128)(2,1)S(1)}, bf16[1,544,256]{2,1,0:T(8,128)(2,1)S(1)}, u32[]{:S(2)}, u32[]{:S(2)}) collective-permute-start(bf16[1,544,256]{2,1,0:T(8,128)(2,1)S(1)} %fusion.97), channel_id=1, source_target_pairs={{0,16},{4,20},{8,24},{12,28},{16,0},{20,4},{24,8},{28,12},{1,17},{... | collective-permute-start | bytes 835592 | tf_op jit(solution)/shard_map/ppermute | solution.py:38
  836.4 23.6 %collective-permute-start.107 = (bf16[256,1024]{1,0:T(8,128)(2,1)}, bf16[256,1024]{1,0:T(8,128)(2,1)}, u32[]{:S(2)}, u32[]{:S(2)}) collective-permute-start(bf16[256,1024]{1,0:T(8,128)(2,1)} %fusion.89), channel_id=1, source_target_pairs={{0,8},{4,12},{8,0},{12,4},{16,24},{20,28},{24,16},{28,20},{1,9},{5... | collective-permute-start | bytes 1572872 | tf_op jit(solution)/shard_map/ppermute | solution.py:38
  838.5 31.6 %collective-permute-start.103 = (bf16[2,512,256]{2,1,0:T(8,128)(2,1)S(1)}, bf16[2,512,256]{2,1,0:T(8,128)(2,1)}, u32[]{:S(2)}, u32[]{:S(2)}) collective-permute-start(bf16[2,512,256]{2,1,0:T(8,128)(2,1)S(1)} %pad_maximum_fusion.16), channel_id=1, source_target_pairs={{0,8},{4,12},{8,0},{12,4},{16,24},{20,28},{24,16},{28,20},{1,9},{5... | collective-permute-start | bytes 1572872 | tf_op jit(solution)/shard_map/ppermute | solution.py:38
  839.3 32.0 %collective-permute-start.104 = (bf16[2,544,256]{2,1,0:T(8,128)(2,1)S(1)}, bf16[2,544,256]{2,1,0:T(8,128)(2,1)}, u32[]{:S(2)}, u32[]{:S(2)}) collective-permute-start(bf16[2,544,256]{2,1,0:T(8,128)(2,1)S(1)} %pad_maximum_fusion.13), channel_id=1, source_target_pairs={{0,4},{4,0},{8,12},{12,8},{16,20},{20,16},{24,28},{28,24},{1,5},{5... | collective-permute-start | bytes 1671176 | tf_op jit(solution)/shard_map/ppermute | solution.py:38
  844.3 28.5 %collective-permute-start.105 = (bf16[1,256,768]{2,1,0:T(8,128)(2,1)}, bf16[1,256,768]{2,1,0:T(8,128)(2,1)S(1)}, u32[]{:S(2)}, u32[]{:S(2)}) collective-permute-start(bf16[1,256,768]{2,1,0:T(8,128)(2,1)} %get-tuple-element.314), channel_id=1, source_target_pairs={{0,16},{4,20},{8,24},{12,28},{16,0},{20,4},{24,8},{28,12},{1,17},{... | collective-permute-start | bytes 1179656 | tf_op jit(solution)/shard_map/ppermute | solution.py:38
  874.5 24.6 %collective-permute-start.109 = (bf16[4,544,256]{2,1,0:T(8,128)(2,1)S(1)}, bf16[4,544,256]{2,1,0:T(8,128)(2,1)S(1)}, u32[]{:S(2)}, u32[]{:S(2)}) collective-permute-start(bf16[4,544,256]{2,1,0:T(8,128)(2,1)S(1)} %pad_maximum_fusion.7.refs_3_), channel_id=1, source_target_pairs={{0,8},{4,12},{8,0},{12,4},{16,24},{20,28},{24,16},{28,20},{1,9},{5... | collective-permute-start | bytes 3342344 | tf_op jit(solution)/shard_map/ppermute | solution.py:38
  (181 other events, 1952.2 us)

commit v4 on v3

--- a/solution.py
+++ b/solution.py
@@ -313,7 +313,7 @@
             out_ref[0, :, 0] = piece[...]
 
 
-def assembled_at(places, pieces):
+def assembled_at(places, pieces, grant):
     count = len(pieces)
     unused, rows, columns = pieces[0].shape
     grid = pltpu.PrefetchScalarGridSpec(
@@ -328,7 +328,7 @@
         lambda *refs: assembled_kernel(count, *refs),
         grid_spec=grid,
         out_shape=jax.ShapeDtypeStruct((count // 2, 2, 2, rows, columns), HALF),
-        compiler_params=pltpu.CompilerParams(vmem_limit_bytes=60 * 2**20),
+        compiler_params=pltpu.CompilerParams(vmem_limit_bytes=grant * 2**20),
         cost_estimate=pl.CostEstimate(
             flops=0, bytes_accessed=4 * count * pieces[0].size, transcendentals=0
         ),
@@ -488,11 +488,11 @@
     def spread_low(pieces):
         return tuple(flip(piece, 1) for piece in pieces)
 
-    def assembled(mine, far, near):
+    def assembled(mine, far, near, grant=40):
         pieces = (mine, *far, *near)
         places = [high ^ (k % highs) if side_at == 0 else low ^ (k // highs)
                   for k in range(len(pieces)) for side_at in range(2)]
-        return assembled_at(jnp.stack(places).astype(jnp.int32), pieces)
+        return assembled_at(jnp.stack(places).astype(jnp.int32), pieces, grant)
 
     mine = [mine_first, None, None, None]
     far = [None] * 4
@@ -529,16 +529,16 @@
         return keep + flip(send, bit)
 
     left = sorted(all_bits, reverse=True)
-    mid = 3 * width // 4
+    mid = width // 2
     picked, mine[0] = tie(picked, mine[0])
     far[0] = spread_high(mine[0])
     part_a = token_hop(picked[..., :mid], 1, left)
     part_b = token_hop(picked[..., mid:], PAIR, left)
-    local[1:] = [sides_of(halves) for halves in local[1:]]
     part_a = token_hop(part_a, PAIR, left[:-1])
     part_b = token_hop(part_b, 1, left[:-2] + left[-1:])
-    part_a, part_b, mine[0], far[0], local[1] = tie(part_a, part_b, mine[0], far[0], local[1])
-    mine[1] = paired(*local[1])
+    part_a, part_b, mine[0], far[0], local[1:] = tie(part_a, part_b, mine[0], far[0], local[1:])
+    local[2:] = [sides_of(halves) for halves in local[2:]]
+    mine[1] = paired(*sides_of(local[1]))
     near_own = spread_low(mine[:1])
     for k, bit in enumerate(high_bits[::-1]):
         part_a = token_hop(part_a, bit, left[k:-2])
@@ -559,7 +559,7 @@
     column_pieces = [[row, [hop(piece, 0, 1) for piece in row]] for row in of_core]
     column_at = jnp.stack([head ^ (2 * y + c) for c in range(2) for y in range(ys)])
     normed_in, embedded_own = joined_norm(column_pieces, column_at, gains_full[0], own)
-    w_first = assembled(mine[0], far[0], near[0])
+    w_first = assembled(mine[0], far[0], near[0], 60)
     head_columns = w_first.shape[-1] // 4
     w_in, w_out = w_first[:, : 3 * head_columns], w_first[:, 3 * head_columns :]
     local_heads = head_columns // HD

time: 984 us -> 956 us (0.972)
  waiting for transfers between devices: 459 us -> 477 us
  starting transfers between devices: 115 us -> 101 us
  other arithmetic: 124 us -> 111 us
  Pallas kernels: 75.3 us -> 64.9 us
    ppermute x51, waiting for transfers between devices: 185 us -> 201 us  [hop(): return lax.ppermute(value, both, pairs)]
    ppermute x59, starting transfers between devices: 67.2 us -> 53.6 us  [flip(): return lax.ppermute(value, 'blk', [(i, i ^ bit) for i in range(count)])]
    pallas_call x4, Pallas kernels: 21.9 us -> 10.3 us  [assembled_at(): pl.pallas_call(lambda *refs: assembled_kernel(count, *refs), grid_spec=gr...]
    unnamed x302 -> x346, local copies, waits for them, and re-layouts: 32.8 us -> 31.7 us
  transfers between devices with their start and end apart: 112 -> 112, of which waited for: 57 -> 59; matrix products, arithmetic and copies ran while one was open for 20% -> 19% of each run, Pallas kernels for 7% -> 6%
where the time goes in v4:
time: 956 us; the launch traced here: 944 us
  waiting for transfers between devices  477 us (50%)
  other arithmetic  111 us (12%)
  starting transfers between devices  101 us (11%)
  matrix products  86 us (9%)
  local copies, waits for them, and re-layouts  81.8 us (9%)
  Pallas kernels  64.9 us (7%)
  between operations  11.4 us (1%)
  blocking collectives  10.3 us (1%)
    ppermute x59, waiting for transfers between devices, flip(): return lax.ppermute(value, 'blk', [(i, i ^ bit) for i in range(count)])  276 us
    ppermute x51, waiting for transfers between devices, hop(): return lax.ppermute(value, both, pairs)  201 us
    dot_general x24, matrix products, dot(): lax.dot_general(left, right, (dims, ((), ())), preferred_element_type=F32)  86 us
    ppermute x59, starting transfers between devices, flip(): return lax.ppermute(value, 'blk', [(i, i ^ bit) for i in range(count)])  53.6 us
    ppermute x51, starting transfers between devices, hop(): return lax.ppermute(value, both, pairs)  42.4 us
    unnamed x346, local copies, waits for them, and re-layouts  31.7 us
    sub x8, other arithmetic, adamw(): weight - rate * (first_hat / (jnp.sqrt(second_hat) + ADAM_EPS) + decay *...  24.8 us
    pallas_call x2, Pallas kernels, attend_back(): pl.pallas_call(lambda *refs: attend_back_kernel(state is None, closing, *...  23.2 us
  transfers between devices with their start and end apart: 112, of which 59 were waited for; matrix products, arithmetic and copies ran while one was open for 19% of the time, Pallas kernels for 6%

profile of v4, /device:TPU:0, one launch (start us, length us, event | category | flops | bytes accessed | tf_op | source)
XLA Modules:
  0.0 943.8 jit_solution(10851152819839930198)
XLA Ops:
  26.3 6.0 fusion.2
  37.4 18.8 %collective-permute-done.4 = bf16[2,2,512,256]{3,2,0,1:T(8,128)(2,1)S(1)} collective-permute-done((bf16[2,2,512,256]{3,2,0,1:T(8,128)(2,1)S(1)}, bf16[2,2,512,256]{3,2,0,1:T(8,128)(2,1)S(1)}, u32[]{:S(2)}, u32[]{:S(2)}) %collective-permute-start.4) | collective-permute-done | bytes 1048608 | tf_op jit(solution)/shard_map/ppermute | solution.py:38
  58.9 21.9 %collective-permute-done.6 = bf16[2,2,512,256]{3,2,0,1:T(8,128)(2,1)S(1)} collective-permute-done((bf16[2,2,512,256]{3,2,0,1:T(8,128)(2,1)S(1)}, bf16[2,2,512,256]{3,2,0,1:T(8,128)(2,1)S(1)}, u32[]{:S(2)}, u32[]{:S(2)}) %collective-permute-start.6) | collective-permute-done | bytes 1048608 | tf_op jit(solution)/shard_map/ppermute | solution.py:38
  107.7 8.8 collective-permute-done.10
  117.4 4.4 collective-permute-done.9
  130.6 16.3 %collective-permute-done.16 = bf16[256,1024]{1,0:T(8,128)(2,1)S(1)} collective-permute-done((bf16[256,1024]{1,0:T(8,128)(2,1)S(1)}, bf16[256,1024]{1,0:T(8,128)(2,1)S(1)}, u32[]{:S(2)}, u32[]{:S(2)}) %collective-permute-start.16) | collective-permute-done | bytes 524320 | tf_op jit(solution)/shard_map/ppermute | solution.py:38
  146.9 6.7 collective-permute-done.15.refs_7_
  153.6 8.3 collective-permute-done.14.refs_6_
  167.4 5.4 shard_map.494
  172.9 7.5 shard_map.493
  182.7 6.6 fusion.56.refs_2_.refs_3_.refs_4_
  189.3 9.4 collective-permute-done.23
  199.8 3.9 collective-permute-start.25
  207.5 6.6 shard_map.495
  215.4 10.8 %collective-permute-done.27 = bf16[256,1024]{1,0:T(8,128)(2,1)S(1)} collective-permute-done((bf16[256,1024]{1,0:T(8,128)(2,1)S(1)}, bf16[256,1024]{1,0:T(8,128)(2,1)S(1)}, u32[]{:S(2)}, u32[]{:S(2)}) %collective-permute-start.27) | collective-permute-done | bytes 524320 | tf_op jit(solution)/shard_map/ppermute | solution.py:38
  226.3 3.7 collective-permute-done.26
  230.1 8.4 shard_map.496
  248.0 17.5 %collective-permute-done.33 = bf16[256,1024]{1,0:T(8,128)(2,1)S(1)} collective-permute-done((bf16[256,1024]{1,0:T(8,128)(2,1)S(1)}, bf16[256,1024]{1,0:T(8,128)(2,1)S(1)}, u32[]{:S(2)}, u32[]{:S(2)}) %collective-permute-start.33) | collective-permute-done | bytes 524320 | tf_op jit(solution)/shard_map/ppermute | solution.py:38
  265.6 13.6 %collective-permute-done.31 = bf16[128,2048]{1,0:T(8,128)(2,1)S(1)} collective-permute-done((bf16[128,2048]{1,0:T(8,128)(2,1)S(1)}, bf16[128,2048]{1,0:T(8,128)(2,1)S(1)}, u32[]{:S(2)}, u32[]{:S(2)}) %collective-permute-start.31) | collective-permute-done | bytes 524320 | tf_op jit(solution)/shard_map/ppermute | solution.py:403
  279.2 13.4 %collective-permute-done.30 = bf16[128,2048]{1,0:T(8,128)(2,1)S(1)} collective-permute-done((bf16[128,2048]{1,0:T(8,128)(2,1)S(1)}, bf16[128,2048]{1,0:T(8,128)(2,1)S(1)}, u32[]{:S(2)}, u32[]{:S(2)}) %collective-permute-start.30) | collective-permute-done | bytes 524320 | tf_op jit(solution)/shard_map/ppermute | solution.py:403
  299.6 9.8 %collective-permute-done.36 = bf16[128,2048]{1,0:T(8,128)(2,1)S(1)} collective-permute-done((bf16[128,2048]{1,0:T(8,128)(2,1)S(1)}, bf16[128,2048]{1,0:T(8,128)(2,1)S(1)}, u32[]{:S(2)}, u32[]{:S(2)}) %collective-permute-start.36) | collective-permute-done | bytes 524320 | tf_op jit(solution)/shard_map/ppermute | solution.py:403
  309.4 9.1 collective-permute-done.35
  323.5 5.5 multiply_convert_fusion
  334.0 5.4 multiply_convert_fusion.1
  346.3 12.6 %collective-permute-done.46 = bf16[256,1024]{1,0:T(8,128)(2,1)S(1)} collective-permute-done((bf16[256,1024]{1,0:T(8,128)(2,1)S(1)}, bf16[256,1024]{1,0:T(8,128)(2,1)S(1)}, u32[]{:S(2)}, u32[]{:S(2)}) %collective-permute-start.46) | collective-permute-done | bytes 524320 | tf_op jit(solution)/shard_map/ppermute | solution.py:38
  359.8 9.8 %collective-permute-done.44 = bf16[128,2048]{1,0:T(8,128)(2,1)S(1)} collective-permute-done((bf16[128,2048]{1,0:T(8,128)(2,1)S(1)}, bf16[128,2048]{1,0:T(8,128)(2,1)S(1)}, u32[]{:S(2)}, u32[]{:S(2)}) %collective-permute-start.44) | collective-permute-done | bytes 524320 | tf_op jit(solution)/shard_map/ppermute | solution.py:403
  369.7 9.4 collective-permute-done.43
  384.7 12.3 %collective-permute-done.49 = bf16[128,2048]{1,0:T(8,128)(2,1)S(1)} collective-permute-done((bf16[128,2048]{1,0:T(8,128)(2,1)S(1)}, bf16[128,2048]{1,0:T(8,128)(2,1)S(1)}, u32[]{:S(2)}, u32[]{:S(2)}) %collective-permute-start.49) | collective-permute-done | bytes 524320 | tf_op jit(solution)/shard_map/ppermute | solution.py:403
  397.0 8.6 collective-permute-done.48
  418.2 4.0 fusion.173
  443.5 5.0 convolution_convert_fusion.1
  457.8 12.4 %collective-permute-done.58 = bf16[128,2048]{1,0:T(8,128)(2,1)S(1)} collective-permute-done((bf16[128,2048]{1,0:T(8,128)(2,1)}, bf16[128,2048]{1,0:T(8,128)(2,1)S(1)}, u32[]{:S(2)}, u32[]{:S(2)}) %collective-permute-start.58) | collective-permute-done | bytes 524320 | tf_op jit(solution)/shard_map/ppermute | solution.py:403
  470.2 10.1 %collective-permute-done.57 = bf16[128,2048]{1,0:T(8,128)(2,1)} collective-permute-done((bf16[128,2048]{1,0:T(8,128)(2,1)}, bf16[128,2048]{1,0:T(8,128)(2,1)}, u32[]{:S(2)}, u32[]{:S(2)}) %collective-permute-start.57) | collective-permute-done | bytes 524320 | tf_op jit(solution)/shard_map/ppermute | solution.py:403
  488.4 20.6 %collective-permute-done.64 = bf16[1,256,1024]{2,1,0:T(8,128)(2,1)S(1)} collective-permute-done((bf16[1,256,1024]{2,1,0:T(8,128)(2,1)S(1)}, bf16[1,256,1024]{2,1,0:T(8,128)(2,1)S(1)}, u32[]{:S(2)}, u32[]{:S(2)}) %collective-permute-start.64) | collective-permute-done | bytes 524320 | tf_op jit(solution)/shard_map/ppermute | solution.py:38
  511.8 9.1 collective-permute-done.61
  523.1 5.5 fusion.28
  539.9 5.1 convolution_convert_fusion
  552.2 7.8 fusion.7
  560.0 4.5 collective-permute-done.70
  564.5 9.8 %collective-permute-done.69 = bf16[128,2048]{1,0:T(8,128)(2,1)S(1)} collective-permute-done((bf16[128,2048]{1,0:T(8,128)(2,1)S(1)}, bf16[128,2048]{1,0:T(8,128)(2,1)S(1)}, u32[]{:S(2)}, u32[]{:S(2)}) %collective-permute-start.69) | collective-permute-done | bytes 524320 | tf_op jit(solution)/shard_map/ppermute | solution.py:403
  583.6 20.3 %collective-permute-done.74 = bf16[128,2048]{1,0:T(8,128)(2,1)S(1)} collective-permute-done((bf16[128,2048]{1,0:T(8,128)(2,1)S(1)}, bf16[128,2048]{1,0:T(8,128)(2,1)S(1)}, u32[]{:S(2)}, u32[]{:S(2)}) %collective-permute-start.74) | collective-permute-done | bytes 524320 | tf_op jit(solution)/shard_map/ppermute | solution.py:403
  603.9 10.1 %collective-permute-done.73 = bf16[128,2048]{1,0:T(8,128)(2,1)S(1)} collective-permute-done((bf16[128,2048]{1,0:T(8,128)(2,1)S(1)}, bf16[128,2048]{1,0:T(8,128)(2,1)S(1)}, u32[]{:S(2)}, u32[]{:S(2)}) %collective-permute-start.73) | collective-permute-done | bytes 524320 | tf_op jit(solution)/shard_map/ppermute | solution.py:403
  629.0 10.9 %shard_map.500 = (f32[2,128,1024]{2,1,0:T(8,128)S(1)}, bf16[1024,512]{1,0:T(8,128)(2,1)S(1)}) custom-call(s32[1,1024]{1,0:T(1,128)S(1)} %bitcast.435, s32[1024,1]{1,0:T(8,128)S(1)} %add_select_fusion.refs_1_, bf16[1024,768]{1,0:T(8,128)(2,1)} %copy-done, bf16[1024,512]{1,0:T(8,128)(2,1)} %collective-permute-done.25.refs_3_.refs_4_, ...), custom_call_target="tpu_custom_call" | custom-call | flops 2684354560 | bytes 5242880 | tf_op jit(solution)/shard_map/pallas_call | solution.py:176
  639.9 7.4 collective-permute-done.79
  657.0 12.3 %shard_map.501 = (bf16[1024,256]{1,0:T(8,128)(2,1)S(1)}, f32[1024,512]{1,0:T(8,128)}) custom-call(s32[1,1024]{1,0:T(1,128)S(1)} %bitcast.436, s32[1024,1]{1,0:T(8,128)S(1)} %copy-done.6, bf16[1024,768]{1,0:T(8,128)(2,1)S(1)} %copy-done.1, bf16[1024,768]{1,0:T(8,128)(2,1)S(1)} %copy-done.1, bf16[1024,768]{1,0:T(8,128)(2,1)S(1)} %copy-done.1, ...), custom_call_target="tpu_custom_call" | custom-call | flops 2684354560 | bytes 5242880 | tf_op jit(solution)/shard_map/pallas_call | solution.py:176
  669.3 7.1 collective-permute-done.82
  680.5 4.0 collective-permute-done.81
  699.1 3.8 convolution_convert_fusion.2
  703.7 9.7 %collective-permute-done.84 = bf16[1,2,256,1024]{3,2,1,0:T(8,128)(2,1)S(1)} collective-permute-done((bf16[1,2,256,1024]{3,2,1,0:T(8,128)(2,1)S(1)}, bf16[1,2,256,1024]{3,2,1,0:T(8,128)(2,1)S(1)}, u32[]{:S(2)}, u32[]{:S(2)}) %collective-permute-start.84) | collective-permute-done | bytes 1048608 | tf_op jit(solution)/shard_map/ppermute | solution.py:38
  724.1 15.3 %collective-permute-done.90 = bf16[1,2,256,256]{2,3,1,0:T(8,128)(2,1)S(1)} collective-permute-done((bf16[1,2,256,256]{2,3,1,0:T(8,128)(2,1)}, bf16[1,2,256,256]{2,3,1,0:T(8,128)(2,1)S(1)}, u32[]{:S(2)}, u32[]{:S(2)}) %collective-permute-start.90) | collective-permute-done | bytes 262176 | tf_op jit(solution)/shard_map/ppermute | solution.py:38
  739.5 4.2 collective-permute-done.87
  773.1 29.0 %collective-permute-done.97 = bf16[1,512,256]{2,1,0:T(8,128)(2,1)S(1)} collective-permute-done((bf16[1,512,256]{2,1,0:T(8,128)(2,1)S(1)}, bf16[1,512,256]{2,1,0:T(8,128)(2,1)S(1)}, u32[]{:S(2)}, u32[]{:S(2)}) %collective-permute-start.97) | collective-permute-done | bytes 262176 | tf_op jit(solution)/shard_map/ppermute | solution.py:38
  802.1 7.4 collective-permute-done.98
  817.3 15.8 %collective-permute-done.107 = bf16[256,1024]{1,0:T(8,128)(2,1)} collective-permute-done((bf16[256,1024]{1,0:T(8,128)(2,1)}, bf16[256,1024]{1,0:T(8,128)(2,1)}, u32[]{:S(2)}, u32[]{:S(2)}) %collective-permute-start.107) | collective-permute-done | bytes 524320 | tf_op jit(solution)/shard_map/ppermute | solution.py:38
  834.9 9.8 %collective-permute-done.103 = bf16[2,512,256]{2,1,0:T(8,128)(2,1)} collective-permute-done((bf16[2,512,256]{2,1,0:T(8,128)(2,1)S(1)}, bf16[2,512,256]{2,1,0:T(8,128)(2,1)}, u32[]{:S(2)}, u32[]{:S(2)}) %collective-permute-start.103) | collective-permute-done | bytes 524320 | tf_op jit(solution)/shard_map/ppermute | solution.py:38
  854.2 14.2 %collective-permute-done.108.refs_2_ = bf16[4,512,256]{2,1,0:T(8,128)(2,1)S(1)} collective-permute-done((bf16[4,512,256]{2,1,0:T(8,128)(2,1)S(1)}, bf16[4,512,256]{2,1,0:T(8,128)(2,1)S(1)}, u32[]{:S(2)}, u32[]{:S(2)}) %collective-permute-start.108) | collective-permute-done | bytes 1048608 | tf_op jit(solution)/shard_map/ppermute | solution.py:38
  868.4 4.0 collective-permute-done.109.refs_4_
  875.4 8.9 shard_map.502
  898.9 10.3 %all_to_all.5 = f32[32,2,128]{2,1,0:T(2,128)S(1)} all-to-all(f32[32,2,128]{2,1,0:T(2,128)S(1)} %broadcast_in_dim.41), channel_id=1, replica_groups=mesh['blk'=8,'head'=4] {'blk','head'}, dimensions={0} | all-to-all | bytes 65536 | tf_op jit(solution)/shard_map/all_to_all | solution.py:896
  916.3 4.6 multiply_subtract_fusion.4
  922.1 3.9 multiply_subtract_fusion.1
  927.7 4.1 multiply_subtract_fusion
  932.8 3.8 multiply_subtract_fusion.2
  938.5 4.0 multiply_subtract_fusion.3
  (781 shorter events, 333.1 us)
Async XLA Ops:
  34.4 46.3 %collective-permute-start.6 = (bf16[2,2,512,256]{3,2,0,1:T(8,128)(2,1)S(1)}, bf16[2,2,512,256]{3,2,0,1:T(8,128)(2,1)S(1)}, u32[]{:S(2)}, u32[]{:S(2)}) collective-permute-start(bf16[2,2,512,256]{3,2,0,1:T(8,128)(2,1)S(1)} %slice_bitcast_fusion), channel_id=1, source_target_pairs={{0,8},{4,12},{8,0},{12,4},{16,24},{20,28},{24,16},{28,20},{1,9},{5... | collective-permute-start | bytes 3145736 | tf_op jit(solution)/shard_map/ppermute | solution.py:38
  34.8 61.3 %collective-permute-start.8 = (bf16[2,256,1024]{2,1,0:T(8,128)(2,1)S(1)}, bf16[2,256,1024]{2,1,0:T(8,128)(2,1)}, u32[]{:S(2)}, u32[]{:S(2)}) collective-permute-start(bf16[2,256,1024]{2,1,0:T(8,128)(2,1)S(1)} %maximum_select_fusion.refs_1_), channel_id=1, source_target_pairs={{0,16},{4,20},{8,24},{12,28},{16,0},{20,4},{24,8},{28,12},{1,17},{... | collective-permute-start | bytes 3145736 | tf_op jit(solution)/shard_map/ppermute | solution.py:38
  58.3 35.3 %collective-permute-start.5 = (bf16[2,512,256]{2,1,0:T(8,128)(2,1)}, bf16[2,512,256]{2,1,0:T(8,128)(2,1)}, u32[]{:S(2)}, u32[]{:S(2)}) collective-permute-start(bf16[2,512,256]{2,1,0:T(8,128)(2,1)} %slice_bitcast_fusion.12), channel_id=1, source_target_pairs={{0,8},{4,12},{8,0},{12,4},{16,24},{20,28},{24,16},{28,20},{1,9},{5... | collective-permute-start | bytes 1572872 | tf_op jit(solution)/shard_map/ppermute | solution.py:38
  97.8 27.8 %collective-permute-start.12 = (bf16[2,256,1024]{2,1,0:T(8,128)(2,1)S(1)}, bf16[2,256,1024]{2,1,0:T(8,128)(2,1)}, u32[]{:S(2)}, u32[]{:S(2)}) collective-permute-start(bf16[2,256,1024]{2,1,0:T(8,128)(2,1)S(1)} %maximum_select_fusion.refs_1_), channel_id=1, source_target_pairs={{0,4},{4,0},{8,12},{12,8},{16,20},{20,16},{24,28},{28,24},{1,5},{5... | collective-permute-start | bytes 3145736 | tf_op jit(solution)/shard_map/ppermute | solution.py:38
  125.7 36.2 %collective-permute-start.17 = (bf16[2,256,1024]{2,1,0:T(8,128)(2,1)}, bf16[2,256,1024]{2,1,0:T(8,128)(2,1)S(1)}, u32[]{:S(2)}, u32[]{:S(2)}) collective-permute-start(bf16[2,256,1024]{2,1,0:T(8,128)(2,1)} %collective-permute-done.8.refs_2_), channel_id=1, source_target_pairs={{0,4},{4,0},{8,12},{12,8},{16,20},{20,16},{24,28},{28,24},{1,5},{5... | collective-permute-start | bytes 3145736 | tf_op jit(solution)/shard_map/ppermute | solution.py:38
  127.0 26.6 %collective-permute-start.15 = (bf16[512,512]{1,0:T(8,128)(2,1)S(1)}, bf16[512,512]{1,0:T(8,128)(2,1)S(1)}, u32[]{:S(2)}, u32[]{:S(2)}) collective-permute-start(bf16[512,512]{1,0:T(8,128)(2,1)S(1)} %pad_maximum_fusion.14.refs_2_), channel_id=1, source_target_pairs={{0,10},{1,11},{2,8},{3,9},{4,14},{5,15},{6,12},{7,13},{8,2},{9,3},... | collective-permute-start | bytes 1572872 | tf_op jit(solution)/shard_map/ppermute | solution.py:403
  128.2 33.6 %collective-permute-start.14 = (bf16[512,512]{1,0:T(8,128)(2,1)S(1)}, bf16[512,512]{1,0:T(8,128)(2,1)S(1)}, u32[]{:S(2)}, u32[]{:S(2)}) collective-permute-start(bf16[512,512]{1,0:T(8,128)(2,1)S(1)} %pad_maximum_fusion.14.refs_2_), channel_id=1, source_target_pairs={{0,8},{1,9},{2,10},{3,11},{4,12},{5,13},{6,14},{7,15},{8,0},{9,1},... | collective-permute-start | bytes 1572872 | tf_op jit(solution)/shard_map/ppermute | solution.py:403
  130.1 31.8 %collective-permute-start.13 = (bf16[512,512]{1,0:T(8,128)(2,1)S(1)}, bf16[512,512]{1,0:T(8,128)(2,1)S(1)}, u32[]{:S(2)}, u32[]{:S(2)}) collective-permute-start(bf16[512,512]{1,0:T(8,128)(2,1)S(1)} %pad_maximum_fusion.14.refs_2_), channel_id=1, source_target_pairs={{0,2},{1,3},{2,0},{3,1},{4,6},{5,7},{6,4},{7,5},{8,10},{9,11},{10,... | collective-permute-start | bytes 1572872 | tf_op jit(solution)/shard_map/ppermute | solution.py:403
  166.4 32.4 %collective-permute-start.22 = (bf16[2,256,1024]{2,1,0:T(8,128)(2,1)S(1)}, bf16[2,256,1024]{2,1,0:T(8,128)(2,1)}, u32[]{:S(2)}, u32[]{:S(2)}) collective-permute-start(bf16[2,256,1024]{2,1,0:T(8,128)(2,1)S(1)} %maximum_select_fusion.1.refs_1_), channel_id=1, source_target_pairs={{0,4},{4,0},{8,12},{12,8},{16,20},{20,16},{24,28},{28,24},{1,5},{5... | collective-permute-start | bytes 3145736 | tf_op jit(solution)/shard_map/ppermute | solution.py:38
  172.8 26.0 %collective-permute-start.23 = (bf16[256,1024]{1,0:T(8,128)(2,1)S(1)}, bf16[256,1024]{1,0:T(8,128)(2,1)}, u32[]{:S(2)}, u32[]{:S(2)}) collective-permute-start(bf16[256,1024]{1,0:T(8,128)(2,1)S(1)} %slice_bitcast_fusion.30), channel_id=1, source_target_pairs={{0,16},{4,20},{8,24},{12,28},{16,0},{20,4},{24,8},{28,12},{1,17},{... | collective-permute-start | bytes 1572872 | tf_op jit(solution)/shard_map/ppermute | solution.py:38
  199.8 30.3 %collective-permute-start.25 = (bf16[1024,512]{1,0:T(8,128)(2,1)}, bf16[1024,512]{1,0:T(8,128)(2,1)}, u32[]{:S(2)}, u32[]{:S(2)}) collective-permute-start(bf16[1024,512]{1,0:T(8,128)(2,1)} %slice.371), channel_id=1, source_target_pairs={{0,4},{8,12},{16,20},{24,28},{1,5},{9,13},{17,21},{25,29},{2,6},{1... | collective-permute-start | bytes 3145736 | tf_op jit(solution)/shard_map/ppermute | solution.py:584
  205.3 24.8 %collective-permute-start.26 = (bf16[256,1024]{1,0:T(8,128)(2,1)S(1)}, bf16[256,1024]{1,0:T(8,128)(2,1)S(1)}, u32[]{:S(2)}, u32[]{:S(2)}) collective-permute-start(bf16[256,1024]{1,0:T(8,128)(2,1)S(1)} %slice_bitcast_fusion.29), channel_id=1, source_target_pairs={{0,16},{4,20},{8,24},{12,28},{16,0},{20,4},{24,8},{28,12},{1,17},{... | collective-permute-start | bytes 1572872 | tf_op jit(solution)/shard_map/ppermute | solution.py:38
  240.0 25.6 %collective-permute-start.33 = (bf16[256,1024]{1,0:T(8,128)(2,1)S(1)}, bf16[256,1024]{1,0:T(8,128)(2,1)S(1)}, u32[]{:S(2)}, u32[]{:S(2)}) collective-permute-start(bf16[256,1024]{1,0:T(8,128)(2,1)S(1)} %slice_bitcast_fusion.25), channel_id=1, source_target_pairs={{0,16},{4,20},{8,24},{12,28},{16,0},{20,4},{24,8},{28,12},{1,17},{... | collective-permute-start | bytes 1572872 | tf_op jit(solution)/shard_map/ppermute | solution.py:38
  240.1 25.5 %collective-permute-start.32 = (bf16[2,256,1024]{2,1,0:T(8,128)(2,1)S(1)}, bf16[2,256,1024]{2,1,0:T(8,128)(2,1)S(1)}, u32[]{:S(2)}, u32[]{:S(2)}) collective-permute-start(bf16[2,256,1024]{2,1,0:T(8,128)(2,1)S(1)} %pad_maximum_fusion.9.refs_2_), channel_id=1, source_target_pairs={{0,4},{4,0},{8,12},{12,8},{16,20},{20,16},{24,28},{28,24},{1,5},{5... | collective-permute-start | bytes 3145736 | tf_op jit(solution)/shard_map/ppermute | solution.py:38
  244.5 34.7 %collective-permute-start.31 = (bf16[128,2048]{1,0:T(8,128)(2,1)S(1)}, bf16[128,2048]{1,0:T(8,128)(2,1)S(1)}, u32[]{:S(2)}, u32[]{:S(2)}) collective-permute-start(bf16[128,2048]{1,0:T(8,128)(2,1)S(1)} %get-tuple-element.415), channel_id=1, source_target_pairs={{0,10},{1,11},{2,8},{3,9},{4,14},{5,15},{6,12},{7,13},{8,2},{9,3},... | collective-permute-start | bytes 1572872 | tf_op jit(solution)/shard_map/ppermute | solution.py:403
  244.5 48.0 %collective-permute-start.30 = (bf16[128,2048]{1,0:T(8,128)(2,1)S(1)}, bf16[128,2048]{1,0:T(8,128)(2,1)S(1)}, u32[]{:S(2)}, u32[]{:S(2)}) collective-permute-start(bf16[128,2048]{1,0:T(8,128)(2,1)S(1)} %get-tuple-element.416), channel_id=1, source_target_pairs={{0,8},{1,9},{2,10},{3,11},{4,12},{5,13},{6,14},{7,15},{8,0},{9,1},... | collective-permute-start | bytes 1572872 | tf_op jit(solution)/shard_map/ppermute | solution.py:403
  247.0 45.6 %collective-permute-start.29 = (bf16[128,2048]{1,0:T(8,128)(2,1)S(1)}, bf16[128,2048]{1,0:T(8,128)(2,1)S(1)}, u32[]{:S(2)}, u32[]{:S(2)}) collective-permute-start(bf16[128,2048]{1,0:T(8,128)(2,1)S(1)} %get-tuple-element.417), channel_id=1, source_target_pairs={{0,2},{1,3},{2,0},{3,1},{4,6},{5,7},{6,4},{7,5},{8,10},{9,11},{10,... | collective-permute-start | bytes 1572872 | tf_op jit(solution)/shard_map/ppermute | solution.py:403
  265.6 30.5 %collective-permute-start.37 = (bf16[256,1024]{1,0:T(8,128)(2,1)S(1)}, bf16[256,1024]{1,0:T(8,128)(2,1)S(1)}, u32[]{:S(2)}, u32[]{:S(2)}) collective-permute-start(bf16[256,1024]{1,0:T(8,128)(2,1)S(1)} %slice_bitcast_fusion.24), channel_id=1, source_target_pairs={{0,16},{4,20},{8,24},{12,28},{16,0},{20,4},{24,8},{28,12},{1,17},{... | collective-permute-start | bytes 1572872 | tf_op jit(solution)/shard_map/ppermute | solution.py:38
  265.6 34.0 %collective-permute-start.39 = (bf16[2,256,1024]{2,1,0:T(8,128)(2,1)S(1)}, bf16[2,256,1024]{2,1,0:T(8,128)(2,1)S(1)}, u32[]{:S(2)}, u32[]{:S(2)}) collective-permute-start(bf16[2,256,1024]{2,1,0:T(8,128)(2,1)S(1)} %copy-done.4), channel_id=1, source_target_pairs={{0,4},{4,0},{8,12},{12,8},{16,20},{20,16},{24,28},{28,24},{1,5},{5... | collective-permute-start | bytes 3145736 | tf_op jit(solution)/shard_map/ppermute | solution.py:38
  292.7 26.2 %collective-permute-start.38 = (bf16[2,256,1024]{2,1,0:T(8,128)(2,1)S(1)}, bf16[2,256,1024]{2,1,0:T(8,128)(2,1)S(1)}, u32[]{:S(2)}, u32[]{:S(2)}) collective-permute-start(bf16[2,256,1024]{2,1,0:T(8,128)(2,1)S(1)} %pad_maximum_fusion.10.refs_2_), channel_id=1, source_target_pairs={{0,4},{4,0},{8,12},{12,8},{16,20},{20,16},{24,28},{28,24},{1,5},{5... | collective-permute-start | bytes 3145736 | tf_op jit(solution)/shard_map/ppermute | solution.py:38
  293.6 24.9 %collective-permute-start.35 = (bf16[128,2048]{1,0:T(8,128)(2,1)S(1)}, bf16[128,2048]{1,0:T(8,128)(2,1)S(1)}, u32[]{:S(2)}, u32[]{:S(2)}) collective-permute-start(bf16[128,2048]{1,0:T(8,128)(2,1)S(1)} %multiply_convert_fusion.3), channel_id=1, source_target_pairs={{0,8},{1,9},{2,10},{3,11},{4,12},{5,13},{6,14},{7,15},{8,0},{9,1},... | collective-permute-start | bytes 1572872 | tf_op jit(solution)/shard_map/ppermute | solution.py:403
  331.6 27.3 %collective-permute-start.45 = (bf16[2,256,1024]{2,1,0:T(8,128)(2,1)S(1)}, bf16[2,256,1024]{2,1,0:T(8,128)(2,1)S(1)}, u32[]{:S(2)}, u32[]{:S(2)}) collective-permute-start(bf16[2,256,1024]{2,1,0:T(8,128)(2,1)S(1)} %maximum_select_fusion.3.refs_1_), channel_id=1, source_target_pairs={{0,4},{4,0},{8,12},{12,8},{16,20},{20,16},{24,28},{28,24},{1,5},{5... | collective-permute-start | bytes 3145736 | tf_op jit(solution)/shard_map/ppermute | solution.py:38
  333.4 25.5 %collective-permute-start.46 = (bf16[256,1024]{1,0:T(8,128)(2,1)S(1)}, bf16[256,1024]{1,0:T(8,128)(2,1)S(1)}, u32[]{:S(2)}, u32[]{:S(2)}) collective-permute-start(bf16[256,1024]{1,0:T(8,128)(2,1)S(1)} %slice_bitcast_fusion.23), channel_id=1, source_target_pairs={{0,16},{4,20},{8,24},{12,28},{16,0},{20,4},{24,8},{28,12},{1,17},{... | collective-permute-start | bytes 1572872 | tf_op jit(solution)/shard_map/ppermute | solution.py:38
  342.7 27.0 %collective-permute-start.44 = (bf16[128,2048]{1,0:T(8,128)(2,1)S(1)}, bf16[128,2048]{1,0:T(8,128)(2,1)S(1)}, u32[]{:S(2)}, u32[]{:S(2)}) collective-permute-start(bf16[128,2048]{1,0:T(8,128)(2,1)S(1)} %get-tuple-element.412), channel_id=1, source_target_pairs={{0,10},{1,11},{2,8},{3,9},{4,14},{5,15},{6,12},{7,13},{8,2},{9,3},... | collective-permute-start | bytes 1572872 | tf_op jit(solution)/shard_map/ppermute | solution.py:403
  345.4 33.7 %collective-permute-start.43 = (bf16[128,2048]{1,0:T(8,128)(2,1)S(1)}, bf16[128,2048]{1,0:T(8,128)(2,1)S(1)}, u32[]{:S(2)}, u32[]{:S(2)}) collective-permute-start(bf16[128,2048]{1,0:T(8,128)(2,1)S(1)} %get-tuple-element.413), channel_id=1, source_target_pairs={{0,8},{1,9},{2,10},{3,11},{4,12},{5,13},{6,14},{7,15},{8,0},{9,1},... | collective-permute-start | bytes 1572872 | tf_op jit(solution)/shard_map/ppermute | solution.py:403
  345.4 33.7 %collective-permute-start.42 = (bf16[128,2048]{1,0:T(8,128)(2,1)S(1)}, bf16[128,2048]{1,0:T(8,128)(2,1)S(1)}, u32[]{:S(2)}, u32[]{:S(2)}) collective-permute-start(bf16[128,2048]{1,0:T(8,128)(2,1)S(1)} %get-tuple-element.414), channel_id=1, source_target_pairs={{0,2},{1,3},{2,0},{3,1},{4,6},{5,7},{6,4},{7,5},{8,10},{9,11},{10,... | collective-permute-start | bytes 1572872 | tf_op jit(solution)/shard_map/ppermute | solution.py:403
  379.2 26.9 %collective-permute-start.50 = (bf16[2,256,1024]{2,1,0:T(8,128)(2,1)S(1)}, bf16[2,256,1024]{2,1,0:T(8,128)(2,1)S(1)}, u32[]{:S(2)}, u32[]{:S(2)}) collective-permute-start(bf16[2,256,1024]{2,1,0:T(8,128)(2,1)S(1)} %pad_maximum_fusion.11.refs_2_), channel_id=1, source_target_pairs={{0,4},{4,0},{8,12},{12,8},{16,20},{20,16},{24,28},{28,24},{1,5},{5... | collective-permute-start | bytes 3145736 | tf_op jit(solution)/shard_map/ppermute | solution.py:38
  381.4 24.2 %collective-permute-start.48 = (bf16[128,2048]{1,0:T(8,128)(2,1)S(1)}, bf16[128,2048]{1,0:T(8,128)(2,1)S(1)}, u32[]{:S(2)}, u32[]{:S(2)}) collective-permute-start(bf16[128,2048]{1,0:T(8,128)(2,1)S(1)} %get-tuple-element.385), channel_id=1, source_target_pairs={{0,8},{1,9},{2,10},{3,11},{4,12},{5,13},{6,14},{7,15},{8,0},{9,1},... | collective-permute-start | bytes 1572872 | tf_op jit(solution)/shard_map/ppermute | solution.py:403
  451.4 29.4 %collective-permute-start.59 = (bf16[1,2,256,1024]{3,2,1,0:T(8,128)(2,1)}, bf16[1,2,256,1024]{3,2,1,0:T(8,128)(2,1)S(1)}, u32[]{:S(2)}, u32[]{:S(2)}) collective-permute-start(bf16[1,2,256,1024]{3,2,1,0:T(8,128)(2,1)} %dynamic-slice_bitcast_fusion.5), channel_id=1, source_target_pairs={{0,4},{4,0},{8,12},{12,8},{16,20},{20,16},{24,28},{28,24},{1,5},{5... | collective-permute-start | bytes 3145736 | tf_op jit(solution)/shard_map/ppermute | solution.py:38
  454.7 25.6 %collective-permute-start.57 = (bf16[128,2048]{1,0:T(8,128)(2,1)}, bf16[128,2048]{1,0:T(8,128)(2,1)}, u32[]{:S(2)}, u32[]{:S(2)}) collective-permute-start(bf16[128,2048]{1,0:T(8,128)(2,1)} %get-tuple-element.410), channel_id=1, source_target_pairs={{0,8},{1,9},{2,10},{3,11},{4,12},{5,13},{6,14},{7,15},{8,0},{9,1},... | collective-permute-start | bytes 1572872 | tf_op jit(solution)/shard_map/ppermute | solution.py:403
  456.7 24.1 %collective-permute-start.56 = (bf16[128,2048]{1,0:T(8,128)(2,1)}, bf16[128,2048]{1,0:T(8,128)(2,1)}, u32[]{:S(2)}, u32[]{:S(2)}) collective-permute-start(bf16[128,2048]{1,0:T(8,128)(2,1)} %get-tuple-element.411), channel_id=1, source_target_pairs={{0,2},{1,3},{2,0},{3,1},{4,6},{5,7},{6,4},{7,5},{8,10},{9,11},{10,... | collective-permute-start | bytes 1572872 | tf_op jit(solution)/shard_map/ppermute | solution.py:403
  483.3 25.7 %collective-permute-start.64 = (bf16[1,256,1024]{2,1,0:T(8,128)(2,1)S(1)}, bf16[1,256,1024]{2,1,0:T(8,128)(2,1)S(1)}, u32[]{:S(2)}, u32[]{:S(2)}) collective-permute-start(bf16[1,256,1024]{2,1,0:T(8,128)(2,1)S(1)} %get-tuple-element.426), channel_id=1, source_target_pairs={{0,16},{4,20},{8,24},{12,28},{16,0},{20,4},{24,8},{28,12},{1,17},{... | collective-permute-start | bytes 1572872 | tf_op jit(solution)/shard_map/ppermute | solution.py:38
  484.1 36.8 %collective-permute-start.63 = (bf16[1,2,256,1024]{3,2,1,0:T(8,128)(2,1)S(1)}, bf16[1,2,256,1024]{3,2,1,0:T(8,128)(2,1)S(1)}, u32[]{:S(2)}, u32[]{:S(2)}) collective-permute-start(bf16[1,2,256,1024]{3,2,1,0:T(8,128)(2,1)S(1)} %dynamic-slice_bitcast_fusion.4), channel_id=1, source_target_pairs={{0,4},{4,0},{8,12},{12,8},{16,20},{20,16},{24,28},{28,24},{1,5},{5... | collective-permute-start | bytes 3145736 | tf_op jit(solution)/shard_map/ppermute | solution.py:38
  484.8 27.0 %collective-permute-start.62 = (bf16[128,2048]{1,0:T(8,128)(2,1)S(1)}, bf16[128,2048]{1,0:T(8,128)(2,1)S(1)}, u32[]{:S(2)}, u32[]{:S(2)}) collective-permute-start(bf16[128,2048]{1,0:T(8,128)(2,1)S(1)} %get-tuple-element.382), channel_id=1, source_target_pairs={{0,10},{1,11},{2,8},{3,9},{4,14},{5,15},{6,12},{7,13},{8,2},{9,3},... | collective-permute-start | bytes 1572872 | tf_op jit(solution)/shard_map/ppermute | solution.py:403
  487.0 34.0 %collective-permute-start.61 = (bf16[128,2048]{1,0:T(8,128)(2,1)S(1)}, bf16[128,2048]{1,0:T(8,128)(2,1)S(1)}, u32[]{:S(2)}, u32[]{:S(2)}) collective-permute-start(bf16[128,2048]{1,0:T(8,128)(2,1)S(1)} %get-tuple-element.382), channel_id=1, source_target_pairs={{0,8},{1,9},{2,10},{3,11},{4,12},{5,13},{6,14},{7,15},{8,0},{9,1},... | collective-permute-start | bytes 1572872 | tf_op jit(solution)/shard_map/ppermute | solution.py:403
  487.2 33.7 %collective-permute-start.60 = (bf16[128,2048]{1,0:T(8,128)(2,1)S(1)}, bf16[128,2048]{1,0:T(8,128)(2,1)S(1)}, u32[]{:S(2)}, u32[]{:S(2)}) collective-permute-start(bf16[128,2048]{1,0:T(8,128)(2,1)S(1)} %get-tuple-element.382), channel_id=1, source_target_pairs={{0,2},{1,3},{2,0},{3,1},{4,6},{5,7},{6,4},{7,5},{8,10},{9,11},{10,... | collective-permute-start | bytes 1572872 | tf_op jit(solution)/shard_map/ppermute | solution.py:403
  521.2 25.6 %collective-permute-start.67 = (bf16[1,256,1024]{2,1,0:T(8,128)(2,1)S(1)}, bf16[1,256,1024]{2,1,0:T(8,128)(2,1)S(1)}, u32[]{:S(2)}, u32[]{:S(2)}) collective-permute-start(bf16[1,256,1024]{2,1,0:T(8,128)(2,1)S(1)} %get-tuple-element.266), channel_id=1, source_target_pairs={{0,16},{4,20},{8,24},{12,28},{16,0},{20,4},{24,8},{28,12},{1,17},{... | collective-permute-start | bytes 1572872 | tf_op jit(solution)/shard_map/ppermute | solution.py:38
  546.9 27.6 %collective-permute-start.71 = (bf16[1,2,256,1024]{3,2,1,0:T(8,128)(2,1)S(1)}, bf16[1,2,256,1024]{3,2,1,0:T(8,128)(2,1)S(1)}, u32[]{:S(2)}, u32[]{:S(2)}) collective-permute-start(bf16[1,2,256,1024]{3,2,1,0:T(8,128)(2,1)S(1)} %dynamic-slice_bitcast_fusion.3), channel_id=1, source_target_pairs={{0,4},{4,0},{8,12},{12,8},{16,20},{20,16},{24,28},{28,24},{1,5},{5... | collective-permute-start | bytes 3145736 | tf_op jit(solution)/shard_map/ppermute | solution.py:38
  549.2 25.1 %collective-permute-start.69 = (bf16[128,2048]{1,0:T(8,128)(2,1)S(1)}, bf16[128,2048]{1,0:T(8,128)(2,1)S(1)}, u32[]{:S(2)}, u32[]{:S(2)}) collective-permute-start(bf16[128,2048]{1,0:T(8,128)(2,1)S(1)} %get-tuple-element.407), channel_id=1, source_target_pairs={{0,8},{1,9},{2,10},{3,11},{4,12},{5,13},{6,14},{7,15},{8,0},{9,1},... | collective-permute-start | bytes 1572872 | tf_op jit(solution)/shard_map/ppermute | solution.py:403
  576.9 27.0 %collective-permute-start.74 = (bf16[128,2048]{1,0:T(8,128)(2,1)S(1)}, bf16[128,2048]{1,0:T(8,128)(2,1)S(1)}, u32[]{:S(2)}, u32[]{:S(2)}) collective-permute-start(bf16[128,2048]{1,0:T(8,128)(2,1)S(1)} %get-tuple-element.379), channel_id=1, source_target_pairs={{0,10},{1,11},{2,8},{3,9},{4,14},{5,15},{6,12},{7,13},{8,2},{9,3},... | collective-permute-start | bytes 1572872 | tf_op jit(solution)/shard_map/ppermute | solution.py:403
  577.7 36.3 %collective-permute-start.73 = (bf16[128,2048]{1,0:T(8,128)(2,1)S(1)}, bf16[128,2048]{1,0:T(8,128)(2,1)S(1)}, u32[]{:S(2)}, u32[]{:S(2)}) collective-permute-start(bf16[128,2048]{1,0:T(8,128)(2,1)S(1)} %get-tuple-element.379), channel_id=1, source_target_pairs={{0,8},{1,9},{2,10},{3,11},{4,12},{5,13},{6,14},{7,15},{8,0},{9,1},... | collective-permute-start | bytes 1572872 | tf_op jit(solution)/shard_map/ppermute | solution.py:403
  579.6 34.3 %collective-permute-start.72 = (bf16[128,2048]{1,0:T(8,128)(2,1)S(1)}, bf16[128,2048]{1,0:T(8,128)(2,1)S(1)}, u32[]{:S(2)}, u32[]{:S(2)}) collective-permute-start(bf16[128,2048]{1,0:T(8,128)(2,1)S(1)} %get-tuple-element.379), channel_id=1, source_target_pairs={{0,2},{1,3},{2,0},{3,1},{4,6},{5,7},{6,4},{7,5},{8,10},{9,11},{10,... | collective-permute-start | bytes 1572872 | tf_op jit(solution)/shard_map/ppermute | solution.py:403
  580.5 33.5 %collective-permute-start.75 = (bf16[1,2,256,1024]{3,2,1,0:T(8,128)(2,1)S(1)}, bf16[1,2,256,1024]{3,2,1,0:T(8,128)(2,1)S(1)}, u32[]{:S(2)}, u32[]{:S(2)}) collective-permute-start(bf16[1,2,256,1024]{3,2,1,0:T(8,128)(2,1)S(1)} %dynamic-slice_bitcast_fusion.2), channel_id=1, source_target_pairs={{0,4},{4,0},{8,12},{12,8},{16,20},{20,16},{24,28},{28,24},{1,5},{5... | collective-permute-start | bytes 3145736 | tf_op jit(solution)/shard_map/ppermute | solution.py:38
  582.3 31.7 %collective-permute-start.76 = (bf16[1,256,1024]{2,1,0:T(8,128)(2,1)S(1)}, bf16[1,256,1024]{2,1,0:T(8,128)(2,1)S(1)}, u32[]{:S(2)}, u32[]{:S(2)}) collective-permute-start(bf16[1,256,1024]{2,1,0:T(8,128)(2,1)S(1)} %get-tuple-element.423), channel_id=1, source_target_pairs={{0,16},{4,20},{8,24},{12,28},{16,0},{20,4},{24,8},{28,12},{1,17},{... | collective-permute-start | bytes 1572872 | tf_op jit(solution)/shard_map/ppermute | solution.py:38
  618.2 29.0 %collective-permute-start.78 = (bf16[1,2,256,1024]{3,2,1,0:T(8,128)(2,1)S(1)}, bf16[1,2,256,1024]{3,2,1,0:T(8,128)(2,1)S(1)}, u32[]{:S(2)}, u32[]{:S(2)}) collective-permute-start(bf16[1,2,256,1024]{3,2,1,0:T(8,128)(2,1)S(1)} %dynamic-slice_bitcast_fusion.1), channel_id=1, source_target_pairs={{0,4},{4,0},{8,12},{12,8},{16,20},{20,16},{24,28},{28,24},{1,5},{5... | collective-permute-start | bytes 3145736 | tf_op jit(solution)/shard_map/ppermute | solution.py:38
  621.3 25.9 %collective-permute-start.79 = (bf16[1,256,1024]{2,1,0:T(8,128)(2,1)S(1)}, bf16[1,256,1024]{2,1,0:T(8,128)(2,1)S(1)}, u32[]{:S(2)}, u32[]{:S(2)}) collective-permute-start(bf16[1,256,1024]{2,1,0:T(8,128)(2,1)S(1)} %copy-done.125), channel_id=1, source_target_pairs={{0,16},{4,20},{8,24},{12,28},{16,0},{20,4},{24,8},{28,12},{1,17},{... | collective-permute-start | bytes 1572872 | tf_op jit(solution)/shard_map/ppermute | solution.py:38
  650.2 26.2 %collective-permute-start.82 = (bf16[256,1024]{1,0:T(8,128)(2,1)S(1)}, bf16[256,1024]{1,0:T(8,128)(2,1)}, u32[]{:S(2)}, u32[]{:S(2)}) collective-permute-start(bf16[256,1024]{1,0:T(8,128)(2,1)S(1)} %fusion.87), channel_id=1, source_target_pairs={{0,8},{4,12},{8,0},{12,4},{16,24},{20,28},{24,16},{28,20},{1,9},{5... | collective-permute-start | bytes 1572872 | tf_op jit(solution)/shard_map/ppermute | solution.py:38
  650.3 40.5 %collective-permute-start.85 = (bf16[256,1024]{1,0:T(8,128)(2,1)S(1)}, bf16[256,1024]{1,0:T(8,128)(2,1)}, u32[]{:S(2)}, u32[]{:S(2)}) collective-permute-start(bf16[256,1024]{1,0:T(8,128)(2,1)S(1)} %fusion.88), channel_id=1, source_target_pairs={{0,8},{4,12},{8,0},{12,4},{16,24},{20,28},{24,16},{28,20},{1,9},{5... | collective-permute-start | bytes 1572872 | tf_op jit(solution)/shard_map/ppermute | solution.py:38
  652.3 26.5 %collective-permute-start.80 = (bf16[1024,512]{1,0:T(8,128)(2,1)S(1)}, bf16[1024,512]{1,0:T(8,128)(2,1)}, u32[]{:S(2)}, u32[]{:S(2)}) collective-permute-start(bf16[1024,512]{1,0:T(8,128)(2,1)S(1)} %get-tuple-element.293), channel_id=1, source_target_pairs={{4,0},{12,8},{20,16},{28,24},{5,1},{13,9},{21,17},{29,25},{6,2},{1... | collective-permute-start | bytes 3145736 | tf_op jit(solution)/shard_map/ppermute | solution.py:783
  656.6 27.9 %collective-permute-start.81 = (bf16[1,256,1024]{2,1,0:T(8,128)(2,1)}, bf16[1,256,1024]{2,1,0:T(8,128)(2,1)}, u32[]{:S(2)}, u32[]{:S(2)}) collective-permute-start(bf16[1,256,1024]{2,1,0:T(8,128)(2,1)} %get-tuple-element.421), channel_id=1, source_target_pairs={{0,16},{4,20},{8,24},{12,28},{16,0},{20,4},{24,8},{28,12},{1,17},{... | collective-permute-start | bytes 1572872 | tf_op jit(solution)/shard_map/ppermute | solution.py:38
  687.8 25.6 %collective-permute-start.84 = (bf16[1,2,256,1024]{3,2,1,0:T(8,128)(2,1)S(1)}, bf16[1,2,256,1024]{3,2,1,0:T(8,128)(2,1)S(1)}, u32[]{:S(2)}, u32[]{:S(2)}) collective-permute-start(bf16[1,2,256,1024]{3,2,1,0:T(8,128)(2,1)S(1)} %dynamic-slice_bitcast_fusion), channel_id=1, source_target_pairs={{0,4},{4,0},{8,12},{12,8},{16,20},{20,16},{24,28},{28,24},{1,5},{5... | collective-permute-start | bytes 3145736 | tf_op jit(solution)/shard_map/ppermute | solution.py:38
  693.9 28.6 %collective-permute-start.91 = (bf16[1,256,1024]{2,1,0:T(8,128)(2,1)}, bf16[1,256,1024]{2,1,0:T(8,128)(2,1)}, u32[]{:S(2)}, u32[]{:S(2)}) collective-permute-start(bf16[1,256,1024]{2,1,0:T(8,128)(2,1)} %get-tuple-element.304), channel_id=1, source_target_pairs={{0,16},{4,20},{8,24},{12,28},{16,0},{20,4},{24,8},{28,12},{1,17},{... | collective-permute-start | bytes 1572872 | tf_op jit(solution)/shard_map/ppermute | solution.py:38
  714.4 29.5 %collective-permute-start.89 = (bf16[1,2,256,768]{3,2,1,0:T(8,128)(2,1)}, bf16[1,2,256,768]{3,2,1,0:T(8,128)(2,1)}, u32[]{:S(2)}, u32[]{:S(2)}) collective-permute-start(bf16[1,2,256,768]{3,2,1,0:T(8,128)(2,1)} %dynamic-slice_bitcast_fusion.7), channel_id=1, source_target_pairs={{0,4},{4,0},{8,12},{12,8},{16,20},{20,16},{24,28},{28,24},{1,5},{5... | collective-permute-start | bytes 2359304 | tf_op jit(solution)/shard_map/ppermute | solution.py:38
  720.2 23.6 %collective-permute-start.86 = (bf16[128,2048]{1,0:T(8,128)(2,1)}, bf16[128,2048]{1,0:T(8,128)(2,1)}, u32[]{:S(2)}, u32[]{:S(2)}) collective-permute-start(bf16[128,2048]{1,0:T(8,128)(2,1)} %get-tuple-element.405), channel_id=1, source_target_pairs={{0,2},{1,3},{2,0},{3,1},{4,6},{5,7},{6,4},{7,5},{8,10},{9,11},{10,... | collective-permute-start | bytes 1572872 | tf_op jit(solution)/shard_map/ppermute | solution.py:403
  759.2 51.7 %collective-permute-start.102 = (bf16[1,2,256,256]{2,3,1,0:T(8,128)(2,1)S(1)}, bf16[1,2,256,256]{2,3,1,0:T(8,128)(2,1)S(1)}, u32[]{:S(2)}, u32[]{:S(2)}) collective-permute-start(bf16[1,2,256,256]{2,3,1,0:T(8,128)(2,1)S(1)} %bitcast.503), channel_id=1, source_target_pairs={{0,4},{4,0},{8,12},{12,8},{16,20},{20,16},{24,28},{28,24},{1,5},{5... | collective-permute-start | bytes 786440 | tf_op jit(solution)/shard_map/ppermute | solution.py:38
  762.9 48.1 %collective-permute-start.99 = (bf16[1,256,768]{2,1,0:T(8,128)(2,1)}, bf16[1,256,768]{2,1,0:T(8,128)(2,1)S(1)}, u32[]{:S(2)}, u32[]{:S(2)}) collective-permute-start(bf16[1,256,768]{2,1,0:T(8,128)(2,1)} %get-tuple-element.442), channel_id=1, source_target_pairs={{0,16},{4,20},{8,24},{12,28},{16,0},{20,4},{24,8},{28,12},{1,17},{... | collective-permute-start | bytes 1179656 | tf_op jit(solution)/shard_map/ppermute | solution.py:38
  765.4 45.5 %collective-permute-start.101 = (bf16[1,2,256,768]{3,2,1,0:T(8,128)(2,1)}, bf16[1,2,256,768]{3,2,1,0:T(8,128)(2,1)S(1)}, u32[]{:S(2)}, u32[]{:S(2)}) collective-permute-start(bf16[1,2,256,768]{3,2,1,0:T(8,128)(2,1)} %dynamic-slice_bitcast_fusion.6), channel_id=1, source_target_pairs={{0,4},{4,0},{8,12},{12,8},{16,20},{20,16},{24,28},{28,24},{1,5},{5... | collective-permute-start | bytes 2359304 | tf_op jit(solution)/shard_map/ppermute | solution.py:38
  767.0 35.1 %collective-permute-start.97 = (bf16[1,512,256]{2,1,0:T(8,128)(2,1)S(1)}, bf16[1,512,256]{2,1,0:T(8,128)(2,1)S(1)}, u32[]{:S(2)}, u32[]{:S(2)}) collective-permute-start(bf16[1,512,256]{2,1,0:T(8,128)(2,1)S(1)} %get-tuple-element.308), channel_id=1, source_target_pairs={{0,16},{4,20},{8,24},{12,28},{16,0},{20,4},{24,8},{28,12},{1,17},{... | collective-permute-start | bytes 786440 | tf_op jit(solution)/shard_map/ppermute | solution.py:38
  768.7 40.8 %collective-permute-start.98 = (bf16[1,544,256]{2,1,0:T(8,128)(2,1)S(1)}, bf16[1,544,256]{2,1,0:T(8,128)(2,1)S(1)}, u32[]{:S(2)}, u32[]{:S(2)}) collective-permute-start(bf16[1,544,256]{2,1,0:T(8,128)(2,1)S(1)} %fusion.98), channel_id=1, source_target_pairs={{0,16},{4,20},{8,24},{12,28},{16,0},{20,4},{24,8},{28,12},{1,17},{... | collective-permute-start | bytes 835592 | tf_op jit(solution)/shard_map/ppermute | solution.py:38
  809.5 23.6 %collective-permute-start.107 = (bf16[256,1024]{1,0:T(8,128)(2,1)}, bf16[256,1024]{1,0:T(8,128)(2,1)}, u32[]{:S(2)}, u32[]{:S(2)}) collective-permute-start(bf16[256,1024]{1,0:T(8,128)(2,1)} %fusion.89), channel_id=1, source_target_pairs={{0,8},{4,12},{8,0},{12,4},{16,24},{20,28},{24,16},{28,20},{1,9},{5... | collective-permute-start | bytes 1572872 | tf_op jit(solution)/shard_map/ppermute | solution.py:38
  811.0 33.7 %collective-permute-start.103 = (bf16[2,512,256]{2,1,0:T(8,128)(2,1)S(1)}, bf16[2,512,256]{2,1,0:T(8,128)(2,1)}, u32[]{:S(2)}, u32[]{:S(2)}) collective-permute-start(bf16[2,512,256]{2,1,0:T(8,128)(2,1)S(1)} %pad_maximum_fusion.16), channel_id=1, source_target_pairs={{0,8},{4,12},{8,0},{12,4},{16,24},{20,28},{24,16},{28,20},{1,9},{5... | collective-permute-start | bytes 1572872 | tf_op jit(solution)/shard_map/ppermute | solution.py:38
  811.8 34.0 %collective-permute-start.104 = (bf16[2,544,256]{2,1,0:T(8,128)(2,1)S(1)}, bf16[2,544,256]{2,1,0:T(8,128)(2,1)}, u32[]{:S(2)}, u32[]{:S(2)}) collective-permute-start(bf16[2,544,256]{2,1,0:T(8,128)(2,1)S(1)} %pad_maximum_fusion.13), channel_id=1, source_target_pairs={{0,4},{4,0},{8,12},{12,8},{16,20},{20,16},{24,28},{28,24},{1,5},{5... | collective-permute-start | bytes 1671176 | tf_op jit(solution)/shard_map/ppermute | solution.py:38
  815.7 31.6 %collective-permute-start.105 = (bf16[1,256,768]{2,1,0:T(8,128)(2,1)}, bf16[1,256,768]{2,1,0:T(8,128)(2,1)S(1)}, u32[]{:S(2)}, u32[]{:S(2)}) collective-permute-start(bf16[1,256,768]{2,1,0:T(8,128)(2,1)} %get-tuple-element.316), channel_id=1, source_target_pairs={{0,16},{4,20},{8,24},{12,28},{16,0},{20,4},{24,8},{28,12},{1,17},{... | collective-permute-start | bytes 1179656 | tf_op jit(solution)/shard_map/ppermute | solution.py:38
  847.9 24.6 %collective-permute-start.109 = (bf16[4,544,256]{2,1,0:T(8,128)(2,1)S(1)}, bf16[4,544,256]{2,1,0:T(8,128)(2,1)S(1)}, u32[]{:S(2)}, u32[]{:S(2)}) collective-permute-start(bf16[4,544,256]{2,1,0:T(8,128)(2,1)S(1)} %pad_maximum_fusion.7.refs_3_), channel_id=1, source_target_pairs={{0,8},{4,12},{8,0},{12,4},{16,24},{20,28},{24,16},{28,20},{1,9},{5... | collective-permute-start | bytes 3342344 | tf_op jit(solution)/shard_map/ppermute | solution.py:38
  (206 other events, 2154.8 us)

commit v5 on v4

--- a/solution.py
+++ b/solution.py
@@ -800,20 +800,13 @@
     grad_mixed, up_first, up_top, grad_read = tie(grad_mixed, up_first, up_top, grad_read)
     up_second = send_high(up_top[1])
     made = core_sum(grad_mixed[:half], grad_mixed[half:], w_in, ((1,), (1,)))
-    made, in_made, out_made, up_near, grad_down = tie(
-        made,
-        made_of(normed_in, grad_mixed),
-        made_of(attn_grad, flat_heads),
-        up_near,
-        grad_down,
+    made, in_made, out_made, grad_down = tie(
+        made, made_of(normed_in, grad_mixed), made_of(attn_grad, flat_heads), grad_down
+    )
+    grad_norm_in, in_made, out_made, up_near, up_second = group_sum(
+        made, in_made, out_made, up_near, up_second
     )
     in_far, out_far = send_low(in_made, 1 - top), send_low(out_made, 1 - top)
-    grad_norm_in, in_made, out_made, in_far, out_far, up_second = group_sum(
-        made, in_made, out_made, in_far, out_far, up_second
-    )
-    in_near, out_near = send_low(in_made, top), send_low(out_made, top)
-    in_top, out_top = for_top(in_made, in_far), for_top(out_made, out_far)
-    in_first, out_first = send_high(in_top[0]), send_high(out_top[0])
     grad_embed_in, gain_in = norm_back(embedded_own, gains_full[0], grad_norm_in)
     grad_embed = (grad_first + grad_embed_in).astype(HALF)
 
@@ -826,6 +819,12 @@
         columns_of(bits) if bits == 0 else hop(columns_of(bits), 0, bits) for bits in head_bits
     ]
     grad_up = sum_sides(add_high(up_made, up_near, (up_first, up_second)))
+    head_parts, in_made, out_made, in_far, out_far = tie(
+        head_parts, in_made, out_made, in_far, out_far
+    )
+    in_near, out_near = send_low(in_made, top), send_low(out_made, top)
+    in_top, out_top = for_top(in_made, in_far), for_top(out_made, out_far)
+    in_first, out_first = send_high(in_top[0]), send_high(out_top[0])
     columns_own = jnp.concatenate(head_parts)
     gain_own = jnp.stack([gain_in, gain_mid, gain_final])
     for k in range(heads.bit_length() - 1):

time: 956 us -> 984 us (1.029)
  waiting for transfers between devices: 477 us -> 495 us
    ppermute x51, waiting for transfers between devices: 201 us -> 217 us  [hop(): return lax.ppermute(value, both, pairs)]
    unnamed x346 -> x345, local copies, waits for them, and re-layouts: 31.7 us -> 39.7 us
  transfers between devices with their start and end apart: 112 -> 112, of which waited for: 59 -> 58; matrix products, arithmetic and copies ran while one was open for 19% -> 19% of each run, Pallas kernels for 6% -> 6%
where the time goes in v5:
time: 984 us; the launch traced here: 971 us
  waiting for transfers between devices  495 us (50%)
  other arithmetic  111 us (11%)
  starting transfers between devices  99.1 us (10%)
  local copies, waits for them, and re-layouts  89.8 us (9%)
  matrix products  88.6 us (9%)
  Pallas kernels  64.9 us (7%)
  between operations  11.4 us (1%)
  blocking collectives  10.9 us (1%)
    ppermute x59, waiting for transfers between devices, flip(): return lax.ppermute(value, 'blk', [(i, i ^ bit) for i in range(count)])  279 us
    ppermute x51, waiting for transfers between devices, hop(): return lax.ppermute(value, both, pairs)  217 us
    dot_general x24, matrix products, dot(): lax.dot_general(left, right, (dims, ((), ())), preferred_element_type=F32)  88.6 us
    ppermute x59, starting transfers between devices, flip(): return lax.ppermute(value, 'blk', [(i, i ^ bit) for i in range(count)])  52.3 us
    ppermute x51, starting transfers between devices, hop(): return lax.ppermute(value, both, pairs)  41.5 us
    unnamed x345, local copies, waits for them, and re-layouts  39.7 us
    sub x8, other arithmetic, adamw(): weight - rate * (first_hat / (jnp.sqrt(second_hat) + ADAM_EPS) + decay *...  24.8 us
    pallas_call x2, Pallas kernels, attend_back(): pl.pallas_call(lambda *refs: attend_back_kernel(state is None, closing, *...  23.2 us
  transfers between devices with their start and end apart: 112, of which 58 were waited for; matrix products, arithmetic and copies ran while one was open for 19% of the time, Pallas kernels for 6%

profile of v5, /device:TPU:0, one launch (start us, length us, event | category | flops | bytes accessed | tf_op | source)
XLA Modules:
  0.0 970.9 jit_solution(16037645215957669129)
XLA Ops:
  26.3 6.0 fusion.2
  37.4 18.8 %collective-permute-done.4 = bf16[2,2,512,256]{3,2,0,1:T(8,128)(2,1)S(1)} collective-permute-done((bf16[2,2,512,256]{3,2,0,1:T(8,128)(2,1)S(1)}, bf16[2,2,512,256]{3,2,0,1:T(8,128)(2,1)S(1)}, u32[]{:S(2)}, u32[]{:S(2)}) %collective-permute-start.4) | collective-permute-done | bytes 1048608 | tf_op jit(solution)/shard_map/ppermute | solution.py:38
  58.9 21.9 %collective-permute-done.6 = bf16[2,2,512,256]{3,2,0,1:T(8,128)(2,1)S(1)} collective-permute-done((bf16[2,2,512,256]{3,2,0,1:T(8,128)(2,1)S(1)}, bf16[2,2,512,256]{3,2,0,1:T(8,128)(2,1)S(1)}, u32[]{:S(2)}, u32[]{:S(2)}) %collective-permute-start.6) | collective-permute-done | bytes 1048608 | tf_op jit(solution)/shard_map/ppermute | solution.py:38
  107.7 8.8 collective-permute-done.10
  117.4 4.4 collective-permute-done.9
  130.5 16.3 %collective-permute-done.16 = bf16[256,1024]{1,0:T(8,128)(2,1)S(1)} collective-permute-done((bf16[256,1024]{1,0:T(8,128)(2,1)S(1)}, bf16[256,1024]{1,0:T(8,128)(2,1)S(1)}, u32[]{:S(2)}, u32[]{:S(2)}) %collective-permute-start.16) | collective-permute-done | bytes 524320 | tf_op jit(solution)/shard_map/ppermute | solution.py:38
  146.9 6.7 collective-permute-done.15.refs_7_
  153.6 8.3 collective-permute-done.14.refs_6_
  167.4 5.3 shard_map.494
  172.8 7.5 shard_map.493
  182.6 6.6 fusion.56.refs_2_.refs_3_.refs_4_
  189.2 9.5 collective-permute-done.23
  199.8 4.0 collective-permute-start.25
  207.5 6.6 shard_map.495
  215.3 10.8 %collective-permute-done.27 = bf16[256,1024]{1,0:T(8,128)(2,1)S(1)} collective-permute-done((bf16[256,1024]{1,0:T(8,128)(2,1)S(1)}, bf16[256,1024]{1,0:T(8,128)(2,1)S(1)}, u32[]{:S(2)}, u32[]{:S(2)}) %collective-permute-start.27) | collective-permute-done | bytes 524320 | tf_op jit(solution)/shard_map/ppermute | solution.py:38
  230.1 8.4 shard_map.496
  248.0 17.5 %collective-permute-done.33 = bf16[256,1024]{1,0:T(8,128)(2,1)S(1)} collective-permute-done((bf16[256,1024]{1,0:T(8,128)(2,1)S(1)}, bf16[256,1024]{1,0:T(8,128)(2,1)S(1)}, u32[]{:S(2)}, u32[]{:S(2)}) %collective-permute-start.33) | collective-permute-done | bytes 524320 | tf_op jit(solution)/shard_map/ppermute | solution.py:38
  265.6 13.6 %collective-permute-done.31 = bf16[128,2048]{1,0:T(8,128)(2,1)S(1)} collective-permute-done((bf16[128,2048]{1,0:T(8,128)(2,1)S(1)}, bf16[128,2048]{1,0:T(8,128)(2,1)S(1)}, u32[]{:S(2)}, u32[]{:S(2)}) %collective-permute-start.31) | collective-permute-done | bytes 524320 | tf_op jit(solution)/shard_map/ppermute | solution.py:403
  279.2 13.4 %collective-permute-done.30 = bf16[128,2048]{1,0:T(8,128)(2,1)S(1)} collective-permute-done((bf16[128,2048]{1,0:T(8,128)(2,1)S(1)}, bf16[128,2048]{1,0:T(8,128)(2,1)S(1)}, u32[]{:S(2)}, u32[]{:S(2)}) %collective-permute-start.30) | collective-permute-done | bytes 524320 | tf_op jit(solution)/shard_map/ppermute | solution.py:403
  300.0 9.8 %collective-permute-done.36 = bf16[128,2048]{1,0:T(8,128)(2,1)S(1)} collective-permute-done((bf16[128,2048]{1,0:T(8,128)(2,1)S(1)}, bf16[128,2048]{1,0:T(8,128)(2,1)S(1)}, u32[]{:S(2)}, u32[]{:S(2)}) %collective-permute-start.36) | collective-permute-done | bytes 524320 | tf_op jit(solution)/shard_map/ppermute | solution.py:403
  309.8 9.1 collective-permute-done.35
  323.9 5.5 multiply_convert_fusion
  334.4 5.4 multiply_convert_fusion.1
  346.7 12.6 %collective-permute-done.46 = bf16[256,1024]{1,0:T(8,128)(2,1)S(1)} collective-permute-done((bf16[256,1024]{1,0:T(8,128)(2,1)S(1)}, bf16[256,1024]{1,0:T(8,128)(2,1)S(1)}, u32[]{:S(2)}, u32[]{:S(2)}) %collective-permute-start.46) | collective-permute-done | bytes 524320 | tf_op jit(solution)/shard_map/ppermute | solution.py:38
  360.3 9.8 %collective-permute-done.44 = bf16[128,2048]{1,0:T(8,128)(2,1)S(1)} collective-permute-done((bf16[128,2048]{1,0:T(8,128)(2,1)S(1)}, bf16[128,2048]{1,0:T(8,128)(2,1)S(1)}, u32[]{:S(2)}, u32[]{:S(2)}) %collective-permute-start.44) | collective-permute-done | bytes 524320 | tf_op jit(solution)/shard_map/ppermute | solution.py:403
  370.1 9.4 collective-permute-done.43
  385.2 12.3 %collective-permute-done.49 = bf16[128,2048]{1,0:T(8,128)(2,1)S(1)} collective-permute-done((bf16[128,2048]{1,0:T(8,128)(2,1)S(1)}, bf16[128,2048]{1,0:T(8,128)(2,1)S(1)}, u32[]{:S(2)}, u32[]{:S(2)}) %collective-permute-start.49) | collective-permute-done | bytes 524320 | tf_op jit(solution)/shard_map/ppermute | solution.py:403
  397.5 8.6 collective-permute-done.48
  418.7 4.0 fusion.173
  443.9 5.0 convolution_convert_fusion.1
  458.2 12.4 %collective-permute-done.58 = bf16[128,2048]{1,0:T(8,128)(2,1)S(1)} collective-permute-done((bf16[128,2048]{1,0:T(8,128)(2,1)}, bf16[128,2048]{1,0:T(8,128)(2,1)S(1)}, u32[]{:S(2)}, u32[]{:S(2)}) %collective-permute-start.58) | collective-permute-done | bytes 524320 | tf_op jit(solution)/shard_map/ppermute | solution.py:403
  470.6 10.2 %collective-permute-done.57 = bf16[128,2048]{1,0:T(8,128)(2,1)} collective-permute-done((bf16[128,2048]{1,0:T(8,128)(2,1)}, bf16[128,2048]{1,0:T(8,128)(2,1)}, u32[]{:S(2)}, u32[]{:S(2)}) %collective-permute-start.57) | collective-permute-done | bytes 524320 | tf_op jit(solution)/shard_map/ppermute | solution.py:403
  488.8 20.6 %collective-permute-done.64 = bf16[1,256,1024]{2,1,0:T(8,128)(2,1)S(1)} collective-permute-done((bf16[1,256,1024]{2,1,0:T(8,128)(2,1)S(1)}, bf16[1,256,1024]{2,1,0:T(8,128)(2,1)S(1)}, u32[]{:S(2)}, u32[]{:S(2)}) %collective-permute-start.64) | collective-permute-done | bytes 524320 | tf_op jit(solution)/shard_map/ppermute | solution.py:38
  512.3 9.1 collective-permute-done.61
  523.6 5.4 fusion.28
  540.3 5.1 convolution_convert_fusion
  552.7 7.8 fusion.7
  560.5 4.4 collective-permute-done.70
  565.0 9.8 %collective-permute-done.69 = bf16[128,2048]{1,0:T(8,128)(2,1)S(1)} collective-permute-done((bf16[128,2048]{1,0:T(8,128)(2,1)S(1)}, bf16[128,2048]{1,0:T(8,128)(2,1)S(1)}, u32[]{:S(2)}, u32[]{:S(2)}) %collective-permute-start.69) | collective-permute-done | bytes 524320 | tf_op jit(solution)/shard_map/ppermute | solution.py:403
  584.0 20.3 %collective-permute-done.74 = bf16[128,2048]{1,0:T(8,128)(2,1)S(1)} collective-permute-done((bf16[128,2048]{1,0:T(8,128)(2,1)S(1)}, bf16[128,2048]{1,0:T(8,128)(2,1)S(1)}, u32[]{:S(2)}, u32[]{:S(2)}) %collective-permute-start.74) | collective-permute-done | bytes 524320 | tf_op jit(solution)/shard_map/ppermute | solution.py:403
  604.4 10.0 %collective-permute-done.73 = bf16[128,2048]{1,0:T(8,128)(2,1)S(1)} collective-permute-done((bf16[128,2048]{1,0:T(8,128)(2,1)S(1)}, bf16[128,2048]{1,0:T(8,128)(2,1)S(1)}, u32[]{:S(2)}, u32[]{:S(2)}) %collective-permute-start.73) | collective-permute-done | bytes 524320 | tf_op jit(solution)/shard_map/ppermute | solution.py:403
  628.7 10.9 %shard_map.500 = (f32[2,128,1024]{2,1,0:T(8,128)S(1)}, bf16[1024,512]{1,0:T(8,128)(2,1)S(1)}) custom-call(s32[1,1024]{1,0:T(1,128)S(1)} %bitcast.435, s32[1024,1]{1,0:T(8,128)S(1)} %add_select_fusion.refs_1_, bf16[1024,768]{1,0:T(8,128)(2,1)} %copy-done, bf16[1024,512]{1,0:T(8,128)(2,1)} %collective-permute-done.25.refs_3_.refs_4_, ...), custom_call_target="tpu_custom_call" | custom-call | flops 2684354560 | bytes 5242880 | tf_op jit(solution)/shard_map/pallas_call | solution.py:176
  639.6 7.4 collective-permute-done.79
  656.7 12.3 %shard_map.501 = (bf16[1024,256]{1,0:T(8,128)(2,1)S(1)}, f32[1024,512]{1,0:T(8,128)}) custom-call(s32[1,1024]{1,0:T(1,128)S(1)} %bitcast.436, s32[1024,1]{1,0:T(8,128)S(1)} %copy-done.6, bf16[1024,768]{1,0:T(8,128)(2,1)S(1)} %copy-done.1, bf16[1024,768]{1,0:T(8,128)(2,1)S(1)} %copy-done.1, bf16[1024,768]{1,0:T(8,128)(2,1)S(1)} %copy-done.1, ...), custom_call_target="tpu_custom_call" | custom-call | flops 2684354560 | bytes 5242880 | tf_op jit(solution)/shard_map/pallas_call | solution.py:176
  669.0 7.1 collective-permute-done.82
  680.5 3.8 collective-permute-done.81
  700.2 5.3 convolution_convert_fusion.2
  715.6 6.7 collective-permute-done.89
  722.3 10.9 %collective-permute-done.87 = bf16[128,2048]{1,0:T(8,128)(2,1)} collective-permute-done((bf16[128,2048]{1,0:T(8,128)(2,1)}, bf16[128,2048]{1,0:T(8,128)(2,1)}, u32[]{:S(2)}, u32[]{:S(2)}) %collective-permute-start.87) | collective-permute-done | bytes 524320 | tf_op jit(solution)/shard_map/ppermute | solution.py:403
  733.2 9.6 collective-permute-done.86
  761.6 19.1 %collective-permute-done.94 = bf16[1,2,256,256]{2,3,1,0:T(8,128)(2,1)S(1)} collective-permute-done((bf16[1,2,256,256]{2,3,1,0:T(8,128)(2,1)S(1)}, bf16[1,2,256,256]{2,3,1,0:T(8,128)(2,1)S(1)}, u32[]{:S(2)}, u32[]{:S(2)}) %collective-permute-start.94) | collective-permute-done | bytes 262176 | tf_op jit(solution)/shard_map/ppermute | solution.py:38
  795.1 23.3 %collective-permute-done.97 = bf16[1,512,256]{2,1,0:T(8,128)(2,1)S(1)} collective-permute-done((bf16[1,512,256]{2,1,0:T(8,128)(2,1)S(1)}, bf16[1,512,256]{2,1,0:T(8,128)(2,1)S(1)}, u32[]{:S(2)}, u32[]{:S(2)}) %collective-permute-start.97) | collective-permute-done | bytes 262176 | tf_op jit(solution)/shard_map/ppermute | solution.py:38
  818.3 6.1 collective-permute-done.98
  826.1 12.3 %collective-permute-done.100 = bf16[1,256,256]{1,2,0:T(8,128)(2,1)S(1)} collective-permute-done((bf16[1,256,256]{1,2,0:T(8,128)(2,1)S(1)}, bf16[1,256,256]{1,2,0:T(8,128)(2,1)S(1)}, u32[]{:S(2)}, u32[]{:S(2)}) %collective-permute-start.100) | collective-permute-done | bytes 131104 | tf_op jit(solution)/shard_map/ppermute | solution.py:38
  845.8 7.8 collective-permute-done.107
  855.4 13.9 %collective-permute-done.103 = bf16[2,512,256]{2,1,0:T(8,128)(2,1)} collective-permute-done((bf16[2,512,256]{2,1,0:T(8,128)(2,1)}, bf16[2,512,256]{2,1,0:T(8,128)(2,1)}, u32[]{:S(2)}, u32[]{:S(2)}) %collective-permute-start.103) | collective-permute-done | bytes 524320 | tf_op jit(solution)/shard_map/ppermute | solution.py:38
  878.3 19.2 %collective-permute-done.108.refs_2_ = bf16[4,512,256]{2,1,0:T(8,128)(2,1)S(1)} collective-permute-done((bf16[4,512,256]{2,1,0:T(8,128)(2,1)S(1)}, bf16[4,512,256]{2,1,0:T(8,128)(2,1)S(1)}, u32[]{:S(2)}, u32[]{:S(2)}) %collective-permute-start.108) | collective-permute-done | bytes 1048608 | tf_op jit(solution)/shard_map/ppermute | solution.py:38
  901.9 9.0 shard_map.502
  925.5 10.9 %all_to_all.5 = f32[32,2,128]{2,1,0:T(2,128)S(1)} all-to-all(f32[32,2,128]{2,1,0:T(2,128)S(1)} %broadcast_in_dim.41), channel_id=1, replica_groups=mesh['blk'=8,'head'=4] {'blk','head'}, dimensions={0} | all-to-all | bytes 65536 | tf_op jit(solution)/shard_map/all_to_all | solution.py:895
  943.5 4.6 multiply_subtract_fusion.4
  949.2 3.9 multiply_subtract_fusion.1
  954.9 4.1 multiply_subtract_fusion
  959.9 3.8 multiply_subtract_fusion.2
  965.6 4.0 multiply_subtract_fusion.3
  (780 shorter events, 342.6 us)
Async XLA Ops:
  34.4 46.3 %collective-permute-start.6 = (bf16[2,2,512,256]{3,2,0,1:T(8,128)(2,1)S(1)}, bf16[2,2,512,256]{3,2,0,1:T(8,128)(2,1)S(1)}, u32[]{:S(2)}, u32[]{:S(2)}) collective-permute-start(bf16[2,2,512,256]{3,2,0,1:T(8,128)(2,1)S(1)} %slice_bitcast_fusion), channel_id=1, source_target_pairs={{0,8},{4,12},{8,0},{12,4},{16,24},{20,28},{24,16},{28,20},{1,9},{5... | collective-permute-start | bytes 3145736 | tf_op jit(solution)/shard_map/ppermute | solution.py:38
  34.8 61.3 %collective-permute-start.8 = (bf16[2,256,1024]{2,1,0:T(8,128)(2,1)S(1)}, bf16[2,256,1024]{2,1,0:T(8,128)(2,1)}, u32[]{:S(2)}, u32[]{:S(2)}) collective-permute-start(bf16[2,256,1024]{2,1,0:T(8,128)(2,1)S(1)} %maximum_select_fusion.refs_1_), channel_id=1, source_target_pairs={{0,16},{4,20},{8,24},{12,28},{16,0},{20,4},{24,8},{28,12},{1,17},{... | collective-permute-start | bytes 3145736 | tf_op jit(solution)/shard_map/ppermute | solution.py:38
  58.3 35.3 %collective-permute-start.5 = (bf16[2,512,256]{2,1,0:T(8,128)(2,1)}, bf16[2,512,256]{2,1,0:T(8,128)(2,1)}, u32[]{:S(2)}, u32[]{:S(2)}) collective-permute-start(bf16[2,512,256]{2,1,0:T(8,128)(2,1)} %slice_bitcast_fusion.12), channel_id=1, source_target_pairs={{0,8},{4,12},{8,0},{12,4},{16,24},{20,28},{24,16},{28,20},{1,9},{5... | collective-permute-start | bytes 1572872 | tf_op jit(solution)/shard_map/ppermute | solution.py:38
  97.8 27.8 %collective-permute-start.12 = (bf16[2,256,1024]{2,1,0:T(8,128)(2,1)S(1)}, bf16[2,256,1024]{2,1,0:T(8,128)(2,1)}, u32[]{:S(2)}, u32[]{:S(2)}) collective-permute-start(bf16[2,256,1024]{2,1,0:T(8,128)(2,1)S(1)} %maximum_select_fusion.refs_1_), channel_id=1, source_target_pairs={{0,4},{4,0},{8,12},{12,8},{16,20},{20,16},{24,28},{28,24},{1,5},{5... | collective-permute-start | bytes 3145736 | tf_op jit(solution)/shard_map/ppermute | solution.py:38
  125.7 36.2 %collective-permute-start.17 = (bf16[2,256,1024]{2,1,0:T(8,128)(2,1)}, bf16[2,256,1024]{2,1,0:T(8,128)(2,1)S(1)}, u32[]{:S(2)}, u32[]{:S(2)}) collective-permute-start(bf16[2,256,1024]{2,1,0:T(8,128)(2,1)} %collective-permute-done.8.refs_2_), channel_id=1, source_target_pairs={{0,4},{4,0},{8,12},{12,8},{16,20},{20,16},{24,28},{28,24},{1,5},{5... | collective-permute-start | bytes 3145736 | tf_op jit(solution)/shard_map/ppermute | solution.py:38
  127.0 26.6 %collective-permute-start.15 = (bf16[512,512]{1,0:T(8,128)(2,1)S(1)}, bf16[512,512]{1,0:T(8,128)(2,1)S(1)}, u32[]{:S(2)}, u32[]{:S(2)}) collective-permute-start(bf16[512,512]{1,0:T(8,128)(2,1)S(1)} %pad_maximum_fusion.14.refs_2_), channel_id=1, source_target_pairs={{0,10},{1,11},{2,8},{3,9},{4,14},{5,15},{6,12},{7,13},{8,2},{9,3},... | collective-permute-start | bytes 1572872 | tf_op jit(solution)/shard_map/ppermute | solution.py:403
  128.2 33.7 %collective-permute-start.14 = (bf16[512,512]{1,0:T(8,128)(2,1)S(1)}, bf16[512,512]{1,0:T(8,128)(2,1)S(1)}, u32[]{:S(2)}, u32[]{:S(2)}) collective-permute-start(bf16[512,512]{1,0:T(8,128)(2,1)S(1)} %pad_maximum_fusion.14.refs_2_), channel_id=1, source_target_pairs={{0,8},{1,9},{2,10},{3,11},{4,12},{5,13},{6,14},{7,15},{8,0},{9,1},... | collective-permute-start | bytes 1572872 | tf_op jit(solution)/shard_map/ppermute | solution.py:403
  130.0 31.9 %collective-permute-start.13 = (bf16[512,512]{1,0:T(8,128)(2,1)S(1)}, bf16[512,512]{1,0:T(8,128)(2,1)S(1)}, u32[]{:S(2)}, u32[]{:S(2)}) collective-permute-start(bf16[512,512]{1,0:T(8,128)(2,1)S(1)} %pad_maximum_fusion.14.refs_2_), channel_id=1, source_target_pairs={{0,2},{1,3},{2,0},{3,1},{4,6},{5,7},{6,4},{7,5},{8,10},{9,11},{10,... | collective-permute-start | bytes 1572872 | tf_op jit(solution)/shard_map/ppermute | solution.py:403
  166.4 32.3 %collective-permute-start.22 = (bf16[2,256,1024]{2,1,0:T(8,128)(2,1)S(1)}, bf16[2,256,1024]{2,1,0:T(8,128)(2,1)}, u32[]{:S(2)}, u32[]{:S(2)}) collective-permute-start(bf16[2,256,1024]{2,1,0:T(8,128)(2,1)S(1)} %maximum_select_fusion.1.refs_1_), channel_id=1, source_target_pairs={{0,4},{4,0},{8,12},{12,8},{16,20},{20,16},{24,28},{28,24},{1,5},{5... | collective-permute-start | bytes 3145736 | tf_op jit(solution)/shard_map/ppermute | solution.py:38
  172.7 26.0 %collective-permute-start.23 = (bf16[256,1024]{1,0:T(8,128)(2,1)S(1)}, bf16[256,1024]{1,0:T(8,128)(2,1)}, u32[]{:S(2)}, u32[]{:S(2)}) collective-permute-start(bf16[256,1024]{1,0:T(8,128)(2,1)S(1)} %slice_bitcast_fusion.30), channel_id=1, source_target_pairs={{0,16},{4,20},{8,24},{12,28},{16,0},{20,4},{24,8},{28,12},{1,17},{... | collective-permute-start | bytes 1572872 | tf_op jit(solution)/shard_map/ppermute | solution.py:38
  199.8 30.3 %collective-permute-start.25 = (bf16[1024,512]{1,0:T(8,128)(2,1)}, bf16[1024,512]{1,0:T(8,128)(2,1)}, u32[]{:S(2)}, u32[]{:S(2)}) collective-permute-start(bf16[1024,512]{1,0:T(8,128)(2,1)} %slice.371), channel_id=1, source_target_pairs={{0,4},{8,12},{16,20},{24,28},{1,5},{9,13},{17,21},{25,29},{2,6},{1... | collective-permute-start | bytes 3145736 | tf_op jit(solution)/shard_map/ppermute | solution.py:584
  240.0 25.6 %collective-permute-start.33 = (bf16[256,1024]{1,0:T(8,128)(2,1)S(1)}, bf16[256,1024]{1,0:T(8,128)(2,1)S(1)}, u32[]{:S(2)}, u32[]{:S(2)}) collective-permute-start(bf16[256,1024]{1,0:T(8,128)(2,1)S(1)} %slice_bitcast_fusion.25), channel_id=1, source_target_pairs={{0,16},{4,20},{8,24},{12,28},{16,0},{20,4},{24,8},{28,12},{1,17},{... | collective-permute-start | bytes 1572872 | tf_op jit(solution)/shard_map/ppermute | solution.py:38
  240.1 25.5 %collective-permute-start.32 = (bf16[2,256,1024]{2,1,0:T(8,128)(2,1)S(1)}, bf16[2,256,1024]{2,1,0:T(8,128)(2,1)S(1)}, u32[]{:S(2)}, u32[]{:S(2)}) collective-permute-start(bf16[2,256,1024]{2,1,0:T(8,128)(2,1)S(1)} %pad_maximum_fusion.9.refs_2_), channel_id=1, source_target_pairs={{0,4},{4,0},{8,12},{12,8},{16,20},{20,16},{24,28},{28,24},{1,5},{5... | collective-permute-start | bytes 3145736 | tf_op jit(solution)/shard_map/ppermute | solution.py:38
  244.4 34.7 %collective-permute-start.31 = (bf16[128,2048]{1,0:T(8,128)(2,1)S(1)}, bf16[128,2048]{1,0:T(8,128)(2,1)S(1)}, u32[]{:S(2)}, u32[]{:S(2)}) collective-permute-start(bf16[128,2048]{1,0:T(8,128)(2,1)S(1)} %get-tuple-element.427), channel_id=1, source_target_pairs={{0,10},{1,11},{2,8},{3,9},{4,14},{5,15},{6,12},{7,13},{8,2},{9,3},... | collective-permute-start | bytes 1572872 | tf_op jit(solution)/shard_map/ppermute | solution.py:403
  244.5 48.0 %collective-permute-start.30 = (bf16[128,2048]{1,0:T(8,128)(2,1)S(1)}, bf16[128,2048]{1,0:T(8,128)(2,1)S(1)}, u32[]{:S(2)}, u32[]{:S(2)}) collective-permute-start(bf16[128,2048]{1,0:T(8,128)(2,1)S(1)} %get-tuple-element.428), channel_id=1, source_target_pairs={{0,8},{1,9},{2,10},{3,11},{4,12},{5,13},{6,14},{7,15},{8,0},{9,1},... | collective-permute-start | bytes 1572872 | tf_op jit(solution)/shard_map/ppermute | solution.py:403
  247.0 45.6 %collective-permute-start.29 = (bf16[128,2048]{1,0:T(8,128)(2,1)S(1)}, bf16[128,2048]{1,0:T(8,128)(2,1)S(1)}, u32[]{:S(2)}, u32[]{:S(2)}) collective-permute-start(bf16[128,2048]{1,0:T(8,128)(2,1)S(1)} %get-tuple-element.429), channel_id=1, source_target_pairs={{0,2},{1,3},{2,0},{3,1},{4,6},{5,7},{6,4},{7,5},{8,10},{9,11},{10,... | collective-permute-start | bytes 1572872 | tf_op jit(solution)/shard_map/ppermute | solution.py:403
  265.5 31.0 %collective-permute-start.37 = (bf16[256,1024]{1,0:T(8,128)(2,1)S(1)}, bf16[256,1024]{1,0:T(8,128)(2,1)S(1)}, u32[]{:S(2)}, u32[]{:S(2)}) collective-permute-start(bf16[256,1024]{1,0:T(8,128)(2,1)S(1)} %slice_bitcast_fusion.24), channel_id=1, source_target_pairs={{0,16},{4,20},{8,24},{12,28},{16,0},{20,4},{24,8},{28,12},{1,17},{... | collective-permute-start | bytes 1572872 | tf_op jit(solution)/shard_map/ppermute | solution.py:38
  265.5 34.5 %collective-permute-start.39 = (bf16[2,256,1024]{2,1,0:T(8,128)(2,1)S(1)}, bf16[2,256,1024]{2,1,0:T(8,128)(2,1)S(1)}, u32[]{:S(2)}, u32[]{:S(2)}) collective-permute-start(bf16[2,256,1024]{2,1,0:T(8,128)(2,1)S(1)} %copy-done.4), channel_id=1, source_target_pairs={{0,4},{4,0},{8,12},{12,8},{16,20},{20,16},{24,28},{28,24},{1,5},{5... | collective-permute-start | bytes 3145736 | tf_op jit(solution)/shard_map/ppermute | solution.py:38
  292.6 26.7 %collective-permute-start.38 = (bf16[2,256,1024]{2,1,0:T(8,128)(2,1)S(1)}, bf16[2,256,1024]{2,1,0:T(8,128)(2,1)S(1)}, u32[]{:S(2)}, u32[]{:S(2)}) collective-permute-start(bf16[2,256,1024]{2,1,0:T(8,128)(2,1)S(1)} %pad_maximum_fusion.10.refs_2_), channel_id=1, source_target_pairs={{0,4},{4,0},{8,12},{12,8},{16,20},{20,16},{24,28},{28,24},{1,5},{5... | collective-permute-start | bytes 3145736 | tf_op jit(solution)/shard_map/ppermute | solution.py:38
  294.1 24.9 %collective-permute-start.35 = (bf16[128,2048]{1,0:T(8,128)(2,1)S(1)}, bf16[128,2048]{1,0:T(8,128)(2,1)S(1)}, u32[]{:S(2)}, u32[]{:S(2)}) collective-permute-start(bf16[128,2048]{1,0:T(8,128)(2,1)S(1)} %multiply_convert_fusion.3), channel_id=1, source_target_pairs={{0,8},{1,9},{2,10},{3,11},{4,12},{5,13},{6,14},{7,15},{8,0},{9,1},... | collective-permute-start | bytes 1572872 | tf_op jit(solution)/shard_map/ppermute | solution.py:403
  332.1 27.3 %collective-permute-start.45 = (bf16[2,256,1024]{2,1,0:T(8,128)(2,1)S(1)}, bf16[2,256,1024]{2,1,0:T(8,128)(2,1)S(1)}, u32[]{:S(2)}, u32[]{:S(2)}) collective-permute-start(bf16[2,256,1024]{2,1,0:T(8,128)(2,1)S(1)} %maximum_select_fusion.3.refs_1_), channel_id=1, source_target_pairs={{0,4},{4,0},{8,12},{12,8},{16,20},{20,16},{24,28},{28,24},{1,5},{5... | collective-permute-start | bytes 3145736 | tf_op jit(solution)/shard_map/ppermute | solution.py:38
  333.8 25.5 %collective-permute-start.46 = (bf16[256,1024]{1,0:T(8,128)(2,1)S(1)}, bf16[256,1024]{1,0:T(8,128)(2,1)S(1)}, u32[]{:S(2)}, u32[]{:S(2)}) collective-permute-start(bf16[256,1024]{1,0:T(8,128)(2,1)S(1)} %slice_bitcast_fusion.23), channel_id=1, source_target_pairs={{0,16},{4,20},{8,24},{12,28},{16,0},{20,4},{24,8},{28,12},{1,17},{... | collective-permute-start | bytes 1572872 | tf_op jit(solution)/shard_map/ppermute | solution.py:38
  343.1 27.0 %collective-permute-start.44 = (bf16[128,2048]{1,0:T(8,128)(2,1)S(1)}, bf16[128,2048]{1,0:T(8,128)(2,1)S(1)}, u32[]{:S(2)}, u32[]{:S(2)}) collective-permute-start(bf16[128,2048]{1,0:T(8,128)(2,1)S(1)} %get-tuple-element.424), channel_id=1, source_target_pairs={{0,10},{1,11},{2,8},{3,9},{4,14},{5,15},{6,12},{7,13},{8,2},{9,3},... | collective-permute-start | bytes 1572872 | tf_op jit(solution)/shard_map/ppermute | solution.py:403
  345.8 33.7 %collective-permute-start.43 = (bf16[128,2048]{1,0:T(8,128)(2,1)S(1)}, bf16[128,2048]{1,0:T(8,128)(2,1)S(1)}, u32[]{:S(2)}, u32[]{:S(2)}) collective-permute-start(bf16[128,2048]{1,0:T(8,128)(2,1)S(1)} %get-tuple-element.425), channel_id=1, source_target_pairs={{0,8},{1,9},{2,10},{3,11},{4,12},{5,13},{6,14},{7,15},{8,0},{9,1},... | collective-permute-start | bytes 1572872 | tf_op jit(solution)/shard_map/ppermute | solution.py:403
  345.8 33.7 %collective-permute-start.42 = (bf16[128,2048]{1,0:T(8,128)(2,1)S(1)}, bf16[128,2048]{1,0:T(8,128)(2,1)S(1)}, u32[]{:S(2)}, u32[]{:S(2)}) collective-permute-start(bf16[128,2048]{1,0:T(8,128)(2,1)S(1)} %get-tuple-element.426), channel_id=1, source_target_pairs={{0,2},{1,3},{2,0},{3,1},{4,6},{5,7},{6,4},{7,5},{8,10},{9,11},{10,... | collective-permute-start | bytes 1572872 | tf_op jit(solution)/shard_map/ppermute | solution.py:403
  379.6 26.9 %collective-permute-start.50 = (bf16[2,256,1024]{2,1,0:T(8,128)(2,1)S(1)}, bf16[2,256,1024]{2,1,0:T(8,128)(2,1)S(1)}, u32[]{:S(2)}, u32[]{:S(2)}) collective-permute-start(bf16[2,256,1024]{2,1,0:T(8,128)(2,1)S(1)} %pad_maximum_fusion.11.refs_2_), channel_id=1, source_target_pairs={{0,4},{4,0},{8,12},{12,8},{16,20},{20,16},{24,28},{28,24},{1,5},{5... | collective-permute-start | bytes 3145736 | tf_op jit(solution)/shard_map/ppermute | solution.py:38
  451.9 29.3 %collective-permute-start.59 = (bf16[1,2,256,1024]{3,2,1,0:T(8,128)(2,1)}, bf16[1,2,256,1024]{3,2,1,0:T(8,128)(2,1)S(1)}, u32[]{:S(2)}, u32[]{:S(2)}) collective-permute-start(bf16[1,2,256,1024]{3,2,1,0:T(8,128)(2,1)} %dynamic-slice_bitcast_fusion.5), channel_id=1, source_target_pairs={{0,4},{4,0},{8,12},{12,8},{16,20},{20,16},{24,28},{28,24},{1,5},{5... | collective-permute-start | bytes 3145736 | tf_op jit(solution)/shard_map/ppermute | solution.py:38
  455.2 25.6 %collective-permute-start.57 = (bf16[128,2048]{1,0:T(8,128)(2,1)}, bf16[128,2048]{1,0:T(8,128)(2,1)}, u32[]{:S(2)}, u32[]{:S(2)}) collective-permute-start(bf16[128,2048]{1,0:T(8,128)(2,1)} %get-tuple-element.422), channel_id=1, source_target_pairs={{0,8},{1,9},{2,10},{3,11},{4,12},{5,13},{6,14},{7,15},{8,0},{9,1},... | collective-permute-start | bytes 1572872 | tf_op jit(solution)/shard_map/ppermute | solution.py:403
  483.6 25.8 %collective-permute-start.64 = (bf16[1,256,1024]{2,1,0:T(8,128)(2,1)S(1)}, bf16[1,256,1024]{2,1,0:T(8,128)(2,1)S(1)}, u32[]{:S(2)}, u32[]{:S(2)}) collective-permute-start(bf16[1,256,1024]{2,1,0:T(8,128)(2,1)S(1)} %get-tuple-element.438), channel_id=1, source_target_pairs={{0,16},{4,20},{8,24},{12,28},{16,0},{20,4},{24,8},{28,12},{1,17},{... | collective-permute-start | bytes 1572872 | tf_op jit(solution)/shard_map/ppermute | solution.py:38
  484.6 36.8 %collective-permute-start.63 = (bf16[1,2,256,1024]{3,2,1,0:T(8,128)(2,1)S(1)}, bf16[1,2,256,1024]{3,2,1,0:T(8,128)(2,1)S(1)}, u32[]{:S(2)}, u32[]{:S(2)}) collective-permute-start(bf16[1,2,256,1024]{3,2,1,0:T(8,128)(2,1)S(1)} %dynamic-slice_bitcast_fusion.4), channel_id=1, source_target_pairs={{0,4},{4,0},{8,12},{12,8},{16,20},{20,16},{24,28},{28,24},{1,5},{5... | collective-permute-start | bytes 3145736 | tf_op jit(solution)/shard_map/ppermute | solution.py:38
  485.3 27.0 %collective-permute-start.62 = (bf16[128,2048]{1,0:T(8,128)(2,1)S(1)}, bf16[128,2048]{1,0:T(8,128)(2,1)S(1)}, u32[]{:S(2)}, u32[]{:S(2)}) collective-permute-start(bf16[128,2048]{1,0:T(8,128)(2,1)S(1)} %get-tuple-element.394), channel_id=1, source_target_pairs={{0,10},{1,11},{2,8},{3,9},{4,14},{5,15},{6,12},{7,13},{8,2},{9,3},... | collective-permute-start | bytes 1572872 | tf_op jit(solution)/shard_map/ppermute | solution.py:403
  487.4 33.9 %collective-permute-start.61 = (bf16[128,2048]{1,0:T(8,128)(2,1)S(1)}, bf16[128,2048]{1,0:T(8,128)(2,1)S(1)}, u32[]{:S(2)}, u32[]{:S(2)}) collective-permute-start(bf16[128,2048]{1,0:T(8,128)(2,1)S(1)} %get-tuple-element.394), channel_id=1, source_target_pairs={{0,8},{1,9},{2,10},{3,11},{4,12},{5,13},{6,14},{7,15},{8,0},{9,1},... | collective-permute-start | bytes 1572872 | tf_op jit(solution)/shard_map/ppermute | solution.py:403
  487.6 33.7 %collective-permute-start.60 = (bf16[128,2048]{1,0:T(8,128)(2,1)S(1)}, bf16[128,2048]{1,0:T(8,128)(2,1)S(1)}, u32[]{:S(2)}, u32[]{:S(2)}) collective-permute-start(bf16[128,2048]{1,0:T(8,128)(2,1)S(1)} %get-tuple-element.394), channel_id=1, source_target_pairs={{0,2},{1,3},{2,0},{3,1},{4,6},{5,7},{6,4},{7,5},{8,10},{9,11},{10,... | collective-permute-start | bytes 1572872 | tf_op jit(solution)/shard_map/ppermute | solution.py:403
  521.6 25.6 %collective-permute-start.67 = (bf16[1,256,1024]{2,1,0:T(8,128)(2,1)S(1)}, bf16[1,256,1024]{2,1,0:T(8,128)(2,1)S(1)}, u32[]{:S(2)}, u32[]{:S(2)}) collective-permute-start(bf16[1,256,1024]{2,1,0:T(8,128)(2,1)S(1)} %get-tuple-element.272), channel_id=1, source_target_pairs={{0,16},{4,20},{8,24},{12,28},{16,0},{20,4},{24,8},{28,12},{1,17},{... | collective-permute-start | bytes 1572872 | tf_op jit(solution)/shard_map/ppermute | solution.py:38
  547.3 27.7 %collective-permute-start.71 = (bf16[1,2,256,1024]{3,2,1,0:T(8,128)(2,1)S(1)}, bf16[1,2,256,1024]{3,2,1,0:T(8,128)(2,1)S(1)}, u32[]{:S(2)}, u32[]{:S(2)}) collective-permute-start(bf16[1,2,256,1024]{3,2,1,0:T(8,128)(2,1)S(1)} %dynamic-slice_bitcast_fusion.3), channel_id=1, source_target_pairs={{0,4},{4,0},{8,12},{12,8},{16,20},{20,16},{24,28},{28,24},{1,5},{5... | collective-permute-start | bytes 3145736 | tf_op jit(solution)/shard_map/ppermute | solution.py:38
  549.7 25.1 %collective-permute-start.69 = (bf16[128,2048]{1,0:T(8,128)(2,1)S(1)}, bf16[128,2048]{1,0:T(8,128)(2,1)S(1)}, u32[]{:S(2)}, u32[]{:S(2)}) collective-permute-start(bf16[128,2048]{1,0:T(8,128)(2,1)S(1)} %get-tuple-element.419), channel_id=1, source_target_pairs={{0,8},{1,9},{2,10},{3,11},{4,12},{5,13},{6,14},{7,15},{8,0},{9,1},... | collective-permute-start | bytes 1572872 | tf_op jit(solution)/shard_map/ppermute | solution.py:403
  577.4 27.0 %collective-permute-start.74 = (bf16[128,2048]{1,0:T(8,128)(2,1)S(1)}, bf16[128,2048]{1,0:T(8,128)(2,1)S(1)}, u32[]{:S(2)}, u32[]{:S(2)}) collective-permute-start(bf16[128,2048]{1,0:T(8,128)(2,1)S(1)} %get-tuple-element.391), channel_id=1, source_target_pairs={{0,10},{1,11},{2,8},{3,9},{4,14},{5,15},{6,12},{7,13},{8,2},{9,3},... | collective-permute-start | bytes 1572872 | tf_op jit(solution)/shard_map/ppermute | solution.py:403
  578.1 36.3 %collective-permute-start.73 = (bf16[128,2048]{1,0:T(8,128)(2,1)S(1)}, bf16[128,2048]{1,0:T(8,128)(2,1)S(1)}, u32[]{:S(2)}, u32[]{:S(2)}) collective-permute-start(bf16[128,2048]{1,0:T(8,128)(2,1)S(1)} %get-tuple-element.391), channel_id=1, source_target_pairs={{0,8},{1,9},{2,10},{3,11},{4,12},{5,13},{6,14},{7,15},{8,0},{9,1},... | collective-permute-start | bytes 1572872 | tf_op jit(solution)/shard_map/ppermute | solution.py:403
  580.1 34.3 %collective-permute-start.72 = (bf16[128,2048]{1,0:T(8,128)(2,1)S(1)}, bf16[128,2048]{1,0:T(8,128)(2,1)S(1)}, u32[]{:S(2)}, u32[]{:S(2)}) collective-permute-start(bf16[128,2048]{1,0:T(8,128)(2,1)S(1)} %get-tuple-element.391), channel_id=1, source_target_pairs={{0,2},{1,3},{2,0},{3,1},{4,6},{5,7},{6,4},{7,5},{8,10},{9,11},{10,... | collective-permute-start | bytes 1572872 | tf_op jit(solution)/shard_map/ppermute | solution.py:403
  581.0 33.5 %collective-permute-start.75 = (bf16[1,2,256,1024]{3,2,1,0:T(8,128)(2,1)S(1)}, bf16[1,2,256,1024]{3,2,1,0:T(8,128)(2,1)S(1)}, u32[]{:S(2)}, u32[]{:S(2)}) collective-permute-start(bf16[1,2,256,1024]{3,2,1,0:T(8,128)(2,1)S(1)} %dynamic-slice_bitcast_fusion.2), channel_id=1, source_target_pairs={{0,4},{4,0},{8,12},{12,8},{16,20},{20,16},{24,28},{28,24},{1,5},{5... | collective-permute-start | bytes 3145736 | tf_op jit(solution)/shard_map/ppermute | solution.py:38
  582.7 31.7 %collective-permute-start.76 = (bf16[1,256,1024]{2,1,0:T(8,128)(2,1)S(1)}, bf16[1,256,1024]{2,1,0:T(8,128)(2,1)S(1)}, u32[]{:S(2)}, u32[]{:S(2)}) collective-permute-start(bf16[1,256,1024]{2,1,0:T(8,128)(2,1)S(1)} %get-tuple-element.435), channel_id=1, source_target_pairs={{0,16},{4,20},{8,24},{12,28},{16,0},{20,4},{24,8},{28,12},{1,17},{... | collective-permute-start | bytes 1572872 | tf_op jit(solution)/shard_map/ppermute | solution.py:38
  618.0 29.0 %collective-permute-start.78 = (bf16[1,2,256,1024]{3,2,1,0:T(8,128)(2,1)S(1)}, bf16[1,2,256,1024]{3,2,1,0:T(8,128)(2,1)S(1)}, u32[]{:S(2)}, u32[]{:S(2)}) collective-permute-start(bf16[1,2,256,1024]{3,2,1,0:T(8,128)(2,1)S(1)} %dynamic-slice_bitcast_fusion.1), channel_id=1, source_target_pairs={{0,4},{4,0},{8,12},{12,8},{16,20},{20,16},{24,28},{28,24},{1,5},{5... | collective-permute-start | bytes 3145736 | tf_op jit(solution)/shard_map/ppermute | solution.py:38
  621.0 25.9 %collective-permute-start.79 = (bf16[1,256,1024]{2,1,0:T(8,128)(2,1)S(1)}, bf16[1,256,1024]{2,1,0:T(8,128)(2,1)S(1)}, u32[]{:S(2)}, u32[]{:S(2)}) collective-permute-start(bf16[1,256,1024]{2,1,0:T(8,128)(2,1)S(1)} %copy-done.121), channel_id=1, source_target_pairs={{0,16},{4,20},{8,24},{12,28},{16,0},{20,4},{24,8},{28,12},{1,17},{... | collective-permute-start | bytes 1572872 | tf_op jit(solution)/shard_map/ppermute | solution.py:38
  649.9 26.2 %collective-permute-start.82 = (bf16[256,1024]{1,0:T(8,128)(2,1)S(1)}, bf16[256,1024]{1,0:T(8,128)(2,1)}, u32[]{:S(2)}, u32[]{:S(2)}) collective-permute-start(bf16[256,1024]{1,0:T(8,128)(2,1)S(1)} %fusion.87), channel_id=1, source_target_pairs={{0,8},{4,12},{8,0},{12,4},{16,24},{20,28},{24,16},{28,20},{1,9},{5... | collective-permute-start | bytes 1572872 | tf_op jit(solution)/shard_map/ppermute | solution.py:38
  650.0 42.4 %collective-permute-start.84 = (bf16[256,1024]{1,0:T(8,128)(2,1)S(1)}, bf16[256,1024]{1,0:T(8,128)(2,1)}, u32[]{:S(2)}, u32[]{:S(2)}) collective-permute-start(bf16[256,1024]{1,0:T(8,128)(2,1)S(1)} %fusion.88), channel_id=1, source_target_pairs={{0,8},{4,12},{8,0},{12,4},{16,24},{20,28},{24,16},{28,20},{1,9},{5... | collective-permute-start | bytes 1572872 | tf_op jit(solution)/shard_map/ppermute | solution.py:38
  652.0 26.8 %collective-permute-start.80 = (bf16[1024,512]{1,0:T(8,128)(2,1)S(1)}, bf16[1024,512]{1,0:T(8,128)(2,1)}, u32[]{:S(2)}, u32[]{:S(2)}) collective-permute-start(bf16[1024,512]{1,0:T(8,128)(2,1)S(1)} %get-tuple-element.299), channel_id=1, source_target_pairs={{4,0},{12,8},{20,16},{28,24},{5,1},{13,9},{21,17},{29,25},{6,2},{1... | collective-permute-start | bytes 3145736 | tf_op jit(solution)/shard_map/ppermute | solution.py:783
  656.3 27.9 %collective-permute-start.81 = (bf16[1,256,1024]{2,1,0:T(8,128)(2,1)}, bf16[1,256,1024]{2,1,0:T(8,128)(2,1)S(1)}, u32[]{:S(2)}, u32[]{:S(2)}) collective-permute-start(bf16[1,256,1024]{2,1,0:T(8,128)(2,1)} %get-tuple-element.433), channel_id=1, source_target_pairs={{0,16},{4,20},{8,24},{12,28},{16,0},{20,4},{24,8},{28,12},{1,17},{... | collective-permute-start | bytes 1572872 | tf_op jit(solution)/shard_map/ppermute | solution.py:38
  688.5 27.1 %collective-permute-start.88 = (bf16[1,2,256,1024]{3,2,1,0:T(8,128)(2,1)}, bf16[1,2,256,1024]{3,2,1,0:T(8,128)(2,1)}, u32[]{:S(2)}, u32[]{:S(2)}) collective-permute-start(bf16[1,2,256,1024]{3,2,1,0:T(8,128)(2,1)} %dynamic-slice_bitcast_fusion), channel_id=1, source_target_pairs={{0,4},{4,0},{8,12},{12,8},{16,20},{20,16},{24,28},{28,24},{1,5},{5... | collective-permute-start | bytes 3145736 | tf_op jit(solution)/shard_map/ppermute | solution.py:38
  695.1 27.2 %collective-permute-start.89 = (bf16[1,256,1024]{2,1,0:T(8,128)(2,1)}, bf16[1,256,1024]{2,1,0:T(8,128)(2,1)}, u32[]{:S(2)}, u32[]{:S(2)}) collective-permute-start(bf16[1,256,1024]{2,1,0:T(8,128)(2,1)} %get-tuple-element.310), channel_id=1, source_target_pairs={{0,16},{4,20},{8,24},{12,28},{16,0},{20,4},{24,8},{28,12},{1,17},{... | collective-permute-start | bytes 1572872 | tf_op jit(solution)/shard_map/ppermute | solution.py:38
  707.5 25.6 %collective-permute-start.87 = (bf16[128,2048]{1,0:T(8,128)(2,1)}, bf16[128,2048]{1,0:T(8,128)(2,1)}, u32[]{:S(2)}, u32[]{:S(2)}) collective-permute-start(bf16[128,2048]{1,0:T(8,128)(2,1)} %get-tuple-element.415), channel_id=1, source_target_pairs={{0,10},{1,11},{2,8},{3,9},{4,14},{5,15},{6,12},{7,13},{8,2},{9,3},... | collective-permute-start | bytes 1572872 | tf_op jit(solution)/shard_map/ppermute | solution.py:403
  707.5 35.3 %collective-permute-start.86 = (bf16[128,2048]{1,0:T(8,128)(2,1)}, bf16[128,2048]{1,0:T(8,128)(2,1)}, u32[]{:S(2)}, u32[]{:S(2)}) collective-permute-start(bf16[128,2048]{1,0:T(8,128)(2,1)} %get-tuple-element.416), channel_id=1, source_target_pairs={{0,8},{1,9},{2,10},{3,11},{4,12},{5,13},{6,14},{7,15},{8,0},{9,1},... | collective-permute-start | bytes 1572872 | tf_op jit(solution)/shard_map/ppermute | solution.py:403
  709.8 33.0 %collective-permute-start.85 = (bf16[128,2048]{1,0:T(8,128)(2,1)}, bf16[128,2048]{1,0:T(8,128)(2,1)}, u32[]{:S(2)}, u32[]{:S(2)}) collective-permute-start(bf16[128,2048]{1,0:T(8,128)(2,1)} %get-tuple-element.417), channel_id=1, source_target_pairs={{0,2},{1,3},{2,0},{3,1},{4,6},{5,7},{6,4},{7,5},{8,10},{9,11},{10,... | collective-permute-start | bytes 1572872 | tf_op jit(solution)/shard_map/ppermute | solution.py:403
  755.5 25.3 %collective-permute-start.93 = (bf16[1,2,256,768]{3,2,1,0:T(8,128)(2,1)S(1)}, bf16[1,2,256,768]{3,2,1,0:T(8,128)(2,1)S(1)}, u32[]{:S(2)}, u32[]{:S(2)}) collective-permute-start(bf16[1,2,256,768]{3,2,1,0:T(8,128)(2,1)S(1)} %dynamic-slice_bitcast_fusion.7), channel_id=1, source_target_pairs={{0,4},{4,0},{8,12},{12,8},{16,20},{20,16},{24,28},{28,24},{1,5},{5... | collective-permute-start | bytes 2359304 | tf_op jit(solution)/shard_map/ppermute | solution.py:38
  787.2 51.2 %collective-permute-start.102 = (bf16[1,2,256,256]{2,3,1,0:T(8,128)(2,1)}, bf16[1,2,256,256]{2,3,1,0:T(8,128)(2,1)S(1)}, u32[]{:S(2)}, u32[]{:S(2)}) collective-permute-start(bf16[1,2,256,256]{2,3,1,0:T(8,128)(2,1)} %bitcast.177), channel_id=1, source_target_pairs={{0,4},{4,0},{8,12},{12,8},{16,20},{20,16},{24,28},{28,24},{1,5},{5... | collective-permute-start | bytes 786440 | tf_op jit(solution)/shard_map/ppermute | solution.py:38
  789.6 48.9 %collective-permute-start.101 = (bf16[1,2,256,768]{3,2,1,0:T(8,128)(2,1)S(1)}, bf16[1,2,256,768]{3,2,1,0:T(8,128)(2,1)}, u32[]{:S(2)}, u32[]{:S(2)}) collective-permute-start(bf16[1,2,256,768]{3,2,1,0:T(8,128)(2,1)S(1)} %dynamic-slice_bitcast_fusion.6), channel_id=1, source_target_pairs={{0,4},{4,0},{8,12},{12,8},{16,20},{20,16},{24,28},{28,24},{1,5},{5... | collective-permute-start | bytes 2359304 | tf_op jit(solution)/shard_map/ppermute | solution.py:38
  791.3 27.1 %collective-permute-start.97 = (bf16[1,512,256]{2,1,0:T(8,128)(2,1)S(1)}, bf16[1,512,256]{2,1,0:T(8,128)(2,1)S(1)}, u32[]{:S(2)}, u32[]{:S(2)}) collective-permute-start(bf16[1,512,256]{2,1,0:T(8,128)(2,1)S(1)} %get-tuple-element.320), channel_id=1, source_target_pairs={{0,16},{4,20},{8,24},{12,28},{16,0},{20,4},{24,8},{28,12},{1,17},{... | collective-permute-start | bytes 786440 | tf_op jit(solution)/shard_map/ppermute | solution.py:38
  791.3 33.1 %collective-permute-start.98 = (bf16[1,544,256]{2,1,0:T(8,128)(2,1)S(1)}, bf16[1,544,256]{2,1,0:T(8,128)(2,1)S(1)}, u32[]{:S(2)}, u32[]{:S(2)}) collective-permute-start(bf16[1,544,256]{2,1,0:T(8,128)(2,1)S(1)} %fusion.98), channel_id=1, source_target_pairs={{0,16},{4,20},{8,24},{12,28},{16,0},{20,4},{24,8},{28,12},{1,17},{... | collective-permute-start | bytes 835592 | tf_op jit(solution)/shard_map/ppermute | solution.py:38
  794.3 44.2 %collective-permute-start.99 = (bf16[1,256,768]{2,1,0:T(8,128)(2,1)S(1)}, bf16[1,256,768]{2,1,0:T(8,128)(2,1)S(1)}, u32[]{:S(2)}, u32[]{:S(2)}) collective-permute-start(bf16[1,256,768]{2,1,0:T(8,128)(2,1)S(1)} %get-tuple-element.454), channel_id=1, source_target_pairs={{0,16},{4,20},{8,24},{12,28},{16,0},{20,4},{24,8},{28,12},{1,17},{... | collective-permute-start | bytes 1179656 | tf_op jit(solution)/shard_map/ppermute | solution.py:38
  818.3 35.3 %collective-permute-start.107 = (bf16[256,1024]{1,0:T(8,128)(2,1)}, bf16[256,1024]{1,0:T(8,128)(2,1)}, u32[]{:S(2)}, u32[]{:S(2)}) collective-permute-start(bf16[256,1024]{1,0:T(8,128)(2,1)} %fusion.89), channel_id=1, source_target_pairs={{0,8},{4,12},{8,0},{12,4},{16,24},{20,28},{24,16},{28,20},{1,9},{5... | collective-permute-start | bytes 1572872 | tf_op jit(solution)/shard_map/ppermute | solution.py:38
  839.2 30.1 %collective-permute-start.103 = (bf16[2,512,256]{2,1,0:T(8,128)(2,1)}, bf16[2,512,256]{2,1,0:T(8,128)(2,1)}, u32[]{:S(2)}, u32[]{:S(2)}) collective-permute-start(bf16[2,512,256]{2,1,0:T(8,128)(2,1)} %pad_maximum_fusion.15), channel_id=1, source_target_pairs={{0,8},{4,12},{8,0},{12,4},{16,24},{20,28},{24,16},{28,20},{1,9},{5... | collective-permute-start | bytes 1572872 | tf_op jit(solution)/shard_map/ppermute | solution.py:38
  839.2 31.4 %collective-permute-start.104 = (bf16[2,544,256]{2,1,0:T(8,128)(2,1)}, bf16[2,544,256]{2,1,0:T(8,128)(2,1)}, u32[]{:S(2)}, u32[]{:S(2)}) collective-permute-start(bf16[2,544,256]{2,1,0:T(8,128)(2,1)} %pad_maximum_fusion.13), channel_id=1, source_target_pairs={{0,4},{4,0},{8,12},{12,8},{16,20},{20,16},{24,28},{28,24},{1,5},{5... | collective-permute-start | bytes 1671176 | tf_op jit(solution)/shard_map/ppermute | solution.py:38
  843.0 29.3 %collective-permute-start.105 = (bf16[1,256,768]{2,1,0:T(8,128)(2,1)}, bf16[1,256,768]{2,1,0:T(8,128)(2,1)S(1)}, u32[]{:S(2)}, u32[]{:S(2)}) collective-permute-start(bf16[1,256,768]{2,1,0:T(8,128)(2,1)} %get-tuple-element.328), channel_id=1, source_target_pairs={{0,16},{4,20},{8,24},{12,28},{16,0},{20,4},{24,8},{28,12},{1,17},{... | collective-permute-start | bytes 1179656 | tf_op jit(solution)/shard_map/ppermute | solution.py:38
  872.3 25.1 %collective-permute-start.108 = (bf16[4,512,256]{2,1,0:T(8,128)(2,1)S(1)}, bf16[4,512,256]{2,1,0:T(8,128)(2,1)S(1)}, u32[]{:S(2)}, u32[]{:S(2)}) collective-permute-start(bf16[4,512,256]{2,1,0:T(8,128)(2,1)S(1)} %pad_maximum_fusion.12.refs_1_), channel_id=1, source_target_pairs={{0,4},{4,0},{8,12},{12,8},{16,20},{20,16},{24,28},{28,24},{1,5},{5... | collective-permute-start | bytes 3145736 | tf_op jit(solution)/shard_map/ppermute | solution.py:38
  872.4 26.5 %collective-permute-start.109 = (bf16[4,544,256]{2,1,0:T(8,128)(2,1)S(1)}, bf16[4,544,256]{2,1,0:T(8,128)(2,1)S(1)}, u32[]{:S(2)}, u32[]{:S(2)}) collective-permute-start(bf16[4,544,256]{2,1,0:T(8,128)(2,1)S(1)} %pad_maximum_fusion.7.refs_3_), channel_id=1, source_target_pairs={{0,8},{4,12},{8,0},{12,4},{16,24},{20,28},{24,16},{28,20},{1,9},{5... | collective-permute-start | bytes 3342344 | tf_op jit(solution)/shard_map/ppermute | solution.py:38
  (204 other events, 2122.5 us)
